TPU v7x, 32 devices: a whole 2x2x4 slice. The times are simulated.
32 devices in a mesh: batch: 4 (over y, core), rows: 8 (over z, x).
Axes of the slice: x: 2, y: 2, z: 4, core: 2. Of those that a mesh axis runs over, the one named last changes fastest.
Arguments:
- params: float32 [8527872], P(('batch', 'rows')), as said below
- moment1: float32 [8527872], P(('batch', 'rows')), as said below
- moment2: float32 [8527872], P(('batch', 'rows')), as said below
- images: float32 [32, 3, 64, 64], P('batch', None, 'rows'), may hold values from -1 to 1
- noise: float32 [32, 3, 64, 64], P('batch', None, 'rows'), may hold values from -6 to 6
- timesteps: int32 [32], P('batch'), may hold values from 2 to 2999
- masks: int32 [32, 64, 64], P('batch', 'rows'), may hold values from 0 to 1, as said below
- weight_index: int32 [32], P('batch'), may hold values from 0 to 3
Outputs:
- params_new: float32 [8527872], P(('batch', 'rows'))
- moment1_new: float32 [8527872], P(('batch', 'rows'))
- moment2_new: float32 [8527872], P(('batch', 'rows'))
- params_low: bfloat16 [8527872], P(('batch', 'rows'))
- loss_sum: float32 [], replicated
- loss_vlb: float32 [], replicated
- count: float32 [], replicated
- grad_norm: float32 [], replicated
Inputs may be any that keep to these rules, and one draw needn't show every extreme that they name: `masks`: 1 marks a valid pixel. `params`: parameters at the usual initial scales. `moment1`: both signs. `moment2`: positive.
All inputs are finite; a program needn't handle non-finite values.
Results may differ from a plain program's by a relative error of at most 0.0019.
The roundings to bfloat16 on the way count: a program that leaves them out, or rounds other values in their place, can miss the bound.
Values may be sent and summed in bfloat16 or wider, within the bound.
No kernel may reach another device: no remote copies, remote signals or barrier semaphores. Data moves between devices by JAX's collectives and lax.ppermute only.
A program may use at most 384 MiB of HBM per device.

v0:
```python
import math

import jax
import jax.numpy as jnp
from jax import lax
from jax.sharding import PartitionSpec as P

IN_CH = 3
C0 = 192
CH = 384
TEMB = 768
HEADS = 4
HEAD_DIM = 96
GROUPS = 32
OUT_CH = 6
DIFF_STEPS = 4000
BLOCKS = 2
MB = 4
STEP = 10


cosine_offset = 0.008
kl_weight = 0.001
clip_limit = 0.05
learn_rate = 0.05
decay_first = 0.9
decay_second = 0.999
weight_decay = 0.01
narrow = jnp.bfloat16


def as_sent(value):

    def short(part):
        return part.astype(jnp.bfloat16) if part.dtype == jnp.float32 else part

    return jax.tree.map(short, value)


def with_halo(value, sides, width):
    for axis, dim in sides:
        size, length = (lax.axis_size(axis), value.shape[dim])
        up = [(i, (i + 1) % size) for i in range(size - 1)]
        down = [(j, i) for i, j in up]
        last = lax.slice_in_dim(value, length - width, length, axis=dim)
        leading = lax.slice_in_dim(value, 0, width, axis=dim)
        before = lax.ppermute(last, axis, up)
        after = lax.ppermute(leading, axis, down)
        value = jnp.concatenate([before, value, after], axis=dim)
    return value


def shifted(block, axis, distance):
    devices = range(lax.axis_size(axis))
    route = [(i - distance, i) for i in devices if i - distance in devices]
    return lax.ppermute(block, axis, route)


def segments():
    return [
        ("stem_w", (3, 3, IN_CH, C0)),
        ("stem_b", (C0,)),
        ("time1_w", (C0, TEMB)),
        ("time1_b", (TEMB,)),
        ("time2_w", (TEMB, TEMB)),
        ("time2_b", (TEMB,)),
        ("down_w", (3, 3, C0, CH)),
        ("down_b", (CH,)),
        ("res_w", (BLOCKS, 2, 3, 3, CH, CH)),
        ("res_b", (BLOCKS, 2, CH)),
        ("emb_w", (BLOCKS, TEMB, 2 * CH)),
        ("emb_b", (BLOCKS, 2 * CH)),
        ("res_gain", (BLOCKS, 2, CH)),
        ("res_shift", (BLOCKS, 2, CH)),
        ("attn_gain", (CH,)),
        ("attn_shift", (CH,)),
        ("qkv_w", (CH, 3 * CH)),
        ("qv_b", (2 * CH,)),
        ("proj_w", (CH, CH)),
        ("proj_b", (CH,)),
        ("head_gain", (C0 + CH,)),
        ("head_shift", (C0 + CH,)),
        ("head_w", (3, 3, C0 + CH, OUT_CH)),
        ("head_b", (OUT_CH,)),
    ]


def unpack(flat):
    table = {}
    offset = 0
    for name, shape in segments():
        amount = math.prod(shape)
        table[name] = flat[offset : offset + amount].reshape(shape)
        offset = offset + amount
    return table


def pack(table, length):
    pieces = [table[name].reshape(-1) for name, shape in segments()]
    used = sum((piece.shape[0] for piece in pieces))
    pieces.append(jnp.zeros((length - used,), jnp.float32))
    return jnp.concatenate(pieces)


def plan(steps):
    timef = steps.astype(jnp.float32)
    angle = math.pi / 2.0 / (1.0 + cosine_offset)
    theta = (timef / DIFF_STEPS + cosine_offset) * angle
    before = ((timef - 1.0) / DIFF_STEPS + cosine_offset) * angle
    anchor = cosine_offset * angle
    base = math.cos(anchor) ** 2
    signal = jnp.cos(theta) ** 2 / base
    one_minus = jnp.sin(theta + anchor) * jnp.sin(timef / DIFF_STEPS * angle) / base
    one_prev = jnp.sin(before + anchor) * jnp.sin((timef - 1.0) / DIFF_STEPS * angle) / base
    beta = jnp.sin(theta + before) * math.sin(angle / DIFF_STEPS) / jnp.cos(before) ** 2
    alpha = 1.0 - beta
    tilde = beta * one_prev / one_minus
    return (signal, one_minus, beta, alpha, tilde)


def silu(value):
    return value * jax.nn.sigmoid(value)


def silu_grad(value):
    gate = jax.nn.sigmoid(value)
    return gate * (1.0 + value * (1.0 - gate))


def column_sum(tensor):
    return jnp.sum(tensor.astype(jnp.float32), axis=(0, 1, 2))


def precise(left, right):
    return jnp.dot(left, right, precision=lax.Precision.HIGHEST)


def per_image(value):
    return value[:, None, None, None]


def conv_apply(padded, kernel, stride):
    return lax.conv_general_dilated(
        padded,
        kernel,
        (stride, stride),
        "VALID",
        dimension_numbers=("NHWC", "HWIO", "NHWC"),
        preferred_element_type=jnp.float32,
    )


def widen(tensor):
    return jnp.pad(tensor, ((0, 0), (0, 0), (1, 1), (0, 0)))


def flipped(kernel):
    return jnp.transpose(kernel[::-1, ::-1], (0, 1, 3, 2))


def kernel_grad(padded, grad, stride):
    batch, rows, cols, outs = grad.shape
    parts = []
    for top in range(3):
        for left in range(3):
            window = lax.slice(
                padded,
                (0, top, left, 0),
                (
                    batch,
                    top + stride * (rows - 1) + 1,
                    left + stride * (cols - 1) + 1,
                    padded.shape[3],
                ),
                (1, stride, stride, 1),
            )
            parts.append(
                jnp.einsum("brci,brco->io", window, grad, preferred_element_type=jnp.float32)
            )
    return jnp.stack(parts).reshape(3, 3, padded.shape[3], outs)


def conv_same(inputs, kernel, bias):
    padded = widen(with_halo(as_sent(inputs), (("rows", 1),), 1).astype(inputs.dtype))
    return (conv_apply(padded, kernel, 1) + bias.astype(jnp.float32), padded)


def conv_same_back(padded, kernel, grad):
    grad_padded = widen(with_halo(as_sent(grad), (("rows", 1),), 1).astype(grad.dtype))
    return (conv_apply(grad_padded, flipped(kernel), 1), kernel_grad(padded, grad, 1))


def conv_down(inputs, kernel, bias):
    above = shifted(as_sent(inputs[:, -1:]), "rows", 1)
    padded = widen(jnp.concatenate([above, inputs], axis=1))
    return (conv_apply(padded, kernel, 2) + bias.astype(jnp.float32), padded)


def conv_down_back(padded, kernel, grad):
    spread = lax.conv_general_dilated(
        grad,
        flipped(kernel),
        (1, 1),
        ((2, 2), (2, 3)),
        lhs_dilation=(2, 2),
        dimension_numbers=("NHWC", "HWIO", "NHWC"),
        preferred_element_type=jnp.float32,
    )
    spread = spread[:, :, 1:-1]
    below = shifted(spread[:, :1].astype(jnp.bfloat16), "rows", -1).astype(jnp.float32)
    rows = spread.shape[1] - 1
    inputs_grad = spread[:, 1:] + jnp.pad(below, ((0, 0), (rows - 1, 0), (0, 0), (0, 0)))
    return (inputs_grad, kernel_grad(padded, grad, 2))


def norm_forward(values, gain, shift):
    batch, rows, cols, chans = values.shape
    grouped = values.reshape(batch, rows, cols, GROUPS, chans // GROUPS)
    totals, squares = lax.psum(
        (jnp.sum(grouped, axis=(1, 2, 4)), jnp.sum(grouped * grouped, axis=(1, 2, 4))), "rows"
    )
    amount = rows * lax.axis_size("rows") * cols * (chans // GROUPS)
    mean = totals / amount
    inverse = lax.rsqrt(squares / amount - mean * mean + 1e-05)
    normed = ((grouped - mean[:, None, None, :, None]) * inverse[:, None, None, :, None]).reshape(
        values.shape
    )
    return (normed * gain + shift, (normed, inverse))


def norm_back(grad, kept, gain):
    normed, inverse = kept
    batch, rows, cols, chans = grad.shape
    gain_grad = jnp.sum(grad * normed, axis=(0, 1, 2))
    shift_grad = jnp.sum(grad, axis=(0, 1, 2))
    shape = (batch, rows, cols, GROUPS, chans // GROUPS)
    scaled = (grad * gain).reshape(shape)
    normed = normed.reshape(shape)
    first, second = lax.psum(
        (jnp.sum(scaled, axis=(1, 2, 4)), jnp.sum(scaled * normed, axis=(1, 2, 4))), "rows"
    )
    amount = rows * lax.axis_size("rows") * cols * (chans // GROUPS)
    inputs_grad = (
        scaled
        - first[:, None, None, :, None] / amount
        - normed * second[:, None, None, :, None] / amount
    ) * inverse[:, None, None, :, None]
    return (inputs_grad.reshape(grad.shape), gain_grad, shift_grad)


def time_forward(steps, weights):
    half = C0 // 2
    freqs = jnp.exp(-math.log(10000.0) * jnp.arange(half).astype(jnp.float32) / half)
    angles = steps.astype(jnp.float32)[:, None] * freqs
    sinus = jnp.concatenate([jnp.cos(angles), jnp.sin(angles)], axis=-1).astype(narrow)
    hidden_pre = (
        jnp.dot(sinus, weights["time1_w"], preferred_element_type=jnp.float32) + weights["time1_b"]
    )
    hidden = silu(hidden_pre).astype(narrow)
    outer_pre = (
        jnp.dot(hidden, weights["time2_w"], preferred_element_type=jnp.float32) + weights["time2_b"]
    )
    return (silu(outer_pre).astype(narrow), (sinus, hidden_pre, hidden, outer_pre))


def time_back(embed_grad, weights, kept):
    sinus, hidden_pre, hidden, outer_pre = kept
    outer_grad = embed_grad * silu_grad(outer_pre)
    hidden_grad = precise(outer_grad, weights["time2_w"].astype(jnp.float32).T) * silu_grad(
        hidden_pre
    )
    return {
        "time2_w": precise(hidden.astype(jnp.float32).T, outer_grad),
        "time2_b": jnp.sum(outer_grad, axis=0),
        "time1_w": precise(sinus.astype(jnp.float32).T, hidden_grad),
        "time1_b": jnp.sum(hidden_grad, axis=0),
    }


def block_forward(state, weights, embed, index):
    modulate = (
        jnp.dot(embed, weights["emb_w"][index], preferred_element_type=jnp.float32)
        + weights["emb_b"][index]
    )
    scale = 1.0 + modulate[:, None, None, :CH]
    offset = modulate[:, None, None, CH:]
    normed_one, saved_one = norm_forward(
        state, weights["res_gain"][index, 0], weights["res_shift"][index, 0]
    )
    inner, padded_one = conv_same(
        silu(normed_one).astype(narrow), weights["res_w"][index, 0], weights["res_b"][index, 0]
    )
    normed_two, saved_two = norm_forward(
        inner, weights["res_gain"][index, 1], weights["res_shift"][index, 1]
    )
    before = normed_two * scale + offset
    outer, padded_two = conv_same(
        silu(before).astype(narrow), weights["res_w"][index, 1], weights["res_b"][index, 1]
    )
    return (
        state + outer,
        (normed_one, saved_one, padded_one, normed_two, saved_two, before, padded_two, scale),
    )


def block_back(grad, weights, embed, index, kept):
    normed_one, saved_one, padded_one, normed_two, saved_two, before, padded_two, scale = kept
    outer_grad = grad.astype(narrow)
    act_two, kernel_two = conv_same_back(padded_two, weights["res_w"][index, 1], outer_grad)
    before_grad = act_two * silu_grad(before)
    modulate_grad = jnp.concatenate(
        [jnp.sum(before_grad * normed_two, axis=(1, 2)), jnp.sum(before_grad, axis=(1, 2))], axis=-1
    )
    inner_grad, gain_two, shift_two = norm_back(
        before_grad * scale, saved_two, weights["res_gain"][index, 1]
    )
    inner_low = inner_grad.astype(narrow)
    act_one, kernel_one = conv_same_back(padded_one, weights["res_w"][index, 0], inner_low)
    state_grad, gain_one, shift_one = norm_back(
        act_one * silu_grad(normed_one), saved_one, weights["res_gain"][index, 0]
    )
    result = {
        "res_w": jnp.stack([kernel_one, kernel_two]),
        "res_b": jnp.stack([column_sum(inner_low), column_sum(outer_grad)]),
        "emb_w": precise(embed.astype(jnp.float32).T, modulate_grad),
        "emb_b": jnp.sum(modulate_grad, axis=0),
        "res_gain": jnp.stack([gain_one, gain_two]),
        "res_shift": jnp.stack([shift_one, shift_two]),
    }
    embed_grad = precise(modulate_grad, weights["emb_w"][index].astype(jnp.float32).T)
    return (grad + state_grad, result, embed_grad)


def to_heads(tensor, thirds):
    batch, places, width = tensor.shape
    split = tensor.reshape(batch, places, thirds, HEADS, HEAD_DIM)
    return jnp.transpose(split, (0, 3, 1, 2, 4)).reshape(batch * HEADS, places, thirds * HEAD_DIM)


def from_heads(tensor, batch, thirds):
    items, places, width = tensor.shape
    split = tensor.reshape(batch, HEADS, places, thirds, HEAD_DIM)
    return jnp.transpose(split, (0, 2, 3, 1, 4)).reshape(batch, places, thirds * CH)


def head_scores(query, keys):
    return jnp.einsum("kqd,kpd->kqp", query, keys, preferred_element_type=jnp.float32) / math.sqrt(
        HEAD_DIM
    )


def attention_forward(state, weights):
    batch, rows, cols, chans = state.shape
    normed, saved = norm_forward(state, weights["attn_gain"], weights["attn_shift"])
    normed_low = normed.astype(narrow).reshape(batch, rows * cols, CH)
    bias = jnp.concatenate([weights["qv_b"][:CH], jnp.zeros((CH,), narrow), weights["qv_b"][CH:]])
    project = (
        jnp.einsum("bpc,cf->bpf", normed_low, weights["qkv_w"], preferred_element_type=jnp.float32)
        + bias
    ).astype(narrow)
    spread = lax.all_to_all(
        as_sent(to_heads(project, 3)), "rows", split_axis=0, concat_axis=1, tiled=True
    )
    query = spread[..., :HEAD_DIM]
    keys = spread[..., HEAD_DIM : 2 * HEAD_DIM]
    values = spread[..., 2 * HEAD_DIM :]
    scores = head_scores(query, keys)
    top = jnp.max(scores, axis=-1, keepdims=True)
    log_total = top + jnp.log(jnp.sum(jnp.exp(scores - top), axis=-1, keepdims=True))
    probs = jnp.exp(scores - log_total).astype(narrow)
    mixed = jnp.einsum("kqp,kpd->kqd", probs, values, preferred_element_type=jnp.float32).astype(
        narrow
    )
    returned = lax.all_to_all(
        as_sent(mixed), "rows", split_axis=1, concat_axis=0, tiled=True
    ).astype(mixed.dtype)
    mixed_local = from_heads(returned, batch, 1)
    out = (
        jnp.einsum(
            "bpc,cf->bpf", mixed_local, weights["proj_w"], preferred_element_type=jnp.float32
        )
        + weights["proj_b"]
    )
    return (state + out.reshape(state.shape), (normed_low, saved, spread, log_total, mixed_local))


def attention_back(grad, weights, kept):
    normed_low, saved, spread, log_total, mixed_local = kept
    batch, rows, cols, chans = grad.shape
    out_grad = grad.reshape(batch, rows * cols, CH).astype(narrow)
    proj_w_grad = jnp.einsum(
        "bpc,bpf->cf", mixed_local, out_grad, preferred_element_type=jnp.float32
    )
    mixed_grad = jnp.einsum(
        "bpf,cf->bpc", out_grad, weights["proj_w"], preferred_element_type=jnp.float32
    )
    mixed_grad = lax.all_to_all(
        as_sent(to_heads(mixed_grad.astype(narrow), 1)),
        "rows",
        split_axis=0,
        concat_axis=1,
        tiled=True,
    )
    query = spread[..., :HEAD_DIM]
    keys = spread[..., HEAD_DIM : 2 * HEAD_DIM]
    values = spread[..., 2 * HEAD_DIM :]
    probs = jnp.exp(head_scores(query, keys) - log_total)
    values_grad = jnp.einsum(
        "kqp,kqd->kpd", probs.astype(narrow), mixed_grad, preferred_element_type=jnp.float32
    )
    probs_grad = jnp.einsum("kqd,kpd->kqp", mixed_grad, values, preferred_element_type=jnp.float32)
    score_grad = (
        probs * (probs_grad - jnp.sum(probs_grad * probs, axis=-1, keepdims=True))
    ).astype(narrow)
    query_grad = jnp.einsum(
        "kqp,kpd->kqd", score_grad, keys, preferred_element_type=jnp.float32
    ) / math.sqrt(HEAD_DIM)
    keys_grad = jnp.einsum(
        "kqp,kqd->kpd", score_grad, query, preferred_element_type=jnp.float32
    ) / math.sqrt(HEAD_DIM)
    item_grad = jnp.concatenate([query_grad, keys_grad, values_grad], axis=-1).astype(narrow)
    item_grad = lax.all_to_all(
        as_sent(item_grad), "rows", split_axis=1, concat_axis=0, tiled=True
    ).astype(item_grad.dtype)
    project_grad = from_heads(item_grad, batch, 3)
    bias_grad = jnp.sum(project_grad.astype(jnp.float32), axis=(0, 1))
    normed_grad = jnp.einsum(
        "bpf,cf->bpc", project_grad, weights["qkv_w"], preferred_element_type=jnp.float32
    )
    state_grad, gain_grad, shift_grad = norm_back(
        normed_grad.reshape(grad.shape), saved, weights["attn_gain"]
    )
    result = {
        "proj_w": proj_w_grad,
        "proj_b": jnp.sum(out_grad.astype(jnp.float32), axis=(0, 1)),
        "qkv_w": jnp.einsum(
            "bpc,bpf->cf", normed_low, project_grad, preferred_element_type=jnp.float32
        ),
        "qv_b": jnp.concatenate([bias_grad[:CH], bias_grad[2 * CH :]]),
        "attn_gain": gain_grad,
        "attn_shift": shift_grad,
    }
    return (grad + state_grad, result)


def head_forward(state, skip, weights):
    upsampled = jnp.repeat(jnp.repeat(state, 2, axis=1), 2, axis=2)
    joined = jnp.concatenate([upsampled, skip.astype(jnp.float32)], axis=-1)
    normed, saved = norm_forward(joined, weights["head_gain"], weights["head_shift"])
    out, padded = conv_same(silu(normed).astype(narrow), weights["head_w"], weights["head_b"])
    return (out, (normed, saved, padded))


def head_back(out_grad, weights, kept):
    normed, saved, padded = kept
    out_low = out_grad.astype(narrow)
    act_grad, kernel = conv_same_back(padded, weights["head_w"], out_low)
    joined_grad, gain_grad, shift_grad = norm_back(
        act_grad * silu_grad(normed), saved, weights["head_gain"]
    )
    batch, rows, cols, chans = joined_grad.shape
    upper = joined_grad[..., :CH].reshape(batch, rows // 2, 2, cols // 2, 2, CH).sum(axis=(2, 4))
    result = {
        "head_w": kernel,
        "head_b": column_sum(out_low),
        "head_gain": gain_grad,
        "head_shift": shift_grad,
    }
    return (upper, joined_grad[..., CH:], result)


def loss_terms(out, noise, mask, sample_weight, beta, alpha, one_minus, tilde):
    error = out[..., :IN_CH] - noise
    fraction = (out[..., IN_CH:] + 1.0) / 2.0
    log_beta = per_image(jnp.log(beta))
    log_tilde = per_image(jnp.log(tilde))
    log_var = fraction * log_beta + (1.0 - fraction) * log_tilde
    coefficient = per_image(beta * beta / (alpha * one_minus))
    inverse = jnp.exp(-log_var)
    ratio = jnp.exp(log_tilde - log_var)
    divergence = 0.5 * (-1.0 + log_var - log_tilde + ratio + coefficient * error * error * inverse)
    each = jnp.sum(error * error + kl_weight * divergence, axis=-1)
    weight = sample_weight[:, None, None] * mask.astype(jnp.float32)
    total = jnp.sum(weight * each)
    vlb = jnp.sum(weight * kl_weight * jnp.sum(divergence, axis=-1))
    weight = weight[..., None]
    predict_grad = weight * (2.0 * error + kl_weight * coefficient * error * inverse)
    spread_grad = (
        weight
        * kl_weight
        * 0.5
        * (1.0 - ratio - coefficient * error * error * inverse)
        * (log_beta - log_tilde)
        / 2.0
    )
    return (total, vlb, jnp.concatenate([predict_grad, spread_grad], axis=-1))


def micro_step(weights, clean, noise, steps, mask, sample_weight):
    clean = jnp.transpose(clean, (0, 2, 3, 1))
    noise = jnp.transpose(noise, (0, 2, 3, 1))
    signal, one_minus, beta, alpha, tilde = plan(steps)
    noisy = jnp.sqrt(per_image(signal)) * clean + jnp.sqrt(per_image(one_minus)) * noise
    embed, time_kept = time_forward(steps, weights)
    stem_out, stem_padded = conv_same(noisy.astype(narrow), weights["stem_w"], weights["stem_b"])
    skip = stem_out.astype(narrow)
    state, down_padded = conv_down(skip, weights["down_w"], weights["down_b"])
    block_kept = []
    for index in range(BLOCKS):
        state, kept = block_forward(state, weights, embed, index)
        block_kept.append(kept)
    state, attention_kept = attention_forward(state, weights)
    out, head_kept = head_forward(state, skip, weights)
    loss, vlb, out_grad = loss_terms(out, noise, mask, sample_weight, beta, alpha, one_minus, tilde)
    state_grad, skip_grad, grads = head_back(out_grad, weights, head_kept)
    state_grad, attention_grads = attention_back(state_grad, weights, attention_kept)
    grads.update(attention_grads)
    embed_grad = jnp.zeros((steps.shape[0], TEMB), jnp.float32)
    block_grads = [None] * BLOCKS
    for index in reversed(range(BLOCKS)):
        state_grad, block_grads[index], part = block_back(
            state_grad, weights, embed, index, block_kept[index]
        )
        embed_grad = embed_grad + part
    for name in block_grads[0]:
        grads[name] = jnp.stack([entry[name] for entry in block_grads])
    down_low = state_grad.astype(narrow)
    skip_more, down_kernel = conv_down_back(down_padded, weights["down_w"], down_low)
    stem_low = (skip_grad + skip_more).astype(narrow)
    grads.update(
        {
            "down_w": down_kernel,
            "down_b": column_sum(down_low),
            "stem_w": kernel_grad(stem_padded, stem_low, 1),
            "stem_b": column_sum(stem_low),
        }
    )
    grads.update(time_back(embed_grad, weights, time_kept))
    return (loss, vlb, grads)


def shards(params, moment1, moment2, images, noise, timesteps, masks, weight_index):
    shard = params.shape[0]
    length = shard * lax.axis_size("batch") * lax.axis_size("rows")
    whole = lax.all_gather(as_sent(params.astype(narrow)), ("batch", "rows"), axis=0, tiled=True)
    weights = unpack(whole)
    group = images.shape[0] // MB
    sample_weight = 0.5 + 0.5 * weight_index.astype(jnp.float32)
    items = (
        images.reshape((MB, group) + images.shape[1:]),
        noise.reshape((MB, group) + noise.shape[1:]),
        timesteps.reshape(MB, group),
        masks.reshape((MB, group) + masks.shape[1:]),
        sample_weight.reshape(MB, group),
    )
    count = lax.psum(jnp.sum(masks).astype(jnp.float32), ("batch", "rows"))

    def one_batch(carry, item):
        summed, loss, vlb_total = carry
        part, vlb_part, grads = micro_step(weights, *item)
        flat = pack(grads, length)
        return ((summed + flat, loss + part, vlb_total + vlb_part), None)

    start = jnp.zeros((length,), jnp.float32)
    zero = jnp.zeros((), jnp.float32)
    (summed, loss_local, vlb_local), unused = lax.scan(one_batch, (start, zero, zero), items)
    summed = lax.psum_scatter(summed, ("batch", "rows"), scatter_dimension=0, tiled=True)
    scaled = summed / count
    squares, loss_sum, loss_vlb = lax.psum(
        (jnp.sum(scaled * scaled), loss_local, vlb_local), ("batch", "rows")
    )
    grad_norm = jnp.sqrt(squares)
    clipped = scaled * jnp.minimum(1.0, clip_limit / (grad_norm + 1e-06))
    first = decay_first * moment1 + (1.0 - decay_first) * clipped
    second = decay_second * moment2 + (1.0 - decay_second) * clipped * clipped
    first_hat = first / (1.0 - decay_first**STEP)
    second_hat = second / (1.0 - decay_second**STEP)
    updated = params - learn_rate * (
        first_hat / (jnp.sqrt(second_hat) + 1e-08) + weight_decay * params
    )
    return (updated, first, second, updated.astype(narrow), loss_sum, loss_vlb, count, grad_norm)


def solution(mesh):
    return jax.shard_map(
        shards,
        mesh=mesh,
        in_specs=(
            P(("batch", "rows")),
            P(("batch", "rows")),
            P(("batch", "rows")),
            P("batch", None, "rows", None),
            P("batch", None, "rows", None),
            P("batch"),
            P("batch", "rows", None),
            P("batch"),
        ),
        out_specs=(
            P(("batch", "rows")),
            P(("batch", "rows")),
            P(("batch", "rows")),
            P(("batch", "rows")),
            P(),
            P(),
            P(),
            P(),
        ),
        check_vma=False,
    )
```

profile of v0, /device:TPU:0, one launch (start us, length us, event | category | flops | bytes accessed | tf_op | source)
XLA Modules:
  0.0 5443.4 jit_solution(6676942511530215583)
XLA Ops:
  17.6 198.2 %all-gather.3.cloned.1.call-done = bf16[32,1,266496]{2,1,0:T(2,128)(2,1)} async-done(((bf16[1,1,266496]{2,1,0:T(2,128)(2,1)}), bf16[32,1,266496]{2,1,0:T(2,128)(2,1)}) %all-gather.3.cloned.1.call-update) | async-done | bytes 17055760 | tf_op jit(solution)/shard_map/all_gather | solution.py:545
  215.8 362.0 %reduce.203 = bf16[32,266496]{1,0:T(8,128)(2,1)} reduce(bf16[32,1,266496]{2,1,0:T(2,128)(2,1)} %all-gather.3.cloned.1.call-done, bf16[]{:T(256)} %constant.392), dimensions={1}, to_apply=%all-gather.reduce_sub_computation | reduce | bytes 34111488 | tf_op jit(solution)/shard_map/all_gather | solution.py:545
  577.8 42.6 reshape.1524
  681.7 4193.9 %while.18 = (s32[]{:T(128)}, f32[8527872]{0:T(1024)}, f32[]{:T(128)}, f32[]{:T(128)}, s32[4,2]{1,0:T(4,128)S(1)}, /*index=5*/f32[4,2,3,8,64]{4,2,3,1,0:T(4,128)}...) while((s32[]{:T(128)}, f32[8527872]{0:T(1024)}, ...), condition=%wide.region_110.111_spmd.clone, body=%wide.region_0.110_spmd.clone.sunk | while | flops 13284588544 | bytes 1083077504 | solution.py:566
  1129.4 21.8 all-reduce.41
  1342.7 22.2 reshape.1857
  1424.0 273.0 %concatenate.312 = f32[8527872]{0:T(1024)} concatenate(f32[5184]{0:T(1024)S(1)} %reshape.1853, f32[192]{0:T(256)S(1)} %get-tuple-element.1704, f32[147456]{0:T(1024)} %reshape.1854, f32[768]{0:T(1024)S(1)} %get-tuple-element.1709, f32[589824]{0:T(1024)} %reshape.1855, f32[768]{0:T(1024)S(1)} %copy-done.188, f32[663552]{0:T(1024)S(1)} %reshape.1856, f32[384]{0:T(512)S(1)} %get-tuple-element.1712, ...), dimensions={0} | concatenate | bytes 68222976 | tf_op jit(solution)/shard_map/while/body/eval_jaxpr/concatenate | solution.py:102
  1697.1 22.9 select_add_fusion.2
  2031.7 20.5 all-reduce.40
  2169.8 21.8 all-reduce.41
  2383.2 22.2 reshape.1857
  2464.5 273.0 %concatenate.312 = f32[8527872]{0:T(1024)} concatenate(f32[5184]{0:T(1024)S(1)} %reshape.1853, f32[192]{0:T(256)S(1)} %get-tuple-element.1704, f32[147456]{0:T(1024)} %reshape.1854, f32[768]{0:T(1024)S(1)} %get-tuple-element.1709, f32[589824]{0:T(1024)} %reshape.1855, f32[768]{0:T(1024)S(1)} %copy-done.188, f32[663552]{0:T(1024)S(1)} %reshape.1856, f32[384]{0:T(512)S(1)} %get-tuple-element.1712, ...), dimensions={0} | concatenate | bytes 68222976 | tf_op jit(solution)/shard_map/while/body/eval_jaxpr/concatenate | solution.py:102
  2737.6 34.0 select_add_fusion.2
  3220.3 21.8 all-reduce.41
  3433.6 22.2 reshape.1857
  3514.9 273.0 %concatenate.312 = f32[8527872]{0:T(1024)} concatenate(f32[5184]{0:T(1024)S(1)} %reshape.1853, f32[192]{0:T(256)S(1)} %get-tuple-element.1704, f32[147456]{0:T(1024)} %reshape.1854, f32[768]{0:T(1024)S(1)} %get-tuple-element.1709, f32[589824]{0:T(1024)} %reshape.1855, f32[768]{0:T(1024)S(1)} %copy-done.188, f32[663552]{0:T(1024)S(1)} %reshape.1856, f32[384]{0:T(512)S(1)} %get-tuple-element.1712, ...), dimensions={0} | concatenate | bytes 68222976 | tf_op jit(solution)/shard_map/while/body/eval_jaxpr/concatenate | solution.py:102
  3788.0 34.0 select_add_fusion.2
  4270.8 21.8 all-reduce.41
  4484.1 22.2 reshape.1857
  4565.4 273.0 %concatenate.312 = f32[8527872]{0:T(1024)} concatenate(f32[5184]{0:T(1024)S(1)} %reshape.1853, f32[192]{0:T(256)S(1)} %get-tuple-element.1704, f32[147456]{0:T(1024)} %reshape.1854, f32[768]{0:T(1024)S(1)} %get-tuple-element.1709, f32[589824]{0:T(1024)} %reshape.1855, f32[768]{0:T(1024)S(1)} %copy-done.188, f32[663552]{0:T(1024)S(1)} %reshape.1856, f32[384]{0:T(512)S(1)} %get-tuple-element.1712, ...), dimensions={0} | concatenate | bytes 68222976 | tf_op jit(solution)/shard_map/while/body/eval_jaxpr/concatenate | solution.py:102
  4838.5 34.0 select_add_fusion.2
  4877.7 40.9 psum.292
  4918.6 468.1 %all-reduce.48.cloned.1.call-done = f32[8527872]{0:T(1024)} async-done(((f32[8527872]{0:T(1024)}), f32[8527872]{0:T(1024)}) %all-reduce.48.cloned.1.call-update) | async-done | bytes 34111504
  5389.5 40.1 all-reduce.21
  (4397 shorter events, 2832.7 us)
Async XLA Ops:
  7.2 208.6 %all-gather.3.cloned.1.call-start = ((), (), s32[]{:S(2)}) async-start(), calls=%async_computation.4 | async-start | bytes 35177472 | tf_op jit(solution)/shard_map/all_gather | solution.py:545
  15.4 5371.2 %all-reduce.48.cloned.1.call-start = ((), (), s32[]{:S(2)}) async-start(), calls=%async_computation.5 | async-start | bytes 68222976
  1025.6 48.2 all-to-all-start.2
  1096.2 22.9 all-to-all-start.3
  1194.9 20.7 collective-permute-start.17
  1196.4 19.2 collective-permute-start.18
  1297.4 71.1 %collective-permute-start.21 = (bf16[2,1,32,384]{3,2,1,0:T(8,128)(2,1)}, bf16[2,1,32,384]{3,2,1,0:T(8,128)(2,1)}, u32[]{:S(2)}, u32[]{:S(2)}) collective-permute-start(bf16[2,1,32,384]{3,2,1,0:T(8,128)(2,1)} %slice_bitcast_fusion.57), channel_id=1, source_target_pairs={{1,0},{2,1},{3,2},{4,3},{5,4},{6,5},{7,6},{9,8},{10,9},{11,10},{12... | collective-permute-start | bytes 147464 | tf_op jit(solution)/shard_map/while/body/eval_jaxpr/ppermute | solution.py:48
  1298.8 69.7 %collective-permute-start.22 = (bf16[2,1,32,384]{3,2,1,0:T(8,128)(2,1)S(1)}, bf16[2,1,32,384]{3,2,1,0:T(8,128)(2,1)S(1)}, u32[]{:S(2)}, u32[]{:S(2)}) collective-permute-start(bf16[2,1,32,384]{3,2,1,0:T(8,128)(2,1)S(1)} %slice_bitcast_fusion.58), channel_id=1, source_target_pairs={{0,1},{1,2},{2,3},{3,4},{4,5},{5,6},{6,7},{8,9},{9,10},{10,11},{11... | collective-permute-start | bytes 147464 | tf_op jit(solution)/shard_map/while/body/eval_jaxpr/ppermute | solution.py:47
  2066.1 48.2 all-to-all-start.2
  2136.7 22.9 all-to-all-start.3
  2235.4 20.7 collective-permute-start.17
  2236.9 19.2 collective-permute-start.18
  2337.9 71.1 %collective-permute-start.21 = (bf16[2,1,32,384]{3,2,1,0:T(8,128)(2,1)}, bf16[2,1,32,384]{3,2,1,0:T(8,128)(2,1)}, u32[]{:S(2)}, u32[]{:S(2)}) collective-permute-start(bf16[2,1,32,384]{3,2,1,0:T(8,128)(2,1)} %slice_bitcast_fusion.57), channel_id=1, source_target_pairs={{1,0},{2,1},{3,2},{4,3},{5,4},{6,5},{7,6},{9,8},{10,9},{11,10},{12... | collective-permute-start | bytes 147464 | tf_op jit(solution)/shard_map/while/body/eval_jaxpr/ppermute | solution.py:48
  2339.3 69.7 %collective-permute-start.22 = (bf16[2,1,32,384]{3,2,1,0:T(8,128)(2,1)S(1)}, bf16[2,1,32,384]{3,2,1,0:T(8,128)(2,1)S(1)}, u32[]{:S(2)}, u32[]{:S(2)}) collective-permute-start(bf16[2,1,32,384]{3,2,1,0:T(8,128)(2,1)S(1)} %slice_bitcast_fusion.58), channel_id=1, source_target_pairs={{0,1},{1,2},{2,3},{3,4},{4,5},{5,6},{6,7},{8,9},{9,10},{10,11},{11... | collective-permute-start | bytes 147464 | tf_op jit(solution)/shard_map/while/body/eval_jaxpr/ppermute | solution.py:47
  3116.5 48.2 all-to-all-start.2
  3187.1 22.9 all-to-all-start.3
  3285.8 20.7 collective-permute-start.17
  3388.4 71.1 %collective-permute-start.21 = (bf16[2,1,32,384]{3,2,1,0:T(8,128)(2,1)}, bf16[2,1,32,384]{3,2,1,0:T(8,128)(2,1)}, u32[]{:S(2)}, u32[]{:S(2)}) collective-permute-start(bf16[2,1,32,384]{3,2,1,0:T(8,128)(2,1)} %slice_bitcast_fusion.57), channel_id=1, source_target_pairs={{1,0},{2,1},{3,2},{4,3},{5,4},{6,5},{7,6},{9,8},{10,9},{11,10},{12... | collective-permute-start | bytes 147464 | tf_op jit(solution)/shard_map/while/body/eval_jaxpr/ppermute | solution.py:48
  3389.8 69.7 %collective-permute-start.22 = (bf16[2,1,32,384]{3,2,1,0:T(8,128)(2,1)S(1)}, bf16[2,1,32,384]{3,2,1,0:T(8,128)(2,1)S(1)}, u32[]{:S(2)}, u32[]{:S(2)}) collective-permute-start(bf16[2,1,32,384]{3,2,1,0:T(8,128)(2,1)S(1)} %slice_bitcast_fusion.58), channel_id=1, source_target_pairs={{0,1},{1,2},{2,3},{3,4},{4,5},{5,6},{6,7},{8,9},{9,10},{10,11},{11... | collective-permute-start | bytes 147464 | tf_op jit(solution)/shard_map/while/body/eval_jaxpr/ppermute | solution.py:47
  4167.0 48.2 all-to-all-start.2
  4237.6 22.9 all-to-all-start.3
  4336.3 20.7 collective-permute-start.17
  4438.8 71.1 %collective-permute-start.21 = (bf16[2,1,32,384]{3,2,1,0:T(8,128)(2,1)}, bf16[2,1,32,384]{3,2,1,0:T(8,128)(2,1)}, u32[]{:S(2)}, u32[]{:S(2)}) collective-permute-start(bf16[2,1,32,384]{3,2,1,0:T(8,128)(2,1)} %slice_bitcast_fusion.57), channel_id=1, source_target_pairs={{1,0},{2,1},{3,2},{4,3},{5,4},{6,5},{7,6},{9,8},{10,9},{11,10},{12... | collective-permute-start | bytes 147464 | tf_op jit(solution)/shard_map/while/body/eval_jaxpr/ppermute | solution.py:48
  4440.2 69.7 %collective-permute-start.22 = (bf16[2,1,32,384]{3,2,1,0:T(8,128)(2,1)S(1)}, bf16[2,1,32,384]{3,2,1,0:T(8,128)(2,1)S(1)}, u32[]{:S(2)}, u32[]{:S(2)}) collective-permute-start(bf16[2,1,32,384]{3,2,1,0:T(8,128)(2,1)S(1)} %slice_bitcast_fusion.58), channel_id=1, source_target_pairs={{0,1},{1,2},{2,3},{3,4},{4,5},{5,6},{6,7},{8,9},{9,10},{10,11},{11... | collective-permute-start | bytes 147464 | tf_op jit(solution)/shard_map/while/body/eval_jaxpr/ppermute | solution.py:47
  (932 other events, 13816.6 us)
Sparse Core Ops, SparseCore 0:
  15.5 200.2 all-gather.2
  4875.8 510.8 all-reduce.47
where the time goes:
time: 5540 us; the launch traced here: 5440 us
  local copies, waits for them, and re-layouts  1890 us (34%)
  blocking collectives  1060 us (19%)
  other arithmetic  874 us (16%)
  waiting for transfers between devices  726 us (13%)
  matrix products  504 us (9%)
  starting transfers between devices  339 us (6%)
    concatenate x4, local copies, waits for them, and re-layouts, pack(): return jnp.concatenate(pieces)  1090 us
    unnamed x3, waiting for transfers between devices  468 us
    psum x24, blocking collectives, norm_back(): lax.psum((jnp.sum(scaled, axis=(1, 2, 4)), jnp.sum(scaled * normed, axis=...  465 us
    psum x24, blocking collectives, norm_forward(): lax.psum((jnp.sum(grouped, axis=(1, 2, 4)), jnp.sum(grouped * grouped, ax...  461 us
    all_gather x1, other arithmetic, shards(): lax.all_gather(as_sent(params.astype(narrow)), ('batch', 'rows'), axis=0,...  362 us
    ppermute x44, starting transfers between devices, with_halo(): before = lax.ppermute(last, axis, up)  202 us
    all_gather x1, waiting for transfers between devices, shards(): lax.all_gather(as_sent(params.astype(narrow)), ('batch', 'rows'), axis=0,...  198 us
    conv_general_dilated x48, matrix products, conv_apply(): lax.conv_general_dilated(padded, kernel, (stride, stride), 'VALID', dimen...  194 us

commit v1 on v0

--- a/solution.py
+++ b/solution.py
@@ -15,7 +15,7 @@
 OUT_CH = 6
 DIFF_STEPS = 4000
 BLOCKS = 2
-MB = 4
+WIDE = 384
 STEP = 10
 
 
@@ -29,31 +29,8 @@
 narrow = jnp.bfloat16
 
 
-def as_sent(value):
-
-    def short(part):
-        return part.astype(jnp.bfloat16) if part.dtype == jnp.float32 else part
-
-    return jax.tree.map(short, value)
-
-
-def with_halo(value, sides, width):
-    for axis, dim in sides:
-        size, length = (lax.axis_size(axis), value.shape[dim])
-        up = [(i, (i + 1) % size) for i in range(size - 1)]
-        down = [(j, i) for i, j in up]
-        last = lax.slice_in_dim(value, length - width, length, axis=dim)
-        leading = lax.slice_in_dim(value, 0, width, axis=dim)
-        before = lax.ppermute(last, axis, up)
-        after = lax.ppermute(leading, axis, down)
-        value = jnp.concatenate([before, value, after], axis=dim)
-    return value
-
-
-def shifted(block, axis, distance):
-    devices = range(lax.axis_size(axis))
-    route = [(i - distance, i) for i in devices if i - distance in devices]
-    return lax.ppermute(block, axis, route)
+def with_halo(value):
+    return jnp.pad(value, ((0, 0), (1, 1), (0, 0), (0, 0)))
 
 
 def segments():
@@ -85,20 +62,32 @@
     ]
 
 
-def unpack(flat):
+def unpack(whole):
     table = {}
     offset = 0
     for name, shape in segments():
         amount = math.prod(shape)
-        table[name] = flat[offset : offset + amount].reshape(shape)
+        first, last = offset // WIDE, -(-(offset + amount) // WIDE)
+        part = whole[first:last].reshape(-1)
+        table[name] = part[offset - first * WIDE : offset - first * WIDE + amount].reshape(shape)
         offset = offset + amount
     return table
 
 
-def pack(table, length):
-    pieces = [table[name].reshape(-1) for name, shape in segments()]
-    used = sum((piece.shape[0] for piece in pieces))
-    pieces.append(jnp.zeros((length - used,), jnp.float32))
+def pack(table, rows):
+    pieces, pending = [], []
+    for name, shape in segments():
+        flat = table[name].reshape(-1)
+        pending.append(flat)
+        held = sum(piece.shape[0] for piece in pending)
+        if held % WIDE == 0:
+            joined = pending[0] if len(pending) == 1 else jnp.concatenate(pending)
+            pieces.append(joined.reshape(-1, WIDE))
+            pending = []
+    used = sum(piece.shape[0] for piece in pieces)
+    held = sum(piece.shape[0] for piece in pending)
+    pending.append(jnp.zeros(((rows - used) * WIDE - held,), jnp.float32))
+    pieces.append(jnp.concatenate(pending).reshape(-1, WIDE))
     return jnp.concatenate(pieces)
 
 
@@ -181,18 +170,17 @@
 
 
 def conv_same(inputs, kernel, bias):
-    padded = widen(with_halo(as_sent(inputs), (("rows", 1),), 1).astype(inputs.dtype))
+    padded = widen(with_halo(inputs))
     return (conv_apply(padded, kernel, 1) + bias.astype(jnp.float32), padded)
 
 
 def conv_same_back(padded, kernel, grad):
-    grad_padded = widen(with_halo(as_sent(grad), (("rows", 1),), 1).astype(grad.dtype))
+    grad_padded = widen(with_halo(grad))
     return (conv_apply(grad_padded, flipped(kernel), 1), kernel_grad(padded, grad, 1))
 
 
 def conv_down(inputs, kernel, bias):
-    above = shifted(as_sent(inputs[:, -1:]), "rows", 1)
-    padded = widen(jnp.concatenate([above, inputs], axis=1))
+    padded = widen(jnp.pad(inputs, ((0, 0), (1, 0), (0, 0), (0, 0))))
     return (conv_apply(padded, kernel, 2) + bias.astype(jnp.float32), padded)
 
 
@@ -206,20 +194,16 @@
         dimension_numbers=("NHWC", "HWIO", "NHWC"),
         preferred_element_type=jnp.float32,
     )
-    spread = spread[:, :, 1:-1]
-    below = shifted(spread[:, :1].astype(jnp.bfloat16), "rows", -1).astype(jnp.float32)
-    rows = spread.shape[1] - 1
-    inputs_grad = spread[:, 1:] + jnp.pad(below, ((0, 0), (rows - 1, 0), (0, 0), (0, 0)))
+    inputs_grad = spread[:, 1:, 1:-1]
     return (inputs_grad, kernel_grad(padded, grad, 2))
 
 
 def norm_forward(values, gain, shift):
     batch, rows, cols, chans = values.shape
     grouped = values.reshape(batch, rows, cols, GROUPS, chans // GROUPS)
-    totals, squares = lax.psum(
-        (jnp.sum(grouped, axis=(1, 2, 4)), jnp.sum(grouped * grouped, axis=(1, 2, 4))), "rows"
-    )
-    amount = rows * lax.axis_size("rows") * cols * (chans // GROUPS)
+    totals = jnp.sum(grouped, axis=(1, 2, 4))
+    squares = jnp.sum(grouped * grouped, axis=(1, 2, 4))
+    amount = rows * cols * (chans // GROUPS)
     mean = totals / amount
     inverse = lax.rsqrt(squares / amount - mean * mean + 1e-05)
     normed = ((grouped - mean[:, None, None, :, None]) * inverse[:, None, None, :, None]).reshape(
@@ -236,10 +220,9 @@
     shape = (batch, rows, cols, GROUPS, chans // GROUPS)
     scaled = (grad * gain).reshape(shape)
     normed = normed.reshape(shape)
-    first, second = lax.psum(
-        (jnp.sum(scaled, axis=(1, 2, 4)), jnp.sum(scaled * normed, axis=(1, 2, 4))), "rows"
-    )
-    amount = rows * lax.axis_size("rows") * cols * (chans // GROUPS)
+    first = jnp.sum(scaled, axis=(1, 2, 4))
+    second = jnp.sum(scaled * normed, axis=(1, 2, 4))
+    amount = rows * cols * (chans // GROUPS)
     inputs_grad = (
         scaled
         - first[:, None, None, :, None] / amount
@@ -358,9 +341,7 @@
         jnp.einsum("bpc,cf->bpf", normed_low, weights["qkv_w"], preferred_element_type=jnp.float32)
         + bias
     ).astype(narrow)
-    spread = lax.all_to_all(
-        as_sent(to_heads(project, 3)), "rows", split_axis=0, concat_axis=1, tiled=True
-    )
+    spread = to_heads(project, 3)
     query = spread[..., :HEAD_DIM]
     keys = spread[..., HEAD_DIM : 2 * HEAD_DIM]
     values = spread[..., 2 * HEAD_DIM :]
@@ -371,10 +352,7 @@
     mixed = jnp.einsum("kqp,kpd->kqd", probs, values, preferred_element_type=jnp.float32).astype(
         narrow
     )
-    returned = lax.all_to_all(
-        as_sent(mixed), "rows", split_axis=1, concat_axis=0, tiled=True
-    ).astype(mixed.dtype)
-    mixed_local = from_heads(returned, batch, 1)
+    mixed_local = from_heads(mixed, batch, 1)
     out = (
         jnp.einsum(
             "bpc,cf->bpf", mixed_local, weights["proj_w"], preferred_element_type=jnp.float32
@@ -394,13 +372,7 @@
     mixed_grad = jnp.einsum(
         "bpf,cf->bpc", out_grad, weights["proj_w"], preferred_element_type=jnp.float32
     )
-    mixed_grad = lax.all_to_all(
-        as_sent(to_heads(mixed_grad.astype(narrow), 1)),
-        "rows",
-        split_axis=0,
-        concat_axis=1,
-        tiled=True,
-    )
+    mixed_grad = to_heads(mixed_grad.astype(narrow), 1)
     query = spread[..., :HEAD_DIM]
     keys = spread[..., HEAD_DIM : 2 * HEAD_DIM]
     values = spread[..., 2 * HEAD_DIM :]
@@ -419,9 +391,6 @@
         "kqp,kqd->kpd", score_grad, query, preferred_element_type=jnp.float32
     ) / math.sqrt(HEAD_DIM)
     item_grad = jnp.concatenate([query_grad, keys_grad, values_grad], axis=-1).astype(narrow)
-    item_grad = lax.all_to_all(
-        as_sent(item_grad), "rows", split_axis=1, concat_axis=0, tiled=True
-    ).astype(item_grad.dtype)
     project_grad = from_heads(item_grad, batch, 3)
     bias_grad = jnp.sum(project_grad.astype(jnp.float32), axis=(0, 1))
     normed_grad = jnp.einsum(
@@ -539,31 +508,32 @@
     return (loss, vlb, grads)
 
 
+def whole_images(value):
+    return lax.all_to_all(value, "rows", split_axis=0, concat_axis=2, tiled=True)
+
+
 def shards(params, moment1, moment2, images, noise, timesteps, masks, weight_index):
     shard = params.shape[0]
-    length = shard * lax.axis_size("batch") * lax.axis_size("rows")
-    whole = lax.all_gather(as_sent(params.astype(narrow)), ("batch", "rows"), axis=0, tiled=True)
+    params, moment1, moment2 = (
+        value.reshape(-1, WIDE) for value in (params, moment1, moment2)
+    )
+    total_rows = params.shape[0] * lax.axis_size("batch") * lax.axis_size("rows")
+    whole = lax.all_gather(params.astype(narrow), ("batch", "rows"), axis=0, tiled=True)
     weights = unpack(whole)
-    group = images.shape[0] // MB
-    sample_weight = 0.5 + 0.5 * weight_index.astype(jnp.float32)
-    items = (
-        images.reshape((MB, group) + images.shape[1:]),
-        noise.reshape((MB, group) + noise.shape[1:]),
-        timesteps.reshape(MB, group),
-        masks.reshape((MB, group) + masks.shape[1:]),
-        sample_weight.reshape(MB, group),
-    )
+    group = images.shape[0] // lax.axis_size("rows")
+    place = lax.axis_index("rows") * group
     count = lax.psum(jnp.sum(masks).astype(jnp.float32), ("batch", "rows"))
-
-    def one_batch(carry, item):
-        summed, loss, vlb_total = carry
-        part, vlb_part, grads = micro_step(weights, *item)
-        flat = pack(grads, length)
-        return ((summed + flat, loss + part, vlb_total + vlb_part), None)
-
-    start = jnp.zeros((length,), jnp.float32)
-    zero = jnp.zeros((), jnp.float32)
-    (summed, loss_local, vlb_local), unused = lax.scan(one_batch, (start, zero, zero), items)
+    own = whole_images(
+        jnp.concatenate([images, noise, masks.astype(jnp.float32)[:, None]], axis=1)
+    )
+    steps = lax.dynamic_slice_in_dim(timesteps, place, group)
+    sample_weight = 0.5 + 0.5 * lax.dynamic_slice_in_dim(weight_index, place, group).astype(
+        jnp.float32
+    )
+    loss_local, vlb_local, grads = micro_step(
+        weights, own[:, :IN_CH], own[:, IN_CH : 2 * IN_CH], steps, own[:, 2 * IN_CH], sample_weight
+    )
+    summed = pack(grads, total_rows)
     summed = lax.psum_scatter(summed, ("batch", "rows"), scatter_dimension=0, tiled=True)
     scaled = summed / count
     squares, loss_sum, loss_vlb = lax.psum(
@@ -578,7 +548,8 @@
     updated = params - learn_rate * (
         first_hat / (jnp.sqrt(second_hat) + 1e-08) + weight_decay * params
     )
-    return (updated, first, second, updated.astype(narrow), loss_sum, loss_vlb, count, grad_norm)
+    arrays = (value.reshape(shard) for value in (updated, first, second, updated.astype(narrow)))
+    return (*arrays, loss_sum, loss_vlb, count, grad_norm)
 
 
 def solution(mesh):

time: 5540 us -> 1960 us (0.35); the launches traced: 5440 us -> 1950 us
  local copies, waits for them, and re-layouts: 1890 us -> 446 us
  other arithmetic: 874 us -> 154 us
  waiting for transfers between devices: 726 us -> 102 us
  starting transfers between devices: 339 us -> 9.5 us
  blocking collectives: 1060 us -> 816 us
  matrix products: 504 us -> 397 us
    concatenate x4 -> x1, local copies, waits for them, and re-layouts: 1090 us -> 102 us  [pack(): return jnp.concatenate(pieces)]
    psum x48 -> x0, blocking collectives: 925 us -> none  [the longest x24 465 us: norm_back(): lax.psum((jnp.sum(scaled, axis=(1, 2, 4)), jnp.sum(scaled * normed, axis=...]
    unnamed x0 -> x1, blocking collectives: none -> 730 us
    unnamed x3 -> x2, waiting for transfers between devices: 468 us -> 0.02 us
    all_gather x1 -> x0, other arithmetic: 362 us -> none  [shards(): lax.all_gather(as_sent(params.astype(narrow)), ('batch', 'rows'), axis=0,...]
    ppermute x96 -> x0, starting transfers between devices: 285 us -> none  [the longest x44 202 us: with_halo(): before = lax.ppermute(last, axis, up)]
    reshape x76 -> x20, local copies, waits for them, and re-layouts: 201 us -> 12 us  [the longest x4 5.57 us: shards(): value.reshape(shard)]
    add x5 -> x0, other arithmetic: 125 us -> none  [the longest x4 125 us: one_batch(): return ((summed + flat, loss + part, vlb_total + vlb_part), None)]
where the time goes in v1:
time: 1960 us; the launch traced here: 1950 us
  blocking collectives  816 us (42%)
  local copies, waits for them, and re-layouts  446 us (23%)
  matrix products  397 us (20%)
  other arithmetic  154 us (8%)
  waiting for transfers between devices  102 us (5%)
  between operations  22.3 us (1%)
    unnamed x1, blocking collectives  730 us
    conv_general_dilated x12, matrix products, conv_apply(): lax.conv_general_dilated(padded, kernel, (stride, stride), 'VALID', dimen...  236 us
    concatenate x1, local copies, waits for them, and re-layouts, pack(): return jnp.concatenate(pieces)  102 us
    all_gather x1, waiting for transfers between devices, shards(): lax.all_gather(params.astype(narrow), ('batch', 'rows'), axis=0, tiled=True)  101 us
    slice x9, local copies, waits for them, and re-layouts, kernel_grad(): lax.slice(padded, (0, top, left, 0), (batch, top + stride * (rows - 1) +...  91.2 us
    dot_general x63, matrix products, kernel_grad(): jnp.einsum('brci,brco->io', window, grad, preferred_element_type=jnp.floa...  81.7 us
    unnamed x405, local copies, waits for them, and re-layouts  73.2 us
    psum x1, blocking collectives, shards(): count = lax.psum(jnp.sum(masks).astype(jnp.float32), ('batch', 'rows'))  44.8 us
  transfers between devices with their start and end apart: 3, of which 2 were waited for; matrix products, arithmetic and copies ran while one was open for 1% of the time, Pallas kernels for 0%

profile of v1, /device:TPU:0, one launch (start us, length us, event | category | flops | bytes accessed | tf_op | source)
XLA Modules:
  0.0 1947.6 jit_solution(12170941123871818908)
XLA Ops:
  29.6 100.9 %all-gather.3.cloned.1.call-done = bf16[32,694,384]{2,1,0:T(8,128)(2,1)} async-done(((bf16[1,694,384]{2,1,0:T(8,128)(2,1)}), bf16[32,694,384]{2,1,0:T(8,128)(2,1)}) %all-gather.3.cloned.1.call-update) | async-done | bytes 17055760 | tf_op jit(solution)/shard_map/all_gather | solution.py:521
  130.6 15.3 reshape.2176
  150.0 11.6 slice.627
  314.8 148.1 %fusion.9 = f32[64,8,9,6]{1,3,2,0:T(8,128)S(1)} fusion(bf16[3,3,576,6]{3,2,1,0:T(8,128)(2,1)} %reshape_reshape.67, bf16[64,1,7,2,576]{4,2,3,0,1:T(8,128)(2,1)} %slice.674, bf16[64,1,8,9,576]{4,2,3,0,1:T(8,128)(2,1)} %copy-done.41), kind=kOutput, calls=%fused_computation.30 | convolution fusion | flops 303132672 | bytes 6513408 | tf_op jit(solution)/shard_map/conv_general_dilated | solution.py:132
  474.9 10.9 copy.392
  485.8 13.1 multiply_reduce_fusion.2
  534.9 14.1 multiply_reduce_fusion
  626.0 12.3 select_reduce_fusion.16
  650.3 10.7 select_reduce_fusion.11
  676.5 12.2 select_reduce_fusion.6
  705.2 10.2 slice.493
  715.4 10.1 slice.494
  735.6 10.1 slice.496
  745.7 10.1 slice.497
  755.8 10.1 slice.498
  765.9 10.2 slice.499
  776.1 10.1 slice.500
  786.3 10.2 slice.501
  843.6 10.6 select_reduce_fusion.1
  975.2 12.7 pad_maximum_fusion
  997.2 102.3 %concatenate.134 = f32[22208,384]{1,0:T(8,128)} concatenate(f32[14,384]{1,0:T(8,128)S(1)} %reshape.1770, f32[384,384]{1,0:T(8,128)} %reshape_reshape.69, f32[2,384]{1,0:T(2,128)S(1)} %reshape.1773, f32[1536,384]{1,0:T(8,128)S(1)} %reshape_reshape.70, f32[2,384]{1,0:T(2,128)S(1)} %copy-done.169, f32[1728,384]{1,0:T(8,128)} %bitcast.1143, f32[1,384]{1,0:T(1,128)S(1)} %reshape.1785, ...), dimensions={0} | concatenate | bytes 68222976 | tf_op jit(solution)/shard_map/concatenate | solution.py:91
  1099.5 730.3 %fusion = f32[704,384]{1,0:T(8,128)S(1)} fusion(f32[22208,384]{1,0:T(8,128)} %concatenate.134), kind=kCustom, calls=%all-reduce-scatter | all-reduce-scatter fusion | flops 8650753 | bytes 35192832
  1834.1 44.8 %psum.28 = f32[]{:T(128)} all-reduce(f32[]{:T(128)S(6)} %convert_element_type.600), channel_id=1, replica_groups=mesh['batch'=4,'rows'=8] {'batch','rows'}, use_global_device_ids=true, to_apply=%region_79.80 | all-reduce | flops 1 | bytes 8 | tf_op jit(solution)/shard_map/psum | solution.py:525
  1887.3 41.2 %all-reduce.17 = (f32[]{:T(128)}, f32[]{:T(128)}, f32[]{:T(128)}) all-reduce(f32[]{:T(128)} %multiply_reduce_fusion.13, f32[]{:T(128)} %get-tuple-element.56, f32[]{:T(128)} %get-tuple-element.55), channel_id=1, replica_groups=mesh['batch'=4,'rows'=8] {'batch','rows'}, use_global_device_ids=true, to_apply=%region_81.82 | all-reduce | flops 3 | bytes 24 | tf_op jit(solution)/shard_map/psum | solution.py:539
  (895 shorter events, 553.1 us)
Async XLA Ops:
  7.2 123.4 %all-gather.3.cloned.1.call-start = ((), (), s32[]{:S(2)}) async-start(), calls=%async_computation.1 | async-start | bytes 17639424 | tf_op jit(solution)/shard_map/all_gather | solution.py:521
  11.2 14.6 all-to-all-start
  27.5 118.4 %copy-start.92 = (f32[1,3,64,64]{2,1,3,0:T(4,128)}, f32[1,3,64,64]{2,1,3,0:T(4,128)S(1)}, u32[]{:S(2)}) copy-start(f32[1,3,64,64]{2,1,3,0:T(4,128)S(1)} %copy.482) | copy-start | bytes 147460
  147.4 89.6 %copy-start.160 = (f32[384]{0:T(512)}, f32[384]{0:T(512)S(1)}, u32[]{:S(2)}) copy-start(f32[384]{0:T(512)S(1)} %get-tuple-element.12) | copy-start | bytes 4612
  149.1 24.0 %copy-start.90 = (bf16[1728,384]{1,0:T(8,128)(2,1)}, bf16[1728,384]{1,0:T(8,128)(2,1)S(1)}, u32[]{:S(2)}) copy-start(bf16[1728,384]{1,0:T(8,128)(2,1)S(1)} %slice.619) | copy-start | bytes 3981316
  177.4 19.8 %copy-start.146 = (f32[384]{0:T(512)}, f32[384]{0:T(512)S(1)}, u32[]{:S(2)}) copy-start(f32[384]{0:T(512)S(1)} %get-tuple-element.65) | copy-start | bytes 4612
  177.4 32.4 %copy-start.120 = (f32[384]{0:T(512)}, f32[384]{0:T(512)S(1)}, u32[]{:S(2)}) copy-start(f32[384]{0:T(512)S(1)} %get-tuple-element.64) | copy-start | bytes 4612
  177.4 44.6 %copy-start.134 = (f32[384]{0:T(512)}, f32[384]{0:T(512)S(1)}, u32[]{:S(2)}) copy-start(f32[384]{0:T(512)S(1)} %get-tuple-element.66) | copy-start | bytes 4612
  177.4 44.6 %copy-start.150 = (f32[384]{0:T(512)}, f32[384]{0:T(512)S(1)}, u32[]{:S(2)}) copy-start(f32[384]{0:T(512)S(1)} %get-tuple-element.63) | copy-start | bytes 4612
  177.5 32.3 %copy-start.136 = (f32[384]{0:T(512)}, f32[384]{0:T(512)S(1)}, u32[]{:S(2)}) copy-start(f32[384]{0:T(512)S(1)} %get-tuple-element.68) | copy-start | bytes 4612
  179.4 42.6 %copy-start.8 = (f32[32,8,4,384]{3,1,2,0:T(8,128)}, f32[32,8,4,384]{3,1,2,0:T(8,128)S(1)}, u32[]{:S(2)}) copy-start(f32[32,8,4,384]{3,1,2,0:T(8,128)S(1)} %get-tuple-element.117) | copy-start | bytes 4718596
  247.0 15.8 copy-start.15
  289.8 196.1 %copy-start.122 = (f32[576]{0:T(1024)}, f32[576]{0:T(1024)S(1)}, u32[]{:S(2)}) copy-start(f32[576]{0:T(1024)S(1)} %get-tuple-element.200) | copy-start | bytes 6916
  465.1 20.8 %slice-start.4 = ((s8[6291456]{0:T(1024)(128)(4,1)}), s8[2097152]{0:T(1024)(128)(4,1)S(1)}, s32[]{:S(2)}) async-start(s8[6291456]{0:T(1024)(128)(4,1)} %bitcast.1066), calls=%async_computation.6 | async-start | bytes 4194304
  466.4 19.5 slice-start.5
  534.9 14.2 slice-start
  534.9 15.5 slice-start.2
  534.9 16.6 slice-start.3
  755.8 40.6 %copy-start.68 = (bf16[32,32,384]{2,1,0:T(8,128)(2,1)S(1)}, bf16[32,32,384]{2,1,0:T(8,128)(2,1)}, u32[]{:S(2)}) copy-start(bf16[32,32,384]{2,1,0:T(8,128)(2,1)} %copy-done.67) | copy-start | bytes 2359300
  799.0 15.9 slice-start.11
  1829.8 50.4 %copy-start.42 = (f32[704,384]{1,0:T(8,128)}, f32[704,384]{1,0:T(8,128)S(1)}, u32[]{:S(2)}) copy-start(f32[704,384]{1,0:T(8,128)S(1)} %fusion) | copy-start | bytes 3244036
  1829.8 49.2 %copy-start.52 = (f32[266496]{0:T(1024)S(1)}, f32[266496]{0:T(1024)}, u32[]{:S(2)}) copy-start(f32[266496]{0:T(1024)} %broadcast_multiply_fusion.2) | copy-start | bytes 3197956
  1830.6 50.8 %collective-permute-start = (f32[310,384]{1,0:T(8,128)}, f32[310,384]{1,0:T(8,128)}, u32[]{:S(2)}, u32[]{:S(2)}) collective-permute-start(f32[310,384]{1,0:T(8,128)} %slice.702), channel_id=1, source_target_pairs={{0,1},{1,2},{2,3},{3,4},{4,5},{5,6},{6,7},{7,8},{8,9},{9,10},{10,1... | collective-permute-start | bytes 1428488
  1881.4 47.8 %copy-start.39 = (f32[694,384]{1,0:T(8,128)S(1)}, f32[694,384]{1,0:T(8,128)}, u32[]{:S(2)}) copy-start(f32[694,384]{1,0:T(8,128)} %copy-done.38) | copy-start | bytes 3197956
  (175 other events, 543.6 us)
Sparse Core Ops, SparseCore 0:
  11.5 119.0 all-gather.2

commit v2 on v1

v2 whole, which is shorter than its diff:
```python
import functools
import math

import jax
import jax.numpy as jnp
from jax import lax
from jax.experimental import pallas as pl
from jax.experimental.pallas import tpu as pltpu
from jax.sharding import Mesh
from jax.sharding import PartitionSpec as P

IN_CH = 3
C0 = 192
CH = 384
TEMB = 768
HEADS = 4
HEAD_DIM = 96
GROUPS = 32
OUT_CH = 6
DIFF_STEPS = 4000
BLOCKS = 2
STEP = 10

cosine_offset = 0.008
kl_weight = 0.001
clip_limit = 0.05
learn_rate = 0.05
decay_first = 0.9
decay_second = 0.999
weight_decay = 0.01
narrow = jnp.bfloat16
f32 = jnp.float32


def segments():
    return [
        ("stem_w", (3, 3, IN_CH, C0)),
        ("stem_b", (C0,)),
        ("time1_w", (C0, TEMB)),
        ("time1_b", (TEMB,)),
        ("time2_w", (TEMB, TEMB)),
        ("time2_b", (TEMB,)),
        ("down_w", (3, 3, C0, CH)),
        ("down_b", (CH,)),
        ("res_w", (BLOCKS, 2, 3, 3, CH, CH)),
        ("res_b", (BLOCKS, 2, CH)),
        ("emb_w", (BLOCKS, TEMB, 2 * CH)),
        ("emb_b", (BLOCKS, 2 * CH)),
        ("res_gain", (BLOCKS, 2, CH)),
        ("res_shift", (BLOCKS, 2, CH)),
        ("attn_gain", (CH,)),
        ("attn_shift", (CH,)),
        ("qkv_w", (CH, 3 * CH)),
        ("qv_b", (2 * CH,)),
        ("proj_w", (CH, CH)),
        ("proj_b", (CH,)),
        ("head_gain", (C0 + CH,)),
        ("head_shift", (C0 + CH,)),
        ("head_w", (3, 3, C0 + CH, OUT_CH)),
        ("head_b", (OUT_CH,)),
    ]


WIDE = 384
TILE = 16
LEAD = 13
ROW = {}
offset = 0
for name, shape in segments():
    ROW[name] = offset // WIDE
    offset += math.prod(shape)
RES = ROW["res_w"]+LEAD
TAIL = ROW["res_b"]


def plan(steps):
    timef = steps.astype(jnp.float32)
    angle = math.pi / 2.0 / (1.0 + cosine_offset)
    theta = (timef / DIFF_STEPS + cosine_offset) * angle
    before = ((timef - 1.0) / DIFF_STEPS + cosine_offset) * angle
    anchor = cosine_offset * angle
    base = math.cos(anchor) ** 2
    signal = jnp.cos(theta) ** 2 / base
    one_minus = jnp.sin(theta + anchor) * jnp.sin(timef / DIFF_STEPS * angle) / base
    one_prev = jnp.sin(before + anchor) * jnp.sin((timef - 1.0) / DIFF_STEPS * angle) / base
    beta = jnp.sin(theta + before) * math.sin(angle / DIFF_STEPS) / jnp.cos(before) ** 2
    alpha = 1.0 - beta
    tilde = beta * one_prev / one_minus
    return (signal, one_minus, beta, alpha, tilde)


def silu(value):
    return value * jax.nn.sigmoid(value)


def silu_grad(value):
    gate = jax.nn.sigmoid(value)
    return gate * (1.0 + value * (1.0 - gate))


def precise(left, right):
    return jnp.dot(left, right, precision=lax.Precision.HIGHEST)


SIDE=32; PIX=SIDE*SIDE
LIMIT=60*1024*1024
VM=pltpu.VMEM

def call(kernel, ins, outs, scratch, flops, away=(), away_out=(), alias={}):
    spec = pl.BlockSpec(memory_space=VM)
    places = [pl.BlockSpec(memory_space=pl.ANY) if i in away else spec for i in range(len(ins))]
    moved = sum(a.size*a.dtype.itemsize for a in ins) + sum(math.prod(o.shape)*o.dtype.itemsize for o in outs)
    return pl.pallas_call(
        kernel, out_shape=outs, in_specs=places,
        out_specs=[pl.BlockSpec(memory_space=pl.ANY) if i in away_out else spec for i in range(len(outs))],
        scratch_shapes=scratch, input_output_aliases=alias,
        compiler_params=pltpu.CompilerParams(vmem_limit_bytes=LIMIT),
        cost_estimate=pl.CostEstimate(flops=flops, bytes_accessed=moved, transcendentals=0),
    )(*ins)

def sds(shape, dtype=f32): return jax.ShapeDtypeStruct(shape, dtype)

def dot(a, b): return jnp.dot(a, b, preferred_element_type=f32)
def dot_nt(a, b): return lax.dot_general(a, b, (((1,), (1,)), ((), ())), preferred_element_type=f32)

def sigmoid(v): return 1.0 / (1.0 + jnp.exp(-v))

def membership(chans, per, first=0):
    c = lax.broadcasted_iota(jnp.int32, (chans, 128), 0) + first
    g = lax.broadcasted_iota(jnp.int32, (chans, 128), 1)
    return ((c >= g*per) & (c < (g+1)*per)).astype(f32).astype(narrow)

def three(v):
    hi = v.astype(narrow); rest = v - hi.astype(f32)
    mid = rest.astype(narrow); low = (rest - mid.astype(f32)).astype(narrow)
    return hi, mid, low

def exact(v, ones):
    return sum(dot(p, ones) for p in three(v))
def exact_nt(v, ones):
    return sum(dot_nt(p, ones) for p in three(v))

def group_totals(stats, member):
    return exact_nt(exact(stats, member), member)

def fold(v):
    return jnp.sum(v.reshape(-1, 8, v.shape[-1]), axis=0)

def rows_of(*rows):
    r = jnp.concatenate(rows, axis=0)
    return jnp.concatenate([r, jnp.zeros((8-r.shape[0], r.shape[1]), f32)], axis=0)

def norm_stats(s1, s2, member, amount):
    stats = rows_of(jnp.sum(s1, axis=0, keepdims=True), jnp.sum(s2, axis=0, keepdims=True))
    tot = group_totals(stats, member) / amount
    mean = tot[0:1]
    return mean, lax.rsqrt(tot[1:2] - mean*mean + 1e-05)

EL=128
def steps(n, body, init=None):
    return lax.fori_loop(0, n, body, init)

def pixel_column(rows, width):
    return lax.broadcasted_iota(jnp.int32, (rows, width), 0) % SIDE

def spread(pad_ref, out_ref, width, backward):
    zero = jnp.zeros((SIDE, 3*width), narrow)
    out_ref[0:SIDE, :] = zero
    out_ref[SIDE+PIX:SIDE+PIX+SIDE, :] = zero
    col = pixel_column(EL, width)
    for r in range(0, PIX, EL):
        before = jnp.where(col == 0, 0.0, pad_ref[r+7:r+7+EL, :]).astype(narrow)
        after = jnp.where(col == SIDE-1, 0.0, pad_ref[r+9:r+9+EL, :]).astype(narrow)
        mid = pad_ref[r+8:r+8+EL, :].astype(narrow)
        first, last = (after, before) if backward else (before, after)
        out_ref[r+SIDE:r+SIDE+EL, 0:width] = first
        out_ref[r+SIDE:r+SIDE+EL, width:2*width] = mid
        out_ref[r+SIDE:r+SIDE+EL, 2*width:3*width] = last

MC=1024
def conv_rows(xs_ref, w_ref, base, r):
    acc = dot(xs_ref[pl.ds(r, MC), :], w_ref[base:base+3*CH, :])
    acc += dot(xs_ref[pl.ds(r+SIDE, MC), :], w_ref[base+3*CH:base+6*CH, :])
    return acc + dot(xs_ref[pl.ds(r+2*SIDE, MC), :], w_ref[base+6*CH:base+9*CH, :])

TAPS=9*CH
def fetch(whole_ref, base, w_ref, sems, order):
    copies = []
    for i in order:
        copy = pltpu.make_async_copy(whole_ref.at[base+i*TAPS:base+(i+1)*TAPS, :], w_ref.at[i*TAPS:(i+1)*TAPS, :], sems.at[i])
        copy.start()
        copies.append(copy)
    return copies

def block_forward_kernel(base, state_ref, whole_ref, vec_ref, out_ref, inner_ref, stat_ref, pad_ref, xs_ref, w_ref, sems):
    first_in, second_in = fetch(whole_ref, base, w_ref, sems, (0, 1))
    bias1, bias2, gain1, shift1, gain2, shift2, scale, offset = (vec_ref[i:i+1, :] for i in range(8))
    member = membership(CH, CH//GROUPS)
    amount = PIX*(CH//GROUPS)
    def sums(i, c):
        v = state_ref[pl.ds(pl.multiple_of(i*EL, EL), EL), :]
        return c[0]+fold(v), c[1]+fold(v*v)
    z = jnp.zeros((8, CH), f32)
    mean1, inv1 = norm_stats(*steps(PIX//EL, sums, (z, z)), member, amount)
    def act1(i, _):
        r = pl.multiple_of(i*EL, EL)
        v = (state_ref[pl.ds(r, EL), :] - mean1)*inv1*gain1 + shift1
        pad_ref[pl.ds(r+8, EL), :] = v*sigmoid(v)
        return _
    steps(PIX//EL, act1, 0)
    spread(pad_ref, xs_ref, CH, False)
    first_in.wait()
    def conv1(i, c):
        r = pl.multiple_of(i*MC, MC)
        v = conv_rows(xs_ref, w_ref, 0, r) + bias1
        inner_ref[pl.ds(r, MC), :] = v
        return c[0]+fold(v), c[1]+fold(v*v)
    mean2, inv2 = norm_stats(*steps(PIX//MC, conv1, (z, z)), member, amount)
    def act2(i, _):
        r = pl.multiple_of(i*EL, EL)
        v = (inner_ref[pl.ds(r, EL), :] - mean2)*inv2*gain2 + shift2
        v = v*scale + offset
        pad_ref[pl.ds(r+8, EL), :] = v*sigmoid(v)
        return _
    steps(PIX//EL, act2, 0)
    spread(pad_ref, xs_ref, CH, False)
    second_in.wait()
    def conv2(i, _):
        r = pl.multiple_of(i*MC, MC)
        out_ref[pl.ds(r, MC), :] = state_ref[pl.ds(r, MC), :] + (conv_rows(xs_ref, w_ref, TAPS, r) + bias2)
        return _
    steps(PIX//MC, conv2, 0)
    stat_ref[...] = rows_of(mean1, inv1, mean2, inv2)

def block_forward(state, whole, base, vectors):
    return call(functools.partial(block_forward_kernel, base), [state, whole, vectors],
        [sds((PIX, CH)), sds((PIX, CH)), sds((8, CH))],
        [pltpu.VMEM((PIX+16, CH), f32), pltpu.VMEM((PIX+2*SIDE, 3*CH), narrow), pltpu.VMEM((2*TAPS, CH), narrow),
         pltpu.SemaphoreType.DMA((2,))], 2*2*PIX*TAPS*CH, away=(1,))

def back_taps(gs_ref, w_ref, base, r):
    acc = None
    for dy in range(3):
        for dx in range(3):
            part = dot_nt(gs_ref[pl.ds(r+SIDE*(2-dy), MC), dx*CH:(dx+1)*CH],
                          w_ref[base+(3*dy+dx)*CH:base+(3*dy+dx+1)*CH, :])
            acc = part if acc is None else acc+part
    return acc

def kernel_grads(xt_ref, gs_ref, dw_ref, base):
    def body(dy, _):
        r = pl.multiple_of(SIDE*(2-dy), SIDE)
        for dx in range(3):
            at = (base+(3*dy+dx)*CH)//TILE
            value = dot(xt_ref[...], gs_ref[pl.ds(r, PIX), dx*CH:(dx+1)*CH])
            dw_ref[pl.ds(at, CH//TILE)] = value.astype(dw_ref.dtype).reshape(CH//TILE, TILE, CH)
        return _
    steps(3, body, 0)

def block_back_kernel(base, grad_ref, state_ref, inner_ref, stat_ref, whole_ref, vec_ref, large_in_ref, out_ref, large_ref, small_ref,
                      pad_ref, gs_ref, xt_ref, keep_ref, w_ref, dw_ref, sems):
    second_in, first_in = fetch(whole_ref, base, w_ref, sems, (1, 0))
    bias1, bias2, gain1, shift1, gain2, shift2, scale, offset = (vec_ref[i:i+1, :] for i in range(8))
    mean1, inv1, mean2, inv2 = (stat_ref[i:i+1, :] for i in range(4))
    member = membership(CH, CH//GROUPS)
    amount = PIX*(CH//GROUPS)
    z = jnp.zeros((8, CH), f32)
    def low(i, c):
        r = pl.multiple_of(i*EL, EL)
        g = grad_ref[pl.ds(r, EL), :].astype(narrow).astype(f32)
        pad_ref[pl.ds(r+8, EL), :] = g
        return c+fold(g)
    bias2_grad = steps(PIX//EL, low, z)
    spread(pad_ref, gs_ref, CH, True)
    for i in range(PIX//EL):
        r = i*EL
        v = (inner_ref[r:r+EL, :] - mean2)*inv2*gain2 + shift2
        v = v*scale + offset
        xt_ref[:, r:r+EL] = jnp.transpose(v*sigmoid(v)).astype(narrow)
    kernel_grads(xt_ref, gs_ref, dw_ref, TAPS)
    half = TAPS//TILE
    second_out = pltpu.make_async_copy(dw_ref.at[half:2*half], large_ref.at[base//TILE+half:base//TILE+2*half], sems.at[2])
    second_out.start()
    second_in.wait()
    def back2(i, c):
        r = pl.multiple_of(i*MC, MC)
        d = back_taps(gs_ref, w_ref, TAPS, r)
        n = (inner_ref[pl.ds(r, MC), :] - mean2)*inv2
        nt = n*gain2 + shift2
        v = nt*scale + offset
        s = sigmoid(v)
        d = d*(s*(1.0+v*(1.0-s)))
        keep_ref[pl.ds(r, MC), :] = d
        return c[0]+fold(d*nt), c[1]+fold(d), c[2]+fold(d*n)
    mod_scale, mod_offset, dn = steps(PIX//MC, back2, (z, z, z))
    one = lambda v: jnp.sum(v, axis=0, keepdims=True)
    mod_scale, mod_offset, dn = one(mod_scale), one(mod_offset), one(dn)
    tot = group_totals(rows_of(mod_offset*scale*gain2, dn*scale*gain2), member)/amount
    first, second = tot[0:1], tot[1:2]
    def inner_back(i, c):
        r = pl.multiple_of(i*EL, EL)
        n = (inner_ref[pl.ds(r, EL), :] - mean2)*inv2
        g = (keep_ref[pl.ds(r, EL), :]*scale*gain2 - first - n*second)*inv2
        g = g.astype(narrow).astype(f32)
        pad_ref[pl.ds(r+8, EL), :] = g
        return c+fold(g)
    bias1_grad = steps(PIX//EL, inner_back, z)
    spread(pad_ref, gs_ref, CH, True)
    for i in range(PIX//EL):
        r = i*EL
        v = (state_ref[r:r+EL, :] - mean1)*inv1*gain1 + shift1
        xt_ref[:, r:r+EL] = jnp.transpose(v*sigmoid(v)).astype(narrow)
    kernel_grads(xt_ref, gs_ref, dw_ref, 0)
    first_out = pltpu.make_async_copy(dw_ref.at[0:half], large_ref.at[base//TILE:base//TILE+half], sems.at[3])
    first_out.start()
    first_in.wait()
    def back1(i, c):
        r = pl.multiple_of(i*MC, MC)
        d = back_taps(gs_ref, w_ref, 0, r)
        n = (state_ref[pl.ds(r, MC), :] - mean1)*inv1
        v = n*gain1 + shift1
        s = sigmoid(v)
        d = d*(s*(1.0+v*(1.0-s)))
        keep_ref[pl.ds(r, MC), :] = d
        return c[0]+fold(d), c[1]+fold(d*n)
    shift1_grad, gain1_grad = (one(v) for v in steps(PIX//MC, back1, (z, z)))
    tot = group_totals(rows_of(shift1_grad*gain1, gain1_grad*gain1), member)/amount
    first1, second1 = tot[0:1], tot[1:2]
    def state_back(i, _):
        r = pl.multiple_of(i*EL, EL)
        n = (state_ref[pl.ds(r, EL), :] - mean1)*inv1
        out_ref[pl.ds(r, EL), :] = grad_ref[pl.ds(r, EL), :] + (keep_ref[pl.ds(r, EL), :]*gain1 - first1 - n*second1)*inv1
        return _
    steps(PIX//EL, state_back, 0)
    first_out.wait()
    second_out.wait()
    small_ref[...] = jnp.concatenate([one(bias1_grad), one(bias2_grad), gain1_grad, dn*scale, shift1_grad, mod_offset*scale, mod_scale, mod_offset], axis=0)

def block_back(grad, state, inner, stat, whole, base, vectors, large):
    return call(functools.partial(block_back_kernel, base), [grad, state, inner, stat, whole, vectors, large],
        [sds((PIX, CH)), sds(large.shape, narrow), sds((8, CH))],
        [pltpu.VMEM((PIX+16, CH), f32), pltpu.VMEM((PIX+2*SIDE, 3*CH), narrow), pltpu.VMEM((CH, PIX), narrow),
         pltpu.VMEM((PIX, CH), f32), pltpu.VMEM((2*TAPS, CH), narrow), pltpu.VMEM((2*TAPS//TILE, TILE, CH), narrow),
         pltpu.SemaphoreType.DMA((4,))], 2*4*PIX*TAPS*CH, away=(4, 6), away_out=(1,), alias={6: 1})

PHASES = [(0, 0), (0, 1), (1, 0), (1, 1)]
OFFSETS = [(dy, dx) for dy in (-1, 0, 1) for dx in (-1, 0, 1)]

def source(a, b, dy, dx):
    return 2*((a+dy) % 2) + (b+dx) % 2, (a+dy)//2, (b+dx)//2

def shift_lanes(v, di, dj):
    if di == 0 and dj == 0:
        return v
    moved = pltpu.roll(v, (-(SIDE*di+dj)) % PIX, 1)
    p = lax.broadcasted_iota(jnp.int32, v.shape, 1)
    i, j = p // SIDE + di, p % SIDE + dj
    return jnp.where((i >= 0) & (i < SIDE) & (j >= 0) & (j < SIDE), moved, 0.0)

def stack(phases, a, b, sign):
    rows = []
    for dy, dx in OFFSETS:
        at, di, dj = source(a, b, sign*dy, sign*dx)
        rows.append(shift_lanes(phases[at], di, dj))
    rows.append(jnp.zeros((128-72, PIX), f32))
    return jnp.concatenate(rows, axis=0)

def stem_down_kernel(noisy_ref, sw_ref, sb_ref, dw_ref, db_ref, skip_ref, state_ref, pad_ref, xs_ref):
    phases = [noisy_ref[i] for i in range(4)]
    col = pixel_column(EL, C0)
    xs_ref[:, 0:SIDE, :] = jnp.zeros((6, SIDE, C0), narrow)
    for a, b in PHASES:
        rows = jnp.transpose(stack(phases, a, b, 1)).astype(narrow)
        v = (dot(rows, sw_ref[...]) + sb_ref[...]).astype(narrow)
        skip_ref[2*a+b] = v
        if b == 0:
            xs_ref[3*a+1, SIDE:SIDE+PIX, :] = v
        else:
            xs_ref[3*a+2, SIDE:SIDE+PIX, :] = v
            pad_ref[8:8+PIX, :] = v.astype(f32)
            for r in range(0, PIX, EL):
                xs_ref[3*a, SIDE+r:SIDE+r+EL, :] = jnp.where(col == 0, 0.0, pad_ref[r+7:r+7+EL, :]).astype(narrow)
    acc = None
    for t, (dy, dx) in enumerate(OFFSETS):
        top = 0 if dy == -1 else SIDE
        part = dot(xs_ref[3*(dy % 2)+dx+1, top:top+PIX, :], dw_ref[t*C0:(t+1)*C0, :])
        acc = part if acc is None else acc+part
    state_ref[...] = acc + db_ref[...]

def stem_down(noisy, stem_w, stem_b, down_w, down_b):
    return call(stem_down_kernel, [noisy, stem_w, stem_b, down_w, down_b],
        [sds((4, PIX, C0), narrow), sds((PIX, CH))],
        [pltpu.VMEM((PIX+16, C0), f32), pltpu.VMEM((6, PIX+SIDE, C0), narrow)], 2*PIX*9*C0*CH)

def down_stem_back_kernel(grad_ref, skip_ref, more_ref, dw_ref, noisy_ref, large_in_ref, large_ref, sdw_ref, small_ref, small_s_ref,
                          pad_ref, gs_ref, ddw_ref, low_ref, sems):
    top_row = ROW["down_w"]+LEAD
    spare = top_row % TILE
    ddw_ref[0:TILE, :] = jnp.zeros((TILE, CH), f32)
    ddw_ref[9*C0:9*C0+TILE, :] = jnp.zeros((TILE, CH), f32)
    z = jnp.zeros((8, CH), f32)
    gs_ref[:, PIX:PIX+SIDE, :] = jnp.zeros((2, SIDE, CH), narrow)
    col = pixel_column(EL, CH)
    total = z
    pad_ref[PIX:PIX+16, :] = jnp.zeros((16, CH), f32)
    for r in range(0, PIX, EL):
        g = grad_ref[r:r+EL, :].astype(narrow)
        gs_ref[0, r:r+EL, :] = g
        g = g.astype(f32)
        pad_ref[r:r+EL, :] = g
        total += fold(g)
    for r in range(0, PIX, EL):
        gs_ref[1, r:r+EL, :] = jnp.where(col == SIDE-1, 0.0, pad_ref[r+1:r+1+EL, :]).astype(narrow)
    small_ref[...] = rows_of(jnp.sum(total, axis=0, keepdims=True))
    def shifted(dy, dx):
        top = SIDE if dy == -1 else 0
        return gs_ref[1 if dx == -1 else 0, top:top+PIX, :]
    phases = [noisy_ref[i] for i in range(4)]
    stem_grad, stem_bias = None, None
    for a, b in PHASES:
        turned = jnp.transpose(skip_ref[2*a+b].astype(f32)).astype(narrow)
        more = more_ref[2*a+b]
        for t, (dy, dx) in enumerate(OFFSETS):
            if (dy % 2, dx % 2) == (a, b):
                g = shifted(dy, dx)
                ddw_ref[spare+t*C0:spare+(t+1)*C0, :] = dot(turned, g)
                more += dot_nt(g, dw_ref[t*C0:(t+1)*C0, :])
        low = more.astype(narrow)
        part = dot(stack(phases, a, b, 1).astype(narrow), low)
        stem_grad = part if stem_grad is None else stem_grad+part
        part = fold(low.astype(f32))
        stem_bias = part if stem_bias is None else stem_bias+part
    for r in range(0, 9*C0+TILE, 16*TILE):
        end = min(r+16*TILE, 9*C0+TILE)
        low_ref[r//TILE:end//TILE] = ddw_ref[r:end, :].astype(narrow).reshape((end-r)//TILE, TILE, CH)
    copy = pltpu.make_async_copy(low_ref, large_ref.at[top_row//TILE:top_row//TILE+9*C0//TILE+1], sems.at[0])
    copy.start()
    copy.wait()
    sdw_ref[...] = stem_grad
    small_s_ref[...] = rows_of(jnp.sum(stem_bias, axis=0, keepdims=True))

def down_stem_back(grad, skip, more, down_w, noisy, large):
    return call(down_stem_back_kernel, [grad, skip, more, down_w, noisy, large],
        [sds(large.shape, narrow), sds((128, C0)), sds((8, CH)), sds((8, C0))],
        [pltpu.VMEM((PIX+16, CH), f32), pltpu.VMEM((2, PIX+SIDE, CH), narrow), pltpu.VMEM((9*C0+TILE, CH), f32),
         pltpu.VMEM((9*C0//TILE+1, TILE, CH), narrow), pltpu.SemaphoreType.DMA((1,))],
        2*2*PIX*9*C0*CH, away=(5,), away_out=(0,), alias={5: 0})

HEAD_PER = (C0+CH)//GROUPS
def silu_slope(v):
    s = sigmoid(v)
    return s*(1.0+v*(1.0-s))

KL = 0.001
def head_kernel(num_ref, state_ref, skip_ref, wu_ref, ws_ref, vu_ref, vs_ref, bias_ref, noise_ref, mask_ref,
                state_grad_ref, skip_grad_ref, gu_ref, gs_ref, small_u_ref, small_s_ref, gb_ref, loss_ref,
                up_ref, side_ref, q_ref):
    log_beta, log_tilde, coefficient, sample = (num_ref[i] for i in range(4))
    gain_u, shift_u = vu_ref[0:1, :], vu_ref[1:2, :]
    gain_s, shift_s = vs_ref[0:1, :], vs_ref[1:2, :]
    mu, ms = membership(CH, HEAD_PER), membership(C0, HEAD_PER, CH)
    amount = 4*PIX*HEAD_PER
    one = lambda v: jnp.sum(v, axis=0, keepdims=True)
    zu, zs = jnp.zeros((8, CH), f32), jnp.zeros((8, C0), f32)
    def sums_u(i, c):
        v = state_ref[pl.ds(pl.multiple_of(i*EL, EL), EL), :]
        return c[0]+fold(v), c[1]+fold(v*v)
    u1, u2 = steps(PIX//EL, sums_u, (zu, zu))
    s1, s2 = zs, zs
    for k in range(4):
        def sums_s(i, c):
            v = skip_ref[k, pl.ds(pl.multiple_of(i*EL, EL), EL), :].astype(f32)
            return c[0]+fold(v), c[1]+fold(v*v)
        s1, s2 = steps(PIX//EL, sums_s, (s1, s2))
    tot = (exact(rows_of(4.0*one(u1), 4.0*one(u2)), mu) + exact(rows_of(one(s1), one(s2)), ms))/amount
    tot_u, tot_s = exact_nt(tot, mu), exact_nt(tot, ms)
    mean_u, inv_u = tot_u[0:1], lax.rsqrt(tot_u[1:2]-tot_u[0:1]*tot_u[0:1]+1e-05)
    mean_s, inv_s = tot_s[0:1], lax.rsqrt(tot_s[1:2]-tot_s[0:1]*tot_s[0:1]+1e-05)
    def act_u(i, _):
        r = pl.ds(pl.multiple_of(i*EL, EL), EL)
        v = (state_ref[r, :]-mean_u)*inv_u*gain_u+shift_u
        up_ref[r, :] = (v*sigmoid(v)).astype(narrow)
        return _
    steps(PIX//EL, act_u, 0)
    for k in range(4):
        def act_s(i, _):
            r = pl.ds(pl.multiple_of(i*EL, EL), EL)
            v = (skip_ref[k, r, :].astype(f32)-mean_s)*inv_s*gain_s+shift_s
            side_ref[k, r, :] = (v*sigmoid(v)).astype(narrow)
            return _
        steps(PIX//EL, act_s, 0)
    from_up = dot_nt(wu_ref[...], up_ref[...])
    for k in range(4):
        q_ref[k] = from_up + dot_nt(ws_ref[...], side_ref[k])
    row = lax.broadcasted_iota(jnp.int32, (8, PIX), 0)
    loss, vlb, outs, bias_grad = jnp.zeros((1, PIX), f32), jnp.zeros((1, PIX), f32), [], jnp.zeros((8, PIX), f32)
    for a, b in PHASES:
        out = jnp.zeros((8, PIX), f32)
        for t, (dy, dx) in enumerate(OFFSETS):
            at, di, dj = source(a, b, dy, dx)
            out += shift_lanes(q_ref[at, 8*t:8*t+8, :], di, dj)
        out += bias_ref[:, 0:1]
        k = 2*a+b
        error = jnp.where(row < 3, out - noise_ref[k], 0.0)
        fraction = jnp.where(row < 3, (pltpu.roll(out, 5, 0)+1.0)/2.0, 0.0)
        log_var = fraction*log_beta + (1.0-fraction)*log_tilde
        inverse = jnp.exp(-log_var)
        ratio = jnp.exp(log_tilde-log_var)
        divergence = 0.5*(-1.0+log_var-log_tilde+ratio+coefficient*error*error*inverse)
        divergence = jnp.where(row < 3, divergence, 0.0)
        weight = sample*mask_ref[k]
        loss += weight*jnp.sum(error*error+KL*divergence, axis=0, keepdims=True)
        vlb += weight*KL*jnp.sum(divergence, axis=0, keepdims=True)
        predict = weight*(2.0*error+KL*coefficient*error*inverse)
        var_grad = weight*KL*0.5*(1.0-ratio-coefficient*error*error*inverse)*(log_beta-log_tilde)/2.0
        og = jnp.where(row < 3, predict, jnp.where(row < 6, pltpu.roll(var_grad, 3, 0), 0.0))
        og = og.astype(narrow).astype(f32)
        bias_grad += og
        outs.append(og)
    gb_ref[...] = jnp.broadcast_to(jnp.sum(bias_grad, axis=1, keepdims=True), (8, 128))
    loss_ref[...] = jnp.concatenate([jnp.broadcast_to(jnp.sum(loss, axis=1, keepdims=True), (1, 128)),
        jnp.broadcast_to(jnp.sum(vlb, axis=1, keepdims=True), (1, 128)), jnp.zeros((6, 128), f32)], axis=0)
    nine_sum, gs_total = None, None
    d1, d2 = zs, zs
    for a, b in PHASES:
        k = 2*a+b
        nine = stack(outs, a, b, -1)
        nine_sum = nine if nine_sum is None else nine_sum+nine
        part = dot(nine.astype(narrow), side_ref[k])
        gs_total = part if gs_total is None else gs_total+part
        d = dot(jnp.transpose(nine).astype(narrow), ws_ref[...])
        n = (skip_ref[k].astype(f32)-mean_s)*inv_s
        d = d*silu_slope(n*gain_s+shift_s)
        skip_grad_ref[k] = d
        d1, d2 = d1+fold(d), d2+fold(d*n)
    gs_ref[...] = gs_total
    hi = nine_sum.astype(narrow); lo = (nine_sum-hi.astype(f32)).astype(narrow)
    gu_ref[...] = dot(hi, up_ref[...])+dot(lo, up_ref[...])
    turned = jnp.transpose(nine_sum)
    hi = turned.astype(narrow); lo = (turned-hi.astype(f32)).astype(narrow)
    d = dot(hi, wu_ref[...])+dot(lo, wu_ref[...])
    n = (state_ref[...]-mean_u)*inv_u
    d = d*silu_slope(n*gain_u+shift_u)
    state_grad_ref[...] = d
    e1, e2 = one(fold(d)), one(fold(d*n))
    d1, d2 = one(d1), one(d2)
    small_u_ref[...] = rows_of(e2, e1)
    small_s_ref[...] = rows_of(d2, d1)
    tot = (exact(rows_of(e1*gain_u, e2*gain_u), mu)+exact(rows_of(d1*gain_s, d2*gain_s), ms))/amount
    tot_u, tot_s = exact_nt(tot, mu), exact_nt(tot, ms)
    def back_u(i, _):
        r = pl.ds(pl.multiple_of(i*EL, EL), EL)
        n = (state_ref[r, :]-mean_u)*inv_u
        state_grad_ref[r, :] = (state_grad_ref[r, :]*gain_u-4.0*tot_u[0:1]-4.0*n*tot_u[1:2])*inv_u
        return _
    steps(PIX//EL, back_u, 0)
    for k in range(4):
        def back_s(i, _):
            r = pl.ds(pl.multiple_of(i*EL, EL), EL)
            n = (skip_ref[k, r, :].astype(f32)-mean_s)*inv_s
            skip_grad_ref[k, r, :] = (skip_grad_ref[k, r, :]*gain_s-tot_s[0:1]-n*tot_s[1:2])*inv_s
            return _
        steps(PIX//EL, back_s, 0)

def head(numbers, state, skip, wu, ws, vu, vs, bias, noise, mask):
    spec = pl.BlockSpec(memory_space=VM)
    ins = [numbers, state, skip, wu, ws, vu, vs, bias, noise, mask]
    outs = [sds((PIX, CH)), sds((4, PIX, C0)), sds((128, CH)), sds((128, C0)), sds((8, CH)), sds((8, C0)), sds((8, 128)), sds((8, 128))]
    return pl.pallas_call(head_kernel, out_shape=outs,
        in_specs=[pl.BlockSpec(memory_space=pltpu.SMEM)]+[spec]*(len(ins)-1), out_specs=[spec]*len(outs),
        scratch_shapes=[pltpu.VMEM((PIX, CH), narrow), pltpu.VMEM((4, PIX, C0), narrow), pltpu.VMEM((4, 128, PIX), f32)],
        compiler_params=pltpu.CompilerParams(vmem_limit_bytes=LIMIT),
        cost_estimate=pl.CostEstimate(flops=4*2*PIX*128*(4*C0+CH), bytes_accessed=12*2**20, transcendentals=0))(*ins)

HP = 128
QW = HEADS*HP
SCALE = 1.0/math.sqrt(HEAD_DIM)
QC = 256
ATTN_FIRST = (ROW["attn_gain"]+LEAD)//TILE
ATTN_TILES = -(-(ROW["proj_b"]+LEAD+1)//TILE)-ATTN_FIRST
ATTN = {name: ROW[name]+LEAD-ATTN_FIRST*TILE for name in ("attn_gain", "attn_shift", "qkv_w", "qv_b", "proj_w", "proj_b")}

def get_rows(ref, at):
    return jnp.concatenate([ref[i, at, :] for i in range(3)], axis=1)

def put_rows(ref, at, value):
    for i in range(3):
        ref[i, at, :] = value[:, i*128:(i+1)*128]

def attention_forward_kernel(state_ref, whole_ref, out_ref, qkv_ref, log_ref, mixed_t_ref, stat_ref, wp_ref, wo_ref, vec_ref,
                             mixed_ref, vt_ref, bp_ref, rows_ref, wide_ref, sems):
    copy = pltpu.make_async_copy(whole_ref.at[ATTN_FIRST*TILE:(ATTN_FIRST+ATTN_TILES)*TILE, :], rows_ref, sems.at[0])
    copy.start()
    copy.wait()
    for r in range(0, ATTN_TILES*TILE, 16*TILE):
        end = min(r+16*TILE, ATTN_TILES*TILE)
        put_rows(wide_ref, slice(r, end), rows_ref[r:end, :].astype(f32))
    one_row = lambda name, i=0: get_rows(wide_ref, slice(ATTN[name]+i, ATTN[name]+i+1))
    gain, shift, bias = one_row("attn_gain"), one_row("attn_shift"), one_row("proj_b")
    vec_ref[...] = rows_of(gain, shift)
    nothing = jnp.zeros((CH, HP-HEAD_DIM), f32)
    for j in range(3):
        third = get_rows(wide_ref, pl.ds(ATTN["qkv_w"]+j, CH, stride=3))
        third_bias = one_row("qv_b", j//2) if j != 1 else jnp.zeros((1, CH), f32)
        for h in range(HEADS):
            to = slice(j*QW+h*HP, j*QW+(h+1)*HP)
            wp_ref[:, to] = jnp.concatenate([third[:, h*HEAD_DIM:(h+1)*HEAD_DIM], nothing], axis=1).astype(narrow)
            bp_ref[:, to] = jnp.concatenate([third_bias[:, h*HEAD_DIM:(h+1)*HEAD_DIM], nothing[0:1]], axis=1)
    for h in range(HEADS):
        at = ATTN["proj_w"]+h*HEAD_DIM
        wo_ref[h*HP:h*HP+HEAD_DIM, :] = get_rows(wide_ref, slice(at, at+HEAD_DIM)).astype(narrow)
        wo_ref[h*HP+HEAD_DIM:(h+1)*HP, :] = jnp.zeros((HP-HEAD_DIM, CH), narrow)
    member = membership(CH, CH//GROUPS)
    def sums(i, c):
        v = state_ref[pl.ds(pl.multiple_of(i*EL, EL), EL), :]
        return c[0]+fold(v), c[1]+fold(v*v)
    z = jnp.zeros((8, CH), f32)
    mean, inv = norm_stats(*steps(PIX//EL, sums, (z, z)), member, PIX*(CH//GROUPS))
    stat_ref[...] = rows_of(mean, inv)
    def project(i, _):
        r = pl.ds(pl.multiple_of(i*256, 256), 256)
        n = ((state_ref[r, :]-mean)*inv*gain+shift).astype(narrow)
        qkv_ref[r, :] = (dot(n, wp_ref[...])+bp_ref[...]).astype(narrow)
        return _
    steps(PIX//256, project, 0)
    for h in range(HEADS):
        vt_ref[...] = jnp.transpose(qkv_ref[:, 2*QW+h*HP:2*QW+(h+1)*HP].astype(f32)).astype(narrow)
        for c in range(0, PIX, QC):
            s = dot_nt(qkv_ref[:, QW+h*HP:QW+(h+1)*HP], qkv_ref[c:c+QC, h*HP:(h+1)*HP])*SCALE
            top = jnp.max(s, axis=0, keepdims=True)
            e = jnp.exp(s-top)
            total = jnp.sum(e, axis=0, keepdims=True)
            log_ref[h:h+1, c:c+QC] = top+jnp.log(total)
            p = (e*(1.0/total)).astype(narrow)
            m = dot(vt_ref[...], p).astype(narrow)
            mixed_t_ref[h*HP:(h+1)*HP, c:c+QC] = m
            mixed_ref[c:c+QC, h*HP:(h+1)*HP] = jnp.transpose(m.astype(f32)).astype(narrow)
    log_ref[HEADS:8, :] = jnp.zeros((8-HEADS, PIX), f32)
    def finish(i, _):
        r = pl.ds(pl.multiple_of(i*256, 256), 256)
        out_ref[r, :] = state_ref[r, :]+(dot(mixed_ref[r, :], wo_ref[...])+bias)
        return _
    steps(PIX//256, finish, 0)

def attention_forward(state, whole):
    return call(attention_forward_kernel, [state, whole],
        [sds((PIX, CH)), sds((PIX, 3*QW), narrow), sds((8, PIX)), sds((QW, PIX), narrow), sds((8, CH)),
         sds((CH, 3*QW), narrow), sds((QW, CH), narrow), sds((8, CH))],
        [pltpu.VMEM((PIX, QW), narrow), pltpu.VMEM((HP, PIX), narrow), pltpu.VMEM((1, 3*QW), f32),
         pltpu.VMEM((ATTN_TILES*TILE, CH), narrow), pltpu.VMEM((3, ATTN_TILES*TILE, 128), f32), pltpu.SemaphoreType.DMA((1,))],
        2*PIX*(CH*4*QW+2*PIX*QW), away=(1,))

def attention_back_kernel(grad_ref, state_ref, stat_ref, qkv_ref, log_ref, mixed_t_ref, wp_ref, wo_ref, vec_ref,
                          out_ref, large_ref, small_ref, bias_ref, dm_ref, pg_ref, kt_ref, dv_ref, dk_ref, nt_ref, keep_ref,
                          wide_ref, rows_ref, sems):
    gain, shift = vec_ref[0:1, :], vec_ref[1:2, :]
    mean, inv = stat_ref[0:1, :], stat_ref[1:2, :]
    member = membership(CH, CH//GROUPS)
    z = jnp.zeros((8, CH), f32)
    one = lambda v: jnp.sum(v, axis=0, keepdims=True)
    def start(i, c):
        r = pl.ds(pl.multiple_of(i*256, 256), 256)
        g = grad_ref[r, :].astype(narrow)
        keep_ref[r, :] = g
        dm_ref[r, :] = dot_nt(g, wo_ref[...]).astype(narrow)
        return c+fold(g.astype(f32))
    proj_bias = steps(PIX//256, start, z)
    for name, after in (("attn_gain", ATTN["qkv_w"]), ("qv_b", ATTN["proj_w"]), ("proj_b", ATTN_TILES*TILE)):
        put_rows(wide_ref, slice(ATTN[name], after), jnp.zeros((after-ATTN[name], CH), f32))
    wo_grad = dot(mixed_t_ref[...], keep_ref[...])
    for h in range(HEADS):
        at = ATTN["proj_w"]+h*HEAD_DIM
        put_rows(wide_ref, slice(at, at+HEAD_DIM), wo_grad[h*HP:h*HP+HEAD_DIM, :])
    for h in range(HEADS):
        q0, k0, v0 = h*HP, QW+h*HP, 2*QW+h*HP
        kt_ref[...] = jnp.transpose(qkv_ref[:, k0:k0+HP].astype(f32)).astype(narrow)
        for c in range(0, PIX, QC):
            q, dm = qkv_ref[c:c+QC, q0:q0+HP], dm_ref[c:c+QC, h*HP:(h+1)*HP]
            s = dot_nt(qkv_ref[:, k0:k0+HP], q)*SCALE
            p = jnp.exp(s-log_ref[h:h+1, c:c+QC])
            dp = dot_nt(qkv_ref[:, v0:v0+HP], dm)
            delta = jnp.sum(dp*p, axis=0, keepdims=True)
            ds = (p*(dp-delta)).astype(narrow)
            dv = dot(p.astype(narrow), dm)
            dk = dot(ds, q)
            if c == 0:
                dv_ref[...] = dv
                dk_ref[...] = dk
            else:
                dv_ref[...] += dv
                dk_ref[...] += dk
            dq = dot(kt_ref[...], ds)
            pg_ref[c:c+QC, q0:q0+HP] = jnp.transpose(dq*SCALE).astype(narrow)
        pg_ref[:, k0:k0+HP] = (dk_ref[...]*SCALE).astype(narrow)
        pg_ref[:, v0:v0+HP] = dv_ref[...].astype(narrow)
    for r in range(0, PIX, 256):
        nt_ref[:, r:r+256] = jnp.transpose((state_ref[r:r+256, :]-mean)*inv*gain+shift).astype(narrow)
    for j in range(3):
        third = dot(nt_ref[...], pg_ref[:, j*QW:(j+1)*QW])
        third = jnp.concatenate([third[:, h*HP:h*HP+HEAD_DIM] for h in range(HEADS)], axis=1)
        put_rows(wide_ref, pl.ds(ATTN["qkv_w"]+j, CH, stride=3), third)
    for r in range(0, ATTN_TILES, 16):
        end = min(r+16, ATTN_TILES)
        rows_ref[r:end] = get_rows(wide_ref, slice(r*TILE, end*TILE)).astype(narrow).reshape(end-r, TILE, CH)
    copy = pltpu.make_async_copy(rows_ref, large_ref.at[ATTN_FIRST:ATTN_FIRST+ATTN_TILES], sems.at[0])
    copy.start()
    zb = jnp.zeros((8, 3*QW), f32)
    def norm_grad(i, c):
        r = pl.ds(pl.multiple_of(i*256, 256), 256)
        d = dot_nt(pg_ref[r, :], wp_ref[...])
        n = (state_ref[r, :]-mean)*inv
        out_ref[r, :] = d
        return c[0]+fold(d), c[1]+fold(d*n), c[2]+fold(pg_ref[r, :].astype(f32))
    shift_grad, gain_grad, bias_grad = (one(v) for v in steps(PIX//256, norm_grad, (z, z, zb)))
    bias_ref[...] = rows_of(bias_grad)
    tot = group_totals(rows_of(shift_grad*gain, gain_grad*gain), member)/(PIX*(CH//GROUPS))
    first, second = tot[0:1], tot[1:2]
    def finish(i, _):
        r = pl.ds(pl.multiple_of(i*EL, EL), EL)
        n = (state_ref[r, :]-mean)*inv
        out_ref[r, :] = grad_ref[r, :]+(out_ref[r, :]*gain-first-n*second)*inv
        return _
    steps(PIX//EL, finish, 0)
    small_ref[...] = rows_of(gain_grad, shift_grad, one(proj_bias))
    copy.wait()

def attention_back(grad, state, stat, qkv, log, mixed_t, wp, wo, vec, tiles):
    return call(attention_back_kernel, [grad, state, stat, qkv, log, mixed_t, wp, wo, vec],
        [sds((PIX, CH)), sds((tiles, TILE, CH), narrow), sds((8, CH)), sds((8, 3*QW))],
        [pltpu.VMEM((PIX, QW), narrow), pltpu.VMEM((PIX, 3*QW), narrow), pltpu.VMEM((HP, PIX), narrow), pltpu.VMEM((PIX, HP), f32),
         pltpu.VMEM((PIX, HP), f32), pltpu.VMEM((CH, PIX), narrow), pltpu.VMEM((PIX, CH), narrow),
         pltpu.VMEM((3, ATTN_TILES*TILE, 128), f32), pltpu.VMEM((ATTN_TILES, TILE, CH), narrow), pltpu.SemaphoreType.DMA((1,))],
        2*PIX*(CH*8*QW+5*PIX*QW), away_out=(1,))


def to_phases(v):
    c = v.shape[0]
    return jnp.transpose(v.reshape(c, SIDE, 2, SIDE, 2), (2, 4, 0, 1, 3)).reshape(4, c, PIX)


def pad_rows8(v):
    return jnp.pad(v, ((0, 0), (0, 8-v.shape[1]), (0, 0)))


def taps_rows(v):
    v = jnp.pad(v, ((0, 0), (0, 8-v.shape[1]), (0, 0))).reshape(72, v.shape[2])
    return jnp.pad(v, ((0, 128-72), (0, 0)))


def heads_unpad(v):
    v = v.reshape(v.shape[:-1]+(-1, HP))[..., :HEAD_DIM]
    return v.reshape(v.shape[:-2]+(-1,))


class Place:
    def __init__(self, sizes, share):
        self.sizes = sizes
        self.share = share
        self.total = sizes["y"]*sizes["c"]*sizes["z"]*sizes["x"]
        firsts = [(share*d+LEAD)//TILE for d in range(self.total)]
        lasts = [-(-(share*(d+1)+LEAD)//TILE) for d in range(self.total)]
        self.block = max(last-first for first, last in zip(firsts, lasts))
        self.tiles = max(first+self.block for first in firsts)
        self.tiles = -(-self.tiles//TILE)*TILE
        self.at = {axis: lax.axis_index(axis) for axis in sizes}

    def device(self, y, c, z, x):
        s = self.sizes
        return ((y*s["c"]+c)*s["z"]+z)*s["x"]+x

    def first(self, device):
        return (self.share*device+LEAD)//TILE

    def me(self):
        a = self.at
        return self.device(a["y"], a["c"], a["z"], a["x"])


def turn(value, axis, size, distance):
    return lax.ppermute(value, axis, [(i, (i+distance) % size) for i in range(size)])


def add_everywhere(value, place):
    for axis in ("c", "x", "y", "z"):
        size, step = place.sizes[axis], 1
        while step < size:
            value = value+lax.ppermute(value, axis, [(i, i ^ step) for i in range(size)])
            step *= 2
    return value


def cut_kernel(count, size, starts_ref, large_ref, out_ref, sems):
    copies = [pltpu.make_async_copy(large_ref.at[pl.ds(starts_ref[i], size)], out_ref.at[i], sems.at[i]) for i in range(count)]
    for copy in copies:
        copy.start()
    for copy in copies:
        copy.wait()


def cut(large, starts, size):
    count = starts.shape[0]
    return pl.pallas_call(
        functools.partial(cut_kernel, count, size),
        out_shape=sds((count, size, TILE, WIDE), narrow),
        in_specs=[pl.BlockSpec(memory_space=pltpu.SMEM), pl.BlockSpec(memory_space=pl.ANY)],
        out_specs=pl.BlockSpec(memory_space=VM),
        scratch_shapes=[pltpu.SemaphoreType.DMA((count,))],
        compiler_params=pltpu.CompilerParams(vmem_limit_bytes=LIMIT),
        cost_estimate=pl.CostEstimate(flops=0, bytes_accessed=4*count*size*TILE*WIDE, transcendentals=0),
    )(starts, large)


def merge_kernel(coords, sends, count, size, starts_ref, large_ref, arrived_ref, *refs):
    outs, (held_ref, sems) = refs[:-2], refs[-2:]
    copies = [pltpu.make_async_copy(large_ref.at[pl.ds(starts_ref[i], size)], held_ref.at[i], sems.at[i]) for i in range(count)]
    for copy in copies:
        copy.start()
    for i in range(count):
        copies[i].wait()
        which, at = sends[i]
        def body(t, _):
            outs[which][at, t] = (held_ref[i, t].astype(f32)+arrived_ref[i, t].astype(f32)).astype(outs[which].dtype)
            return _
        lax.fori_loop(0, size, body, 0)


def share_out(large, place, parts):
    s, a, block = place.sizes, place.at, place.block
    half = (s["z"]+1)//2
    coords = [(y, z, x) for y in range(s["y"]) for z in range(s["z"]) for x in range(s["x"])]

    def starts(core):
        return jnp.stack([
            place.first(place.device((a["y"]+y) % s["y"], core, (a["z"]+z) % s["z"], (a["x"]+x) % s["x"])) for y, z, x in coords
        ]).astype(jnp.int32)

    other, mine = starts(1-a["c"]), starts(a["c"])
    bounds = [block*i//parts for i in range(parts+1)]
    groups = [("y", [(0, z, x) for z in range(half) for x in range(s["x"])])]
    groups += [("y%d" % k, [(k, z, x) for z in range(half) for x in range(s["x"])]) for k in range(1, s["y"])]
    groups += [("x", [(y, z, 0) for z in range(half, s["z"]) for y in range(s["y"])])]
    groups += [("x%d" % k, [(y, z, k) for z in range(half, s["z"]) for y in range(s["y"])]) for k in range(1, s["x"])]
    names = [name for name, members in groups]
    sends = [None]*len(coords)
    for g, (name, members) in enumerate(groups):
        for at, member in enumerate(members):
            sends[coords.index(member)] = (g, at)
    results = []
    for part in range(parts):
        begin, size = bounds[part], bounds[part+1]-bounds[part]
        arrived = turn(cut(large, other+begin, size), "c", 2, 1)
        outs = [sds((len(members), size, TILE, WIDE), f32 if name in ("y", "x") else narrow) for name, members in groups]
        merged = pl.pallas_call(
            functools.partial(merge_kernel, coords, sends, len(coords), size),
            out_shape=outs,
            in_specs=[pl.BlockSpec(memory_space=pltpu.SMEM), pl.BlockSpec(memory_space=pl.ANY), pl.BlockSpec(memory_space=VM)],
            out_specs=[pl.BlockSpec(memory_space=VM)]*len(outs),
            scratch_shapes=[pltpu.VMEM((len(coords), size, TILE, WIDE), narrow), pltpu.SemaphoreType.DMA((len(coords),))],
            compiler_params=pltpu.CompilerParams(vmem_limit_bytes=LIMIT),
            cost_estimate=pl.CostEstimate(flops=0, bytes_accessed=8*len(coords)*size*TILE*WIDE, transcendentals=0),
        )(mine+begin, large, arrived)
        merged = dict(zip(names, merged))
        near, far = merged["y"], merged["x"]
        near = near+sum(turn(merged["y%d" % k], "y", s["y"], k).astype(f32) for k in range(1, s["y"]))
        far = far+sum(turn(merged["x%d" % k], "x", s["x"], k).astype(f32) for k in range(1, s["x"]))
        near = near.reshape((half, s["x"])+near.shape[1:])
        far = far.reshape((s["z"]-half, s["y"])+far.shape[1:])
        near = near[:, 0]+sum(turn(near[:, k].astype(narrow), "x", s["x"], k).astype(f32) for k in range(1, s["x"]))
        far = far[:, 0]+sum(turn(far[:, k].astype(narrow), "y", s["y"], k).astype(f32) for k in range(1, s["y"]))
        total = near[0]
        for z in range(1, s["z"]):
            value = near[z] if z < half else far[z-half]
            total = total+turn(value.astype(narrow), "z", s["z"], z).astype(f32)
        results.append(total)
    return jnp.concatenate(results, axis=0)


def assemble_kernel(share, count, block, pieces_ref, out_ref, held_ref, sems):
    firsts = [(share*d+LEAD)//TILE for d in range(count)]
    firsts.append(firsts[-1]+block)
    arriving, leaving = [], []
    for d in range(count):
        copy = pltpu.make_async_copy(pieces_ref.at[d], held_ref.at[d], sems.at[0, d])
        copy.start()
        arriving.append(copy)
    for d in range(count):
        arriving[d].wait()
        if d:
            held_ref[d, 0] = held_ref[d, 0]+held_ref[d-1, firsts[d]-firsts[d-1]]
        size = firsts[d+1]-firsts[d]
        copy = pltpu.make_async_copy(held_ref.at[d, 0:size], out_ref.at[firsts[d]:firsts[d]+size], sems.at[1, d])
        copy.start()
        leaving.append(copy)
    for copy in leaving:
        copy.wait()


def assemble(pieces, place):
    count, block = place.total, place.block
    anywhere = pl.BlockSpec(memory_space=pl.ANY)
    return pl.pallas_call(
        functools.partial(assemble_kernel, place.share, count, block),
        out_shape=sds((place.tiles, TILE, WIDE), narrow),
        in_specs=[anywhere],
        out_specs=anywhere,
        scratch_shapes=[pltpu.VMEM((count, block, TILE, WIDE), narrow), pltpu.SemaphoreType.DMA((2, count))],
        compiler_params=pltpu.CompilerParams(vmem_limit_bytes=LIMIT),
        cost_estimate=pl.CostEstimate(flops=0, bytes_accessed=4*count*block*TILE*WIDE, transcendentals=0),
    )(pieces)


SPOTS = (
    list(range(14))
    + [ROW["time1_b"], ROW["time1_b"]+1, ROW["time2_b"], ROW["time2_b"]+1, ROW["down_b"]]
    + [ROW["res_b"]+i for i in range(4)]
    + [ROW["emb_b"]+i for i in range(4)]
    + [ROW["res_gain"]+i for i in range(4)]
    + [ROW["res_shift"]+i for i in range(4)]
    + [ROW["attn_gain"], ROW["attn_shift"], ROW["qv_b"], ROW["qv_b"]+1, ROW["proj_b"]]
    + [ROW["head_gain"]+i for i in range(85)]
)


def time_forward(steps, w1, b1, w2, b2):
    half = C0 // 2
    freqs = jnp.exp(-math.log(10000.0) * jnp.arange(half).astype(f32) / half)
    angles = steps[:, None] * freqs
    sinus = jnp.concatenate([jnp.cos(angles), jnp.sin(angles)], axis=-1).astype(narrow)
    hidden_pre = dot(sinus, w1) + b1
    hidden = silu(hidden_pre).astype(narrow)
    outer_pre = dot(hidden, w2) + b2
    return silu(outer_pre).astype(narrow), (sinus, hidden_pre, hidden, outer_pre)


def rank_one_share(place, kept, embed, hidden_grad, outer_grad, moved, small):
    share, n = place.share, place.total
    sinus, hidden_pre, hidden, outer_pre = kept
    row = share*place.me()+jnp.arange(share)

    def left(parts, first):
        length = sum(part.shape[0] for part in parts)
        table = jnp.concatenate([jnp.zeros((share, n), f32)]+parts+[jnp.zeros((share, n), f32)])
        return lax.dynamic_slice_in_dim(table, jnp.clip(share*place.me()-first+share, 0, length+share), share)

    def twice(value):
        return jnp.repeat(value.astype(f32).T, 2, axis=0)

    time_left = left([twice(sinus), jnp.zeros((2, n), f32), twice(hidden)], ROW["time1_w"])
    emb_left = left([twice(embed), twice(embed)], ROW["emb_w"])
    time_left = time_left+emb_left
    columns, right = [], []
    for begin, length, value in (
        (ROW["time1_w"], 2*C0, hidden_grad),
        (ROW["time2_w"], 2*TEMB, outer_grad),
        (ROW["emb_w"], 2*TEMB, moved[:, :2*CH]),
        (ROW["emb_w"]+2*TEMB, 2*TEMB, moved[:, 2*CH:]),
    ):
        for part in range(2):
            held = (row >= begin) & (row < begin+length) & ((row-begin) % 2 == part)
            columns.append(jnp.where(held[:, None], time_left, 0.0))
            right.append(value[:, part*CH:(part+1)*CH])
    spots = jnp.array(SPOTS+[-1]*(128-len(SPOTS)))
    columns.append((row[:, None] == spots[None]).astype(f32))
    right.append(small)
    return precise(jnp.concatenate(columns, axis=1), jnp.concatenate(right))


def step(sizes, params, moment1, moment2, images, noise, timesteps, masks, weight_index):
    flat = params.shape[0]
    share = flat // WIDE
    params, moment1, moment2 = (value.reshape(share, WIDE) for value in (params, moment1, moment2))
    place = Place(sizes, share)
    a, me = place.at, place.me()
    spare = (share*me+LEAD) % TILE
    piece = jnp.zeros((place.block*TILE, WIDE), narrow)
    piece = lax.dynamic_update_slice_in_dim(piece, params.astype(narrow), spare, axis=0)
    pieces = lax.all_gather(piece.reshape(place.block, TILE, WIDE), ("y", "c", "z", "x"), axis=0)

    own = jnp.concatenate([images, noise, masks.astype(f32)[:, None]], axis=1)
    own = lax.all_to_all(own, ("z", "x"), split_axis=0, concat_axis=2, tiled=True)[0]
    index = a["z"]*sizes["x"]+a["x"]
    own_step = lax.dynamic_index_in_dim(timesteps, index, keepdims=False).astype(f32)
    sample_weight = 0.5+0.5*lax.dynamic_index_in_dim(weight_index, index, keepdims=False).astype(f32)
    clean, own_noise, mask = own[:IN_CH], own[IN_CH:2*IN_CH], own[2*IN_CH:]
    early = jnp.stack([
        jnp.where(jnp.arange(WIDE) == me, own_step, 0.0),
        jnp.full((WIDE,), jnp.sum(mask)),
    ] + [jnp.zeros((WIDE,), f32)]*6)
    early = add_everywhere(early, place)
    all_steps, count = early[0, :place.total], early[1, 0]
    signal, one_minus, beta, alpha, tilde = plan(own_step)
    noisy = (jnp.sqrt(signal)*clean+jnp.sqrt(one_minus)*own_noise).astype(narrow).astype(f32)
    noisy = pad_rows8(to_phases(noisy))
    noise_phases, mask_phases = pad_rows8(to_phases(own_noise)), to_phases(mask)

    whole = assemble(pieces, place).reshape(-1, WIDE)

    def rows(name, length, extra=0):
        first = ROW[name]+extra+LEAD
        return whole[first:first+length]

    stem = rows("stem_w", 14).reshape(-1)
    stem_w = taps_rows(stem[:27*C0].reshape(9, IN_CH, C0))
    stem_b = stem[27*C0:].reshape(1, C0).astype(f32)
    w1, b1 = rows("time1_w", 2*C0).reshape(C0, TEMB), rows("time1_b", 2).reshape(TEMB).astype(f32)
    w2, b2 = rows("time2_w", 2*TEMB).reshape(TEMB, TEMB), rows("time2_b", 2).reshape(TEMB).astype(f32)
    down_w, down_b = rows("down_w", 9*C0), rows("down_b", 1).astype(f32)
    vectors = whole[ROW["emb_b"]+LEAD:ROW["qkv_w"]+LEAD].astype(f32)
    res_b = rows("res_b", 4).astype(f32)
    emb_w = rows("emb_w", 4*TEMB).reshape(BLOCKS, TEMB, TEMB)

    skip, state = stem_down(noisy, stem_w, stem_b, down_w, down_b)
    embed, kept = time_forward(all_steps, w1, b1, w2, b2)
    own_embed = lax.dynamic_slice_in_dim(embed, me, 1)
    blocks = []
    for b in range(BLOCKS):
        modulate = dot(own_embed, emb_w[b]).reshape(2, CH)+vectors[2*b:2*b+2]
        vec = jnp.stack([
            res_b[2*b], res_b[2*b+1], vectors[4+2*b], vectors[8+2*b], vectors[5+2*b], vectors[9+2*b],
            1.0+modulate[0], modulate[1],
        ])
        base = RES+2*TAPS*b
        after, inner, stat = block_forward(state, whole, base, vec)
        blocks.append((state, inner, stat, base, vec))
        state = after
    before = state
    state, qkv, log, mixed_t, attn_stat, wp, wo, attn_vec = attention_forward(before, whole)

    ends = rows("head_gain", 85).reshape(-1)
    norm_u = jnp.stack([ends[:CH], ends[C0+CH:C0+2*CH]]).astype(f32)
    norm_s = jnp.stack([ends[CH:C0+CH], ends[C0+2*CH:2*(C0+CH)]]).astype(f32)
    head_size = 9*(C0+CH)*OUT_CH
    head_w = ends[2*(C0+CH):2*(C0+CH)+head_size].reshape(9, C0+CH, OUT_CH)
    head_w = jnp.transpose(head_w, (0, 2, 1))
    wu, ws = taps_rows(head_w[..., :CH]), taps_rows(head_w[..., CH:])
    head_b = ends[2*(C0+CH)+head_size:2*(C0+CH)+head_size+OUT_CH].astype(f32)
    head_b = jnp.broadcast_to(jnp.pad(head_b, (0, 8-OUT_CH))[:, None], (8, 128))
    numbers = jnp.stack([jnp.log(beta), jnp.log(tilde), beta*beta/(alpha*one_minus), sample_weight])
    grad, skip_grad, gu, gs, small_u, small_s, gb, losses = head(
        numbers, state, skip, wu, ws, norm_u, norm_s, head_b, noise_phases, mask_phases)
    grad, large, attn_small, qkv_bias = attention_back(
        grad, before, attn_stat, qkv, log, mixed_t, wp, wo, attn_vec, place.tiles)
    block_grads = [None]*BLOCKS
    for b in reversed(range(BLOCKS)):
        begin, inner, stat, base, vec = blocks[b]
        grad, large, block_grads[b] = block_back(grad, begin, inner, stat, whole, base, vec, large)
    large, d_stem, down_small, stem_small = down_stem_back(grad, skip, skip_grad, down_w, noisy, large)

    total = share_out(large, place, 2).reshape(-1, WIDE)
    total = lax.dynamic_slice_in_dim(total, spare, share)
    row = share*me+jnp.arange(share)
    dense = functools.reduce(jnp.logical_or, [
        (row >= ROW[name]) & (row < ROW[name]+length)
        for name, length in (("down_w", 9*C0), ("res_w", 4*TAPS), ("qkv_w", 3*CH), ("proj_w", CH))
    ])
    total = jnp.where(dense[:, None], total, 0.0)

    d_head = jnp.concatenate([gu[:72].reshape(9, 8, CH)[:, :OUT_CH], gs[:72].reshape(9, 8, C0)[:, :OUT_CH]], axis=-1)
    d_ends = jnp.concatenate([
        small_u[0], small_s[0], small_u[1], small_s[1], jnp.transpose(d_head, (0, 2, 1)).reshape(-1), gb[:OUT_CH, 0],
    ])
    d_ends = jnp.pad(d_ends, (0, 85*WIDE-d_ends.shape[0])).reshape(85, WIDE)
    d_stem = jnp.concatenate([d_stem[:72].reshape(9, 8, C0)[:, :IN_CH].reshape(-1), stem_small[0]]).reshape(14, WIDE)
    qkv_bias = heads_unpad(qkv_bias[0]).reshape(3, CH)
    none = jnp.zeros((4, WIDE), f32)
    s0, s1 = block_grads
    small = jnp.concatenate([
        d_stem, none, down_small[:1], s0[:2], s1[:2], none, s0[2:4], s1[2:4], s0[4:6], s1[4:6],
        attn_small[:2], qkv_bias[:1], qkv_bias[2:], attn_small[2:3], d_ends, jnp.zeros((3, WIDE), f32),
    ])
    moved = jnp.concatenate([s0[6:8], s1[6:8]])
    slots = jnp.where(jnp.arange(place.total)[:, None, None] == me, moved[None], 0.0).reshape(-1, WIDE)
    merged = add_everywhere(jnp.concatenate([small, slots]), place)
    small, moved = merged[:128], merged[128:].reshape(place.total, 4*CH)
    sinus, hidden_pre, hidden, outer_pre = kept
    embed_grad = sum(
        precise(moved[:, 2*CH*b:2*CH*(b+1)], emb_w[b].astype(f32).T) for b in range(BLOCKS))
    outer_grad = embed_grad*silu_grad(outer_pre)
    hidden_grad = precise(outer_grad, w2.astype(f32).T)*silu_grad(hidden_pre)
    filled = jnp.concatenate([
        small[:14], jnp.sum(hidden_grad, axis=0).reshape(2, WIDE), jnp.sum(outer_grad, axis=0).reshape(2, WIDE), small[18:23],
        jnp.sum(moved, axis=0).reshape(4, WIDE), small[27:],
    ])
    total = total+rank_one_share(place, kept, embed, hidden_grad, outer_grad, moved, filled)

    scaled = total/count
    sums = jnp.concatenate([losses[:2], jnp.full((1, 128), jnp.sum(scaled*scaled)), losses[3:]])
    sums = add_everywhere(sums, place)
    loss_sum, loss_vlb, grad_norm = sums[0, 0], sums[1, 0], jnp.sqrt(sums[2, 0])
    clipped = scaled*jnp.minimum(1.0, clip_limit/(grad_norm+1e-06))
    first = decay_first*moment1+(1.0-decay_first)*clipped
    second = decay_second*moment2+(1.0-decay_second)*clipped*clipped
    first_hat = first/(1.0-decay_first**STEP)
    second_hat = second/(1.0-decay_second**STEP)
    updated = params-learn_rate*(first_hat/(jnp.sqrt(second_hat)+1e-08)+weight_decay*params)
    arrays = (value.reshape(flat) for value in (updated, first, second, updated.astype(narrow)))
    return (*arrays, loss_sum, loss_vlb, count, grad_norm)


def solution(mesh):
    y = mesh.shape["batch"] // 2
    sizes = {"y": y, "c": 2, "z": mesh.shape["rows"] // y, "x": y}
    fine = Mesh(mesh.devices.reshape(tuple(sizes.values())), tuple(sizes))
    every, batch, rows = ("y", "c", "z", "x"), ("y", "c"), ("z", "x")
    return jax.shard_map(
        functools.partial(step, sizes),
        mesh=fine,
        in_specs=(P(every), P(every), P(every), P(batch, None, rows, None), P(batch, None, rows, None),
                  P(batch), P(batch, rows, None), P(batch)),
        out_specs=(P(every), P(every), P(every), P(every), P(), P(), P(), P()),
        check_vma=False,
    )
```

time: 1960 us -> 611 us (0.31)
  blocking collectives: 816 us -> 0 us
  matrix products: 397 us -> 14.5 us
  local copies, waits for them, and re-layouts: 446 us -> 111 us
  Pallas kernels: 0 us -> 210 us
  other arithmetic: 154 us -> 37.2 us
  waiting for transfers between devices: 102 us -> 170 us
  starting transfers between devices: 9.5 us -> 39.4 us
    unnamed x1 -> x0, blocking collectives: 730 us -> none
    conv_general_dilated x12 -> x0, matrix products: 236 us -> none  [conv_apply(): lax.conv_general_dilated(padded, kernel, (stride, stride), 'VALID', dimen...]
    pallas_call x0 -> x14, Pallas kernels: none -> 210 us  [the longest x8 152 us: call(): pl.pallas_call(kernel, out_shape=outs, in_specs=places, out_specs=[pl.Blo...]
    dot_general x79 -> x4, matrix products: 154 us -> 5.68 us  [dot(): return jnp.dot(a, b, preferred_element_type=f32)]
    ppermute x0 -> x31, waiting for transfers between devices: none -> 91.3 us  [the longest x16 59.7 us: turn(): lax.ppermute(value, axis, [(i, (i + distance) % size) for i in range(size)])]
    concatenate x7, local copies, waits for them, and re-layouts: 106 us -> 15.9 us  [the longest x2 13.1 us: rank_one_share(): return precise(jnp.concatenate(columns, axis=1), jnp.concatenate(right))]
    slice x27 -> x39, local copies, waits for them, and re-layouts: 115 us -> 27 us  [the longest x3 4.65 us: rows(): return whole[first:first + length]]
    psum x2 -> x0, blocking collectives: 86 us -> none  [the longest x1 44.8 us: shards(): count = lax.psum(jnp.sum(masks).astype(jnp.float32), ('batch', 'rows'))]
  transfers between devices with their start and end apart: 3 -> 33, of which waited for: 2 -> 20; matrix products, arithmetic and copies ran while one was open for 1% -> 16% of each run, Pallas kernels for 0% -> 4%
where the time goes in v2:
time: 611 us; the launch traced here: 603 us
  Pallas kernels  210 us (34%)
  waiting for transfers between devices  170 us (28%)
  local copies, waits for them, and re-layouts  111 us (18%)
  starting transfers between devices  39.4 us (6%)
  other arithmetic  37.2 us (6%)
  between operations  20.2 us (3%)
  matrix products  14.5 us (2%)
    pallas_call x8, Pallas kernels, call(): pl.pallas_call(kernel, out_shape=outs, in_specs=places, out_specs=[pl.Blo...  152 us
    all_gather x1, waiting for transfers between devices, step(): lax.all_gather(piece.reshape(place.block, TILE, WIDE), ('y', 'c', 'z', 'x...  73.8 us
    ppermute x16, waiting for transfers between devices, turn(): lax.ppermute(value, axis, [(i, (i + distance) % size) for i in range(size)])  59.7 us
    ppermute x15, waiting for transfers between devices, add_everywhere(): lax.ppermute(value, axis, [(i, i ^ step) for i in range(size)])  31.6 us
    pallas_call x1, Pallas kernels, head(): pl.pallas_call(head_kernel, out_shape=outs, in_specs=[pl.BlockSpec(memory...  17.4 us
    pallas_call x2, Pallas kernels, share_out(): pl.pallas_call(functools.partial(merge_kernel, coords, sends, len(coords)...  17.2 us
    ppermute x16, starting transfers between devices, turn(): lax.ppermute(value, axis, [(i, (i + distance) % size) for i in range(size)])  16.3 us
    ppermute x15, starting transfers between devices, add_everywhere(): lax.ppermute(value, axis, [(i, i ^ step) for i in range(size)])  15.8 us
  transfers between devices with their start and end apart: 33, of which 20 were waited for; matrix products, arithmetic and copies ran while one was open for 16% of the time, Pallas kernels for 4%

profile of v2, /device:TPU:0, one launch (start us, length us, event | category | flops | bytes accessed | tf_op | source)
XLA Modules:
  0.0 602.5 jit_solution(7521035378979163460)
XLA Ops:
  13.3 7.3 %all-to-all-start = ((f32[8,1,3584]{2,1,0:T(1,128)}), f32[8,1,3584]{2,1,0:T(1,128)S(1)}, u32[]{:S(2)}, u32[]{:S(2)}) async-start(f32[8,1,3584]{2,1,0:T(1,128)} %reshape.408), calls=%async_computation | async-start | bytes 229376 | tf_op jit(solution)/shard_map/all_to_all | solution.py:980
  60.5 73.8 %all-gather.2.cloned.1.call-done.pieces_ref = bf16[32,45,16,384]{3,2,1,0:T(8,128)(2,1)} async-done(((bf16[1,45,16,384]{3,2,1,0:T(8,128)(2,1)}), bf16[32,45,16,384]{3,2,1,0:T(8,128)(2,1)}) %all-gather.2.cloned.1.call-update) | async-done | bytes 17694736 | tf_op jit(solution)/shard_map/all_gather | solution.py:977
  134.3 12.6 %shard_map.152 = bf16[1392,16,384]{2,1,0:T(8,128)(2,1)} custom-call(bf16[32,45,16,384]{3,2,1,0:T(8,128)(2,1)} %all-gather.2.cloned.1.call-done.pieces_ref), custom_call_target="tpu_custom_call" | custom-call | bytes 35389440 | tf_op jit(solution)/shard_map/pallas_call | solution.py:901
  181.0 6.1 %shard_map.153 = (bf16[4,1024,192]{2,1,0:T(8,128)(2,1)}, f32[1024,384]{1,0:T(8,128)}) custom-call(f32[4,8,1024]{2,1,0:T(8,128)} %pad_convert_fusion.noisy_ref, bf16[128,192]{1,0:T(8,128)(2,1)} %pad.46.sw_ref, f32[1,192]{1,0:T(1,128)} %bitcast.262, bf16[1728,384]{1,0:T(8,128)(2,1)} %slice.473.dw_ref, f32[1,384]{1,0:T(1,128)} %get-tuple-element.109.db_ref), custom_call_target="tpu_custom_call" | custom-call | flops 1358954496 | bytes 4655360 | tf_op jit(solution)/shard_map/pallas_call | solution.py:113
  187.8 15.2 %shard_map.154 = (f32[1024,384]{1,0:T(8,128)}, f32[1024,384]{1,0:T(8,128)}, f32[8,384]{1,0:T(8,128)}) custom-call(f32[1024,384]{1,0:T(8,128)} %get-tuple-element.54.state_ref, bf16[22272,384]{1,0:T(8,128)(2,1)} %bitcast.229, f32[8,384]{1,0:T(8,128)} %stack.169.vec_ref), custom_call_target="tpu_custom_call" | custom-call | flops 5435817984 | bytes 21848064 | tf_op jit(solution)/shard_map/pallas_call | solution.py:113
  203.5 14.8 %shard_map.155 = (f32[1024,384]{1,0:T(8,128)}, f32[1024,384]{1,0:T(8,128)}, f32[8,384]{1,0:T(8,128)}) custom-call(f32[1024,384]{1,0:T(8,128)} %get-tuple-element.55.state_ref, bf16[22272,384]{1,0:T(8,128)(2,1)} %bitcast.230, f32[8,384]{1,0:T(8,128)} %stack.170.vec_ref), custom_call_target="tpu_custom_call" | custom-call | flops 5435817984 | bytes 21848064 | tf_op jit(solution)/shard_map/pallas_call | solution.py:113
  218.3 23.7 %shard_map.156 = (f32[1024,384]{1,0:T(8,128)}, bf16[1024,1536]{1,0:T(8,128)(2,1)}, f32[8,1024]{1,0:T(8,128)}, bf16[512,1024]{1,0:T(8,128)(2,1)}, f32[8,384]{1,0:...) custom-call(f32[1024,384]{1,0:T(8,128)} %get-tuple-element.56.state_ref, ...), custom_call_target="tpu_custom_call" | custom-call | flops 3758096384 | bytes 26075136 | tf_op jit(solution)/shard_map/pallas_call | solution.py:113
  246.9 17.4 %shard_map.157 = (f32[1024,384]{1,0:T(8,128)}, f32[4,1024,192]{2,1,0:T(8,128)}, f32[128,384]{1,0:T(8,128)}, f32[128,192]{1,0:T(8,128)}, f32[8,384]{1,0:T(8,128)}...) custom-call(f32[4]{0:T(128)} %pad_maximum_fusion.8.num_ref, f32[1024,384]{1,0:T(8,128)} %get-tuple-element.57.state_ref, ...), custom_call_target="tpu_custom_call" | custom-call | flops 1207959552 | bytes 12582912 | tf_op jit(solution)/shard_map/pallas_call | solution.py:569
  264.3 25.8 %shard_map.158 = (f32[1024,384]{1,0:T(8,128)}, bf16[1392,16,384]{2,1,0:T(8,128)(2,1)}, f32[8,384]{1,0:T(8,128)}, f32[8,1536]{1,0:T(8,128)}) custom-call(f32[1024,384]{1,0:T(8,128)} %get-tuple-element.59.grad_ref, f32[1024,384]{1,0:T(8,128)} %get-tuple-element.56.state_ref, f32[8,384]{1,0:T(8,128)} %get-tuple-element.60.stat_ref, ...), custom_call_target="tpu_custom_call" | custom-call | flops 8589934592 | bytes 27709440 | tf_op jit(solution)/shard_map/pallas_call | solution.py:113
  291.5 27.4 %shard_map.159 = (f32[1024,384]{1,0:T(8,128)}, bf16[1392,16,384]{2,1,0:T(8,128)(2,1)}, f32[8,384]{1,0:T(8,128)}) custom-call(f32[1024,384]{1,0:T(8,128)} %get-tuple-element.67.grad_ref, f32[1024,384]{1,0:T(8,128)} %get-tuple-element.55.state_ref, f32[1024,384]{1,0:T(8,128)} %get-tuple-element.68.inner_ref, ...), custom_call_target="tpu_custom_call", output_to_operand_aliasing={{1}: (6, {})} | custom-call | flops 10871635968 | bytes 57643008 | tf_op jit(solution)/shard_map/pallas_call | solution.py:113
  318.9 27.7 %shard_map.160 = (f32[1024,384]{1,0:T(8,128)}, bf16[1392,16,384]{2,1,0:T(8,128)(2,1)}, f32[8,384]{1,0:T(8,128)}) custom-call(f32[1024,384]{1,0:T(8,128)} %get-tuple-element.71.grad_ref, f32[1024,384]{1,0:T(8,128)} %get-tuple-element.54.state_ref, f32[1024,384]{1,0:T(8,128)} %get-tuple-element.72.inner_ref, ...), custom_call_target="tpu_custom_call", output_to_operand_aliasing={{1}: (6, {})} | custom-call | flops 10871635968 | bytes 57643008 | tf_op jit(solution)/shard_map/pallas_call | solution.py:113
  346.7 11.9 %shard_map.161 = (bf16[1392,16,384]{2,1,0:T(8,128)(2,1)}, f32[128,192]{1,0:T(8,128)}, f32[8,384]{1,0:T(8,128)}, f32[8,192]{1,0:T(8,128)}) custom-call(f32[1024,384]{1,0:T(8,128)} %get-tuple-element.75.grad_ref, bf16[4,1024,192]{2,1,0:T(8,128)(2,1)} %get-tuple-element.58.skip_ref, ...), custom_call_target="tpu_custom_call", output_to_operand_aliasing={{0}: (5, {})} | custom-call | flops 2717908992 | bytes 42076160 | tf_op jit(solution)/shard_map/pallas_call | solution.py:113
  358.6 5.0 shard_map.162
  363.9 5.2 shard_map.164
  386.6 7.5 %collective-permute-done.22 = f32[256,384]{1,0:T(8,128)S(1)} collective-permute-done((f32[256,384]{1,0:T(8,128)S(1)}, f32[256,384]{1,0:T(8,128)S(1)}, u32[]{:S(2)}, u32[]{:S(2)}) %collective-permute-start.22) | collective-permute-done | bytes 393248 | tf_op jit(solution)/shard_map/ppermute | solution.py:787
  396.8 7.9 %collective-permute-done.23 = f32[256,384]{1,0:T(8,128)S(1)} collective-permute-done((f32[256,384]{1,0:T(8,128)S(1)}, f32[256,384]{1,0:T(8,128)S(1)}, u32[]{:S(2)}, u32[]{:S(2)}) %collective-permute-start.23) | collective-permute-done | bytes 393248 | tf_op jit(solution)/shard_map/ppermute | solution.py:787
  436.0 8.5 %shard_map.163 = (f32[4,22,16,384]{3,2,1,0:T(8,128)}, bf16[4,22,16,384]{3,2,1,0:T(8,128)(2,1)}, f32[4,22,16,384]{3,2,1,0:T(8,128)}, bf16[4,22,16,384]{3,2,1,0:T(8,128)(2,1)}) custom-call(s32[16]{0:T(128)} %stack.162.starts_ref, bf16[1392,16,384]{2,1,0:T(8,128)(2,1)} %get-tuple-element.78.large_ref, bf16[16,22,16,384]{3,2,1,0:T(8,128)(2,1)} %collective-permute-done.5.arrived_ref), custom_call_target="tpu_custom_call" | custom-call | bytes 17301504 | tf_op jit(solution)/shard_map/pallas_call | solution.py:853
  452.1 8.8 %shard_map.165 = (f32[4,23,16,384]{3,2,1,0:T(8,128)}, bf16[4,23,16,384]{3,2,1,0:T(8,128)(2,1)}, f32[4,23,16,384]{3,2,1,0:T(8,128)}, bf16[4,23,16,384]{3,2,1,0:T(8,128)(2,1)}) custom-call(s32[16]{0:T(128)} %broadcast_add_fusion.1.starts_ref, bf16[1392,16,384]{2,1,0:T(8,128)(2,1)} %get-tuple-element.78.large_ref, ...), custom_call_target="tpu_custom_call" | custom-call | bytes 18087936 | tf_op jit(solution)/shard_map/pallas_call | solution.py:853
  462.9 8.8 %collective-permute-done.9 = bf16[4,22,16,384]{3,2,1,0:T(8,128)(2,1)} collective-permute-done((bf16[4,22,16,384]{3,2,1,0:T(8,128)(2,1)}, bf16[4,22,16,384]{3,2,1,0:T(8,128)(2,1)}, u32[]{:S(2)}, u32[]{:S(2)}) %collective-permute-start.9) | collective-permute-done | bytes 1081376 | tf_op jit(solution)/shard_map/ppermute | solution.py:780
  478.5 17.3 %collective-permute-done.17 = bf16[4,23,16,384]{3,2,1,0:T(8,128)(2,1)S(1)} collective-permute-done((bf16[4,23,16,384]{3,2,1,0:T(8,128)(2,1)}, bf16[4,23,16,384]{3,2,1,0:T(8,128)(2,1)S(1)}, u32[]{:S(2)}, u32[]{:S(2)}) %collective-permute-start.17) | collective-permute-done | bytes 1130528 | tf_op jit(solution)/shard_map/ppermute | solution.py:780
  501.2 10.6 %collective-permute-done.10 = bf16[2,22,16,384]{3,2,1,0:T(8,128)(2,1)S(1)} collective-permute-done((bf16[2,22,16,384]{3,2,1,0:T(8,128)(2,1)S(1)}, bf16[2,22,16,384]{3,2,1,0:T(8,128)(2,1)S(1)}, u32[]{:S(2)}, u32[]{:S(2)}) %collective-permute-start.10) | collective-permute-done | bytes 540704 | tf_op jit(solution)/shard_map/ppermute | solution.py:780
  526.5 8.5 %collective-permute-done.11 = bf16[22,16,384]{2,1,0:T(8,128)(2,1)S(1)} collective-permute-done((bf16[22,16,384]{2,1,0:T(8,128)(2,1)S(1)}, bf16[22,16,384]{2,1,0:T(8,128)(2,1)S(1)}, u32[]{:S(2)}, u32[]{:S(2)}) %collective-permute-start.11) | collective-permute-done | bytes 270368 | tf_op jit(solution)/shard_map/ppermute | solution.py:780
  539.5 9.1 %concatenate.51 = f32[384,384]{1,0:T(8,128)S(1)} concatenate(f32[32,384]{1,0:T(8,128)} %get-tuple-element.132, f32[32,384]{1,0:T(8,128)} %get-tuple-element.131, f32[32,384]{1,0:T(8,128)} %get-tuple-element.130, f32[32,384]{1,0:T(8,128)} %get-tuple-element.129, f32[32,384]{1,0:T(8,128)} %get-tuple-element.128, f32[32,384]{1,0:T(8,128)} %get-tuple-element.127, ...), dimensions={0} | concatenate | bytes 1179648 | tf_op jit(solution)/shard_map/concatenate | solution.py:965
  549.8 5.8 collective-permute-done.19
  (405 shorter events, 215.8 us)
Async XLA Ops:
  7.2 127.2 %all-gather.2.cloned.1.call-start = ((), (), s32[]{:S(2)}) async-start(), calls=%async_computation.1 | async-start | bytes 18247680 | tf_op jit(solution)/shard_map/all_gather | solution.py:977
  13.3 14.6 %all-to-all-start = ((f32[8,1,3584]{2,1,0:T(1,128)}), f32[8,1,3584]{2,1,0:T(1,128)S(1)}, u32[]{:S(2)}, u32[]{:S(2)}) async-start(f32[8,1,3584]{2,1,0:T(1,128)} %reshape.408), calls=%async_computation | async-start | bytes 229376 | tf_op jit(solution)/shard_map/all_to_all | solution.py:980
  36.7 9.7 %collective-permute-start.2 = (f32[8,384]{1,0:T(8,128)S(1)}, f32[8,384]{1,0:T(8,128)S(1)}, u32[]{:S(2)}, u32[]{:S(2)}) collective-permute-start(f32[8,384]{1,0:T(8,128)S(1)} %fusion.112), channel_id=1, source_target_pairs={{0,16},{16,0},{1,17},{17,1},{2,18},{18,2},{3,19},{19,3},{4,20},{20... | collective-permute-start | bytes 36872 | tf_op jit(solution)/shard_map/ppermute | solution.py:787
  53.0 6.8 %collective-permute-start.4 = (f32[8,384]{1,0:T(8,128)S(1)}, f32[8,384]{1,0:T(8,128)S(1)}, u32[]{:S(2)}, u32[]{:S(2)}) collective-permute-start(f32[8,384]{1,0:T(8,128)S(1)} %add.982), channel_id=1, source_target_pairs={{0,4},{2,6},{4,0},{6,2},{1,5},{3,7},{5,1},{7,3},{8,12},{10,14},{12... | collective-permute-start | bytes 36872 | tf_op jit(solution)/shard_map/ppermute | solution.py:787
  363.6 72.4 %collective-permute-start.5 = (bf16[16,22,16,384]{3,2,1,0:T(8,128)(2,1)}, bf16[16,22,16,384]{3,2,1,0:T(8,128)(2,1)}, u32[]{:S(2)}, u32[]{:S(2)}) collective-permute-start(bf16[16,22,16,384]{3,2,1,0:T(8,128)(2,1)} %shard_map.162), channel_id=1, source_target_pairs={{0,8},{8,0},{1,9},{9,1},{2,10},{10,2},{3,11},{11,3},{4,12},{12,4},... | collective-permute-start | bytes 12976136 | tf_op jit(solution)/shard_map/ppermute | solution.py:780
  369.1 82.9 %collective-permute-start.13 = (bf16[16,23,16,384]{3,2,1,0:T(8,128)(2,1)}, bf16[16,23,16,384]{3,2,1,0:T(8,128)(2,1)}, u32[]{:S(2)}, u32[]{:S(2)}) collective-permute-start(bf16[16,23,16,384]{3,2,1,0:T(8,128)(2,1)} %shard_map.164), channel_id=1, source_target_pairs={{0,8},{8,0},{1,9},{9,1},{2,10},{10,2},{3,11},{11,3},{4,12},{12,4},... | collective-permute-start | bytes 13565960 | tf_op jit(solution)/shard_map/ppermute | solution.py:780
  382.7 11.3 %collective-permute-start.22 = (f32[256,384]{1,0:T(8,128)S(1)}, f32[256,384]{1,0:T(8,128)S(1)}, u32[]{:S(2)}, u32[]{:S(2)}) collective-permute-start(f32[256,384]{1,0:T(8,128)S(1)} %add.1064), channel_id=1, source_target_pairs={{0,1},{1,0},{2,3},{3,2},{4,5},{5,4},{6,7},{7,6},{8,9},{9,8},{10,11... | collective-permute-start | bytes 1179656 | tf_op jit(solution)/shard_map/ppermute | solution.py:787
  394.1 10.5 %collective-permute-start.23 = (f32[256,384]{1,0:T(8,128)S(1)}, f32[256,384]{1,0:T(8,128)S(1)}, u32[]{:S(2)}, u32[]{:S(2)}) collective-permute-start(f32[256,384]{1,0:T(8,128)S(1)} %add.1065), channel_id=1, source_target_pairs={{0,16},{16,0},{1,17},{17,1},{2,18},{18,2},{3,19},{19,3},{4,20},{20... | collective-permute-start | bytes 1179656 | tf_op jit(solution)/shard_map/ppermute | solution.py:787
  405.4 9.8 %collective-permute-start.24 = (f32[256,384]{1,0:T(8,128)}, f32[256,384]{1,0:T(8,128)}, u32[]{:S(2)}, u32[]{:S(2)}) collective-permute-start(f32[256,384]{1,0:T(8,128)} %add.1066), channel_id=1, source_target_pairs={{0,2},{2,0},{4,6},{6,4},{1,3},{3,1},{5,7},{7,5},{8,10},{10,8},{12,... | collective-permute-start | bytes 1179656 | tf_op jit(solution)/shard_map/ppermute | solution.py:787
  416.5 18.4 %collective-permute-start.25 = (f32[256,384]{1,0:T(8,128)S(1)}, f32[256,384]{1,0:T(8,128)}, u32[]{:S(2)}, u32[]{:S(2)}) collective-permute-start(f32[256,384]{1,0:T(8,128)S(1)} %add.1067), channel_id=1, source_target_pairs={{0,4},{2,6},{4,0},{6,2},{1,5},{3,7},{5,1},{7,3},{8,12},{10,14},{12... | collective-permute-start | bytes 1179656 | tf_op jit(solution)/shard_map/ppermute | solution.py:787
  444.5 27.2 %collective-permute-start.9 = (bf16[4,22,16,384]{3,2,1,0:T(8,128)(2,1)}, bf16[4,22,16,384]{3,2,1,0:T(8,128)(2,1)}, u32[]{:S(2)}, u32[]{:S(2)}) collective-permute-start(bf16[4,22,16,384]{3,2,1,0:T(8,128)(2,1)} %get-tuple-element.82), channel_id=1, source_target_pairs={{0,1},{1,0},{2,3},{3,2},{4,5},{5,4},{6,7},{7,6},{8,9},{9,8},{10,11... | collective-permute-start | bytes 3244040 | tf_op jit(solution)/shard_map/ppermute | solution.py:780
  449.0 27.2 %collective-permute-start.6 = (bf16[4,22,16,384]{3,2,1,0:T(8,128)(2,1)}, bf16[4,22,16,384]{3,2,1,0:T(8,128)(2,1)}, u32[]{:S(2)}, u32[]{:S(2)}) collective-permute-start(bf16[4,22,16,384]{3,2,1,0:T(8,128)(2,1)} %get-tuple-element.80), channel_id=1, source_target_pairs={{0,16},{16,0},{1,17},{17,1},{2,18},{18,2},{3,19},{19,3},{4,20},{20... | collective-permute-start | bytes 3244040 | tf_op jit(solution)/shard_map/ppermute | solution.py:780
  460.8 34.9 %collective-permute-start.17 = (bf16[4,23,16,384]{3,2,1,0:T(8,128)(2,1)}, bf16[4,23,16,384]{3,2,1,0:T(8,128)(2,1)S(1)}, u32[]{:S(2)}, u32[]{:S(2)}) collective-permute-start(bf16[4,23,16,384]{3,2,1,0:T(8,128)(2,1)} %get-tuple-element.86), channel_id=1, source_target_pairs={{0,1},{1,0},{2,3},{3,2},{4,5},{5,4},{6,7},{7,6},{8,9},{9,8},{10,11... | collective-permute-start | bytes 3391496 | tf_op jit(solution)/shard_map/ppermute | solution.py:780
  462.4 37.9 %collective-permute-start.14 = (bf16[4,23,16,384]{3,2,1,0:T(8,128)(2,1)}, bf16[4,23,16,384]{3,2,1,0:T(8,128)(2,1)S(1)}, u32[]{:S(2)}, u32[]{:S(2)}) collective-permute-start(bf16[4,23,16,384]{3,2,1,0:T(8,128)(2,1)} %get-tuple-element.84), channel_id=1, source_target_pairs={{0,16},{16,0},{1,17},{17,1},{2,18},{18,2},{3,19},{19,3},{4,20},{20... | collective-permute-start | bytes 3391496 | tf_op jit(solution)/shard_map/ppermute | solution.py:780
  473.3 38.5 %collective-permute-start.10 = (bf16[2,22,16,384]{3,2,1,0:T(8,128)(2,1)S(1)}, bf16[2,22,16,384]{3,2,1,0:T(8,128)(2,1)S(1)}, u32[]{:S(2)}, u32[]{:S(2)}) collective-permute-start(bf16[2,22,16,384]{3,2,1,0:T(8,128)(2,1)S(1)} %fusion.22), channel_id=1, source_target_pairs={{0,16},{16,0},{1,17},{17,1},{2,18},{18,2},{3,19},{19,3},{4,20},{20... | collective-permute-start | bytes 1622024 | tf_op jit(solution)/shard_map/ppermute | solution.py:780
  477.8 37.5 %collective-permute-start.7 = (bf16[2,22,16,384]{3,2,1,0:T(8,128)(2,1)S(1)}, bf16[2,22,16,384]{3,2,1,0:T(8,128)(2,1)S(1)}, u32[]{:S(2)}, u32[]{:S(2)}) collective-permute-start(bf16[2,22,16,384]{3,2,1,0:T(8,128)(2,1)S(1)} %fusion.21), channel_id=1, source_target_pairs={{0,1},{1,0},{2,3},{3,2},{4,5},{5,4},{6,7},{7,6},{8,9},{9,8},{10,11... | collective-permute-start | bytes 1622024 | tf_op jit(solution)/shard_map/ppermute | solution.py:780
  496.1 25.4 %collective-permute-start.18 = (bf16[2,23,16,384]{3,2,1,0:T(8,128)(2,1)S(1)}, bf16[2,23,16,384]{3,2,1,0:T(8,128)(2,1)S(1)}, u32[]{:S(2)}, u32[]{:S(2)}) collective-permute-start(bf16[2,23,16,384]{3,2,1,0:T(8,128)(2,1)S(1)} %fusion.16), channel_id=1, source_target_pairs={{0,16},{16,0},{1,17},{17,1},{2,18},{18,2},{3,19},{19,3},{4,20},{20... | collective-permute-start | bytes 1695752 | tf_op jit(solution)/shard_map/ppermute | solution.py:780
  500.6 21.2 %collective-permute-start.15 = (bf16[2,23,16,384]{3,2,1,0:T(8,128)(2,1)S(1)}, bf16[2,23,16,384]{3,2,1,0:T(8,128)(2,1)S(1)}, u32[]{:S(2)}, u32[]{:S(2)}) collective-permute-start(bf16[2,23,16,384]{3,2,1,0:T(8,128)(2,1)S(1)} %fusion.17), channel_id=1, source_target_pairs={{0,1},{1,0},{2,3},{3,2},{4,5},{5,4},{6,7},{7,6},{8,9},{9,8},{10,11... | collective-permute-start | bytes 1695752 | tf_op jit(solution)/shard_map/ppermute | solution.py:780
  512.8 22.2 %collective-permute-start.11 = (bf16[22,16,384]{2,1,0:T(8,128)(2,1)S(1)}, bf16[22,16,384]{2,1,0:T(8,128)(2,1)S(1)}, u32[]{:S(2)}, u32[]{:S(2)}) collective-permute-start(bf16[22,16,384]{2,1,0:T(8,128)(2,1)S(1)} %get-tuple-element.119), channel_id=1, source_target_pairs={{0,4},{2,6},{4,0},{6,2},{1,5},{3,7},{5,1},{7,3},{8,12},{10,14},{12... | collective-permute-start | bytes 811016 | tf_op jit(solution)/shard_map/ppermute | solution.py:780
  512.8 35.8 %collective-permute-start.12 = (bf16[22,16,384]{2,1,0:T(8,128)(2,1)}, bf16[22,16,384]{2,1,0:T(8,128)(2,1)}, u32[]{:S(2)}, u32[]{:S(2)}) collective-permute-start(bf16[22,16,384]{2,1,0:T(8,128)(2,1)} %get-tuple-element.120), channel_id=1, source_target_pairs={{0,6},{2,0},{4,2},{6,4},{1,7},{3,1},{5,3},{7,5},{8,14},{10,8},{12,... | collective-permute-start | bytes 811016 | tf_op jit(solution)/shard_map/ppermute | solution.py:780
  516.1 32.5 %collective-permute-start.8 = (bf16[22,16,384]{2,1,0:T(8,128)(2,1)}, bf16[22,16,384]{2,1,0:T(8,128)(2,1)}, u32[]{:S(2)}, u32[]{:S(2)}) collective-permute-start(bf16[22,16,384]{2,1,0:T(8,128)(2,1)} %fusion.27), channel_id=1, source_target_pairs={{0,2},{2,4},{4,6},{6,0},{1,3},{3,5},{5,7},{7,1},{8,10},{10,12},{12... | collective-permute-start | bytes 811016 | tf_op jit(solution)/shard_map/ppermute | solution.py:780
  521.7 34.0 %collective-permute-start.19 = (bf16[23,16,384]{2,1,0:T(8,128)(2,1)S(1)}, bf16[23,16,384]{2,1,0:T(8,128)(2,1)}, u32[]{:S(2)}, u32[]{:S(2)}) collective-permute-start(bf16[23,16,384]{2,1,0:T(8,128)(2,1)S(1)} %get-tuple-element.117), channel_id=1, source_target_pairs={{0,4},{2,6},{4,0},{6,2},{1,5},{3,7},{5,1},{7,3},{8,12},{10,14},{12... | collective-permute-start | bytes 847880 | tf_op jit(solution)/shard_map/ppermute | solution.py:780
  521.7 33.9 %collective-permute-start.20 = (bf16[23,16,384]{2,1,0:T(8,128)(2,1)S(1)}, bf16[23,16,384]{2,1,0:T(8,128)(2,1)}, u32[]{:S(2)}, u32[]{:S(2)}) collective-permute-start(bf16[23,16,384]{2,1,0:T(8,128)(2,1)S(1)} %get-tuple-element.118), channel_id=1, source_target_pairs={{0,6},{2,0},{4,2},{6,4},{1,7},{3,1},{5,3},{7,5},{8,14},{10,8},{12,... | collective-permute-start | bytes 847880 | tf_op jit(solution)/shard_map/ppermute | solution.py:780
  535.7 20.0 %collective-permute-start.16 = (bf16[23,16,384]{2,1,0:T(8,128)(2,1)}, bf16[23,16,384]{2,1,0:T(8,128)(2,1)}, u32[]{:S(2)}, u32[]{:S(2)}) collective-permute-start(bf16[23,16,384]{2,1,0:T(8,128)(2,1)} %fusion.26), channel_id=1, source_target_pairs={{0,2},{2,4},{4,6},{6,0},{1,3},{3,5},{5,7},{7,1},{8,10},{10,12},{12... | collective-permute-start | bytes 847880 | tf_op jit(solution)/shard_map/ppermute | solution.py:780
  (70 other events, 550.6 us)
Sparse Core Ops, SparseCore 0:
  12.5 121.7 all-gather.1

commit v3 on v2

--- a/solution.py
+++ b/solution.py
@@ -89,26 +89,13 @@
     return (signal, one_minus, beta, alpha, tilde)
 
 
-def silu(value):
-    return value * jax.nn.sigmoid(value)
-
-
-def silu_grad(value):
-    gate = jax.nn.sigmoid(value)
-    return gate * (1.0 + value * (1.0 - gate))
-
-
-def precise(left, right):
-    return jnp.dot(left, right, precision=lax.Precision.HIGHEST)
-
-
 SIDE=32; PIX=SIDE*SIDE
 LIMIT=60*1024*1024
 VM=pltpu.VMEM
 
-def call(kernel, ins, outs, scratch, flops, away=(), away_out=(), alias={}):
+def call(kernel, ins, outs, scratch, flops, away=(), away_out=(), alias={}, scalar=()):
     spec = pl.BlockSpec(memory_space=VM)
-    places = [pl.BlockSpec(memory_space=pl.ANY) if i in away else spec for i in range(len(ins))]
+    places = [pl.BlockSpec(memory_space=pl.ANY if i in away else pltpu.SMEM if i in scalar else VM) for i in range(len(ins))]
     moved = sum(a.size*a.dtype.itemsize for a in ins) + sum(math.prod(o.shape)*o.dtype.itemsize for o in outs)
     return pl.pallas_call(
         kernel, out_shape=outs, in_specs=places,
@@ -184,16 +171,47 @@
     return acc + dot(xs_ref[pl.ds(r+2*SIDE, MC), :], w_ref[base+6*CH:base+9*CH, :])
 
 TAPS=9*CH
-def fetch(whole_ref, base, w_ref, sems, order):
-    copies = []
-    for i in order:
-        copy = pltpu.make_async_copy(whole_ref.at[base+i*TAPS:base+(i+1)*TAPS, :], w_ref.at[i*TAPS:(i+1)*TAPS, :], sems.at[i])
-        copy.start()
-        copies.append(copy)
-    return copies
-
-def block_forward_kernel(base, state_ref, whole_ref, vec_ref, out_ref, inner_ref, stat_ref, pad_ref, xs_ref, w_ref, sems):
-    first_in, second_in = fetch(whole_ref, base, w_ref, sems, (0, 1))
+class Rows:
+    def __init__(self, place, first, tiles):
+        starts = [place.first(d) for d in range(place.total)]
+        self.tiles, self.parts, self.edges = tiles, [], []
+        for d in range(place.total):
+            begin = starts[d]+1 if d else 0
+            end = starts[d+1]+1 if d+1 < place.total else starts[d]+place.block
+            begin, end = max(begin, first), min(end, first+tiles)
+            if begin < end:
+                self.parts.append((d, begin-starts[d], end-starts[d], begin-first))
+            if d and first <= starts[d] < first+tiles:
+                self.edges.append((d, starts[d]-first))
+
+    def scratch(self):
+        return [pltpu.VMEM((self.tiles*TILE, CH), narrow), pltpu.VMEM((max(len(self.edges), 1), TILE, CH), narrow),
+                pltpu.SemaphoreType.DMA((len(self.parts)+len(self.edges),))]
+
+    def copies(self, pieces_ref, low_ref, edge_ref, sems):
+        made = []
+        for d, begin, end, to in self.parts:
+            made.append(pltpu.make_async_copy(pieces_ref.at[d, begin*TILE:end*TILE, :],
+                                              low_ref.at[to*TILE:(to+end-begin)*TILE, :], sems.at[len(made)]))
+        for i, (d, to) in enumerate(self.edges):
+            made.append(pltpu.make_async_copy(pieces_ref.at[d, 0:TILE, :], edge_ref.at[i], sems.at[len(made)]))
+        return made
+
+    def start(self, *refs):
+        for copy in self.copies(*refs):
+            copy.start()
+
+    def finish(self, pieces_ref, low_ref, edge_ref, sems):
+        for copy in self.copies(pieces_ref, low_ref, edge_ref, sems):
+            copy.wait()
+        for i, (d, to) in enumerate(self.edges):
+            low_ref[to*TILE:(to+1)*TILE, :] = low_ref[to*TILE:(to+1)*TILE, :]+edge_ref[i]
+
+def block_forward_kernel(rows, state_ref, pieces_ref, vec_ref, out_ref, inner_ref, stat_ref, pad_ref, xs_ref, *held):
+    one, two = (pieces_ref,)+held[:3], (pieces_ref,)+held[3:]
+    rows[0].start(*one)
+    rows[1].start(*two)
+    w1_ref, w2_ref = held[0], held[3]
     bias1, bias2, gain1, shift1, gain2, shift2, scale, offset = (vec_ref[i:i+1, :] for i in range(8))
     member = membership(CH, CH//GROUPS)
     amount = PIX*(CH//GROUPS)
@@ -209,10 +227,10 @@
         return _
     steps(PIX//EL, act1, 0)
     spread(pad_ref, xs_ref, CH, False)
-    first_in.wait()
+    rows[0].finish(*one)
     def conv1(i, c):
         r = pl.multiple_of(i*MC, MC)
-        v = conv_rows(xs_ref, w_ref, 0, r) + bias1
+        v = conv_rows(xs_ref, w1_ref, 0, r) + bias1
         inner_ref[pl.ds(r, MC), :] = v
         return c[0]+fold(v), c[1]+fold(v*v)
     mean2, inv2 = norm_stats(*steps(PIX//MC, conv1, (z, z)), member, amount)
@@ -224,19 +242,23 @@
         return _
     steps(PIX//EL, act2, 0)
     spread(pad_ref, xs_ref, CH, False)
-    second_in.wait()
+    rows[1].finish(*two)
     def conv2(i, _):
         r = pl.multiple_of(i*MC, MC)
-        out_ref[pl.ds(r, MC), :] = state_ref[pl.ds(r, MC), :] + (conv_rows(xs_ref, w_ref, TAPS, r) + bias2)
+        out_ref[pl.ds(r, MC), :] = state_ref[pl.ds(r, MC), :] + (conv_rows(xs_ref, w2_ref, 0, r) + bias2)
         return _
     steps(PIX//MC, conv2, 0)
     stat_ref[...] = rows_of(mean1, inv1, mean2, inv2)
 
-def block_forward(state, whole, base, vectors):
-    return call(functools.partial(block_forward_kernel, base), [state, whole, vectors],
+def block_rows(place, base):
+    return [Rows(place, (base+i*TAPS)//TILE, TAPS//TILE) for i in range(2)]
+
+def block_forward(place, state, pieces, base, vectors):
+    rows = block_rows(place, base)
+    return call(functools.partial(block_forward_kernel, rows), [state, pieces, vectors],
         [sds((PIX, CH)), sds((PIX, CH)), sds((8, CH))],
-        [pltpu.VMEM((PIX+16, CH), f32), pltpu.VMEM((PIX+2*SIDE, 3*CH), narrow), pltpu.VMEM((2*TAPS, CH), narrow),
-         pltpu.SemaphoreType.DMA((2,))], 2*2*PIX*TAPS*CH, away=(1,))
+        [pltpu.VMEM((PIX+16, CH), f32), pltpu.VMEM((PIX+2*SIDE, 3*CH), narrow)]+rows[0].scratch()+rows[1].scratch(),
+        2*2*PIX*TAPS*CH, away=(1,))
 
 def back_taps(gs_ref, w_ref, base, r):
     acc = None
@@ -257,9 +279,12 @@
         return _
     steps(3, body, 0)
 
-def block_back_kernel(base, grad_ref, state_ref, inner_ref, stat_ref, whole_ref, vec_ref, large_in_ref, out_ref, large_ref, small_ref,
-                      pad_ref, gs_ref, xt_ref, keep_ref, w_ref, dw_ref, sems):
-    second_in, first_in = fetch(whole_ref, base, w_ref, sems, (1, 0))
+def block_back_kernel(base, rows, grad_ref, state_ref, inner_ref, stat_ref, pieces_ref, vec_ref, large_in_ref, out_ref, large_ref, small_ref,
+                      pad_ref, gs_ref, xt_ref, keep_ref, dw_ref, sems, *held):
+    first_in, second_in = (pieces_ref,)+held[:3], (pieces_ref,)+held[3:]
+    rows[1].start(*second_in)
+    rows[0].start(*first_in)
+    w1_ref, w2_ref = held[0], held[3]
     bias1, bias2, gain1, shift1, gain2, shift2, scale, offset = (vec_ref[i:i+1, :] for i in range(8))
     mean1, inv1, mean2, inv2 = (stat_ref[i:i+1, :] for i in range(4))
     member = membership(CH, CH//GROUPS)
@@ -279,12 +304,12 @@
         xt_ref[:, r:r+EL] = jnp.transpose(v*sigmoid(v)).astype(narrow)
     kernel_grads(xt_ref, gs_ref, dw_ref, TAPS)
     half = TAPS//TILE
-    second_out = pltpu.make_async_copy(dw_ref.at[half:2*half], large_ref.at[base//TILE+half:base//TILE+2*half], sems.at[2])
+    second_out = pltpu.make_async_copy(dw_ref.at[half:2*half], large_ref.at[base//TILE+half:base//TILE+2*half], sems.at[0])
     second_out.start()
-    second_in.wait()
+    rows[1].finish(*second_in)
     def back2(i, c):
         r = pl.multiple_of(i*MC, MC)
-        d = back_taps(gs_ref, w_ref, TAPS, r)
+        d = back_taps(gs_ref, w2_ref, 0, r)
         n = (inner_ref[pl.ds(r, MC), :] - mean2)*inv2
         nt = n*gain2 + shift2
         v = nt*scale + offset
@@ -311,12 +336,12 @@
         v = (state_ref[r:r+EL, :] - mean1)*inv1*gain1 + shift1
         xt_ref[:, r:r+EL] = jnp.transpose(v*sigmoid(v)).astype(narrow)
     kernel_grads(xt_ref, gs_ref, dw_ref, 0)
-    first_out = pltpu.make_async_copy(dw_ref.at[0:half], large_ref.at[base//TILE:base//TILE+half], sems.at[3])
+    first_out = pltpu.make_async_copy(dw_ref.at[0:half], large_ref.at[base//TILE:base//TILE+half], sems.at[1])
     first_out.start()
-    first_in.wait()
+    rows[0].finish(*first_in)
     def back1(i, c):
         r = pl.multiple_of(i*MC, MC)
-        d = back_taps(gs_ref, w_ref, 0, r)
+        d = back_taps(gs_ref, w1_ref, 0, r)
         n = (state_ref[pl.ds(r, MC), :] - mean1)*inv1
         v = n*gain1 + shift1
         s = sigmoid(v)
@@ -336,12 +361,13 @@
     second_out.wait()
     small_ref[...] = jnp.concatenate([one(bias1_grad), one(bias2_grad), gain1_grad, dn*scale, shift1_grad, mod_offset*scale, mod_scale, mod_offset], axis=0)
 
-def block_back(grad, state, inner, stat, whole, base, vectors, large):
-    return call(functools.partial(block_back_kernel, base), [grad, state, inner, stat, whole, vectors, large],
+def block_back(place, grad, state, inner, stat, pieces, base, vectors, large):
+    rows = block_rows(place, base)
+    return call(functools.partial(block_back_kernel, base, rows), [grad, state, inner, stat, pieces, vectors, large],
         [sds((PIX, CH)), sds(large.shape, narrow), sds((8, CH))],
         [pltpu.VMEM((PIX+16, CH), f32), pltpu.VMEM((PIX+2*SIDE, 3*CH), narrow), pltpu.VMEM((CH, PIX), narrow),
-         pltpu.VMEM((PIX, CH), f32), pltpu.VMEM((2*TAPS, CH), narrow), pltpu.VMEM((2*TAPS//TILE, TILE, CH), narrow),
-         pltpu.SemaphoreType.DMA((4,))], 2*4*PIX*TAPS*CH, away=(4, 6), away_out=(1,), alias={6: 1})
+         pltpu.VMEM((PIX, CH), f32), pltpu.VMEM((2*TAPS//TILE, TILE, CH), narrow),
+         pltpu.SemaphoreType.DMA((2,))]+rows[0].scratch()+rows[1].scratch(), 2*4*PIX*TAPS*CH, away=(4, 6), away_out=(1,), alias={6: 1})
 
 PHASES = [(0, 0), (0, 1), (1, 0), (1, 1)]
 OFFSETS = [(dy, dx) for dy in (-1, 0, 1) for dx in (-1, 0, 1)]
@@ -365,7 +391,11 @@
     rows.append(jnp.zeros((128-72, PIX), f32))
     return jnp.concatenate(rows, axis=0)
 
-def stem_down_kernel(noisy_ref, sw_ref, sb_ref, dw_ref, db_ref, skip_ref, state_ref, pad_ref, xs_ref):
+DOWN_FIRST = (ROW["down_w"]+LEAD)//TILE
+DOWN_TILES = -(-(ROW["down_b"]+1+LEAD)//TILE)-DOWN_FIRST
+
+def stem_down_kernel(source_rows, noisy_ref, sw_ref, sb_ref, pieces_ref, skip_ref, state_ref, dw_ref, pad_ref, xs_ref, wide_ref, *held):
+    source_rows.start(pieces_ref, *held)
     phases = [noisy_ref[i] for i in range(4)]
     col = pixel_column(EL, C0)
     xs_ref[:, 0:SIDE, :] = jnp.zeros((6, SIDE, C0), narrow)
@@ -380,19 +410,26 @@
             pad_ref[8:8+PIX, :] = v.astype(f32)
             for r in range(0, PIX, EL):
                 xs_ref[3*a, SIDE+r:SIDE+r+EL, :] = jnp.where(col == 0, 0.0, pad_ref[r+7:r+7+EL, :]).astype(narrow)
+    source_rows.finish(pieces_ref, *held)
+    wide_ref[...] = held[0][...].astype(f32)
+    at = ROW["down_w"]+LEAD-DOWN_FIRST*TILE
+    dw_ref[...] = wide_ref[at:at+9*C0, :].astype(narrow)
     acc = None
     for t, (dy, dx) in enumerate(OFFSETS):
         top = 0 if dy == -1 else SIDE
         part = dot(xs_ref[3*(dy % 2)+dx+1, top:top+PIX, :], dw_ref[t*C0:(t+1)*C0, :])
         acc = part if acc is None else acc+part
-    state_ref[...] = acc + db_ref[...]
-
-def stem_down(noisy, stem_w, stem_b, down_w, down_b):
-    return call(stem_down_kernel, [noisy, stem_w, stem_b, down_w, down_b],
-        [sds((4, PIX, C0), narrow), sds((PIX, CH))],
-        [pltpu.VMEM((PIX+16, C0), f32), pltpu.VMEM((6, PIX+SIDE, C0), narrow)], 2*PIX*9*C0*CH)
-
-def down_stem_back_kernel(grad_ref, skip_ref, more_ref, dw_ref, noisy_ref, large_in_ref, large_ref, sdw_ref, small_ref, small_s_ref,
+    state_ref[...] = acc + wide_ref[at+9*C0:at+9*C0+1, :]
+
+def stem_down(place, noisy, stem_w, stem_b, pieces):
+    rows = Rows(place, DOWN_FIRST, DOWN_TILES)
+    return call(functools.partial(stem_down_kernel, rows), [noisy, stem_w, stem_b, pieces],
+        [sds((4, PIX, C0), narrow), sds((PIX, CH)), sds((9*C0, CH), narrow)],
+        [pltpu.VMEM((PIX+16, C0), f32), pltpu.VMEM((6, PIX+SIDE, C0), narrow), pltpu.VMEM((DOWN_TILES*TILE, CH), f32)]+rows.scratch(),
+        2*PIX*9*C0*CH, away=(3,))
+
+def down_stem_back_kernel(n, me_ref, grad_ref, skip_ref, more_ref, dw_ref, noisy_ref, head_ref, attn_ref, s1_ref, s0_ref,
+                          large_in_ref, large_ref, small_ref,
                           pad_ref, gs_ref, ddw_ref, low_ref, sems):
     top_row = ROW["down_w"]+LEAD
     spare = top_row % TILE
@@ -411,7 +448,7 @@
         total += fold(g)
     for r in range(0, PIX, EL):
         gs_ref[1, r:r+EL, :] = jnp.where(col == SIDE-1, 0.0, pad_ref[r+1:r+1+EL, :]).astype(narrow)
-    small_ref[...] = rows_of(jnp.sum(total, axis=0, keepdims=True))
+    down_bias = jnp.sum(total, axis=0, keepdims=True)
     def shifted(dy, dx):
         top = SIDE if dy == -1 else 0
         return gs_ref[1 if dx == -1 else 0, top:top+PIX, :]
@@ -436,15 +473,27 @@
     copy = pltpu.make_async_copy(low_ref, large_ref.at[top_row//TILE:top_row//TILE+9*C0//TILE+1], sems.at[0])
     copy.start()
     copy.wait()
-    sdw_ref[...] = stem_grad
-    small_s_ref[...] = rows_of(jnp.sum(stem_bias, axis=0, keepdims=True))
-
-def down_stem_back(grad, skip, more, down_w, noisy, large):
-    return call(down_stem_back_kernel, [grad, skip, more, down_w, noisy, large],
-        [sds(large.shape, narrow), sds((128, C0)), sds((8, CH)), sds((8, C0))],
+    small_ref[SMALL_STEM:SMALL_STEM+40, :] = jnp.concatenate(
+        [stem_grad[0:40, :], jnp.concatenate([stem_grad[40:72, :], jnp.zeros((8, C0), f32)], axis=0)], axis=1)
+    stem_bias = jnp.sum(stem_bias, axis=0, keepdims=True)
+    small_ref[SMALL_HEAD:SMALL_HEAD+120, :] = head_ref[...]
+    small_ref[SMALL_ATTN:SMALL_ATTN+8, :] = attn_ref[...]
+    small_ref[SMALL_S1:SMALL_S1+8, :] = s1_ref[...]
+    small_ref[SMALL_S0:SMALL_S0+8, :] = s0_ref[...]
+    mine = lax.broadcasted_iota(jnp.int32, (n, CH), 0) == me_ref[0]
+    for b, from_ref in enumerate((s0_ref, s1_ref)):
+        for h in range(2):
+            at = SMALL_MOVED+(2*b+h)*n
+            small_ref[at:at+n, :] = jnp.where(mine, from_ref[6+h:7+h, :], 0.0)
+    small_ref[SMALL_STEM+40:SMALL_STEM+48, :] = rows_of(down_bias, jnp.concatenate([stem_bias, jnp.zeros((1, C0), f32)], axis=1))
+
+def down_stem_back(me, n, grad, skip, more, down_w, noisy, head_tail, attn_small, s1, s0, large):
+    return call(functools.partial(down_stem_back_kernel, n),
+        [me.reshape(1), grad, skip, more, down_w, noisy, head_tail, attn_small, s1, s0, large],
+        [sds(large.shape, narrow), sds((SMALL_MOVED+4*n, CH))],
         [pltpu.VMEM((PIX+16, CH), f32), pltpu.VMEM((2, PIX+SIDE, CH), narrow), pltpu.VMEM((9*C0+TILE, CH), f32),
          pltpu.VMEM((9*C0//TILE+1, TILE, CH), narrow), pltpu.SemaphoreType.DMA((1,))],
-        2*2*PIX*9*C0*CH, away=(5,), away_out=(0,), alias={5: 0})
+        2*2*PIX*9*C0*CH, away=(10,), away_out=(0,), alias={10: 0}, scalar=(0,))
 
 HEAD_PER = (C0+CH)//GROUPS
 def silu_slope(v):
@@ -453,7 +502,7 @@
 
 KL = 0.001
 def head_kernel(num_ref, state_ref, skip_ref, wu_ref, ws_ref, vu_ref, vs_ref, bias_ref, noise_ref, mask_ref,
-                state_grad_ref, skip_grad_ref, gu_ref, gs_ref, small_u_ref, small_s_ref, gb_ref, loss_ref,
+                state_grad_ref, skip_grad_ref, tail_ref, loss_ref,
                 up_ref, side_ref, q_ref):
     log_beta, log_tilde, coefficient, sample = (num_ref[i] for i in range(4))
     gain_u, shift_u = vu_ref[0:1, :], vu_ref[1:2, :]
@@ -517,7 +566,9 @@
         og = og.astype(narrow).astype(f32)
         bias_grad += og
         outs.append(og)
-    gb_ref[...] = jnp.broadcast_to(jnp.sum(bias_grad, axis=1, keepdims=True), (8, 128))
+    bias_grad = jnp.broadcast_to(jnp.sum(bias_grad, axis=1, keepdims=True), (8, CH))
+    diagonal = lax.broadcasted_iota(jnp.int32, (8, CH), 0) == lax.broadcasted_iota(jnp.int32, (8, CH), 1)
+    bias_grad = jnp.sum(jnp.where(diagonal, bias_grad, 0.0), axis=0, keepdims=True)
     loss_ref[...] = jnp.concatenate([jnp.broadcast_to(jnp.sum(loss, axis=1, keepdims=True), (1, 128)),
         jnp.broadcast_to(jnp.sum(vlb, axis=1, keepdims=True), (1, 128)), jnp.zeros((6, 128), f32)], axis=0)
     nine_sum, gs_total = None, None
@@ -533,9 +584,10 @@
         d = d*silu_slope(n*gain_s+shift_s)
         skip_grad_ref[k] = d
         d1, d2 = d1+fold(d), d2+fold(d*n)
-    gs_ref[...] = gs_total
+    tail_ref[72:112, :] = jnp.concatenate(
+        [gs_total[0:40, :], jnp.concatenate([gs_total[40:72, :], jnp.zeros((8, C0), f32)], axis=0)], axis=1)
     hi = nine_sum.astype(narrow); lo = (nine_sum-hi.astype(f32)).astype(narrow)
-    gu_ref[...] = dot(hi, up_ref[...])+dot(lo, up_ref[...])
+    tail_ref[0:72, :] = (dot(hi, up_ref[...])+dot(lo, up_ref[...]))[0:72, :]
     turned = jnp.transpose(nine_sum)
     hi = turned.astype(narrow); lo = (turned-hi.astype(f32)).astype(narrow)
     d = dot(hi, wu_ref[...])+dot(lo, wu_ref[...])
@@ -544,8 +596,7 @@
     state_grad_ref[...] = d
     e1, e2 = one(fold(d)), one(fold(d*n))
     d1, d2 = one(d1), one(d2)
-    small_u_ref[...] = rows_of(e2, e1)
-    small_s_ref[...] = rows_of(d2, d1)
+    tail_ref[112:120, :] = rows_of(e2, e1, jnp.concatenate([d2, d1], axis=1), bias_grad)
     tot = (exact(rows_of(e1*gain_u, e2*gain_u), mu)+exact(rows_of(d1*gain_s, d2*gain_s), ms))/amount
     tot_u, tot_s = exact_nt(tot, mu), exact_nt(tot, ms)
     def back_u(i, _):
@@ -565,7 +616,7 @@
 def head(numbers, state, skip, wu, ws, vu, vs, bias, noise, mask):
     spec = pl.BlockSpec(memory_space=VM)
     ins = [numbers, state, skip, wu, ws, vu, vs, bias, noise, mask]
-    outs = [sds((PIX, CH)), sds((4, PIX, C0)), sds((128, CH)), sds((128, C0)), sds((8, CH)), sds((8, C0)), sds((8, 128)), sds((8, 128))]
+    outs = [sds((PIX, CH)), sds((4, PIX, C0)), sds((120, CH)), sds((8, 128))]
     return pl.pallas_call(head_kernel, out_shape=outs,
         in_specs=[pl.BlockSpec(memory_space=pltpu.SMEM)]+[spec]*(len(ins)-1), out_specs=[spec]*len(outs),
         scratch_shapes=[pltpu.VMEM((PIX, CH), narrow), pltpu.VMEM((4, PIX, C0), narrow), pltpu.VMEM((4, 128, PIX), f32)],
@@ -587,11 +638,10 @@
     for i in range(3):
         ref[i, at, :] = value[:, i*128:(i+1)*128]
 
-def attention_forward_kernel(state_ref, whole_ref, out_ref, qkv_ref, log_ref, mixed_t_ref, stat_ref, wp_ref, wo_ref, vec_ref,
-                             mixed_ref, vt_ref, bp_ref, rows_ref, wide_ref, sems):
-    copy = pltpu.make_async_copy(whole_ref.at[ATTN_FIRST*TILE:(ATTN_FIRST+ATTN_TILES)*TILE, :], rows_ref, sems.at[0])
-    copy.start()
-    copy.wait()
+def attention_forward_kernel(rows, state_ref, pieces_ref, out_ref, qkv_ref, log_ref, mixed_t_ref, stat_ref, wp_ref, wo_ref, vec_ref,
+                             mixed_ref, vt_ref, bp_ref, wide_ref, rows_ref, edge_ref, sems):
+    rows.start(pieces_ref, rows_ref, edge_ref, sems)
+    rows.finish(pieces_ref, rows_ref, edge_ref, sems)
     for r in range(0, ATTN_TILES*TILE, 16*TILE):
         end = min(r+16*TILE, ATTN_TILES*TILE)
         put_rows(wide_ref, slice(r, end), rows_ref[r:end, :].astype(f32))
@@ -642,16 +692,17 @@
         return _
     steps(PIX//256, finish, 0)
 
-def attention_forward(state, whole):
-    return call(attention_forward_kernel, [state, whole],
+def attention_forward(place, state, pieces):
+    rows = Rows(place, ATTN_FIRST, ATTN_TILES)
+    return call(functools.partial(attention_forward_kernel, rows), [state, pieces],
         [sds((PIX, CH)), sds((PIX, 3*QW), narrow), sds((8, PIX)), sds((QW, PIX), narrow), sds((8, CH)),
          sds((CH, 3*QW), narrow), sds((QW, CH), narrow), sds((8, CH))],
         [pltpu.VMEM((PIX, QW), narrow), pltpu.VMEM((HP, PIX), narrow), pltpu.VMEM((1, 3*QW), f32),
-         pltpu.VMEM((ATTN_TILES*TILE, CH), narrow), pltpu.VMEM((3, ATTN_TILES*TILE, 128), f32), pltpu.SemaphoreType.DMA((1,))],
+         pltpu.VMEM((3, ATTN_TILES*TILE, 128), f32)]+rows.scratch(),
         2*PIX*(CH*4*QW+2*PIX*QW), away=(1,))
 
 def attention_back_kernel(grad_ref, state_ref, stat_ref, qkv_ref, log_ref, mixed_t_ref, wp_ref, wo_ref, vec_ref,
-                          out_ref, large_ref, small_ref, bias_ref, dm_ref, pg_ref, kt_ref, dv_ref, dk_ref, nt_ref, keep_ref,
+                          out_ref, large_ref, small_ref, dm_ref, pg_ref, kt_ref, dv_ref, dk_ref, nt_ref, keep_ref,
                           wide_ref, rows_ref, sems):
     gain, shift = vec_ref[0:1, :], vec_ref[1:2, :]
     mean, inv = stat_ref[0:1, :], stat_ref[1:2, :]
@@ -712,7 +763,7 @@
         out_ref[r, :] = d
         return c[0]+fold(d), c[1]+fold(d*n), c[2]+fold(pg_ref[r, :].astype(f32))
     shift_grad, gain_grad, bias_grad = (one(v) for v in steps(PIX//256, norm_grad, (z, z, zb)))
-    bias_ref[...] = rows_of(bias_grad)
+    compact = [jnp.concatenate([bias_grad[:, j*QW+h*HP:j*QW+h*HP+HEAD_DIM] for h in range(HEADS)], axis=1) for j in (0, 2)]
     tot = group_totals(rows_of(shift_grad*gain, gain_grad*gain), member)/(PIX*(CH//GROUPS))
     first, second = tot[0:1], tot[1:2]
     def finish(i, _):
@@ -721,12 +772,12 @@
         out_ref[r, :] = grad_ref[r, :]+(out_ref[r, :]*gain-first-n*second)*inv
         return _
     steps(PIX//EL, finish, 0)
-    small_ref[...] = rows_of(gain_grad, shift_grad, one(proj_bias))
+    small_ref[...] = rows_of(gain_grad, shift_grad, compact[0], compact[1], one(proj_bias))
     copy.wait()
 
 def attention_back(grad, state, stat, qkv, log, mixed_t, wp, wo, vec, tiles):
     return call(attention_back_kernel, [grad, state, stat, qkv, log, mixed_t, wp, wo, vec],
-        [sds((PIX, CH)), sds((tiles, TILE, CH), narrow), sds((8, CH)), sds((8, 3*QW))],
+        [sds((PIX, CH)), sds((tiles, TILE, CH), narrow), sds((8, CH))],
         [pltpu.VMEM((PIX, QW), narrow), pltpu.VMEM((PIX, 3*QW), narrow), pltpu.VMEM((HP, PIX), narrow), pltpu.VMEM((PIX, HP), f32),
          pltpu.VMEM((PIX, HP), f32), pltpu.VMEM((CH, PIX), narrow), pltpu.VMEM((PIX, CH), narrow),
          pltpu.VMEM((3, ATTN_TILES*TILE, 128), f32), pltpu.VMEM((ATTN_TILES, TILE, CH), narrow), pltpu.SemaphoreType.DMA((1,))],
@@ -745,11 +796,6 @@
 def taps_rows(v):
     v = jnp.pad(v, ((0, 0), (0, 8-v.shape[1]), (0, 0))).reshape(72, v.shape[2])
     return jnp.pad(v, ((0, 128-72), (0, 0)))
-
-
-def heads_unpad(v):
-    v = v.reshape(v.shape[:-1]+(-1, HP))[..., :HEAD_DIM]
-    return v.reshape(v.shape[:-2]+(-1,))
 
 
 class Place:
@@ -780,8 +826,16 @@
     return lax.ppermute(value, axis, [(i, (i+distance) % size) for i in range(size)])
 
 
+def hold_for(value, others):
+    return lax.optimization_barrier((value, others))[0]
+
+
 def add_everywhere(value, place):
-    for axis in ("c", "x", "y", "z"):
+    return add_over(value, place, ("c", "x", "y", "z"))
+
+
+def add_over(value, place, axes):
+    for axis in axes:
         size, step = place.sizes[axis], 1
         while step < size:
             value = value+lax.ppermute(value, axis, [(i, i ^ step) for i in range(size)])
@@ -806,7 +860,7 @@
         out_specs=pl.BlockSpec(memory_space=VM),
         scratch_shapes=[pltpu.SemaphoreType.DMA((count,))],
         compiler_params=pltpu.CompilerParams(vmem_limit_bytes=LIMIT),
-        cost_estimate=pl.CostEstimate(flops=0, bytes_accessed=4*count*size*TILE*WIDE, transcendentals=0),
+        cost_estimate=pl.CostEstimate(flops=0, bytes_accessed=1024, transcendentals=0),
     )(starts, large)
 
 
@@ -818,13 +872,10 @@
     for i in range(count):
         copies[i].wait()
         which, at = sends[i]
-        def body(t, _):
-            outs[which][at, t] = (held_ref[i, t].astype(f32)+arrived_ref[i, t].astype(f32)).astype(outs[which].dtype)
-            return _
-        lax.fori_loop(0, size, body, 0)
-
-
-def share_out(large, place, parts):
+        outs[which][at] = (held_ref[i].astype(f32)+arrived_ref[i].astype(f32)).astype(outs[which].dtype)
+
+
+def share_out(large, small, place, parts):
     s, a, block = place.sizes, place.at, place.block
     half = (s["z"]+1)//2
     coords = [(y, z, x) for y in range(s["y"]) for z in range(s["z"]) for x in range(s["x"])]
@@ -834,7 +885,7 @@
             place.first(place.device((a["y"]+y) % s["y"], core, (a["z"]+z) % s["z"], (a["x"]+x) % s["x"])) for y, z, x in coords
         ]).astype(jnp.int32)
 
-    other, mine = starts(1-a["c"]), starts(a["c"])
+    far_starts, own_starts = starts(1-a["c"]), starts(a["c"])
     bounds = [block*i//parts for i in range(parts+1)]
     groups = [("y", [(0, z, x) for z in range(half) for x in range(s["x"])])]
     groups += [("y%d" % k, [(k, z, x) for z in range(half) for x in range(s["x"])]) for k in range(1, s["y"])]
@@ -845,68 +896,67 @@
     for g, (name, members) in enumerate(groups):
         for at, member in enumerate(members):
             sends[coords.index(member)] = (g, at)
-    results = []
+    length = small.shape[0]//2
+    half_small, other_small = (lax.dynamic_slice_in_dim(small, core*length, length) for core in (a["c"], 1-a["c"]))
+    arrived, merged = [], []
     for part in range(parts):
-        begin, size = bounds[part], bounds[part+1]-bounds[part]
-        arrived = turn(cut(large, other+begin, size), "c", 2, 1)
+        sent = cut(large, far_starts+bounds[part], bounds[part+1]-bounds[part])
+        arrived.append(turn(sent, "c", 2, 1))
+        far_starts = hold_for(far_starts, sent)
+    half_small = add_over(half_small+turn(other_small, "c", 2, 1), place, ("x",))
+    for part in range(parts):
+        size = bounds[part+1]-bounds[part]
         outs = [sds((len(members), size, TILE, WIDE), f32 if name in ("y", "x") else narrow) for name, members in groups]
-        merged = pl.pallas_call(
+        out = pl.pallas_call(
             functools.partial(merge_kernel, coords, sends, len(coords), size),
             out_shape=outs,
             in_specs=[pl.BlockSpec(memory_space=pltpu.SMEM), pl.BlockSpec(memory_space=pl.ANY), pl.BlockSpec(memory_space=VM)],
             out_specs=[pl.BlockSpec(memory_space=VM)]*len(outs),
             scratch_shapes=[pltpu.VMEM((len(coords), size, TILE, WIDE), narrow), pltpu.SemaphoreType.DMA((len(coords),))],
             compiler_params=pltpu.CompilerParams(vmem_limit_bytes=LIMIT),
-            cost_estimate=pl.CostEstimate(flops=0, bytes_accessed=8*len(coords)*size*TILE*WIDE, transcendentals=0),
-        )(mine+begin, large, arrived)
-        merged = dict(zip(names, merged))
-        near, far = merged["y"], merged["x"]
-        near = near+sum(turn(merged["y%d" % k], "y", s["y"], k).astype(f32) for k in range(1, s["y"]))
-        far = far+sum(turn(merged["x%d" % k], "x", s["x"], k).astype(f32) for k in range(1, s["x"]))
-        near = near.reshape((half, s["x"])+near.shape[1:])
-        far = far.reshape((s["z"]-half, s["y"])+far.shape[1:])
+            cost_estimate=pl.CostEstimate(flops=0, bytes_accessed=1024, transcendentals=0),
+        )(own_starts+bounds[part], large, arrived[part])
+        own_starts = hold_for(own_starts, out)
+        merged.append(dict(zip(names, out)))
+
+    def first_stage(sums):
+        return ([turn(sums["y%d" % k], "y", s["y"], k) for k in range(1, s["y"])],
+                [turn(sums["x%d" % k], "x", s["x"], k) for k in range(1, s["x"])])
+
+    def first_sums(sums, came):
+        near = sums["y"]+sum(value.astype(f32) for value in came[0])
+        far = sums["x"]+sum(value.astype(f32) for value in came[1])
+        return near.reshape((half, s["x"])+near.shape[1:]), far.reshape((s["z"]-half, s["y"])+far.shape[1:])
+
+    def second_sums(near, far):
         near = near[:, 0]+sum(turn(near[:, k].astype(narrow), "x", s["x"], k).astype(f32) for k in range(1, s["x"]))
         far = far[:, 0]+sum(turn(far[:, k].astype(narrow), "y", s["y"], k).astype(f32) for k in range(1, s["y"]))
+        return near, far
+
+    def third_sum(near, far):
         total = near[0]
         for z in range(1, s["z"]):
             value = near[z] if z < half else far[z-half]
             total = total+turn(value.astype(narrow), "z", s["z"], z).astype(f32)
-        results.append(total)
-    return jnp.concatenate(results, axis=0)
-
-
-def assemble_kernel(share, count, block, pieces_ref, out_ref, held_ref, sems):
-    firsts = [(share*d+LEAD)//TILE for d in range(count)]
-    firsts.append(firsts[-1]+block)
-    arriving, leaving = [], []
-    for d in range(count):
-        copy = pltpu.make_async_copy(pieces_ref.at[d], held_ref.at[d], sems.at[0, d])
-        copy.start()
-        arriving.append(copy)
-    for d in range(count):
-        arriving[d].wait()
-        if d:
-            held_ref[d, 0] = held_ref[d, 0]+held_ref[d-1, firsts[d]-firsts[d-1]]
-        size = firsts[d+1]-firsts[d]
-        copy = pltpu.make_async_copy(held_ref.at[d, 0:size], out_ref.at[firsts[d]:firsts[d]+size], sems.at[1, d])
-        copy.start()
-        leaving.append(copy)
-    for copy in leaving:
-        copy.wait()
-
-
-def assemble(pieces, place):
-    count, block = place.total, place.block
-    anywhere = pl.BlockSpec(memory_space=pl.ANY)
-    return pl.pallas_call(
-        functools.partial(assemble_kernel, place.share, count, block),
-        out_shape=sds((place.tiles, TILE, WIDE), narrow),
-        in_specs=[anywhere],
-        out_specs=anywhere,
-        scratch_shapes=[pltpu.VMEM((count, block, TILE, WIDE), narrow), pltpu.SemaphoreType.DMA((2, count))],
-        compiler_params=pltpu.CompilerParams(vmem_limit_bytes=LIMIT),
-        cost_estimate=pl.CostEstimate(flops=0, bytes_accessed=4*count*block*TILE*WIDE, transcendentals=0),
-    )(pieces)
+        return total
+
+    waiting = [first_stage(merged[part]) for part in range(min(2, parts))]
+    results, ready = [], None
+    for part in range(parts):
+        if part == 0:
+            waiting[0] = hold_for(waiting[0], merged[-1])
+        near, far = first_sums(merged[part], waiting[part])
+        if part == 0:
+            half_small = add_over(hold_for(half_small, (near, far)), place, ("y",))
+        if part == min(1, parts-1):
+            half_small = add_over(hold_for(half_small, (near, far)), place, ("z",))
+        if part+2 < parts:
+            waiting.append(first_stage(hold_for(merged[part+2], (near, far))))
+        results.append(third_sum(*second_sums(near, far)))
+    other_small = turn(half_small, "c", 2, 1)
+    first = a["c"] == 0
+    small = jnp.concatenate([jnp.where(first, half_small, other_small), jnp.where(first, other_small, half_small)])
+    return jnp.concatenate(results, axis=0), small
 
 
 SPOTS = (
@@ -917,63 +967,195 @@
     + [ROW["res_gain"]+i for i in range(4)]
     + [ROW["res_shift"]+i for i in range(4)]
     + [ROW["attn_gain"], ROW["attn_shift"], ROW["qv_b"], ROW["qv_b"]+1, ROW["proj_b"]]
-    + [ROW["head_gain"]+i for i in range(85)]
+    + [ROW["head_gain"]+i for i in range(3)] + [ROW["head_b"]] + [-1]*4
+    + [ROW["head_gain"]+3+9*tap+part if tap < 9 else -1 for part in range(9) for tap in range(16)]
 )
-
-
-def time_forward(steps, w1, b1, w2, b2):
-    half = C0 // 2
-    freqs = jnp.exp(-math.log(10000.0) * jnp.arange(half).astype(f32) / half)
-    angles = steps[:, None] * freqs
-    sinus = jnp.concatenate([jnp.cos(angles), jnp.sin(angles)], axis=-1).astype(narrow)
-    hidden_pre = dot(sinus, w1) + b1
-    hidden = silu(hidden_pre).astype(narrow)
-    outer_pre = dot(hidden, w2) + b2
-    return silu(outer_pre).astype(narrow), (sinus, hidden_pre, hidden, outer_pre)
-
-
-def rank_one_share(place, kept, embed, hidden_grad, outer_grad, moved, small):
+SPOTS += [-1]*(256-len(SPOTS))
+
+TIME_FIRST = (ROW["time1_w"]+LEAD)//TILE
+TIME_TILES = -(-(ROW["time2_b"]+2+LEAD)//TILE)-TIME_FIRST
+EMB_FIRST = (ROW["res_b"]+LEAD)//TILE
+EMB_TILES = -(-(ROW["res_shift"]+4+LEAD)//TILE)-EMB_FIRST
+
+
+def widen_rows(low_ref, wide_ref, count):
+    for r in range(0, count, 16*TILE):
+        end = min(r+16*TILE, count)
+        put_rows(wide_ref, slice(r, end), low_ref[r:end, :].astype(f32))
+
+
+def time_kernel(n, rows, me_ref, sinus_ref, pieces_ref, hidden_pre_ref, hidden_ref, outer_pre_ref, embed_ref, vec_ref, w2_ref, we_ref,
+                time_ref, emb_ref, *held):
+    one, two = (pieces_ref,)+held[:3], (pieces_ref,)+held[3:]
+    rows[0].start(*one)
+    rows[1].start(*two)
+    rows[0].finish(*one)
+    time_low_ref, emb_low_ref = held[0], held[3]
+    widen_rows(time_low_ref, time_ref, TIME_TILES*TILE)
+
+    def in_time(name, i=0):
+        return ROW[name]+LEAD-TIME_FIRST*TILE+i
+
+    def in_emb(name, i=0):
+        return ROW[name]+LEAD-EMB_FIRST*TILE+i
+
+    def row(ref, at):
+        return get_rows(ref, slice(at, at+1))
+
+    for h in range(2):
+        w1 = get_rows(time_ref, pl.ds(in_time("time1_w", h), C0, stride=2)).astype(narrow)
+        hidden_pre_ref[:, h*CH:(h+1)*CH] = dot(sinus_ref[...], w1)+row(time_ref, in_time("time1_b", h))
+        w2_ref[h] = get_rows(time_ref, pl.ds(in_time("time2_w", h), TEMB, stride=2)).astype(narrow)
+    v = hidden_pre_ref[...]
+    hidden_ref[...] = (v*sigmoid(v)).astype(narrow)
+    for h in range(2):
+        outer_pre_ref[:, h*CH:(h+1)*CH] = dot(hidden_ref[...], w2_ref[h])+row(time_ref, in_time("time2_b", h))
+    v = outer_pre_ref[...]
+    embed = (v*sigmoid(v)).astype(narrow)
+    embed_ref[...] = embed
+    mine = lax.broadcasted_iota(jnp.int32, (n, TEMB), 0) == me_ref[0]
+    own = jnp.sum(jnp.where(mine, embed.astype(f32), 0.0), axis=0, keepdims=True)
+    own = jnp.broadcast_to(own, (8, TEMB)).astype(narrow)
+    rows[1].finish(*two)
+    widen_rows(emb_low_ref, emb_ref, EMB_TILES*TILE)
+    for b in range(BLOCKS):
+        modulate = []
+        for h in range(2):
+            we_ref[b, h] = get_rows(emb_ref, pl.ds(in_emb("emb_w", 2*TEMB*b+h), TEMB, stride=2)).astype(narrow)
+            modulate.append(dot(own, we_ref[b, h])[0:1]+row(emb_ref, in_emb("emb_b", 2*b+h)))
+        vec_ref[b] = jnp.concatenate([
+            row(emb_ref, in_emb("res_b", 2*b)), row(emb_ref, in_emb("res_b", 2*b+1)),
+            row(emb_ref, in_emb("res_gain", 2*b)), row(emb_ref, in_emb("res_shift", 2*b)),
+            row(emb_ref, in_emb("res_gain", 2*b+1)), row(emb_ref, in_emb("res_shift", 2*b+1)),
+            1.0+modulate[0], modulate[1],
+        ], axis=0)
+
+
+def time_and_modulation(place, sinus, pieces):
+    rows = [Rows(place, TIME_FIRST, TIME_TILES), Rows(place, EMB_FIRST, EMB_TILES)]
+    n = sinus.shape[0]
+    spec = pl.BlockSpec(memory_space=VM)
+    return pl.pallas_call(
+        functools.partial(time_kernel, n, rows),
+        out_shape=[sds((n, TEMB)), sds((n, TEMB), narrow), sds((n, TEMB)), sds((n, TEMB), narrow), sds((BLOCKS, 8, CH)),
+                   sds((2, TEMB, CH), narrow), sds((BLOCKS, 2, TEMB, CH), narrow)],
+        in_specs=[pl.BlockSpec(memory_space=pltpu.SMEM), spec, pl.BlockSpec(memory_space=pl.ANY)],
+        out_specs=[spec]*7,
+        scratch_shapes=[pltpu.VMEM((3, TIME_TILES*TILE, 128), f32), pltpu.VMEM((3, EMB_TILES*TILE, 128), f32)]
+        + rows[0].scratch()+rows[1].scratch(),
+        compiler_params=pltpu.CompilerParams(vmem_limit_bytes=LIMIT),
+        cost_estimate=pl.CostEstimate(flops=2**27, bytes_accessed=8*2**20, transcendentals=0),
+    )(place.me().reshape(1), sinus, pieces)
+
+
+SMALL_HEAD, SMALL_ATTN, SMALL_S1, SMALL_STEM, SMALL_S0, SMALL_MOVED = 0, 120, 128, 136, 184, 192
+
+
+def owner_kernel(share, n, me_ref, small_ref, sinus_ref, hidden_pre_ref, hidden_ref, outer_pre_ref, embed_ref, w2_ref, we_ref, spot_ref,
+                 out_ref, time_ref, emb_ref, mixed_time_ref, mixed_emb_ref):
+    row0 = me_ref[0]*share
+    half_rows = mixed_time_ref.shape[1]//2
+    one = lambda v: jnp.sum(v, axis=0, keepdims=True)
+    moved = [[small_ref[SMALL_MOVED+(2*b+h)*n:SMALL_MOVED+(2*b+h+1)*n, :] for h in range(2)] for b in range(BLOCKS)]
+    embed_grad = sum(exact_nt(moved[b][h], we_ref[b, h]) for b in range(BLOCKS) for h in range(2))
+    outer_grad = embed_grad*silu_slope(outer_pre_ref[...])
+    hidden_grad = sum(exact_nt(outer_grad[:, h*CH:(h+1)*CH], w2_ref[h]) for h in range(2))*silu_slope(hidden_pre_ref[...])
+
+    def table(ref, values):
+        ref[...] = jnp.zeros(ref.shape, f32)
+        width = min(n, 128)
+        for family, (value_ref, at) in enumerate(values):
+            turned = jnp.transpose(value_ref[...].astype(f32))
+            for first in range(0, n, width):
+                group, lane = divmod(family*n+first, 128)
+                ref[group, half_rows+at:half_rows+at+turned.shape[0], lane:lane+width] = turned[:, first:first+width]
+
+    def products(ref, begin, factors, mixed_ref):
+        away = row0-begin+(1 << 20)
+        place = away // 2 - (1 << 19)
+        start = jnp.clip(place+half_rows, 0, ref.shape[1]-half_rows)
+        for h in range(2):
+            right = jnp.concatenate([factors[0][h], factors[1][h]], axis=0)
+            if right.shape[0] < 128:
+                right = jnp.concatenate([right, jnp.zeros((128-right.shape[0], CH), f32)], axis=0)
+            total = None
+            for group in range(ref.shape[0]):
+                left = ref[group, pl.ds(start, half_rows), :].astype(narrow)
+                part = sum(dot(left, p) for p in three(right[group*128:(group+1)*128]))
+                total = part if total is None else total+part
+            put_rows(mixed_ref, pl.ds(h, half_rows, stride=2), total)
+        odd = away-2*(away//2)
+        return jnp.where(odd == 1, get_rows(mixed_ref, slice(1, 1+share)), get_rows(mixed_ref, slice(0, share)))
+
+    halves = lambda v: [v[:, :CH], v[:, CH:]]
+    table(time_ref, [(sinus_ref, 0), (hidden_ref, (ROW["time2_w"]-ROW["time1_w"])//2)])
+    table(emb_ref, [(embed_ref, 0), (embed_ref, TEMB)])
+    total = products(time_ref, ROW["time1_w"], [halves(hidden_grad), halves(outer_grad)], mixed_time_ref)
+    total += products(emb_ref, ROW["emb_w"], moved, mixed_emb_ref)
+
+    def small(at, count=1):
+        return small_ref[at:at+count, :]
+
+    def pairs(at):
+        return jnp.concatenate([small_ref[at:at+40, :C0], small_ref[at:at+32, C0:]], axis=0)
+
+    stem = pairs(SMALL_STEM)
+    stem_rows = [stem[8*tap+c:8*tap+c+1, :] for tap in range(9) for c in range(IN_CH)]+[small(SMALL_STEM+41)[:, :C0]]
+    rows = [jnp.concatenate(stem_rows[2*i:2*i+2], axis=1) for i in range(14)]
+    rows += halves(one(hidden_grad))+halves(one(outer_grad))+[small(SMALL_STEM+40)]
+    rows += [small(SMALL_S0, 2), small(SMALL_S1, 2)]+[one(moved[b][h]) for b in range(BLOCKS) for h in range(2)]
+    rows += [small(SMALL_S0+2, 2), small(SMALL_S1+2, 2), small(SMALL_S0+4, 2), small(SMALL_S1+4, 2), small(SMALL_ATTN, 5)]
+    ends = SMALL_HEAD+112
+    gain_u, shift_u, side = small(ends), small(ends+1), small(ends+2)
+    rows += [gain_u, jnp.concatenate([side[:, :C0], shift_u[:, :C0]], axis=1), jnp.concatenate([shift_u[:, C0:], side[:, C0:]], axis=1)]
+    rows += [small(ends+3), jnp.zeros((4, CH), f32)]
+    q = lax.broadcasted_iota(jnp.int32, (96, 72), 0)
+    pick = (lax.broadcasted_iota(jnp.int32, (96, 72), 1) == (q % 16)*8+q//16).astype(f32).astype(narrow)
+    up = sum(dot(pick, p) for p in three(small_ref[SMALL_HEAD:SMALL_HEAD+72, :]))
+    side = sum(dot(pick, p) for p in three(pairs(SMALL_HEAD+72)))
+    columns = [up[:, 64*i:64*i+64] for i in range(6)]+[side[:, 64*i:64*i+64] for i in range(3)]
+    head_rows = None
+    for o in range(OUT_CH):
+        block = jnp.concatenate([column[16*o:16*o+16] for column in columns], axis=0)
+        lane = lax.broadcasted_iota(jnp.int32, (64, CH), 1)
+        to = (lane == 6*lax.broadcasted_iota(jnp.int32, (64, CH), 0)+o).astype(f32).astype(narrow)
+        part = exact(block, to)
+        head_rows = part if head_rows is None else head_rows+part
+    rows = jnp.concatenate(rows+[head_rows, jnp.zeros((256-48-144, CH), f32)], axis=0)
+    at = lax.broadcasted_iota(jnp.int32, (share, 256), 0)+row0
+    chosen = (at == spot_ref[...]).astype(f32).astype(narrow)
+    out_ref[...] = total+sum(dot(chosen, p) for p in three(rows))
+
+
+def owner_rows(place, small, sinus, kept, w2, we):
     share, n = place.share, place.total
-    sinus, hidden_pre, hidden, outer_pre = kept
-    row = share*place.me()+jnp.arange(share)
-
-    def left(parts, first):
-        length = sum(part.shape[0] for part in parts)
-        table = jnp.concatenate([jnp.zeros((share, n), f32)]+parts+[jnp.zeros((share, n), f32)])
-        return lax.dynamic_slice_in_dim(table, jnp.clip(share*place.me()-first+share, 0, length+share), share)
-
-    def twice(value):
-        return jnp.repeat(value.astype(f32).T, 2, axis=0)
-
-    time_left = left([twice(sinus), jnp.zeros((2, n), f32), twice(hidden)], ROW["time1_w"])
-    emb_left = left([twice(embed), twice(embed)], ROW["emb_w"])
-    time_left = time_left+emb_left
-    columns, right = [], []
-    for begin, length, value in (
-        (ROW["time1_w"], 2*C0, hidden_grad),
-        (ROW["time2_w"], 2*TEMB, outer_grad),
-        (ROW["emb_w"], 2*TEMB, moved[:, :2*CH]),
-        (ROW["emb_w"]+2*TEMB, 2*TEMB, moved[:, 2*CH:]),
-    ):
-        for part in range(2):
-            held = (row >= begin) & (row < begin+length) & ((row-begin) % 2 == part)
-            columns.append(jnp.where(held[:, None], time_left, 0.0))
-            right.append(value[:, part*CH:(part+1)*CH])
-    spots = jnp.array(SPOTS+[-1]*(128-len(SPOTS)))
-    columns.append((row[:, None] == spots[None]).astype(f32))
-    right.append(small)
-    return precise(jnp.concatenate(columns, axis=1), jnp.concatenate(right))
+    hidden_pre, hidden, outer_pre, embed = kept
+    half_rows = -(-(share+2)//16)*8
+    groups = -(-2*n//128)
+    spec = pl.BlockSpec(memory_space=VM)
+    time_rows = (ROW["time2_b"]-ROW["time1_w"])//2
+    lengths = [-(-(time_rows+2*half_rows)//8)*8, -(-(2*TEMB+2*half_rows)//8)*8]
+    spots = jnp.array(SPOTS, jnp.int32)[None]
+    return pl.pallas_call(
+        functools.partial(owner_kernel, share, n),
+        out_shape=sds((share, WIDE)),
+        in_specs=[pl.BlockSpec(memory_space=pltpu.SMEM)]+[spec]*9,
+        out_specs=spec,
+        scratch_shapes=[pltpu.VMEM((groups, lengths[0], 128), f32), pltpu.VMEM((groups, lengths[1], 128), f32),
+                        pltpu.VMEM((3, 2*half_rows, 128), f32), pltpu.VMEM((3, 2*half_rows, 128), f32)],
+        compiler_params=pltpu.CompilerParams(vmem_limit_bytes=LIMIT),
+        cost_estimate=pl.CostEstimate(flops=0, bytes_accessed=1024, transcendentals=0),
+    )(place.me().reshape(1), small, sinus, hidden_pre, hidden, outer_pre, embed, w2, we, spots)
 
 
 def step(sizes, params, moment1, moment2, images, noise, timesteps, masks, weight_index):
     flat = params.shape[0]
     share = flat // WIDE
-    params, moment1, moment2 = (value.reshape(share, WIDE) for value in (params, moment1, moment2))
     place = Place(sizes, share)
     a, me = place.at, place.me()
     spare = (share*me+LEAD) % TILE
     piece = jnp.zeros((place.block*TILE, WIDE), narrow)
-    piece = lax.dynamic_update_slice_in_dim(piece, params.astype(narrow), spare, axis=0)
+    piece = lax.dynamic_update_slice_in_dim(piece, params.astype(narrow).reshape(share, WIDE), spare, axis=0)
     pieces = lax.all_gather(piece.reshape(place.block, TILE, WIDE), ("y", "c", "z", "x"), axis=0)
 
     own = jnp.concatenate([images, noise, masks.astype(f32)[:, None]], axis=1)
@@ -993,38 +1175,34 @@
     noisy = pad_rows8(to_phases(noisy))
     noise_phases, mask_phases = pad_rows8(to_phases(own_noise)), to_phases(mask)
 
-    whole = assemble(pieces, place).reshape(-1, WIDE)
-
-    def rows(name, length, extra=0):
-        first = ROW[name]+extra+LEAD
-        return whole[first:first+length]
+    half = C0 // 2
+    freqs = jnp.exp(-math.log(10000.0) * jnp.arange(half).astype(f32) / half)
+    angles = all_steps[:, None] * freqs
+    sinus = jnp.concatenate([jnp.cos(angles), jnp.sin(angles)], axis=-1).astype(narrow)
+    pieces = pieces.reshape(place.total, place.block*TILE, WIDE)
+
+    def rows(name, length):
+        first, found = ROW[name], []
+        for d in range(first//share, (first+length-1)//share+1):
+            begin, end = max(first, d*share), min(first+length, (d+1)*share)
+            shifted = (d*share+LEAD) % TILE-d*share
+            found.append(pieces[d, begin+shifted:end+shifted])
+        return found[0] if len(found) == 1 else jnp.concatenate(found)
 
     stem = rows("stem_w", 14).reshape(-1)
     stem_w = taps_rows(stem[:27*C0].reshape(9, IN_CH, C0))
     stem_b = stem[27*C0:].reshape(1, C0).astype(f32)
-    w1, b1 = rows("time1_w", 2*C0).reshape(C0, TEMB), rows("time1_b", 2).reshape(TEMB).astype(f32)
-    w2, b2 = rows("time2_w", 2*TEMB).reshape(TEMB, TEMB), rows("time2_b", 2).reshape(TEMB).astype(f32)
-    down_w, down_b = rows("down_w", 9*C0), rows("down_b", 1).astype(f32)
-    vectors = whole[ROW["emb_b"]+LEAD:ROW["qkv_w"]+LEAD].astype(f32)
-    res_b = rows("res_b", 4).astype(f32)
-    emb_w = rows("emb_w", 4*TEMB).reshape(BLOCKS, TEMB, TEMB)
-
-    skip, state = stem_down(noisy, stem_w, stem_b, down_w, down_b)
-    embed, kept = time_forward(all_steps, w1, b1, w2, b2)
-    own_embed = lax.dynamic_slice_in_dim(embed, me, 1)
+    skip, state, down_w = stem_down(place, noisy, stem_w, stem_b, pieces)
+    hidden_pre, hidden, outer_pre, embed, vectors, w2, we = time_and_modulation(place, sinus, pieces)
     blocks = []
     for b in range(BLOCKS):
-        modulate = dot(own_embed, emb_w[b]).reshape(2, CH)+vectors[2*b:2*b+2]
-        vec = jnp.stack([
-            res_b[2*b], res_b[2*b+1], vectors[4+2*b], vectors[8+2*b], vectors[5+2*b], vectors[9+2*b],
-            1.0+modulate[0], modulate[1],
-        ])
+        vec = vectors[b]
         base = RES+2*TAPS*b
-        after, inner, stat = block_forward(state, whole, base, vec)
+        after, inner, stat = block_forward(place, state, pieces, base, vec)
         blocks.append((state, inner, stat, base, vec))
         state = after
     before = state
-    state, qkv, log, mixed_t, attn_stat, wp, wo, attn_vec = attention_forward(before, whole)
+    state, qkv, log, mixed_t, attn_stat, wp, wo, attn_vec = attention_forward(place, before, pieces)
 
     ends = rows("head_gain", 85).reshape(-1)
     norm_u = jnp.stack([ends[:CH], ends[C0+CH:C0+2*CH]]).astype(f32)
@@ -1036,18 +1214,17 @@
     head_b = ends[2*(C0+CH)+head_size:2*(C0+CH)+head_size+OUT_CH].astype(f32)
     head_b = jnp.broadcast_to(jnp.pad(head_b, (0, 8-OUT_CH))[:, None], (8, 128))
     numbers = jnp.stack([jnp.log(beta), jnp.log(tilde), beta*beta/(alpha*one_minus), sample_weight])
-    grad, skip_grad, gu, gs, small_u, small_s, gb, losses = head(
+    grad, skip_grad, head_tail, losses = head(
         numbers, state, skip, wu, ws, norm_u, norm_s, head_b, noise_phases, mask_phases)
-    grad, large, attn_small, qkv_bias = attention_back(
+    grad, large, attn_small = attention_back(
         grad, before, attn_stat, qkv, log, mixed_t, wp, wo, attn_vec, place.tiles)
-    block_grads = [None]*BLOCKS
-    for b in reversed(range(BLOCKS)):
-        begin, inner, stat, base, vec = blocks[b]
-        grad, large, block_grads[b] = block_back(grad, begin, inner, stat, whole, base, vec, large)
-    large, d_stem, down_small, stem_small = down_stem_back(grad, skip, skip_grad, down_w, noisy, large)
-
-    total = share_out(large, place, 2).reshape(-1, WIDE)
-    total = lax.dynamic_slice_in_dim(total, spare, share)
+    begin, inner, stat, base, vec = blocks[1]
+    grad, large, s1 = block_back(place, grad, begin, inner, stat, pieces, base, vec, large)
+    begin, inner, stat, base, vec = blocks[0]
+    grad, large, s0 = block_back(place, grad, begin, inner, stat, pieces, base, vec, large)
+    large, small = down_stem_back(me, place.total, grad, skip, skip_grad, down_w, noisy, head_tail, attn_small, s1, s0, large)
+    total, small = share_out(large, small, place, 3)
+    total = lax.dynamic_slice_in_dim(total.reshape(-1, WIDE), spare, share)
     row = share*me+jnp.arange(share)
     dense = functools.reduce(jnp.logical_or, [
         (row >= ROW[name]) & (row < ROW[name]+length)
@@ -1055,46 +1232,20 @@
     ])
     total = jnp.where(dense[:, None], total, 0.0)
 
-    d_head = jnp.concatenate([gu[:72].reshape(9, 8, CH)[:, :OUT_CH], gs[:72].reshape(9, 8, C0)[:, :OUT_CH]], axis=-1)
-    d_ends = jnp.concatenate([
-        small_u[0], small_s[0], small_u[1], small_s[1], jnp.transpose(d_head, (0, 2, 1)).reshape(-1), gb[:OUT_CH, 0],
-    ])
-    d_ends = jnp.pad(d_ends, (0, 85*WIDE-d_ends.shape[0])).reshape(85, WIDE)
-    d_stem = jnp.concatenate([d_stem[:72].reshape(9, 8, C0)[:, :IN_CH].reshape(-1), stem_small[0]]).reshape(14, WIDE)
-    qkv_bias = heads_unpad(qkv_bias[0]).reshape(3, CH)
-    none = jnp.zeros((4, WIDE), f32)
-    s0, s1 = block_grads
-    small = jnp.concatenate([
-        d_stem, none, down_small[:1], s0[:2], s1[:2], none, s0[2:4], s1[2:4], s0[4:6], s1[4:6],
-        attn_small[:2], qkv_bias[:1], qkv_bias[2:], attn_small[2:3], d_ends, jnp.zeros((3, WIDE), f32),
-    ])
-    moved = jnp.concatenate([s0[6:8], s1[6:8]])
-    slots = jnp.where(jnp.arange(place.total)[:, None, None] == me, moved[None], 0.0).reshape(-1, WIDE)
-    merged = add_everywhere(jnp.concatenate([small, slots]), place)
-    small, moved = merged[:128], merged[128:].reshape(place.total, 4*CH)
-    sinus, hidden_pre, hidden, outer_pre = kept
-    embed_grad = sum(
-        precise(moved[:, 2*CH*b:2*CH*(b+1)], emb_w[b].astype(f32).T) for b in range(BLOCKS))
-    outer_grad = embed_grad*silu_grad(outer_pre)
-    hidden_grad = precise(outer_grad, w2.astype(f32).T)*silu_grad(hidden_pre)
-    filled = jnp.concatenate([
-        small[:14], jnp.sum(hidden_grad, axis=0).reshape(2, WIDE), jnp.sum(outer_grad, axis=0).reshape(2, WIDE), small[18:23],
-        jnp.sum(moved, axis=0).reshape(4, WIDE), small[27:],
-    ])
-    total = total+rank_one_share(place, kept, embed, hidden_grad, outer_grad, moved, filled)
+    total = total+owner_rows(place, small, sinus, (hidden_pre, hidden, outer_pre, embed), w2, we)
 
     scaled = total/count
     sums = jnp.concatenate([losses[:2], jnp.full((1, 128), jnp.sum(scaled*scaled)), losses[3:]])
     sums = add_everywhere(sums, place)
     loss_sum, loss_vlb, grad_norm = sums[0, 0], sums[1, 0], jnp.sqrt(sums[2, 0])
+    scaled = scaled.reshape(flat)
     clipped = scaled*jnp.minimum(1.0, clip_limit/(grad_norm+1e-06))
     first = decay_first*moment1+(1.0-decay_first)*clipped
     second = decay_second*moment2+(1.0-decay_second)*clipped*clipped
     first_hat = first/(1.0-decay_first**STEP)
     second_hat = second/(1.0-decay_second**STEP)
     updated = params-learn_rate*(first_hat/(jnp.sqrt(second_hat)+1e-08)+weight_decay*params)
-    arrays = (value.reshape(flat) for value in (updated, first, second, updated.astype(narrow)))
-    return (*arrays, loss_sum, loss_vlb, count, grad_norm)
+    return (updated, first, second, updated.astype(narrow), loss_sum, loss_vlb, count, grad_norm)
 
 
 def solution(mesh):

time: 611 us -> 523 us (0.86)
  local copies, waits for them, and re-layouts: 111 us -> 42.5 us
  matrix products: 14.5 us -> 0 us
  other arithmetic: 37.2 us -> 27.2 us
  Pallas kernels: 210 us -> 220 us
    reshape x23 -> x1, local copies, waits for them, and re-layouts: 18.3 us -> 0.25 us  [step(): params.astype(narrow).reshape(share, WIDE)]
    slice x27 -> x2, local copies, waits for them, and re-layouts: 17 us -> 1.63 us  [rows(): found.append(pieces[d, begin + shifted:end + shifted])]
    concatenate x6 -> x0, local copies, waits for them, and re-layouts: 15.1 us -> none  [the longest x2 13.1 us: rank_one_share(): return precise(jnp.concatenate(columns, axis=1), jnp.concatenate(right))]
    dot_general x8 -> x0, matrix products: 14.5 us -> none  [the longest x4 8.79 us: precise(): return jnp.dot(left, right, precision=lax.Precision.HIGHEST)]
    select_n x8 -> x0, local copies, waits for them, and re-layouts: 7.25 us -> none  [rank_one_share(): columns.append(jnp.where(held[:, None], time_left, 0.0))]
    ppermute x16 -> x26, waiting for transfers between devices: 59.7 us -> 53.9 us  [turn(): lax.ppermute(value, axis, [(i, (i + distance) % size) for i in range(size)])]
    ppermute x16 -> x26, starting transfers between devices: 16.3 us -> 20.6 us  [turn(): lax.ppermute(value, axis, [(i, (i + distance) % size) for i in range(size)])]
    pallas_call x1 -> x2, Pallas kernels: 12.6 us -> 16.2 us  [the longest x1 10.4 us: owner_rows(): pl.pallas_call(functools.partial(owner_kernel, share, n), out_shape=sds((...]
  transfers between devices with their start and end apart: 33 -> 42, of which waited for: 20 -> 21; matrix products, arithmetic and copies ran while one was open for 16% -> 8% of each run, Pallas kernels for 4% -> 7%
where the time goes in v3:
time: 523 us; the launch traced here: 515 us
  Pallas kernels  220 us (42%)
  waiting for transfers between devices  166 us (32%)
  local copies, waits for them, and re-layouts  42.5 us (8%)
  starting transfers between devices  40.9 us (8%)
  other arithmetic  27.2 us (5%)
  between operations  19.7 us (4%)
    pallas_call x8, Pallas kernels, call(): pl.pallas_call(kernel, out_shape=outs, in_specs=places, out_specs=[pl.Blo...  155 us
    all_gather x1, waiting for transfers between devices, step(): lax.all_gather(piece.reshape(place.block, TILE, WIDE), ('y', 'c', 'z', 'x...  74.5 us
    ppermute x26, waiting for transfers between devices, turn(): lax.ppermute(value, axis, [(i, (i + distance) % size) for i in range(size)])  53.9 us
    ppermute x14, waiting for transfers between devices, add_over(): lax.ppermute(value, axis, [(i, i ^ step) for i in range(size)])  33.1 us
    ppermute x26, starting transfers between devices, turn(): lax.ppermute(value, axis, [(i, (i + distance) % size) for i in range(size)])  20.6 us
    pallas_call x3, Pallas kernels, share_out(): pl.pallas_call(functools.partial(merge_kernel, coords, sends, len(coords)...  17.8 us
    pallas_call x1, Pallas kernels, head(): pl.pallas_call(head_kernel, out_shape=outs, in_specs=[pl.BlockSpec(memory...  17.3 us
    pallas_call x3, Pallas kernels, cut(): pl.pallas_call(functools.partial(cut_kernel, count, size), out_shape=sds(...  13 us
  transfers between devices with their start and end apart: 42, of which 21 were waited for; matrix products, arithmetic and copies ran while one was open for 8% of the time, Pallas kernels for 7%

profile of v3, /device:TPU:0, one launch (start us, length us, event | category | flops | bytes accessed | tf_op | source)
XLA Modules:
  0.0 515.5 jit_solution(4478481518240954098)
XLA Ops:
  13.3 7.3 %all-to-all-start = ((f32[8,1,3584]{2,1,0:T(1,128)}), f32[8,1,3584]{2,1,0:T(1,128)S(1)}, u32[]{:S(2)}, u32[]{:S(2)}) async-start(f32[8,1,3584]{2,1,0:T(1,128)} %reshape.183), calls=%async_computation | async-start | bytes 229376 | tf_op jit(solution)/shard_map/all_to_all | solution.py:1162
  37.4 4.9 mul.432
  60.0 74.5 %all-gather.2.cloned.1.call-done = bf16[32,45,16,384]{3,2,1,0:T(8,128)(2,1)} async-done(((bf16[1,45,16,384]{3,2,1,0:T(8,128)(2,1)}), bf16[32,45,16,384]{3,2,1,0:T(8,128)(2,1)}) %all-gather.2.cloned.1.call-update) | async-done | bytes 17694736 | tf_op jit(solution)/shard_map/all_gather | solution.py:1159
  142.4 5.8 %shard_map.153 = (f32[32,768]{1,0:T(8,128)}, bf16[32,768]{1,0:T(8,128)(2,1)}, f32[32,768]{1,0:T(8,128)}, bf16[32,768]{1,0:T(8,128)(2,1)}, f32[2,8,384]{2,1,0:T(8...) custom-call(s32[1]{0:T(128)} %bitcast.16.me_ref, bf16[32,192]{1,0:T(8,128)(2,1)} %pad_maximum_fusion.3.sinus_ref, ...), custom_call_target="tpu_custom_call" | custom-call | flops 134217728 | bytes 8388608 | tf_op jit(solution)/shard_map/pallas_call | solution.py:1038
  149.6 7.2 %shard_map.152 = (bf16[4,1024,192]{2,1,0:T(8,128)(2,1)}, f32[1024,384]{1,0:T(8,128)}, bf16[1728,384]{1,0:T(8,128)(2,1)}) custom-call(f32[4,8,1024]{2,1,0:T(8,128)} %pad_convert_fusion.noisy_ref, bf16[128,192]{1,0:T(8,128)(2,1)} %pad.42.sw_ref, f32[1,192]{1,0:T(1,128)} %bitcast.212, bf16[32,720,384]{2,1,0:T(8,128)(2,1)} %bitcast.185), custom_call_target="tpu_custom_call" | custom-call | flops 1358954496 | bytes 22348544 | tf_op jit(solution)/shard_map/pallas_call | solution.py:100
  156.8 15.7 %shard_map.154 = (f32[1024,384]{1,0:T(8,128)}, f32[1024,384]{1,0:T(8,128)}, f32[8,384]{1,0:T(8,128)}) custom-call(f32[1024,384]{1,0:T(8,128)} %get-tuple-element.69.state_ref, bf16[32,720,384]{2,1,0:T(8,128)(2,1)} %bitcast.186, f32[8,384]{1,0:T(8,128)} %get-tuple-element.151.vec_ref), custom_call_target="tpu_custom_call" | custom-call | flops 5435817984 | bytes 22437888 | tf_op jit(solution)/shard_map/pallas_call | solution.py:100
  172.4 15.8 %shard_map.155 = (f32[1024,384]{1,0:T(8,128)}, f32[1024,384]{1,0:T(8,128)}, f32[8,384]{1,0:T(8,128)}) custom-call(f32[1024,384]{1,0:T(8,128)} %get-tuple-element.71.state_ref, bf16[32,720,384]{2,1,0:T(8,128)(2,1)} %bitcast.187, f32[8,384]{1,0:T(8,128)} %get-tuple-element.150.vec_ref), custom_call_target="tpu_custom_call" | custom-call | flops 5435817984 | bytes 22437888 | tf_op jit(solution)/shard_map/pallas_call | solution.py:100
  188.3 23.5 %shard_map.156 = (f32[1024,384]{1,0:T(8,128)}, bf16[1024,1536]{1,0:T(8,128)(2,1)}, f32[8,1024]{1,0:T(8,128)}, bf16[512,1024]{1,0:T(8,128)(2,1)}, f32[8,384]{1,0:...) custom-call(f32[1024,384]{1,0:T(8,128)} %get-tuple-element.72.state_ref, ...), custom_call_target="tpu_custom_call" | custom-call | flops 3758096384 | bytes 26664960 | tf_op jit(solution)/shard_map/pallas_call | solution.py:100
  215.6 17.3 %shard_map.157 = (f32[1024,384]{1,0:T(8,128)}, f32[4,1024,192]{2,1,0:T(8,128)}, f32[120,384]{1,0:T(8,128)}, f32[8,128]{1,0:T(8,128)}) custom-call(f32[4]{0:T(128)} %pad_maximum_fusion.5.num_ref, f32[1024,384]{1,0:T(8,128)} %get-tuple-element.73.state_ref, bf16[4,1024,192]{2,1,0:T(8,128)(2,1)} %get-tuple-element.74.skip_ref, bf16[128,384]{1,0:T(8,128)(2,1)} %pad.44.wu_ref, ...), custom_call_target="tpu_custom_call" | custom-call | flops 1207959552 | bytes 12582912 | tf_op jit(solution)/shard_map/pallas_call | solution.py:620
  232.9 25.6 %shard_map.158 = (f32[1024,384]{1,0:T(8,128)}, bf16[1392,16,384]{2,1,0:T(8,128)(2,1)}, f32[8,384]{1,0:T(8,128)}) custom-call(f32[1024,384]{1,0:T(8,128)} %get-tuple-element.75.grad_ref, f32[1024,384]{1,0:T(8,128)} %get-tuple-element.72.state_ref, f32[8,384]{1,0:T(8,128)} %get-tuple-element.76.stat_ref, bf16[1024,1536]{1,0:T(8,128)(2,1)} %get-tuple-element.77.qkv_ref, ...), custom_call_target="tpu_custom_call" | custom-call | flops 8589934592 | bytes 27660288 | tf_op jit(solution)/shard_map/pallas_call | solution.py:100
  258.5 27.5 %shard_map.159 = (f32[1024,384]{1,0:T(8,128)}, bf16[1392,16,384]{2,1,0:T(8,128)(2,1)}, f32[8,384]{1,0:T(8,128)}) custom-call(f32[1024,384]{1,0:T(8,128)} %get-tuple-element.83.grad_ref, f32[1024,384]{1,0:T(8,128)} %get-tuple-element.71.state_ref, f32[1024,384]{1,0:T(8,128)} %get-tuple-element.84.inner_ref, ...), custom_call_target="tpu_custom_call", output_to_operand_aliasing={{1}: (6, {})} | custom-call | flops 10871635968 | bytes 58232832 | tf_op jit(solution)/shard_map/pallas_call | solution.py:100
  286.1 27.9 %shard_map.160 = (f32[1024,384]{1,0:T(8,128)}, bf16[1392,16,384]{2,1,0:T(8,128)(2,1)}, f32[8,384]{1,0:T(8,128)}) custom-call(f32[1024,384]{1,0:T(8,128)} %get-tuple-element.87.grad_ref, f32[1024,384]{1,0:T(8,128)} %get-tuple-element.69.state_ref, f32[1024,384]{1,0:T(8,128)} %get-tuple-element.88.inner_ref, ...), custom_call_target="tpu_custom_call", output_to_operand_aliasing={{1}: (6, {})} | custom-call | flops 10871635968 | bytes 58232832 | tf_op jit(solution)/shard_map/pallas_call | solution.py:100
  314.0 12.2 %shard_map.161 = (bf16[1392,16,384]{2,1,0:T(8,128)(2,1)}, f32[320,384]{1,0:T(8,128)}) custom-call(s32[1]{0:T(128)} %bitcast.16.me_ref, f32[1024,384]{1,0:T(8,128)} %get-tuple-element.91.grad_ref, bf16[4,1024,192]{2,1,0:T(8,128)(2,1)} %get-tuple-element.74.skip_ref, f32[4,1024,192]{2,1,0:T(8,128)} %get-tuple-element.92.more_ref, ...), custom_call_target="tpu_custom_call", output_to_operand_aliasing={{0}: (10, {})} | custom-call | flops 2717908992 | bytes 42672132 | tf_op jit(solution)/shard_map/pallas_call | solution.py:100
  336.5 4.4 shard_map.166
  342.8 5.9 %shard_map.163 = (f32[4,15,16,384]{3,2,1,0:T(8,128)}, bf16[4,15,16,384]{3,2,1,0:T(8,128)(2,1)}, f32[4,15,16,384]{3,2,1,0:T(8,128)}, bf16[4,15,16,384]{3,2,1,0:T(8,128)(2,1)}) custom-call(s32[16]{0:T(128)} %stack.159.starts_ref, bf16[1392,16,384]{2,1,0:T(8,128)(2,1)} %get-tuple-element.99.large_ref, bf16[16,15,16,384]{3,2,1,0:T(8,128)(2,1)} %collective-permute-done.5.arrived_ref), custom_call_target="tpu_custom_call" | custom-call | bytes 1024 | tf_op jit(solution)/shard_map/pallas_call | solution.py:910
  353.9 5.9 %shard_map.165 = (f32[4,15,16,384]{3,2,1,0:T(8,128)}, bf16[4,15,16,384]{3,2,1,0:T(8,128)(2,1)}, f32[4,15,16,384]{3,2,1,0:T(8,128)}, bf16[4,15,16,384]{3,2,1,0:T(8,128)(2,1)}) custom-call(s32[16]{0:T(128)} %broadcast_add_fusion.3.starts_ref, bf16[1392,16,384]{2,1,0:T(8,128)(2,1)} %get-tuple-element.99.large_ref, ...), custom_call_target="tpu_custom_call" | custom-call | bytes 1024 | tf_op jit(solution)/shard_map/pallas_call | solution.py:910
  361.0 14.2 %collective-permute-done.30 = f32[160,384]{1,0:T(8,128)S(1)} collective-permute-done((f32[160,384]{1,0:T(8,128)S(1)}, f32[160,384]{1,0:T(8,128)S(1)}, u32[]{:S(2)}, u32[]{:S(2)}) %collective-permute-start.30) | collective-permute-done | bytes 245792 | tf_op jit(solution)/shard_map/ppermute | solution.py:841
  377.8 5.9 %shard_map.167 = (f32[4,15,16,384]{3,2,1,0:T(8,128)}, bf16[4,15,16,384]{3,2,1,0:T(8,128)(2,1)}, f32[4,15,16,384]{3,2,1,0:T(8,128)}, bf16[4,15,16,384]{3,2,1,0:T(8,128)(2,1)}) custom-call(s32[16]{0:T(128)} %broadcast_add_fusion.1.starts_ref, bf16[1392,16,384]{2,1,0:T(8,128)(2,1)} %get-tuple-element.99.large_ref, bf16[16,15,16,384]{3,2,1,0:T(8,128)(2,1)} %copy-done.2), custom_call_target="tpu_custom_call" | custom-call | bytes 1024 | tf_op jit(solution)/shard_map/pallas_call | solution.py:910
  400.7 7.3 %collective-permute-done.19 = bf16[2,15,16,384]{3,2,1,0:T(8,128)(2,1)S(1)} collective-permute-done((bf16[2,15,16,384]{3,2,1,0:T(8,128)(2,1)S(1)}, bf16[2,15,16,384]{3,2,1,0:T(8,128)(2,1)S(1)}, u32[]{:S(2)}, u32[]{:S(2)}) %collective-permute-start.19) | collective-permute-done | bytes 368672 | tf_op jit(solution)/shard_map/ppermute | solution.py:826
  408.5 6.9 %collective-permute-done.16 = bf16[2,15,16,384]{3,2,1,0:T(8,128)(2,1)S(1)} collective-permute-done((bf16[2,15,16,384]{3,2,1,0:T(8,128)(2,1)S(1)}, bf16[2,15,16,384]{3,2,1,0:T(8,128)(2,1)S(1)}, u32[]{:S(2)}, u32[]{:S(2)}) %collective-permute-start.16) | collective-permute-done | bytes 368672 | tf_op jit(solution)/shard_map/ppermute | solution.py:826
  416.9 4.6 collective-permute-done.10
  427.9 13.7 %collective-permute-done.20 = bf16[15,16,384]{2,1,0:T(8,128)(2,1)S(1)} collective-permute-done((bf16[15,16,384]{2,1,0:T(8,128)(2,1)S(1)}, bf16[15,16,384]{2,1,0:T(8,128)(2,1)S(1)}, u32[]{:S(2)}, u32[]{:S(2)}) %collective-permute-start.20) | collective-permute-done | bytes 184352 | tf_op jit(solution)/shard_map/ppermute | solution.py:826
  445.2 12.2 %collective-permute-done.13 = bf16[15,16,384]{2,1,0:T(8,128)(2,1)S(1)} collective-permute-done((bf16[15,16,384]{2,1,0:T(8,128)(2,1)S(1)}, bf16[15,16,384]{2,1,0:T(8,128)(2,1)S(1)}, u32[]{:S(2)}, u32[]{:S(2)}) %collective-permute-start.13) | collective-permute-done | bytes 184352 | tf_op jit(solution)/shard_map/ppermute | solution.py:826
  470.0 10.4 %shard_map.168 = f32[694,384]{1,0:T(8,128)} custom-call(s32[1]{0:T(128)} %bitcast.16.me_ref, f32[320,384]{1,0:T(8,128)} %pad_maximum_fusion.1.small_ref, bf16[32,192]{1,0:T(8,128)(2,1)} %pad_maximum_fusion.3.sinus_ref, f32[32,768]{1,0:T(8,128)} %get-tuple-element.123.hidden_pre_ref, bf16[32,768]{1,0:T(8,128)(2,1)} %get-tuple-element.124.hidden_ref, ...), custom_call_target="tpu_custom_call" | custom-call | bytes 1024 | tf_op jit(solution)/shard_map/pallas_call | solution.py:1139
  (248 shorter events, 139.0 us)
Async XLA Ops:
  7.2 127.4 %all-gather.2.cloned.1.call-start = ((), (), s32[]{:S(2)}) async-start(), calls=%async_computation.1 | async-start | bytes 18247680 | tf_op jit(solution)/shard_map/all_gather | solution.py:1159
  13.3 14.6 %all-to-all-start = ((f32[8,1,3584]{2,1,0:T(1,128)}), f32[8,1,3584]{2,1,0:T(1,128)S(1)}, u32[]{:S(2)}, u32[]{:S(2)}) async-start(f32[8,1,3584]{2,1,0:T(1,128)} %reshape.183), calls=%async_computation | async-start | bytes 229376 | tf_op jit(solution)/shard_map/all_to_all | solution.py:1162
  335.7 18.2 %collective-permute-start.8 = (bf16[16,15,16,384]{3,2,1,0:T(8,128)(2,1)}, bf16[16,15,16,384]{3,2,1,0:T(8,128)(2,1)}, u32[]{:S(2)}, u32[]{:S(2)}) collective-permute-start(bf16[16,15,16,384]{3,2,1,0:T(8,128)(2,1)} %shard_map.164), channel_id=1, source_target_pairs={{0,8},{8,0},{1,9},{9,1},{2,10},{10,2},{3,11},{11,3},{4,12},{12,4},... | collective-permute-start | bytes 8847368 | tf_op jit(solution)/shard_map/ppermute | solution.py:826
  340.9 35.4 %collective-permute-start.9 = (bf16[16,15,16,384]{3,2,1,0:T(8,128)(2,1)}, bf16[16,15,16,384]{3,2,1,0:T(8,128)(2,1)S(1)}, u32[]{:S(2)}, u32[]{:S(2)}) collective-permute-start(bf16[16,15,16,384]{3,2,1,0:T(8,128)(2,1)} %shard_map.166), channel_id=1, source_target_pairs={{0,8},{8,0},{1,9},{9,1},{2,10},{10,2},{3,11},{11,3},{4,12},{12,4},... | collective-permute-start | bytes 8847368 | tf_op jit(solution)/shard_map/ppermute | solution.py:826
  348.7 35.0 %collective-permute-start.6 = (bf16[4,15,16,384]{3,2,1,0:T(8,128)(2,1)}, bf16[4,15,16,384]{3,2,1,0:T(8,128)(2,1)}, u32[]{:S(2)}, u32[]{:S(2)}) collective-permute-start(bf16[4,15,16,384]{3,2,1,0:T(8,128)(2,1)} %get-tuple-element.101), channel_id=1, source_target_pairs={{0,16},{16,0},{1,17},{17,1},{2,18},{18,2},{3,19},{19,3},{4,20},{20... | collective-permute-start | bytes 2211848 | tf_op jit(solution)/shard_map/ppermute | solution.py:826
  350.3 33.5 %collective-permute-start.7 = (bf16[4,15,16,384]{3,2,1,0:T(8,128)(2,1)}, bf16[4,15,16,384]{3,2,1,0:T(8,128)(2,1)}, u32[]{:S(2)}, u32[]{:S(2)}) collective-permute-start(bf16[4,15,16,384]{3,2,1,0:T(8,128)(2,1)} %get-tuple-element.102), channel_id=1, source_target_pairs={{0,1},{1,0},{2,3},{3,2},{4,5},{5,4},{6,7},{7,6},{8,9},{9,8},{10,11... | collective-permute-start | bytes 2211848 | tf_op jit(solution)/shard_map/ppermute | solution.py:826
  351.8 23.3 %collective-permute-start.30 = (f32[160,384]{1,0:T(8,128)S(1)}, f32[160,384]{1,0:T(8,128)S(1)}, u32[]{:S(2)}, u32[]{:S(2)}) collective-permute-start(f32[160,384]{1,0:T(8,128)S(1)} %dynamic-slice_add_fusion), channel_id=1, source_target_pairs={{0,1},{1,0},{2,3},{3,2},{4,5},{5,4},{6,7},{7,6},{8,9},{9,8},{10,11... | collective-permute-start | bytes 737288 | tf_op jit(solution)/shard_map/ppermute | solution.py:841
  359.8 31.2 %collective-permute-start.18 = (bf16[4,15,16,384]{3,2,1,0:T(8,128)(2,1)}, bf16[4,15,16,384]{3,2,1,0:T(8,128)(2,1)}, u32[]{:S(2)}, u32[]{:S(2)}) collective-permute-start(bf16[4,15,16,384]{3,2,1,0:T(8,128)(2,1)} %get-tuple-element.109), channel_id=1, source_target_pairs={{0,1},{1,0},{2,3},{3,2},{4,5},{5,4},{6,7},{7,6},{8,9},{9,8},{10,11... | collective-permute-start | bytes 2211848 | tf_op jit(solution)/shard_map/ppermute | solution.py:826
  375.2 19.8 %collective-permute-start.15 = (bf16[4,15,16,384]{3,2,1,0:T(8,128)(2,1)}, bf16[4,15,16,384]{3,2,1,0:T(8,128)(2,1)}, u32[]{:S(2)}, u32[]{:S(2)}) collective-permute-start(bf16[4,15,16,384]{3,2,1,0:T(8,128)(2,1)} %get-tuple-element.107), channel_id=1, source_target_pairs={{0,16},{16,0},{1,17},{17,1},{2,18},{18,2},{3,19},{19,3},{4,20},{20... | collective-permute-start | bytes 2211848 | tf_op jit(solution)/shard_map/ppermute | solution.py:826
  388.0 69.5 %collective-permute-start.25 = (bf16[4,15,16,384]{3,2,1,0:T(8,128)(2,1)S(1)}, bf16[4,15,16,384]{3,2,1,0:T(8,128)(2,1)S(1)}, u32[]{:S(2)}, u32[]{:S(2)}) collective-permute-start(bf16[4,15,16,384]{3,2,1,0:T(8,128)(2,1)S(1)} %copy-done.16), channel_id=1, source_target_pairs={{0,1},{1,0},{2,3},{3,2},{4,5},{5,4},{6,7},{7,6},{8,9},{9,8},{10,11... | collective-permute-start | bytes 2211848 | tf_op jit(solution)/shard_map/ppermute | solution.py:826
  392.4 15.6 %collective-permute-start.19 = (bf16[2,15,16,384]{3,2,1,0:T(8,128)(2,1)S(1)}, bf16[2,15,16,384]{3,2,1,0:T(8,128)(2,1)S(1)}, u32[]{:S(2)}, u32[]{:S(2)}) collective-permute-start(bf16[2,15,16,384]{3,2,1,0:T(8,128)(2,1)S(1)} %fusion.14), channel_id=1, source_target_pairs={{0,16},{16,0},{1,17},{17,1},{2,18},{18,2},{3,19},{19,3},{4,20},{20... | collective-permute-start | bytes 1105928 | tf_op jit(solution)/shard_map/ppermute | solution.py:826
  396.3 19.0 %collective-permute-start.16 = (bf16[2,15,16,384]{3,2,1,0:T(8,128)(2,1)S(1)}, bf16[2,15,16,384]{3,2,1,0:T(8,128)(2,1)S(1)}, u32[]{:S(2)}, u32[]{:S(2)}) collective-permute-start(bf16[2,15,16,384]{3,2,1,0:T(8,128)(2,1)S(1)} %fusion.13), channel_id=1, source_target_pairs={{0,1},{1,0},{2,3},{3,2},{4,5},{5,4},{6,7},{7,6},{8,9},{9,8},{10,11... | collective-permute-start | bytes 1105928 | tf_op jit(solution)/shard_map/ppermute | solution.py:826
  396.9 24.6 %collective-permute-start.10 = (bf16[2,15,16,384]{3,2,1,0:T(8,128)(2,1)S(1)}, bf16[2,15,16,384]{3,2,1,0:T(8,128)(2,1)S(1)}, u32[]{:S(2)}, u32[]{:S(2)}) collective-permute-start(bf16[2,15,16,384]{3,2,1,0:T(8,128)(2,1)S(1)} %fusion.11), channel_id=1, source_target_pairs={{0,1},{1,0},{2,3},{3,2},{4,5},{5,4},{6,7},{7,6},{8,9},{9,8},{10,11... | collective-permute-start | bytes 1105928 | tf_op jit(solution)/shard_map/ppermute | solution.py:826
  400.1 23.0 %collective-permute-start.12 = (bf16[2,15,16,384]{3,2,1,0:T(8,128)(2,1)S(1)}, bf16[2,15,16,384]{3,2,1,0:T(8,128)(2,1)S(1)}, u32[]{:S(2)}, u32[]{:S(2)}) collective-permute-start(bf16[2,15,16,384]{3,2,1,0:T(8,128)(2,1)S(1)} %fusion.12), channel_id=1, source_target_pairs={{0,16},{16,0},{1,17},{17,1},{2,18},{18,2},{3,19},{19,3},{4,20},{20... | collective-permute-start | bytes 1105928 | tf_op jit(solution)/shard_map/ppermute | solution.py:826
  408.0 15.9 %collective-permute-start.32 = (f32[160,384]{1,0:T(8,128)S(1)}, f32[160,384]{1,0:T(8,128)S(1)}, u32[]{:S(2)}, u32[]{:S(2)}) collective-permute-start(f32[160,384]{1,0:T(8,128)S(1)} %add.887), channel_id=1, source_target_pairs={{0,2},{2,0},{4,6},{6,4},{1,3},{3,1},{5,7},{7,5},{8,10},{10,8},{12,... | collective-permute-start | bytes 737288 | tf_op jit(solution)/shard_map/ppermute | solution.py:841
  421.5 20.1 %collective-permute-start.20 = (bf16[15,16,384]{2,1,0:T(8,128)(2,1)S(1)}, bf16[15,16,384]{2,1,0:T(8,128)(2,1)S(1)}, u32[]{:S(2)}, u32[]{:S(2)}) collective-permute-start(bf16[15,16,384]{2,1,0:T(8,128)(2,1)S(1)} %get-tuple-element.140), channel_id=1, source_target_pairs={{0,4},{2,6},{4,0},{6,2},{1,5},{3,7},{5,1},{7,3},{8,12},{10,14},{12... | collective-permute-start | bytes 552968 | tf_op jit(solution)/shard_map/ppermute | solution.py:826
  423.1 18.5 %collective-permute-start.17 = (bf16[15,16,384]{2,1,0:T(8,128)(2,1)S(1)}, bf16[15,16,384]{2,1,0:T(8,128)(2,1)S(1)}, u32[]{:S(2)}, u32[]{:S(2)}) collective-permute-start(bf16[15,16,384]{2,1,0:T(8,128)(2,1)S(1)} %fusion.27), channel_id=1, source_target_pairs={{0,2},{2,4},{4,6},{6,0},{1,3},{3,5},{5,7},{7,1},{8,10},{10,12},{12... | collective-permute-start | bytes 552968 | tf_op jit(solution)/shard_map/ppermute | solution.py:826
  424.2 34.2 %collective-permute-start.22 = (bf16[4,15,16,384]{3,2,1,0:T(8,128)(2,1)S(1)}, bf16[4,15,16,384]{3,2,1,0:T(8,128)(2,1)S(1)}, u32[]{:S(2)}, u32[]{:S(2)}) collective-permute-start(bf16[4,15,16,384]{3,2,1,0:T(8,128)(2,1)S(1)} %copy-done.15), channel_id=1, source_target_pairs={{0,16},{16,0},{1,17},{17,1},{2,18},{18,2},{3,19},{19,3},{4,20},{20... | collective-permute-start | bytes 2211848 | tf_op jit(solution)/shard_map/ppermute | solution.py:826
  424.8 17.1 %collective-permute-start.14 = (bf16[15,16,384]{2,1,0:T(8,128)(2,1)S(1)}, bf16[15,16,384]{2,1,0:T(8,128)(2,1)S(1)}, u32[]{:S(2)}, u32[]{:S(2)}) collective-permute-start(bf16[15,16,384]{2,1,0:T(8,128)(2,1)S(1)} %get-tuple-element.139), channel_id=1, source_target_pairs={{0,6},{2,0},{4,2},{6,4},{1,7},{3,1},{5,3},{7,5},{8,14},{10,8},{12,... | collective-permute-start | bytes 552968 | tf_op jit(solution)/shard_map/ppermute | solution.py:826
  441.7 15.7 %collective-permute-start.13 = (bf16[15,16,384]{2,1,0:T(8,128)(2,1)S(1)}, bf16[15,16,384]{2,1,0:T(8,128)(2,1)S(1)}, u32[]{:S(2)}, u32[]{:S(2)}) collective-permute-start(bf16[15,16,384]{2,1,0:T(8,128)(2,1)S(1)} %get-tuple-element.138), channel_id=1, source_target_pairs={{0,4},{2,6},{4,0},{6,2},{1,5},{3,7},{5,1},{7,3},{8,12},{10,14},{12... | collective-permute-start | bytes 552968 | tf_op jit(solution)/shard_map/ppermute | solution.py:826
  441.7 15.7 %collective-permute-start.11 = (bf16[15,16,384]{2,1,0:T(8,128)(2,1)S(1)}, bf16[15,16,384]{2,1,0:T(8,128)(2,1)S(1)}, u32[]{:S(2)}, u32[]{:S(2)}) collective-permute-start(bf16[15,16,384]{2,1,0:T(8,128)(2,1)S(1)} %fusion.26), channel_id=1, source_target_pairs={{0,2},{2,4},{4,6},{6,0},{1,3},{3,5},{5,7},{7,1},{8,10},{10,12},{12... | collective-permute-start | bytes 552968 | tf_op jit(solution)/shard_map/ppermute | solution.py:826
  442.0 19.3 %collective-permute-start.33 = (f32[160,384]{1,0:T(8,128)S(1)}, f32[160,384]{1,0:T(8,128)S(1)}, u32[]{:S(2)}, u32[]{:S(2)}) collective-permute-start(f32[160,384]{1,0:T(8,128)S(1)} %add.888), channel_id=1, source_target_pairs={{0,4},{2,6},{4,0},{6,2},{1,5},{3,7},{5,1},{7,3},{8,12},{10,14},{12... | collective-permute-start | bytes 737288 | tf_op jit(solution)/shard_map/ppermute | solution.py:841
  465.8 14.7 %collective-permute-start.28 = (bf16[15,16,384]{2,1,0:T(8,128)(2,1)S(1)}, bf16[15,16,384]{2,1,0:T(8,128)(2,1)S(1)}, u32[]{:S(2)}, u32[]{:S(2)}) collective-permute-start(bf16[15,16,384]{2,1,0:T(8,128)(2,1)S(1)} %get-tuple-element.143), channel_id=1, source_target_pairs={{0,6},{2,0},{4,2},{6,4},{1,7},{3,1},{5,3},{7,5},{8,14},{10,8},{12,... | collective-permute-start | bytes 552968 | tf_op jit(solution)/shard_map/ppermute | solution.py:826
  465.9 15.1 %collective-permute-start.27 = (bf16[15,16,384]{2,1,0:T(8,128)(2,1)S(1)}, bf16[15,16,384]{2,1,0:T(8,128)(2,1)S(1)}, u32[]{:S(2)}, u32[]{:S(2)}) collective-permute-start(bf16[15,16,384]{2,1,0:T(8,128)(2,1)S(1)} %get-tuple-element.142), channel_id=1, source_target_pairs={{0,4},{2,6},{4,0},{6,2},{1,5},{3,7},{5,1},{7,3},{8,12},{10,14},{12... | collective-permute-start | bytes 552968 | tf_op jit(solution)/shard_map/ppermute | solution.py:826
  (37 other events, 244.2 us)
Sparse Core Ops, SparseCore 0:
  12.5 121.9 all-gather.1

commit v4 on v3

--- a/solution.py
+++ b/solution.py
@@ -145,7 +145,9 @@
 
 EL=128
 def steps(n, body, init=None):
-    return lax.fori_loop(0, n, body, init)
+    for i in range(n):
+        init = body(i, init)
+    return init
 
 def pixel_column(rows, width):
     return lax.broadcasted_iota(jnp.int32, (rows, width), 0) % SIDE
@@ -164,7 +166,7 @@
         out_ref[r+SIDE:r+SIDE+EL, width:2*width] = mid
         out_ref[r+SIDE:r+SIDE+EL, 2*width:3*width] = last
 
-MC=1024
+MC=256
 def conv_rows(xs_ref, w_ref, base, r):
     acc = dot(xs_ref[pl.ds(r, MC), :], w_ref[base:base+3*CH, :])
     acc += dot(xs_ref[pl.ds(r+SIDE, MC), :], w_ref[base+3*CH:base+6*CH, :])
@@ -216,12 +218,12 @@
     member = membership(CH, CH//GROUPS)
     amount = PIX*(CH//GROUPS)
     def sums(i, c):
-        v = state_ref[pl.ds(pl.multiple_of(i*EL, EL), EL), :]
+        v = state_ref[pl.ds(i*EL, EL), :]
         return c[0]+fold(v), c[1]+fold(v*v)
     z = jnp.zeros((8, CH), f32)
     mean1, inv1 = norm_stats(*steps(PIX//EL, sums, (z, z)), member, amount)
     def act1(i, _):
-        r = pl.multiple_of(i*EL, EL)
+        r = i*EL
         v = (state_ref[pl.ds(r, EL), :] - mean1)*inv1*gain1 + shift1
         pad_ref[pl.ds(r+8, EL), :] = v*sigmoid(v)
         return _
@@ -229,13 +231,13 @@
     spread(pad_ref, xs_ref, CH, False)
     rows[0].finish(*one)
     def conv1(i, c):
-        r = pl.multiple_of(i*MC, MC)
+        r = i*MC
         v = conv_rows(xs_ref, w1_ref, 0, r) + bias1
         inner_ref[pl.ds(r, MC), :] = v
         return c[0]+fold(v), c[1]+fold(v*v)
     mean2, inv2 = norm_stats(*steps(PIX//MC, conv1, (z, z)), member, amount)
     def act2(i, _):
-        r = pl.multiple_of(i*EL, EL)
+        r = i*EL
         v = (inner_ref[pl.ds(r, EL), :] - mean2)*inv2*gain2 + shift2
         v = v*scale + offset
         pad_ref[pl.ds(r+8, EL), :] = v*sigmoid(v)
@@ -244,7 +246,7 @@
     spread(pad_ref, xs_ref, CH, False)
     rows[1].finish(*two)
     def conv2(i, _):
-        r = pl.multiple_of(i*MC, MC)
+        r = i*MC
         out_ref[pl.ds(r, MC), :] = state_ref[pl.ds(r, MC), :] + (conv_rows(xs_ref, w2_ref, 0, r) + bias2)
         return _
     steps(PIX//MC, conv2, 0)
@@ -271,11 +273,11 @@
 
 def kernel_grads(xt_ref, gs_ref, dw_ref, base):
     def body(dy, _):
-        r = pl.multiple_of(SIDE*(2-dy), SIDE)
+        r = SIDE*(2-dy)
+        value = dot(xt_ref[...], gs_ref[pl.ds(r, PIX), :]).astype(dw_ref.dtype)
         for dx in range(3):
             at = (base+(3*dy+dx)*CH)//TILE
-            value = dot(xt_ref[...], gs_ref[pl.ds(r, PIX), dx*CH:(dx+1)*CH])
-            dw_ref[pl.ds(at, CH//TILE)] = value.astype(dw_ref.dtype).reshape(CH//TILE, TILE, CH)
+            dw_ref[pl.ds(at, CH//TILE)] = value[:, dx*CH:(dx+1)*CH].reshape(CH//TILE, TILE, CH)
         return _
     steps(3, body, 0)
 
@@ -291,7 +293,7 @@
     amount = PIX*(CH//GROUPS)
     z = jnp.zeros((8, CH), f32)
     def low(i, c):
-        r = pl.multiple_of(i*EL, EL)
+        r = i*EL
         g = grad_ref[pl.ds(r, EL), :].astype(narrow).astype(f32)
         pad_ref[pl.ds(r+8, EL), :] = g
         return c+fold(g)
@@ -308,7 +310,7 @@
     second_out.start()
     rows[1].finish(*second_in)
     def back2(i, c):
-        r = pl.multiple_of(i*MC, MC)
+        r = i*MC
         d = back_taps(gs_ref, w2_ref, 0, r)
         n = (inner_ref[pl.ds(r, MC), :] - mean2)*inv2
         nt = n*gain2 + shift2
@@ -323,7 +325,7 @@
     tot = group_totals(rows_of(mod_offset*scale*gain2, dn*scale*gain2), member)/amount
     first, second = tot[0:1], tot[1:2]
     def inner_back(i, c):
-        r = pl.multiple_of(i*EL, EL)
+        r = i*EL
         n = (inner_ref[pl.ds(r, EL), :] - mean2)*inv2
         g = (keep_ref[pl.ds(r, EL), :]*scale*gain2 - first - n*second)*inv2
         g = g.astype(narrow).astype(f32)
@@ -340,7 +342,7 @@
     first_out.start()
     rows[0].finish(*first_in)
     def back1(i, c):
-        r = pl.multiple_of(i*MC, MC)
+        r = i*MC
         d = back_taps(gs_ref, w1_ref, 0, r)
         n = (state_ref[pl.ds(r, MC), :] - mean1)*inv1
         v = n*gain1 + shift1
@@ -352,7 +354,7 @@
     tot = group_totals(rows_of(shift1_grad*gain1, gain1_grad*gain1), member)/amount
     first1, second1 = tot[0:1], tot[1:2]
     def state_back(i, _):
-        r = pl.multiple_of(i*EL, EL)
+        r = i*EL
         n = (state_ref[pl.ds(r, EL), :] - mean1)*inv1
         out_ref[pl.ds(r, EL), :] = grad_ref[pl.ds(r, EL), :] + (keep_ref[pl.ds(r, EL), :]*gain1 - first1 - n*second1)*inv1
         return _
@@ -512,13 +514,13 @@
     one = lambda v: jnp.sum(v, axis=0, keepdims=True)
     zu, zs = jnp.zeros((8, CH), f32), jnp.zeros((8, C0), f32)
     def sums_u(i, c):
-        v = state_ref[pl.ds(pl.multiple_of(i*EL, EL), EL), :]
+        v = state_ref[pl.ds(i*EL, EL), :]
         return c[0]+fold(v), c[1]+fold(v*v)
     u1, u2 = steps(PIX//EL, sums_u, (zu, zu))
     s1, s2 = zs, zs
     for k in range(4):
         def sums_s(i, c):
-            v = skip_ref[k, pl.ds(pl.multiple_of(i*EL, EL), EL), :].astype(f32)
+            v = skip_ref[k, pl.ds(i*EL, EL), :].astype(f32)
             return c[0]+fold(v), c[1]+fold(v*v)
         s1, s2 = steps(PIX//EL, sums_s, (s1, s2))
     tot = (exact(rows_of(4.0*one(u1), 4.0*one(u2)), mu) + exact(rows_of(one(s1), one(s2)), ms))/amount
@@ -526,14 +528,14 @@
     mean_u, inv_u = tot_u[0:1], lax.rsqrt(tot_u[1:2]-tot_u[0:1]*tot_u[0:1]+1e-05)
     mean_s, inv_s = tot_s[0:1], lax.rsqrt(tot_s[1:2]-tot_s[0:1]*tot_s[0:1]+1e-05)
     def act_u(i, _):
-        r = pl.ds(pl.multiple_of(i*EL, EL), EL)
+        r = pl.ds(i*EL, EL)
         v = (state_ref[r, :]-mean_u)*inv_u*gain_u+shift_u
         up_ref[r, :] = (v*sigmoid(v)).astype(narrow)
         return _
     steps(PIX//EL, act_u, 0)
     for k in range(4):
         def act_s(i, _):
-            r = pl.ds(pl.multiple_of(i*EL, EL), EL)
+            r = pl.ds(i*EL, EL)
             v = (skip_ref[k, r, :].astype(f32)-mean_s)*inv_s*gain_s+shift_s
             side_ref[k, r, :] = (v*sigmoid(v)).astype(narrow)
             return _
@@ -600,14 +602,14 @@
     tot = (exact(rows_of(e1*gain_u, e2*gain_u), mu)+exact(rows_of(d1*gain_s, d2*gain_s), ms))/amount
     tot_u, tot_s = exact_nt(tot, mu), exact_nt(tot, ms)
     def back_u(i, _):
-        r = pl.ds(pl.multiple_of(i*EL, EL), EL)
+        r = pl.ds(i*EL, EL)
         n = (state_ref[r, :]-mean_u)*inv_u
         state_grad_ref[r, :] = (state_grad_ref[r, :]*gain_u-4.0*tot_u[0:1]-4.0*n*tot_u[1:2])*inv_u
         return _
     steps(PIX//EL, back_u, 0)
     for k in range(4):
         def back_s(i, _):
-            r = pl.ds(pl.multiple_of(i*EL, EL), EL)
+            r = pl.ds(i*EL, EL)
             n = (skip_ref[k, r, :].astype(f32)-mean_s)*inv_s
             skip_grad_ref[k, r, :] = (skip_grad_ref[k, r, :]*gain_s-tot_s[0:1]-n*tot_s[1:2])*inv_s
             return _
@@ -626,6 +628,7 @@
 HP = 128
 QW = HEADS*HP
 SCALE = 1.0/math.sqrt(HEAD_DIM)
+POWER = SCALE*math.log2(math.e)
 QC = 256
 ATTN_FIRST = (ROW["attn_gain"]+LEAD)//TILE
 ATTN_TILES = -(-(ROW["proj_b"]+LEAD+1)//TILE)-ATTN_FIRST
@@ -662,13 +665,13 @@
         wo_ref[h*HP+HEAD_DIM:(h+1)*HP, :] = jnp.zeros((HP-HEAD_DIM, CH), narrow)
     member = membership(CH, CH//GROUPS)
     def sums(i, c):
-        v = state_ref[pl.ds(pl.multiple_of(i*EL, EL), EL), :]
+        v = state_ref[pl.ds(i*EL, EL), :]
         return c[0]+fold(v), c[1]+fold(v*v)
     z = jnp.zeros((8, CH), f32)
     mean, inv = norm_stats(*steps(PIX//EL, sums, (z, z)), member, PIX*(CH//GROUPS))
     stat_ref[...] = rows_of(mean, inv)
     def project(i, _):
-        r = pl.ds(pl.multiple_of(i*256, 256), 256)
+        r = pl.ds(i*256, 256)
         n = ((state_ref[r, :]-mean)*inv*gain+shift).astype(narrow)
         qkv_ref[r, :] = (dot(n, wp_ref[...])+bp_ref[...]).astype(narrow)
         return _
@@ -676,18 +679,17 @@
     for h in range(HEADS):
         vt_ref[...] = jnp.transpose(qkv_ref[:, 2*QW+h*HP:2*QW+(h+1)*HP].astype(f32)).astype(narrow)
         for c in range(0, PIX, QC):
-            s = dot_nt(qkv_ref[:, QW+h*HP:QW+(h+1)*HP], qkv_ref[c:c+QC, h*HP:(h+1)*HP])*SCALE
+            s = dot_nt(qkv_ref[:, QW+h*HP:QW+(h+1)*HP], qkv_ref[c:c+QC, h*HP:(h+1)*HP])
             top = jnp.max(s, axis=0, keepdims=True)
-            e = jnp.exp(s-top)
+            e = jnp.exp2((s-top)*POWER)
             total = jnp.sum(e, axis=0, keepdims=True)
-            log_ref[h:h+1, c:c+QC] = top+jnp.log(total)
-            p = (e*(1.0/total)).astype(narrow)
-            m = dot(vt_ref[...], p).astype(narrow)
+            log_ref[h:h+1, c:c+QC] = top*POWER+jnp.log2(total)
+            m = (dot(vt_ref[...], e.astype(narrow))*(1.0/total)).astype(narrow)
             mixed_t_ref[h*HP:(h+1)*HP, c:c+QC] = m
             mixed_ref[c:c+QC, h*HP:(h+1)*HP] = jnp.transpose(m.astype(f32)).astype(narrow)
     log_ref[HEADS:8, :] = jnp.zeros((8-HEADS, PIX), f32)
     def finish(i, _):
-        r = pl.ds(pl.multiple_of(i*256, 256), 256)
+        r = pl.ds(i*256, 256)
         out_ref[r, :] = state_ref[r, :]+(dot(mixed_ref[r, :], wo_ref[...])+bias)
         return _
     steps(PIX//256, finish, 0)
@@ -710,7 +712,7 @@
     z = jnp.zeros((8, CH), f32)
     one = lambda v: jnp.sum(v, axis=0, keepdims=True)
     def start(i, c):
-        r = pl.ds(pl.multiple_of(i*256, 256), 256)
+        r = pl.ds(i*256, 256)
         g = grad_ref[r, :].astype(narrow)
         keep_ref[r, :] = g
         dm_ref[r, :] = dot_nt(g, wo_ref[...]).astype(narrow)
@@ -727,10 +729,11 @@
         kt_ref[...] = jnp.transpose(qkv_ref[:, k0:k0+HP].astype(f32)).astype(narrow)
         for c in range(0, PIX, QC):
             q, dm = qkv_ref[c:c+QC, q0:q0+HP], dm_ref[c:c+QC, h*HP:(h+1)*HP]
-            s = dot_nt(qkv_ref[:, k0:k0+HP], q)*SCALE
-            p = jnp.exp(s-log_ref[h:h+1, c:c+QC])
+            s = dot_nt(qkv_ref[:, k0:k0+HP], q)
+            p = jnp.exp2(s*POWER-log_ref[h:h+1, c:c+QC])
             dp = dot_nt(qkv_ref[:, v0:v0+HP], dm)
-            delta = jnp.sum(dp*p, axis=0, keepdims=True)
+            dm_t = dot_nt(wo_ref[h*HP:(h+1)*HP, :], keep_ref[c:c+QC, :]).astype(narrow).astype(f32)
+            delta = jnp.sum(dm_t*mixed_t_ref[h*HP:(h+1)*HP, c:c+QC].astype(f32), axis=0, keepdims=True)
             ds = (p*(dp-delta)).astype(narrow)
             dv = dot(p.astype(narrow), dm)
             dk = dot(ds, q)
@@ -757,7 +760,7 @@
     copy.start()
     zb = jnp.zeros((8, 3*QW), f32)
     def norm_grad(i, c):
-        r = pl.ds(pl.multiple_of(i*256, 256), 256)
+        r = pl.ds(i*256, 256)
         d = dot_nt(pg_ref[r, :], wp_ref[...])
         n = (state_ref[r, :]-mean)*inv
         out_ref[r, :] = d
@@ -767,7 +770,7 @@
     tot = group_totals(rows_of(shift_grad*gain, gain_grad*gain), member)/(PIX*(CH//GROUPS))
     first, second = tot[0:1], tot[1:2]
     def finish(i, _):
-        r = pl.ds(pl.multiple_of(i*EL, EL), EL)
+        r = pl.ds(i*EL, EL)
         n = (state_ref[r, :]-mean)*inv
         out_ref[r, :] = grad_ref[r, :]+(out_ref[r, :]*gain-first-n*second)*inv
         return _
@@ -898,12 +901,13 @@
             sends[coords.index(member)] = (g, at)
     length = small.shape[0]//2
     half_small, other_small = (lax.dynamic_slice_in_dim(small, core*length, length) for core in (a["c"], 1-a["c"]))
+    half_small = half_small+turn(other_small, "c", 2, 1)
+    far_starts = hold_for(far_starts, half_small)
     arrived, merged = [], []
     for part in range(parts):
         sent = cut(large, far_starts+bounds[part], bounds[part+1]-bounds[part])
         arrived.append(turn(sent, "c", 2, 1))
         far_starts = hold_for(far_starts, sent)
-    half_small = add_over(half_small+turn(other_small, "c", 2, 1), place, ("x",))
     for part in range(parts):
         size = bounds[part+1]-bounds[part]
         outs = [sds((len(members), size, TILE, WIDE), f32 if name in ("y", "x") else narrow) for name, members in groups]
@@ -947,11 +951,13 @@
             waiting[0] = hold_for(waiting[0], merged[-1])
         near, far = first_sums(merged[part], waiting[part])
         if part == 0:
-            half_small = add_over(hold_for(half_small, (near, far)), place, ("y",))
-        if part == min(1, parts-1):
-            half_small = add_over(hold_for(half_small, (near, far)), place, ("z",))
+            half_small = add_over(hold_for(half_small, merged[-1]), place, ("z",))
+        if part == parts-1:
+            half_small = add_over(hold_for(half_small, (near, far)), place, ("x", "y"))
         if part+2 < parts:
             waiting.append(first_stage(hold_for(merged[part+2], (near, far))))
+        if 0 < part < parts-1:
+            near, far = hold_for((near, far), waiting[part+1])
         results.append(third_sum(*second_sums(near, far)))
     other_small = turn(half_small, "c", 2, 1)
     first = a["c"] == 0
@@ -1223,7 +1229,7 @@
     begin, inner, stat, base, vec = blocks[0]
     grad, large, s0 = block_back(place, grad, begin, inner, stat, pieces, base, vec, large)
     large, small = down_stem_back(me, place.total, grad, skip, skip_grad, down_w, noisy, head_tail, attn_small, s1, s0, large)
-    total, small = share_out(large, small, place, 3)
+    total, small = share_out(large, small, place, 2)
     total = lax.dynamic_slice_in_dim(total.reshape(-1, WIDE), spare, share)
     row = share*me+jnp.arange(share)
     dense = functools.reduce(jnp.logical_or, [

time: 523 us -> 491 us (0.939)
  Pallas kernels: 220 us -> 196 us
  waiting for transfers between devices: 166 us -> 160 us
    ppermute x26 -> x18, waiting for transfers between devices: 53.9 us -> 32.4 us  [turn(): lax.ppermute(value, axis, [(i, (i + distance) % size) for i in range(size)])]
    pallas_call x8, Pallas kernels: 155 us -> 139 us  [call(): pl.pallas_call(kernel, out_shape=outs, in_specs=places, out_specs=[pl.Blo...]
    ppermute x14, waiting for transfers between devices: 33.1 us -> 48.8 us  [add_over(): lax.ppermute(value, axis, [(i, i ^ step) for i in range(size)])]
    pallas_call x3 -> x2, Pallas kernels: 17.8 us -> 14.9 us  [share_out(): pl.pallas_call(functools.partial(merge_kernel, coords, sends, len(coords)...]
    pallas_call x3 -> x2, Pallas kernels: 13 us -> 10.3 us  [cut(): pl.pallas_call(functools.partial(cut_kernel, count, size), out_shape=sds(...]
    ppermute x26 -> x18, starting transfers between devices: 20.6 us -> 21.5 us  [turn(): lax.ppermute(value, axis, [(i, (i + distance) % size) for i in range(size)])]
  transfers between devices with their start and end apart: 42 -> 34, of which waited for: 21 -> 19; matrix products, arithmetic and copies ran while one was open for 8% -> 8% of each run, Pallas kernels for 7% -> 6%
where the time goes in v4:
time: 491 us; the launch traced here: 484 us
  Pallas kernels  196 us (40%)
  waiting for transfers between devices  160 us (33%)
  starting transfers between devices  42 us (9%)
  local copies, waits for them, and re-layouts  41.4 us (8%)
  other arithmetic  24.3 us (5%)
  between operations  19.7 us (4%)
    pallas_call x8, Pallas kernels, call(): pl.pallas_call(kernel, out_shape=outs, in_specs=places, out_specs=[pl.Blo...  139 us
    all_gather x1, waiting for transfers between devices, step(): lax.all_gather(piece.reshape(place.block, TILE, WIDE), ('y', 'c', 'z', 'x...  73.3 us
    ppermute x14, waiting for transfers between devices, add_over(): lax.ppermute(value, axis, [(i, i ^ step) for i in range(size)])  48.8 us
    ppermute x18, waiting for transfers between devices, turn(): lax.ppermute(value, axis, [(i, (i + distance) % size) for i in range(size)])  32.4 us
    ppermute x18, starting transfers between devices, turn(): lax.ppermute(value, axis, [(i, (i + distance) % size) for i in range(size)])  21.5 us
    pallas_call x1, Pallas kernels, head(): pl.pallas_call(head_kernel, out_shape=outs, in_specs=[pl.BlockSpec(memory...  15.3 us
    pallas_call x2, Pallas kernels, share_out(): pl.pallas_call(functools.partial(merge_kernel, coords, sends, len(coords)...  14.9 us
    ppermute x14, starting transfers between devices, add_over(): lax.ppermute(value, axis, [(i, i ^ step) for i in range(size)])  13.2 us
  transfers between devices with their start and end apart: 34, of which 19 were waited for; matrix products, arithmetic and copies ran while one was open for 8% of the time, Pallas kernels for 6%

profile of v4, /device:TPU:0, one launch (start us, length us, event | category | flops | bytes accessed | tf_op | source)
XLA Modules:
  0.0 483.8 jit_solution(2413112193481810488)
XLA Ops:
  13.2 7.3 %all-to-all-start = ((f32[8,1,3584]{2,1,0:T(1,128)}), f32[8,1,3584]{2,1,0:T(1,128)S(1)}, u32[]{:S(2)}, u32[]{:S(2)}) async-start(f32[8,1,3584]{2,1,0:T(1,128)} %reshape.170), calls=%async_computation | async-start | bytes 229376 | tf_op jit(solution)/shard_map/all_to_all | solution.py:1168
  21.9 5.9 %all-to-all-done = f32[8,1,3584]{2,1,0:T(1,128)S(1)} async-done(((f32[8,1,3584]{2,1,0:T(1,128)}), f32[8,1,3584]{2,1,0:T(1,128)S(1)}, u32[]{:S(2)}, u32[]{:S(2)}) %all-to-all-start) | async-done | bytes 114720 | tf_op jit(solution)/shard_map/all_to_all | solution.py:1168
  60.9 73.3 %all-gather.2.cloned.1.call-done = bf16[32,45,16,384]{3,2,1,0:T(8,128)(2,1)} async-done(((bf16[1,45,16,384]{3,2,1,0:T(8,128)(2,1)}), bf16[32,45,16,384]{3,2,1,0:T(8,128)(2,1)}) %all-gather.2.cloned.1.call-update) | async-done | bytes 17694736 | tf_op jit(solution)/shard_map/all_gather | solution.py:1165
  142.2 5.8 %shard_map.153 = (f32[32,768]{1,0:T(8,128)}, bf16[32,768]{1,0:T(8,128)(2,1)}, f32[32,768]{1,0:T(8,128)}, bf16[32,768]{1,0:T(8,128)(2,1)}, f32[2,8,384]{2,1,0:T(8...) custom-call(s32[1]{0:T(128)} %bitcast.16.me_ref, bf16[32,192]{1,0:T(8,128)(2,1)} %pad_maximum_fusion.3.sinus_ref, ...), custom_call_target="tpu_custom_call" | custom-call | flops 134217728 | bytes 8388608 | tf_op jit(solution)/shard_map/pallas_call | solution.py:1044
  149.3 7.2 %shard_map.152 = (bf16[4,1024,192]{2,1,0:T(8,128)(2,1)}, f32[1024,384]{1,0:T(8,128)}, bf16[1728,384]{1,0:T(8,128)(2,1)}) custom-call(f32[4,8,1024]{2,1,0:T(8,128)} %pad_convert_fusion.noisy_ref, bf16[128,192]{1,0:T(8,128)(2,1)} %pad.42.sw_ref, f32[1,192]{1,0:T(1,128)} %bitcast.178, bf16[32,720,384]{2,1,0:T(8,128)(2,1)} %bitcast.155), custom_call_target="tpu_custom_call" | custom-call | flops 1358954496 | bytes 22348544 | tf_op jit(solution)/shard_map/pallas_call | solution.py:100
  156.5 15.1 %shard_map.154 = (f32[1024,384]{1,0:T(8,128)}, f32[1024,384]{1,0:T(8,128)}, f32[8,384]{1,0:T(8,128)}) custom-call(f32[1024,384]{1,0:T(8,128)} %get-tuple-element.62.state_ref, bf16[32,720,384]{2,1,0:T(8,128)(2,1)} %bitcast.156, f32[8,384]{1,0:T(8,128)} %get-tuple-element.135.vec_ref), custom_call_target="tpu_custom_call" | custom-call | flops 5435817984 | bytes 22437888 | tf_op jit(solution)/shard_map/pallas_call | solution.py:100
  171.7 15.2 %shard_map.155 = (f32[1024,384]{1,0:T(8,128)}, f32[1024,384]{1,0:T(8,128)}, f32[8,384]{1,0:T(8,128)}) custom-call(f32[1024,384]{1,0:T(8,128)} %get-tuple-element.64.state_ref, bf16[32,720,384]{2,1,0:T(8,128)(2,1)} %bitcast.157, f32[8,384]{1,0:T(8,128)} %get-tuple-element.134.vec_ref), custom_call_target="tpu_custom_call" | custom-call | flops 5435817984 | bytes 22437888 | tf_op jit(solution)/shard_map/pallas_call | solution.py:100
  186.9 18.4 %shard_map.156 = (f32[1024,384]{1,0:T(8,128)}, bf16[1024,1536]{1,0:T(8,128)(2,1)}, f32[8,1024]{1,0:T(8,128)}, bf16[512,1024]{1,0:T(8,128)(2,1)}, f32[8,384]{1,0:...) custom-call(f32[1024,384]{1,0:T(8,128)} %get-tuple-element.65.state_ref, ...), custom_call_target="tpu_custom_call" | custom-call | flops 3758096384 | bytes 26664960 | tf_op jit(solution)/shard_map/pallas_call | solution.py:100
  209.0 15.3 %shard_map.157 = (f32[1024,384]{1,0:T(8,128)}, f32[4,1024,192]{2,1,0:T(8,128)}, f32[120,384]{1,0:T(8,128)}, f32[8,128]{1,0:T(8,128)}) custom-call(f32[4]{0:T(128)} %pad_maximum_fusion.5.num_ref, f32[1024,384]{1,0:T(8,128)} %get-tuple-element.66.state_ref, bf16[4,1024,192]{2,1,0:T(8,128)(2,1)} %get-tuple-element.67.skip_ref, bf16[128,384]{1,0:T(8,128)(2,1)} %pad.44.wu_ref, ...), custom_call_target="tpu_custom_call" | custom-call | flops 1207959552 | bytes 12582912 | tf_op jit(solution)/shard_map/pallas_call | solution.py:622
  224.4 22.8 %shard_map.158 = (f32[1024,384]{1,0:T(8,128)}, bf16[1392,16,384]{2,1,0:T(8,128)(2,1)}, f32[8,384]{1,0:T(8,128)}) custom-call(f32[1024,384]{1,0:T(8,128)} %get-tuple-element.68.grad_ref, f32[1024,384]{1,0:T(8,128)} %get-tuple-element.65.state_ref, f32[8,384]{1,0:T(8,128)} %get-tuple-element.69.stat_ref, bf16[1024,1536]{1,0:T(8,128)(2,1)} %get-tuple-element.70.qkv_ref, ...), custom_call_target="tpu_custom_call" | custom-call | flops 8589934592 | bytes 27660288 | tf_op jit(solution)/shard_map/pallas_call | solution.py:100
  247.2 24.3 %shard_map.159 = (f32[1024,384]{1,0:T(8,128)}, bf16[1392,16,384]{2,1,0:T(8,128)(2,1)}, f32[8,384]{1,0:T(8,128)}) custom-call(f32[1024,384]{1,0:T(8,128)} %get-tuple-element.76.grad_ref, f32[1024,384]{1,0:T(8,128)} %get-tuple-element.64.state_ref, f32[1024,384]{1,0:T(8,128)} %get-tuple-element.77.inner_ref, ...), custom_call_target="tpu_custom_call", output_to_operand_aliasing={{1}: (6, {})} | custom-call | flops 10871635968 | bytes 58232832 | tf_op jit(solution)/shard_map/pallas_call | solution.py:100
  271.5 24.0 %shard_map.160 = (f32[1024,384]{1,0:T(8,128)}, bf16[1392,16,384]{2,1,0:T(8,128)(2,1)}, f32[8,384]{1,0:T(8,128)}) custom-call(f32[1024,384]{1,0:T(8,128)} %get-tuple-element.80.grad_ref, f32[1024,384]{1,0:T(8,128)} %get-tuple-element.62.state_ref, f32[1024,384]{1,0:T(8,128)} %get-tuple-element.81.inner_ref, ...), custom_call_target="tpu_custom_call", output_to_operand_aliasing={{1}: (6, {})} | custom-call | flops 10871635968 | bytes 58232832 | tf_op jit(solution)/shard_map/pallas_call | solution.py:100
  295.5 12.2 %shard_map.161 = (bf16[1392,16,384]{2,1,0:T(8,128)(2,1)}, f32[320,384]{1,0:T(8,128)}) custom-call(s32[1]{0:T(128)} %bitcast.16.me_ref, f32[1024,384]{1,0:T(8,128)} %get-tuple-element.84.grad_ref, bf16[4,1024,192]{2,1,0:T(8,128)(2,1)} %get-tuple-element.67.skip_ref, f32[4,1024,192]{2,1,0:T(8,128)} %get-tuple-element.85.more_ref, ...), custom_call_target="tpu_custom_call", output_to_operand_aliasing={{0}: (10, {})} | custom-call | flops 2717908992 | bytes 42672132 | tf_op jit(solution)/shard_map/pallas_call | solution.py:100
  310.3 5.1 %shard_map.162 = bf16[16,22,16,384]{3,2,1,0:T(8,128)(2,1)} custom-call(s32[16]{0:T(128)} %stack.189.starts_ref, bf16[1392,16,384]{2,1,0:T(8,128)(2,1)} %get-tuple-element.92.large_ref), custom_call_target="tpu_custom_call" | custom-call | bytes 1024 | tf_op jit(solution)/shard_map/pallas_call | solution.py:859
  323.2 7.3 %shard_map.163 = (f32[4,22,16,384]{3,2,1,0:T(8,128)}, bf16[4,22,16,384]{3,2,1,0:T(8,128)(2,1)}, f32[4,22,16,384]{3,2,1,0:T(8,128)}, bf16[4,22,16,384]{3,2,1,0:T(8,128)(2,1)}) custom-call(s32[16]{0:T(128)} %stack.159.starts_ref, bf16[1392,16,384]{2,1,0:T(8,128)(2,1)} %get-tuple-element.92.large_ref, bf16[16,22,16,384]{3,2,1,0:T(8,128)(2,1)} %collective-permute-done.6.arrived_ref), custom_call_target="tpu_custom_call" | custom-call | bytes 1024 | tf_op jit(solution)/shard_map/pallas_call | solution.py:914
  333.1 7.6 %shard_map.165 = (f32[4,23,16,384]{3,2,1,0:T(8,128)}, bf16[4,23,16,384]{3,2,1,0:T(8,128)(2,1)}, f32[4,23,16,384]{3,2,1,0:T(8,128)}, bf16[4,23,16,384]{3,2,1,0:T(8,128)(2,1)}) custom-call(s32[16]{0:T(128)} %broadcast_add_fusion.1.starts_ref, bf16[1392,16,384]{2,1,0:T(8,128)(2,1)} %get-tuple-element.92.large_ref, ...), custom_call_target="tpu_custom_call" | custom-call | bytes 1024 | tf_op jit(solution)/shard_map/pallas_call | solution.py:914
  341.1 7.3 %collective-permute-done.22 = f32[160,384]{1,0:T(8,128)S(1)} collective-permute-done((f32[160,384]{1,0:T(8,128)S(1)}, f32[160,384]{1,0:T(8,128)S(1)}, u32[]{:S(2)}, u32[]{:S(2)}) %collective-permute-start.22) | collective-permute-done | bytes 245792 | tf_op jit(solution)/shard_map/ppermute | solution.py:844
  353.2 8.8 %collective-permute-done.23 = f32[160,384]{1,0:T(8,128)S(1)} collective-permute-done((f32[160,384]{1,0:T(8,128)}, f32[160,384]{1,0:T(8,128)S(1)}, u32[]{:S(2)}, u32[]{:S(2)}) %collective-permute-start.23) | collective-permute-done | bytes 245792 | tf_op jit(solution)/shard_map/ppermute | solution.py:844
  367.7 14.0 %collective-permute-done.15 = bf16[4,23,16,384]{3,2,1,0:T(8,128)(2,1)S(1)} collective-permute-done((bf16[4,23,16,384]{3,2,1,0:T(8,128)(2,1)}, bf16[4,23,16,384]{3,2,1,0:T(8,128)(2,1)S(1)}, u32[]{:S(2)}, u32[]{:S(2)}) %collective-permute-start.15) | collective-permute-done | bytes 1130528 | tf_op jit(solution)/shard_map/ppermute | solution.py:829
  387.4 12.7 %collective-permute-done.24 = f32[160,384]{1,0:T(8,128)S(1)} collective-permute-done((f32[160,384]{1,0:T(8,128)S(1)}, f32[160,384]{1,0:T(8,128)S(1)}, u32[]{:S(2)}, u32[]{:S(2)}) %collective-permute-start.24) | collective-permute-done | bytes 245792 | tf_op jit(solution)/shard_map/ppermute | solution.py:844
  402.9 7.1 %collective-permute-done.25 = f32[160,384]{1,0:T(8,128)S(1)} collective-permute-done((f32[160,384]{1,0:T(8,128)S(1)}, f32[160,384]{1,0:T(8,128)S(1)}, u32[]{:S(2)}, u32[]{:S(2)}) %collective-permute-start.25) | collective-permute-done | bytes 245792 | tf_op jit(solution)/shard_map/ppermute | solution.py:844
  414.4 6.7 %collective-permute-start.20 = (bf16[23,16,384]{2,1,0:T(8,128)(2,1)S(1)}, bf16[23,16,384]{2,1,0:T(8,128)(2,1)S(1)}, u32[]{:S(2)}, u32[]{:S(2)}) collective-permute-start(bf16[23,16,384]{2,1,0:T(8,128)(2,1)S(1)} %get-tuple-element.122), channel_id=1, source_target_pairs={{0,4},{2,6},{4,0},{6,2},{1,5},{3,7},{5,1},{7,3},{8,12},{10,14},{12... | collective-permute-start | bytes 847880 | tf_op jit(solution)/shard_map/ppermute | solution.py:829
  421.1 15.5 %collective-permute-done.13 = bf16[22,16,384]{2,1,0:T(8,128)(2,1)S(1)} collective-permute-done((bf16[22,16,384]{2,1,0:T(8,128)(2,1)S(1)}, bf16[22,16,384]{2,1,0:T(8,128)(2,1)S(1)}, u32[]{:S(2)}, u32[]{:S(2)}) %collective-permute-start.13) | collective-permute-done | bytes 270368 | tf_op jit(solution)/shard_map/ppermute | solution.py:829
  437.8 10.4 %shard_map.166 = f32[694,384]{1,0:T(8,128)} custom-call(s32[1]{0:T(128)} %bitcast.16.me_ref, f32[320,384]{1,0:T(8,128)} %pad_maximum_fusion.1.small_ref, bf16[32,192]{1,0:T(8,128)(2,1)} %pad_maximum_fusion.3.sinus_ref, f32[32,768]{1,0:T(8,128)} %get-tuple-element.109.hidden_pre_ref, bf16[32,768]{1,0:T(8,128)(2,1)} %get-tuple-element.110.hidden_ref, ...), custom_call_target="tpu_custom_call" | custom-call | bytes 1024 | tf_op jit(solution)/shard_map/pallas_call | solution.py:1145
  (211 shorter events, 114.8 us)
Async XLA Ops:
  7.2 127.1 %all-gather.2.cloned.1.call-start = ((), (), s32[]{:S(2)}) async-start(), calls=%async_computation.1 | async-start | bytes 18247680 | tf_op jit(solution)/shard_map/all_gather | solution.py:1165
  13.2 14.6 %all-to-all-start = ((f32[8,1,3584]{2,1,0:T(1,128)}), f32[8,1,3584]{2,1,0:T(1,128)S(1)}, u32[]{:S(2)}, u32[]{:S(2)}) async-start(f32[8,1,3584]{2,1,0:T(1,128)} %reshape.170), calls=%async_computation | async-start | bytes 229376 | tf_op jit(solution)/shard_map/all_to_all | solution.py:1168
  36.6 9.7 %collective-permute-start.2 = (f32[8,384]{1,0:T(8,128)S(1)}, f32[8,384]{1,0:T(8,128)S(1)}, u32[]{:S(2)}, u32[]{:S(2)}) collective-permute-start(f32[8,384]{1,0:T(8,128)S(1)} %fusion.45), channel_id=1, source_target_pairs={{0,16},{16,0},{1,17},{17,1},{2,18},{18,2},{3,19},{19,3},{4,20},{20... | collective-permute-start | bytes 36872 | tf_op jit(solution)/shard_map/ppermute | solution.py:844
  315.5 7.8 %collective-permute-start.6 = (bf16[16,22,16,384]{3,2,1,0:T(8,128)(2,1)}, bf16[16,22,16,384]{3,2,1,0:T(8,128)(2,1)}, u32[]{:S(2)}, u32[]{:S(2)}) collective-permute-start(bf16[16,22,16,384]{3,2,1,0:T(8,128)(2,1)} %shard_map.162), channel_id=1, source_target_pairs={{0,8},{8,0},{1,9},{9,1},{2,10},{10,2},{3,11},{11,3},{4,12},{12,4},... | collective-permute-start | bytes 12976136 | tf_op jit(solution)/shard_map/ppermute | solution.py:829
  321.5 11.7 %collective-permute-start.9 = (bf16[16,23,16,384]{3,2,1,0:T(8,128)(2,1)}, bf16[16,23,16,384]{3,2,1,0:T(8,128)(2,1)}, u32[]{:S(2)}, u32[]{:S(2)}) collective-permute-start(bf16[16,23,16,384]{3,2,1,0:T(8,128)(2,1)} %shard_map.164), channel_id=1, source_target_pairs={{0,8},{8,0},{1,9},{9,1},{2,10},{10,2},{3,11},{11,3},{4,12},{12,4},... | collective-permute-start | bytes 13565960 | tf_op jit(solution)/shard_map/ppermute | solution.py:829
  330.5 32.4 %collective-permute-start.7 = (bf16[4,22,16,384]{3,2,1,0:T(8,128)(2,1)}, bf16[4,22,16,384]{3,2,1,0:T(8,128)(2,1)S(1)}, u32[]{:S(2)}, u32[]{:S(2)}) collective-permute-start(bf16[4,22,16,384]{3,2,1,0:T(8,128)(2,1)} %get-tuple-element.96), channel_id=1, source_target_pairs={{0,16},{16,0},{1,17},{17,1},{2,18},{18,2},{3,19},{19,3},{4,20},{20... | collective-permute-start | bytes 3244040 | tf_op jit(solution)/shard_map/ppermute | solution.py:829
  332.1 30.9 %collective-permute-start.8 = (bf16[4,22,16,384]{3,2,1,0:T(8,128)(2,1)}, bf16[4,22,16,384]{3,2,1,0:T(8,128)(2,1)}, u32[]{:S(2)}, u32[]{:S(2)}) collective-permute-start(bf16[4,22,16,384]{3,2,1,0:T(8,128)(2,1)} %get-tuple-element.97), channel_id=1, source_target_pairs={{0,1},{1,0},{2,3},{3,2},{4,5},{5,4},{6,7},{7,6},{8,9},{9,8},{10,11... | collective-permute-start | bytes 3244040 | tf_op jit(solution)/shard_map/ppermute | solution.py:829
  340.7 7.6 %collective-permute-start.22 = (f32[160,384]{1,0:T(8,128)S(1)}, f32[160,384]{1,0:T(8,128)S(1)}, u32[]{:S(2)}, u32[]{:S(2)}) collective-permute-start(f32[160,384]{1,0:T(8,128)S(1)} %dynamic-slice_add_fusion), channel_id=1, source_target_pairs={{0,2},{2,0},{4,6},{6,4},{1,3},{3,1},{5,7},{7,5},{8,10},{10,8},{12,... | collective-permute-start | bytes 737288 | tf_op jit(solution)/shard_map/ppermute | solution.py:844
  349.1 12.9 %collective-permute-start.23 = (f32[160,384]{1,0:T(8,128)}, f32[160,384]{1,0:T(8,128)S(1)}, u32[]{:S(2)}, u32[]{:S(2)}) collective-permute-start(f32[160,384]{1,0:T(8,128)} %add.850), channel_id=1, source_target_pairs={{0,4},{2,6},{4,0},{6,2},{1,5},{3,7},{5,1},{7,3},{8,12},{10,14},{12... | collective-permute-start | bytes 737288 | tf_op jit(solution)/shard_map/ppermute | solution.py:844
  350.6 31.1 %collective-permute-start.15 = (bf16[4,23,16,384]{3,2,1,0:T(8,128)(2,1)}, bf16[4,23,16,384]{3,2,1,0:T(8,128)(2,1)S(1)}, u32[]{:S(2)}, u32[]{:S(2)}) collective-permute-start(bf16[4,23,16,384]{3,2,1,0:T(8,128)(2,1)} %get-tuple-element.104), channel_id=1, source_target_pairs={{0,16},{16,0},{1,17},{17,1},{2,18},{18,2},{3,19},{19,3},{4,20},{20... | collective-permute-start | bytes 3391496 | tf_op jit(solution)/shard_map/ppermute | solution.py:829
  352.5 30.7 %collective-permute-start.18 = (bf16[4,23,16,384]{3,2,1,0:T(8,128)(2,1)}, bf16[4,23,16,384]{3,2,1,0:T(8,128)(2,1)S(1)}, u32[]{:S(2)}, u32[]{:S(2)}) collective-permute-start(bf16[4,23,16,384]{3,2,1,0:T(8,128)(2,1)} %get-tuple-element.102), channel_id=1, source_target_pairs={{0,1},{1,0},{2,3},{3,2},{4,5},{5,4},{6,7},{7,6},{8,9},{9,8},{10,11... | collective-permute-start | bytes 3391496 | tf_op jit(solution)/shard_map/ppermute | solution.py:829
  365.5 36.9 %collective-permute-start.10 = (bf16[2,22,16,384]{3,2,1,0:T(8,128)(2,1)S(1)}, bf16[2,22,16,384]{3,2,1,0:T(8,128)(2,1)S(1)}, u32[]{:S(2)}, u32[]{:S(2)}) collective-permute-start(bf16[2,22,16,384]{3,2,1,0:T(8,128)(2,1)S(1)} %fusion.13), channel_id=1, source_target_pairs={{0,1},{1,0},{2,3},{3,2},{4,5},{5,4},{6,7},{7,6},{8,9},{9,8},{10,11... | collective-permute-start | bytes 1622024 | tf_op jit(solution)/shard_map/ppermute | solution.py:829
  367.1 33.6 %collective-permute-start.12 = (bf16[2,22,16,384]{3,2,1,0:T(8,128)(2,1)S(1)}, bf16[2,22,16,384]{3,2,1,0:T(8,128)(2,1)S(1)}, u32[]{:S(2)}, u32[]{:S(2)}) collective-permute-start(bf16[2,22,16,384]{3,2,1,0:T(8,128)(2,1)S(1)} %fusion.14), channel_id=1, source_target_pairs={{0,16},{16,0},{1,17},{17,1},{2,18},{18,2},{3,19},{19,3},{4,20},{20... | collective-permute-start | bytes 1622024 | tf_op jit(solution)/shard_map/ppermute | solution.py:829
  383.6 16.4 %collective-permute-start.24 = (f32[160,384]{1,0:T(8,128)S(1)}, f32[160,384]{1,0:T(8,128)S(1)}, u32[]{:S(2)}, u32[]{:S(2)}) collective-permute-start(f32[160,384]{1,0:T(8,128)S(1)} %add.851), channel_id=1, source_target_pairs={{0,1},{1,0},{2,3},{3,2},{4,5},{5,4},{6,7},{7,6},{8,9},{9,8},{10,11... | collective-permute-start | bytes 737288 | tf_op jit(solution)/shard_map/ppermute | solution.py:844
  385.3 25.9 %collective-permute-start.16 = (bf16[2,23,16,384]{3,2,1,0:T(8,128)(2,1)S(1)}, bf16[2,23,16,384]{3,2,1,0:T(8,128)(2,1)S(1)}, u32[]{:S(2)}, u32[]{:S(2)}) collective-permute-start(bf16[2,23,16,384]{3,2,1,0:T(8,128)(2,1)S(1)} %fusion.8), channel_id=1, source_target_pairs={{0,1},{1,0},{2,3},{3,2},{4,5},{5,4},{6,7},{7,6},{8,9},{9,8},{10,11... | collective-permute-start | bytes 1695752 | tf_op jit(solution)/shard_map/ppermute | solution.py:829
  385.9 24.4 %collective-permute-start.19 = (bf16[2,23,16,384]{3,2,1,0:T(8,128)(2,1)S(1)}, bf16[2,23,16,384]{3,2,1,0:T(8,128)(2,1)S(1)}, u32[]{:S(2)}, u32[]{:S(2)}) collective-permute-start(bf16[2,23,16,384]{3,2,1,0:T(8,128)(2,1)S(1)} %fusion.9), channel_id=1, source_target_pairs={{0,16},{16,0},{1,17},{17,1},{2,18},{18,2},{3,19},{19,3},{4,20},{20... | collective-permute-start | bytes 1695752 | tf_op jit(solution)/shard_map/ppermute | solution.py:829
  400.1 9.9 %collective-permute-start.25 = (f32[160,384]{1,0:T(8,128)S(1)}, f32[160,384]{1,0:T(8,128)S(1)}, u32[]{:S(2)}, u32[]{:S(2)}) collective-permute-start(f32[160,384]{1,0:T(8,128)S(1)} %add.852), channel_id=1, source_target_pairs={{0,16},{16,0},{1,17},{17,1},{2,18},{18,2},{3,19},{19,3},{4,20},{20... | collective-permute-start | bytes 737288 | tf_op jit(solution)/shard_map/ppermute | solution.py:844
  400.9 13.5 %collective-permute-start.14 = (bf16[22,16,384]{2,1,0:T(8,128)(2,1)S(1)}, bf16[22,16,384]{2,1,0:T(8,128)(2,1)S(1)}, u32[]{:S(2)}, u32[]{:S(2)}) collective-permute-start(bf16[22,16,384]{2,1,0:T(8,128)(2,1)S(1)} %get-tuple-element.125), channel_id=1, source_target_pairs={{0,6},{2,0},{4,2},{6,4},{1,7},{3,1},{5,3},{7,5},{8,14},{10,8},{12,... | collective-permute-start | bytes 811016 | tf_op jit(solution)/shard_map/ppermute | solution.py:829
  402.4 34.2 %collective-permute-start.13 = (bf16[22,16,384]{2,1,0:T(8,128)(2,1)S(1)}, bf16[22,16,384]{2,1,0:T(8,128)(2,1)S(1)}, u32[]{:S(2)}, u32[]{:S(2)}) collective-permute-start(bf16[22,16,384]{2,1,0:T(8,128)(2,1)S(1)} %get-tuple-element.124), channel_id=1, source_target_pairs={{0,4},{2,6},{4,0},{6,2},{1,5},{3,7},{5,1},{7,3},{8,12},{10,14},{12... | collective-permute-start | bytes 811016 | tf_op jit(solution)/shard_map/ppermute | solution.py:829
  410.0 26.8 %collective-permute-start.11 = (bf16[22,16,384]{2,1,0:T(8,128)(2,1)S(1)}, bf16[22,16,384]{2,1,0:T(8,128)(2,1)S(1)}, u32[]{:S(2)}, u32[]{:S(2)}) collective-permute-start(bf16[22,16,384]{2,1,0:T(8,128)(2,1)S(1)} %fusion.19), channel_id=1, source_target_pairs={{0,2},{2,4},{4,6},{6,0},{1,3},{3,5},{5,7},{7,1},{8,10},{10,12},{12... | collective-permute-start | bytes 811016 | tf_op jit(solution)/shard_map/ppermute | solution.py:829
  410.3 26.6 %collective-permute-start.26 = (f32[160,384]{1,0:T(8,128)S(1)}, f32[160,384]{1,0:T(8,128)S(1)}, u32[]{:S(2)}, u32[]{:S(2)}) collective-permute-start(f32[160,384]{1,0:T(8,128)S(1)} %add.853), channel_id=1, source_target_pairs={{0,8},{8,0},{1,9},{9,1},{2,10},{10,2},{3,11},{11,3},{4,12},{12,4},... | collective-permute-start | bytes 737288 | tf_op jit(solution)/shard_map/ppermute | solution.py:829
  411.2 37.0 %collective-permute-start.21 = (bf16[23,16,384]{2,1,0:T(8,128)(2,1)S(1)}, bf16[23,16,384]{2,1,0:T(8,128)(2,1)S(1)}, u32[]{:S(2)}, u32[]{:S(2)}) collective-permute-start(bf16[23,16,384]{2,1,0:T(8,128)(2,1)S(1)} %get-tuple-element.123), channel_id=1, source_target_pairs={{0,6},{2,0},{4,2},{6,4},{1,7},{3,1},{5,3},{7,5},{8,14},{10,8},{12,... | collective-permute-start | bytes 847880 | tf_op jit(solution)/shard_map/ppermute | solution.py:829
  414.4 34.2 %collective-permute-start.20 = (bf16[23,16,384]{2,1,0:T(8,128)(2,1)S(1)}, bf16[23,16,384]{2,1,0:T(8,128)(2,1)S(1)}, u32[]{:S(2)}, u32[]{:S(2)}) collective-permute-start(bf16[23,16,384]{2,1,0:T(8,128)(2,1)S(1)} %get-tuple-element.122), channel_id=1, source_target_pairs={{0,4},{2,6},{4,0},{6,2},{1,5},{3,7},{5,1},{7,3},{8,12},{10,14},{12... | collective-permute-start | bytes 847880 | tf_op jit(solution)/shard_map/ppermute | solution.py:829
  436.6 12.0 %collective-permute-start.17 = (bf16[23,16,384]{2,1,0:T(8,128)(2,1)S(1)}, bf16[23,16,384]{2,1,0:T(8,128)(2,1)S(1)}, u32[]{:S(2)}, u32[]{:S(2)}) collective-permute-start(bf16[23,16,384]{2,1,0:T(8,128)(2,1)S(1)} %fusion.18), channel_id=1, source_target_pairs={{0,2},{2,4},{4,6},{6,0},{1,3},{3,5},{5,7},{7,1},{8,10},{10,12},{12... | collective-permute-start | bytes 847880 | tf_op jit(solution)/shard_map/ppermute | solution.py:829
  (25 other events, 170.2 us)
Sparse Core Ops, SparseCore 0:
  12.5 121.7 all-gather.1

commit v5 on v4

--- a/solution.py
+++ b/solution.py
@@ -90,10 +90,10 @@
 
 
 SIDE=32; PIX=SIDE*SIDE
-LIMIT=60*1024*1024
+MIB=1024*1024
 VM=pltpu.VMEM
 
-def call(kernel, ins, outs, scratch, flops, away=(), away_out=(), alias={}, scalar=()):
+def call(kernel, ins, outs, scratch, flops, away=(), away_out=(), alias={}, scalar=(), room=32):
     spec = pl.BlockSpec(memory_space=VM)
     places = [pl.BlockSpec(memory_space=pl.ANY if i in away else pltpu.SMEM if i in scalar else VM) for i in range(len(ins))]
     moved = sum(a.size*a.dtype.itemsize for a in ins) + sum(math.prod(o.shape)*o.dtype.itemsize for o in outs)
@@ -101,7 +101,7 @@
         kernel, out_shape=outs, in_specs=places,
         out_specs=[pl.BlockSpec(memory_space=pl.ANY) if i in away_out else spec for i in range(len(outs))],
         scratch_shapes=scratch, input_output_aliases=alias,
-        compiler_params=pltpu.CompilerParams(vmem_limit_bytes=LIMIT),
+        compiler_params=pltpu.CompilerParams(vmem_limit_bytes=room*MIB),
         cost_estimate=pl.CostEstimate(flops=flops, bytes_accessed=moved, transcendentals=0),
     )(*ins)
 
@@ -110,7 +110,7 @@
 def dot(a, b): return jnp.dot(a, b, preferred_element_type=f32)
 def dot_nt(a, b): return lax.dot_general(a, b, (((1,), (1,)), ((), ())), preferred_element_type=f32)
 
-def sigmoid(v): return 1.0 / (1.0 + jnp.exp(-v))
+def sigmoid(v): return 0.5*jnp.tanh(0.5*v) + 0.5
 
 def membership(chans, per, first=0):
     c = lax.broadcasted_iota(jnp.int32, (chans, 128), 0) + first
@@ -152,19 +152,20 @@
 def pixel_column(rows, width):
     return lax.broadcasted_iota(jnp.int32, (rows, width), 0) % SIDE
 
-def spread(pad_ref, out_ref, width, backward):
+def clear_edges(out_ref, width):
     zero = jnp.zeros((SIDE, 3*width), narrow)
     out_ref[0:SIDE, :] = zero
     out_ref[SIDE+PIX:SIDE+PIX+SIDE, :] = zero
-    col = pixel_column(EL, width)
-    for r in range(0, PIX, EL):
-        before = jnp.where(col == 0, 0.0, pad_ref[r+7:r+7+EL, :]).astype(narrow)
-        after = jnp.where(col == SIDE-1, 0.0, pad_ref[r+9:r+9+EL, :]).astype(narrow)
-        mid = pad_ref[r+8:r+8+EL, :].astype(narrow)
-        first, last = (after, before) if backward else (before, after)
-        out_ref[r+SIDE:r+SIDE+EL, 0:width] = first
-        out_ref[r+SIDE:r+SIDE+EL, width:2*width] = mid
-        out_ref[r+SIDE:r+SIDE+EL, 2*width:3*width] = last
+
+def put_spread(out_ref, r, v, backward):
+    count, width = v.shape
+    col = pixel_column(count, width)
+    before = jnp.where(col == 0, 0.0, pltpu.roll(v, 1, 0)).astype(narrow)
+    after = jnp.where(col == SIDE-1, 0.0, pltpu.roll(v, count-1, 0)).astype(narrow)
+    first, last = (after, before) if backward else (before, after)
+    out_ref[SIDE+r:SIDE+r+count, 0:width] = first
+    out_ref[SIDE+r:SIDE+r+count, width:2*width] = v.astype(narrow)
+    out_ref[SIDE+r:SIDE+r+count, 2*width:3*width] = last
 
 MC=256
 def conv_rows(xs_ref, w_ref, base, r):
@@ -209,7 +210,7 @@
         for i, (d, to) in enumerate(self.edges):
             low_ref[to*TILE:(to+1)*TILE, :] = low_ref[to*TILE:(to+1)*TILE, :]+edge_ref[i]
 
-def block_forward_kernel(rows, state_ref, pieces_ref, vec_ref, out_ref, inner_ref, stat_ref, pad_ref, xs_ref, *held):
+def block_forward_kernel(rows, state_ref, pieces_ref, vec_ref, out_ref, inner_ref, stat_ref, xs_ref, *held):
     one, two = (pieces_ref,)+held[:3], (pieces_ref,)+held[3:]
     rows[0].start(*one)
     rows[1].start(*two)
@@ -222,13 +223,11 @@
         return c[0]+fold(v), c[1]+fold(v*v)
     z = jnp.zeros((8, CH), f32)
     mean1, inv1 = norm_stats(*steps(PIX//EL, sums, (z, z)), member, amount)
-    def act1(i, _):
-        r = i*EL
-        v = (state_ref[pl.ds(r, EL), :] - mean1)*inv1*gain1 + shift1
-        pad_ref[pl.ds(r+8, EL), :] = v*sigmoid(v)
-        return _
-    steps(PIX//EL, act1, 0)
-    spread(pad_ref, xs_ref, CH, False)
+    clear_edges(xs_ref, CH)
+    factor, term = inv1*gain1, shift1 - mean1*inv1*gain1
+    for r in range(0, PIX, EL):
+        v = state_ref[r:r+EL, :]*factor + term
+        put_spread(xs_ref, r, v*sigmoid(v), False)
     rows[0].finish(*one)
     def conv1(i, c):
         r = i*MC
@@ -236,14 +235,10 @@
         inner_ref[pl.ds(r, MC), :] = v
         return c[0]+fold(v), c[1]+fold(v*v)
     mean2, inv2 = norm_stats(*steps(PIX//MC, conv1, (z, z)), member, amount)
-    def act2(i, _):
-        r = i*EL
-        v = (inner_ref[pl.ds(r, EL), :] - mean2)*inv2*gain2 + shift2
-        v = v*scale + offset
-        pad_ref[pl.ds(r+8, EL), :] = v*sigmoid(v)
-        return _
-    steps(PIX//EL, act2, 0)
-    spread(pad_ref, xs_ref, CH, False)
+    factor, term = inv2*gain2*scale, (shift2 - mean2*inv2*gain2)*scale + offset
+    for r in range(0, PIX, EL):
+        v = inner_ref[r:r+EL, :]*factor + term
+        put_spread(xs_ref, r, v*sigmoid(v), False)
     rows[1].finish(*two)
     def conv2(i, _):
         r = i*MC
@@ -259,8 +254,8 @@
     rows = block_rows(place, base)
     return call(functools.partial(block_forward_kernel, rows), [state, pieces, vectors],
         [sds((PIX, CH)), sds((PIX, CH)), sds((8, CH))],
-        [pltpu.VMEM((PIX+16, CH), f32), pltpu.VMEM((PIX+2*SIDE, 3*CH), narrow)]+rows[0].scratch()+rows[1].scratch(),
-        2*2*PIX*TAPS*CH, away=(1,))
+        [pltpu.VMEM((PIX+2*SIDE, 3*CH), narrow)]+rows[0].scratch()+rows[1].scratch(),
+        2*2*PIX*TAPS*CH, away=(1,), room=39)
 
 def back_taps(gs_ref, w_ref, base, r):
     acc = None
@@ -282,7 +277,7 @@
     steps(3, body, 0)
 
 def block_back_kernel(base, rows, grad_ref, state_ref, inner_ref, stat_ref, pieces_ref, vec_ref, large_in_ref, out_ref, large_ref, small_ref,
-                      pad_ref, gs_ref, xt_ref, keep_ref, dw_ref, sems, *held):
+                      gs_ref, xt_ref, keep_ref, dw_ref, sems, *held):
     first_in, second_in = (pieces_ref,)+held[:3], (pieces_ref,)+held[3:]
     rows[1].start(*second_in)
     rows[0].start(*first_in)
@@ -292,73 +287,61 @@
     member = membership(CH, CH//GROUPS)
     amount = PIX*(CH//GROUPS)
     z = jnp.zeros((8, CH), f32)
-    def low(i, c):
-        r = i*EL
-        g = grad_ref[pl.ds(r, EL), :].astype(narrow).astype(f32)
-        pad_ref[pl.ds(r+8, EL), :] = g
-        return c+fold(g)
-    bias2_grad = steps(PIX//EL, low, z)
-    spread(pad_ref, gs_ref, CH, True)
-    for i in range(PIX//EL):
-        r = i*EL
-        v = (inner_ref[r:r+EL, :] - mean2)*inv2*gain2 + shift2
-        v = v*scale + offset
+    one = lambda v: jnp.sum(v, axis=0, keepdims=True)
+    clear_edges(gs_ref, CH)
+    factor2, term2 = inv2*gain2*scale, (shift2 - mean2*inv2*gain2)*scale + offset
+    bias2_grad = z
+    for r in range(0, PIX, EL):
+        g = grad_ref[r:r+EL, :].astype(narrow).astype(f32)
+        put_spread(gs_ref, r, g, True)
+        bias2_grad += fold(g)
+        v = inner_ref[r:r+EL, :]*factor2 + term2
         xt_ref[:, r:r+EL] = jnp.transpose(v*sigmoid(v)).astype(narrow)
     kernel_grads(xt_ref, gs_ref, dw_ref, TAPS)
     half = TAPS//TILE
     second_out = pltpu.make_async_copy(dw_ref.at[half:2*half], large_ref.at[base//TILE+half:base//TILE+2*half], sems.at[0])
     second_out.start()
     rows[1].finish(*second_in)
-    def back2(i, c):
-        r = i*MC
+    d_sum, dn_sum = z, z
+    for r in range(0, PIX, MC):
         d = back_taps(gs_ref, w2_ref, 0, r)
-        n = (inner_ref[pl.ds(r, MC), :] - mean2)*inv2
-        nt = n*gain2 + shift2
-        v = nt*scale + offset
-        s = sigmoid(v)
-        d = d*(s*(1.0+v*(1.0-s)))
-        keep_ref[pl.ds(r, MC), :] = d
-        return c[0]+fold(d*nt), c[1]+fold(d), c[2]+fold(d*n)
-    mod_scale, mod_offset, dn = steps(PIX//MC, back2, (z, z, z))
-    one = lambda v: jnp.sum(v, axis=0, keepdims=True)
-    mod_scale, mod_offset, dn = one(mod_scale), one(mod_offset), one(dn)
+        x = inner_ref[r:r+MC, :]
+        d = d*silu_slope(x*factor2 + term2)
+        keep_ref[r:r+MC, :] = d
+        d_sum += fold(d)
+        dn_sum += fold(d*(x*inv2 - mean2*inv2))
+    mod_offset, dn = one(d_sum), one(dn_sum)
+    mod_scale = gain2*dn + shift2*mod_offset
     tot = group_totals(rows_of(mod_offset*scale*gain2, dn*scale*gain2), member)/amount
-    first, second = tot[0:1], tot[1:2]
-    def inner_back(i, c):
-        r = i*EL
-        n = (inner_ref[pl.ds(r, EL), :] - mean2)*inv2
-        g = (keep_ref[pl.ds(r, EL), :]*scale*gain2 - first - n*second)*inv2
+    first, second = tot[0:1]*inv2, tot[1:2]*inv2*inv2
+    by_keep, by_term = scale*gain2*inv2, second*mean2 - first
+    bias1_grad = z
+    factor1, term1 = inv1*gain1, shift1 - mean1*inv1*gain1
+    for r in range(0, PIX, EL):
+        g = keep_ref[r:r+EL, :]*by_keep - inner_ref[r:r+EL, :]*second + by_term
         g = g.astype(narrow).astype(f32)
-        pad_ref[pl.ds(r+8, EL), :] = g
-        return c+fold(g)
-    bias1_grad = steps(PIX//EL, inner_back, z)
-    spread(pad_ref, gs_ref, CH, True)
-    for i in range(PIX//EL):
-        r = i*EL
-        v = (state_ref[r:r+EL, :] - mean1)*inv1*gain1 + shift1
+        put_spread(gs_ref, r, g, True)
+        bias1_grad += fold(g)
+        v = state_ref[r:r+EL, :]*factor1 + term1
         xt_ref[:, r:r+EL] = jnp.transpose(v*sigmoid(v)).astype(narrow)
     kernel_grads(xt_ref, gs_ref, dw_ref, 0)
     first_out = pltpu.make_async_copy(dw_ref.at[0:half], large_ref.at[base//TILE:base//TILE+half], sems.at[1])
     first_out.start()
     rows[0].finish(*first_in)
-    def back1(i, c):
-        r = i*MC
+    d_sum, dn_sum = z, z
+    for r in range(0, PIX, MC):
         d = back_taps(gs_ref, w1_ref, 0, r)
-        n = (state_ref[pl.ds(r, MC), :] - mean1)*inv1
-        v = n*gain1 + shift1
-        s = sigmoid(v)
-        d = d*(s*(1.0+v*(1.0-s)))
-        keep_ref[pl.ds(r, MC), :] = d
-        return c[0]+fold(d), c[1]+fold(d*n)
-    shift1_grad, gain1_grad = (one(v) for v in steps(PIX//MC, back1, (z, z)))
+        x = state_ref[r:r+MC, :]
+        d = d*silu_slope(x*factor1 + term1)
+        keep_ref[r:r+MC, :] = d
+        d_sum += fold(d)
+        dn_sum += fold(d*(x*inv1 - mean1*inv1))
+    shift1_grad, gain1_grad = one(d_sum), one(dn_sum)
     tot = group_totals(rows_of(shift1_grad*gain1, gain1_grad*gain1), member)/amount
-    first1, second1 = tot[0:1], tot[1:2]
-    def state_back(i, _):
-        r = i*EL
-        n = (state_ref[pl.ds(r, EL), :] - mean1)*inv1
-        out_ref[pl.ds(r, EL), :] = grad_ref[pl.ds(r, EL), :] + (keep_ref[pl.ds(r, EL), :]*gain1 - first1 - n*second1)*inv1
-        return _
-    steps(PIX//EL, state_back, 0)
+    first1, second1 = tot[0:1]*inv1, tot[1:2]*inv1*inv1
+    by_keep1, by_term1 = gain1*inv1, second1*mean1 - first1
+    for r in range(0, PIX, EL):
+        out_ref[r:r+EL, :] = grad_ref[r:r+EL, :] + (keep_ref[r:r+EL, :]*by_keep1 - state_ref[r:r+EL, :]*second1 + by_term1)
     first_out.wait()
     second_out.wait()
     small_ref[...] = jnp.concatenate([one(bias1_grad), one(bias2_grad), gain1_grad, dn*scale, shift1_grad, mod_offset*scale, mod_scale, mod_offset], axis=0)
@@ -367,9 +350,9 @@
     rows = block_rows(place, base)
     return call(functools.partial(block_back_kernel, base, rows), [grad, state, inner, stat, pieces, vectors, large],
         [sds((PIX, CH)), sds(large.shape, narrow), sds((8, CH))],
-        [pltpu.VMEM((PIX+16, CH), f32), pltpu.VMEM((PIX+2*SIDE, 3*CH), narrow), pltpu.VMEM((CH, PIX), narrow),
+        [pltpu.VMEM((PIX+2*SIDE, 3*CH), narrow), pltpu.VMEM((CH, PIX), narrow),
          pltpu.VMEM((PIX, CH), f32), pltpu.VMEM((2*TAPS//TILE, TILE, CH), narrow),
-         pltpu.SemaphoreType.DMA((2,))]+rows[0].scratch()+rows[1].scratch(), 2*4*PIX*TAPS*CH, away=(4, 6), away_out=(1,), alias={6: 1})
+         pltpu.SemaphoreType.DMA((2,))]+rows[0].scratch()+rows[1].scratch(), 2*4*PIX*TAPS*CH, away=(4, 6), away_out=(1,), alias={6: 1}, room=39)
 
 PHASES = [(0, 0), (0, 1), (1, 0), (1, 1)]
 OFFSETS = [(dy, dx) for dy in (-1, 0, 1) for dx in (-1, 0, 1)]
@@ -428,7 +411,7 @@
     return call(functools.partial(stem_down_kernel, rows), [noisy, stem_w, stem_b, pieces],
         [sds((4, PIX, C0), narrow), sds((PIX, CH)), sds((9*C0, CH), narrow)],
         [pltpu.VMEM((PIX+16, C0), f32), pltpu.VMEM((6, PIX+SIDE, C0), narrow), pltpu.VMEM((DOWN_TILES*TILE, CH), f32)]+rows.scratch(),
-        2*PIX*9*C0*CH, away=(3,))
+        2*PIX*9*C0*CH, away=(3,), room=39)
 
 def down_stem_back_kernel(n, me_ref, grad_ref, skip_ref, more_ref, dw_ref, noisy_ref, head_ref, attn_ref, s1_ref, s0_ref,
                           large_in_ref, large_ref, small_ref,
@@ -495,7 +478,7 @@
         [sds(large.shape, narrow), sds((SMALL_MOVED+4*n, CH))],
         [pltpu.VMEM((PIX+16, CH), f32), pltpu.VMEM((2, PIX+SIDE, CH), narrow), pltpu.VMEM((9*C0+TILE, CH), f32),
          pltpu.VMEM((9*C0//TILE+1, TILE, CH), narrow), pltpu.SemaphoreType.DMA((1,))],
-        2*2*PIX*9*C0*CH, away=(10,), away_out=(0,), alias={10: 0}, scalar=(0,))
+        2*2*PIX*9*C0*CH, away=(10,), away_out=(0,), alias={10: 0}, scalar=(0,), room=39)
 
 HEAD_PER = (C0+CH)//GROUPS
 def silu_slope(v):
@@ -527,16 +510,18 @@
     tot_u, tot_s = exact_nt(tot, mu), exact_nt(tot, ms)
     mean_u, inv_u = tot_u[0:1], lax.rsqrt(tot_u[1:2]-tot_u[0:1]*tot_u[0:1]+1e-05)
     mean_s, inv_s = tot_s[0:1], lax.rsqrt(tot_s[1:2]-tot_s[0:1]*tot_s[0:1]+1e-05)
+    factor_u, term_u = inv_u*gain_u, shift_u-mean_u*inv_u*gain_u
+    factor_s, term_s = inv_s*gain_s, shift_s-mean_s*inv_s*gain_s
     def act_u(i, _):
         r = pl.ds(i*EL, EL)
-        v = (state_ref[r, :]-mean_u)*inv_u*gain_u+shift_u
+        v = state_ref[r, :]*factor_u+term_u
         up_ref[r, :] = (v*sigmoid(v)).astype(narrow)
         return _
     steps(PIX//EL, act_u, 0)
     for k in range(4):
         def act_s(i, _):
             r = pl.ds(i*EL, EL)
-            v = (skip_ref[k, r, :].astype(f32)-mean_s)*inv_s*gain_s+shift_s
+            v = skip_ref[k, r, :].astype(f32)*factor_s+term_s
             side_ref[k, r, :] = (v*sigmoid(v)).astype(narrow)
             return _
         steps(PIX//EL, act_s, 0)
@@ -582,8 +567,9 @@
         part = dot(nine.astype(narrow), side_ref[k])
         gs_total = part if gs_total is None else gs_total+part
         d = dot(jnp.transpose(nine).astype(narrow), ws_ref[...])
-        n = (skip_ref[k].astype(f32)-mean_s)*inv_s
-        d = d*silu_slope(n*gain_s+shift_s)
+        x = skip_ref[k].astype(f32)
+        n = x*inv_s-mean_s*inv_s
+        d = d*silu_slope(x*factor_s+term_s)
         skip_grad_ref[k] = d
         d1, d2 = d1+fold(d), d2+fold(d*n)
     tail_ref[72:112, :] = jnp.concatenate(
@@ -601,17 +587,17 @@
     tail_ref[112:120, :] = rows_of(e2, e1, jnp.concatenate([d2, d1], axis=1), bias_grad)
     tot = (exact(rows_of(e1*gain_u, e2*gain_u), mu)+exact(rows_of(d1*gain_s, d2*gain_s), ms))/amount
     tot_u, tot_s = exact_nt(tot, mu), exact_nt(tot, ms)
+    second_u, second_s = 4.0*tot_u[1:2]*inv_u*inv_u, tot_s[1:2]*inv_s*inv_s
+    by_term_u, by_term_s = second_u*mean_u-4.0*tot_u[0:1]*inv_u, second_s*mean_s-tot_s[0:1]*inv_s
     def back_u(i, _):
         r = pl.ds(i*EL, EL)
-        n = (state_ref[r, :]-mean_u)*inv_u
-        state_grad_ref[r, :] = (state_grad_ref[r, :]*gain_u-4.0*tot_u[0:1]-4.0*n*tot_u[1:2])*inv_u
+        state_grad_ref[r, :] = state_grad_ref[r, :]*factor_u-state_ref[r, :]*second_u+by_term_u
         return _
     steps(PIX//EL, back_u, 0)
     for k in range(4):
         def back_s(i, _):
             r = pl.ds(i*EL, EL)
-            n = (skip_ref[k, r, :].astype(f32)-mean_s)*inv_s
-            skip_grad_ref[k, r, :] = (skip_grad_ref[k, r, :]*gain_s-tot_s[0:1]-n*tot_s[1:2])*inv_s
+            skip_grad_ref[k, r, :] = skip_grad_ref[k, r, :]*factor_s-skip_ref[k, r, :].astype(f32)*second_s+by_term_s
             return _
         steps(PIX//EL, back_s, 0)
 
@@ -622,7 +608,7 @@
     return pl.pallas_call(head_kernel, out_shape=outs,
         in_specs=[pl.BlockSpec(memory_space=pltpu.SMEM)]+[spec]*(len(ins)-1), out_specs=[spec]*len(outs),
         scratch_shapes=[pltpu.VMEM((PIX, CH), narrow), pltpu.VMEM((4, PIX, C0), narrow), pltpu.VMEM((4, 128, PIX), f32)],
-        compiler_params=pltpu.CompilerParams(vmem_limit_bytes=LIMIT),
+        compiler_params=pltpu.CompilerParams(vmem_limit_bytes=26*MIB),
         cost_estimate=pl.CostEstimate(flops=4*2*PIX*128*(4*C0+CH), bytes_accessed=12*2**20, transcendentals=0))(*ins)
 
 HP = 128
@@ -670,9 +656,10 @@
     z = jnp.zeros((8, CH), f32)
     mean, inv = norm_stats(*steps(PIX//EL, sums, (z, z)), member, PIX*(CH//GROUPS))
     stat_ref[...] = rows_of(mean, inv)
+    factor, term = inv*gain, shift-mean*inv*gain
     def project(i, _):
         r = pl.ds(i*256, 256)
-        n = ((state_ref[r, :]-mean)*inv*gain+shift).astype(narrow)
+        n = (state_ref[r, :]*factor+term).astype(narrow)
         qkv_ref[r, :] = (dot(n, wp_ref[...])+bp_ref[...]).astype(narrow)
         return _
     steps(PIX//256, project, 0)
@@ -701,7 +688,7 @@
          sds((CH, 3*QW), narrow), sds((QW, CH), narrow), sds((8, CH))],
         [pltpu.VMEM((PIX, QW), narrow), pltpu.VMEM((HP, PIX), narrow), pltpu.VMEM((1, 3*QW), f32),
          pltpu.VMEM((3, ATTN_TILES*TILE, 128), f32)]+rows.scratch(),
-        2*PIX*(CH*4*QW+2*PIX*QW), away=(1,))
+        2*PIX*(CH*4*QW+2*PIX*QW), away=(1,), room=39)
 
 def attention_back_kernel(grad_ref, state_ref, stat_ref, qkv_ref, log_ref, mixed_t_ref, wp_ref, wo_ref, vec_ref,
                           out_ref, large_ref, small_ref, dm_ref, pg_ref, kt_ref, dv_ref, dk_ref, nt_ref, keep_ref,
@@ -747,8 +734,9 @@
             pg_ref[c:c+QC, q0:q0+HP] = jnp.transpose(dq*SCALE).astype(narrow)
         pg_ref[:, k0:k0+HP] = (dk_ref[...]*SCALE).astype(narrow)
         pg_ref[:, v0:v0+HP] = dv_ref[...].astype(narrow)
+    factor, term = inv*gain, shift-mean*inv*gain
     for r in range(0, PIX, 256):
-        nt_ref[:, r:r+256] = jnp.transpose((state_ref[r:r+256, :]-mean)*inv*gain+shift).astype(narrow)
+        nt_ref[:, r:r+256] = jnp.transpose(state_ref[r:r+256, :]*factor+term).astype(narrow)
     for j in range(3):
         third = dot(nt_ref[...], pg_ref[:, j*QW:(j+1)*QW])
         third = jnp.concatenate([third[:, h*HP:h*HP+HEAD_DIM] for h in range(HEADS)], axis=1)
@@ -762,17 +750,17 @@
     def norm_grad(i, c):
         r = pl.ds(i*256, 256)
         d = dot_nt(pg_ref[r, :], wp_ref[...])
-        n = (state_ref[r, :]-mean)*inv
+        n = state_ref[r, :]*inv-mean*inv
         out_ref[r, :] = d
         return c[0]+fold(d), c[1]+fold(d*n), c[2]+fold(pg_ref[r, :].astype(f32))
     shift_grad, gain_grad, bias_grad = (one(v) for v in steps(PIX//256, norm_grad, (z, z, zb)))
     compact = [jnp.concatenate([bias_grad[:, j*QW+h*HP:j*QW+h*HP+HEAD_DIM] for h in range(HEADS)], axis=1) for j in (0, 2)]
     tot = group_totals(rows_of(shift_grad*gain, gain_grad*gain), member)/(PIX*(CH//GROUPS))
-    first, second = tot[0:1], tot[1:2]
+    second = tot[1:2]*inv*inv
+    by_term = second*mean-tot[0:1]*inv
     def finish(i, _):
         r = pl.ds(i*EL, EL)
-        n = (state_ref[r, :]-mean)*inv
-        out_ref[r, :] = grad_ref[r, :]+(out_ref[r, :]*gain-first-n*second)*inv
+        out_ref[r, :] = grad_ref[r, :]+(out_ref[r, :]*factor-state_ref[r, :]*second+by_term)
         return _
     steps(PIX//EL, finish, 0)
     small_ref[...] = rows_of(gain_grad, shift_grad, compact[0], compact[1], one(proj_bias))
@@ -784,7 +772,7 @@
         [pltpu.VMEM((PIX, QW), narrow), pltpu.VMEM((PIX, 3*QW), narrow), pltpu.VMEM((HP, PIX), narrow), pltpu.VMEM((PIX, HP), f32),
          pltpu.VMEM((PIX, HP), f32), pltpu.VMEM((CH, PIX), narrow), pltpu.VMEM((PIX, CH), narrow),
          pltpu.VMEM((3, ATTN_TILES*TILE, 128), f32), pltpu.VMEM((ATTN_TILES, TILE, CH), narrow), pltpu.SemaphoreType.DMA((1,))],
-        2*PIX*(CH*8*QW+5*PIX*QW), away_out=(1,))
+        2*PIX*(CH*8*QW+5*PIX*QW), away_out=(1,), room=39)
 
 
 def to_phases(v):
@@ -862,7 +850,7 @@
         in_specs=[pl.BlockSpec(memory_space=pltpu.SMEM), pl.BlockSpec(memory_space=pl.ANY)],
         out_specs=pl.BlockSpec(memory_space=VM),
         scratch_shapes=[pltpu.SemaphoreType.DMA((count,))],
-        compiler_params=pltpu.CompilerParams(vmem_limit_bytes=LIMIT),
+        compiler_params=pltpu.CompilerParams(vmem_limit_bytes=39*MIB),
         cost_estimate=pl.CostEstimate(flops=0, bytes_accessed=1024, transcendentals=0),
     )(starts, large)
 
@@ -917,7 +905,7 @@
             in_specs=[pl.BlockSpec(memory_space=pltpu.SMEM), pl.BlockSpec(memory_space=pl.ANY), pl.BlockSpec(memory_space=VM)],
             out_specs=[pl.BlockSpec(memory_space=VM)]*len(outs),
             scratch_shapes=[pltpu.VMEM((len(coords), size, TILE, WIDE), narrow), pltpu.SemaphoreType.DMA((len(coords),))],
-            compiler_params=pltpu.CompilerParams(vmem_limit_bytes=LIMIT),
+            compiler_params=pltpu.CompilerParams(vmem_limit_bytes=39*MIB),
             cost_estimate=pl.CostEstimate(flops=0, bytes_accessed=1024, transcendentals=0),
         )(own_starts+bounds[part], large, arrived[part])
         own_starts = hold_for(own_starts, out)
@@ -1049,7 +1037,7 @@
         out_specs=[spec]*7,
         scratch_shapes=[pltpu.VMEM((3, TIME_TILES*TILE, 128), f32), pltpu.VMEM((3, EMB_TILES*TILE, 128), f32)]
         + rows[0].scratch()+rows[1].scratch(),
-        compiler_params=pltpu.CompilerParams(vmem_limit_bytes=LIMIT),
+        compiler_params=pltpu.CompilerParams(vmem_limit_bytes=39*MIB),
         cost_estimate=pl.CostEstimate(flops=2**27, bytes_accessed=8*2**20, transcendentals=0),
     )(place.me().reshape(1), sinus, pieces)
 
@@ -1149,7 +1137,7 @@
         out_specs=spec,
         scratch_shapes=[pltpu.VMEM((groups, lengths[0], 128), f32), pltpu.VMEM((groups, lengths[1], 128), f32),
                         pltpu.VMEM((3, 2*half_rows, 128), f32), pltpu.VMEM((3, 2*half_rows, 128), f32)],
-        compiler_params=pltpu.CompilerParams(vmem_limit_bytes=LIMIT),
+        compiler_params=pltpu.CompilerParams(vmem_limit_bytes=26*MIB),
         cost_estimate=pl.CostEstimate(flops=0, bytes_accessed=1024, transcendentals=0),
     )(place.me().reshape(1), small, sinus, hidden_pre, hidden, outer_pre, embed, w2, we, spots)
 

time: 491 us -> 475 us (0.967)
  Pallas kernels: 196 us -> 156 us
  local copies, waits for them, and re-layouts: 41.4 us -> 65.4 us
  waiting for transfers between devices: 160 us -> 166 us
    unnamed x34 -> x90, local copies, waits for them, and re-layouts: 4.77 us -> 31.4 us
    pallas_call x8, Pallas kernels: 139 us -> 114 us  [call(): pl.pallas_call(kernel, out_shape=outs, in_specs=places, out_specs=[pl.Blo...]
    pallas_call x1, Pallas kernels: 15.3 us -> 10.4 us  [head(): pl.pallas_call(head_kernel, out_shape=outs, in_specs=[pl.BlockSpec(memory...]
  transfers between devices with their start and end apart: 34 -> 34, of which waited for: 19 -> 19; matrix products, arithmetic and copies ran while one was open for 8% -> 7% of each run, Pallas kernels for 6% -> 5%
where the time goes in v5:
time: 475 us; the launch traced here: 468 us
  waiting for transfers between devices  166 us (35%)
  Pallas kernels  156 us (33%)
  local copies, waits for them, and re-layouts  65.4 us (14%)
  starting transfers between devices  41.2 us (9%)
  between operations  20.5 us (4%)
  other arithmetic  19.4 us (4%)
    pallas_call x8, Pallas kernels, call(): pl.pallas_call(kernel, out_shape=outs, in_specs=places, out_specs=[pl.Blo...  114 us
    all_gather x1, waiting for transfers between devices, step(): lax.all_gather(piece.reshape(place.block, TILE, WIDE), ('y', 'c', 'z', 'x...  74.4 us
    ppermute x14, waiting for transfers between devices, add_over(): lax.ppermute(value, axis, [(i, i ^ step) for i in range(size)])  49.5 us
    ppermute x18, waiting for transfers between devices, turn(): lax.ppermute(value, axis, [(i, (i + distance) % size) for i in range(size)])  36.4 us
    unnamed x90, local copies, waits for them, and re-layouts  31.4 us
    ppermute x18, starting transfers between devices, turn(): lax.ppermute(value, axis, [(i, (i + distance) % size) for i in range(size)])  21.2 us
    ppermute x14, starting transfers between devices, add_over(): lax.ppermute(value, axis, [(i, i ^ step) for i in range(size)])  12.8 us
    pallas_call x2, Pallas kernels, share_out(): pl.pallas_call(functools.partial(merge_kernel, coords, sends, len(coords)...  10.6 us
  transfers between devices with their start and end apart: 34, of which 19 were waited for; matrix products, arithmetic and copies ran while one was open for 7% of the time, Pallas kernels for 5%

profile of v5, /device:TPU:0, one launch (start us, length us, event | category | flops | bytes accessed | tf_op | source)
XLA Modules:
  0.0 468.3 jit_solution(16003239298090500013)
XLA Ops:
  13.2 7.3 %all-to-all-start = ((f32[8,1,3584]{2,1,0:T(1,128)}), f32[8,1,3584]{2,1,0:T(1,128)S(1)}, u32[]{:S(2)}, u32[]{:S(2)}) async-start(f32[8,1,3584]{2,1,0:T(1,128)} %reshape.170), calls=%async_computation | async-start | bytes 229376 | tf_op jit(solution)/shard_map/all_to_all | solution.py:1156
  21.9 5.9 %all-to-all-done = f32[8,1,3584]{2,1,0:T(1,128)S(1)} async-done(((f32[8,1,3584]{2,1,0:T(1,128)}), f32[8,1,3584]{2,1,0:T(1,128)S(1)}, u32[]{:S(2)}, u32[]{:S(2)}) %all-to-all-start) | async-done | bytes 114720 | tf_op jit(solution)/shard_map/all_to_all | solution.py:1156
  38.2 4.9 %mul.432 = f32[3,32,2,32,2]{4,3,2,1,0:T(8,128)} reshape(f32[1,3,8,8,64]{4,3,2,1,0:T(8,128)S(1)} %copy.51) | data formatting | bytes 98304 | tf_op jit(solution)/shard_map/mul | solution.py:1168
  43.1 4.9 %slice.141 = f32[3,32,2,32,2]{4,3,2,1,0:T(8,128)} reshape(f32[1,3,8,8,64]{4,3,2,1,0:T(8,128)S(1)} %copy.52) | data formatting | bytes 98304 | tf_op jit(solution)/shard_map/slice | solution.py:1160
  59.9 74.4 %all-gather.2.cloned.1.call-done = bf16[32,45,16,384]{3,2,1,0:T(8,128)(2,1)} async-done(((bf16[1,45,16,384]{3,2,1,0:T(8,128)(2,1)}), bf16[32,45,16,384]{3,2,1,0:T(8,128)(2,1)}) %all-gather.2.cloned.1.call-update) | async-done | bytes 17694736 | tf_op jit(solution)/shard_map/all_gather | solution.py:1153
  154.7 13.1 %shard_map.154 = (f32[1024,384]{1,0:T(8,128)S(1)}, f32[1024,384]{1,0:T(8,128)S(1)}, f32[8,384]{1,0:T(8,128)S(1)}) custom-call(f32[1024,384]{1,0:T(8,128)S(1)} %get-tuple-element.62.state_ref, bf16[32,720,384]{2,1,0:T(8,128)(2,1)} %bitcast.157, f32[8,384]{1,0:T(8,128)S(1)} %get-tuple-element.135.vec_ref), custom_call_target="tpu_custom_call" | custom-call | flops 5435817984 | bytes 22437888 | tf_op jit(solution)/shard_map/pallas_call | solution.py:100
  169.0 13.2 %shard_map.155 = (f32[1024,384]{1,0:T(8,128)S(1)}, f32[1024,384]{1,0:T(8,128)S(1)}, f32[8,384]{1,0:T(8,128)S(1)}) custom-call(f32[1024,384]{1,0:T(8,128)S(1)} %get-tuple-element.64.state_ref, bf16[32,720,384]{2,1,0:T(8,128)(2,1)} %bitcast.158, f32[8,384]{1,0:T(8,128)S(1)} %get-tuple-element.134.vec_ref), custom_call_target="tpu_custom_call" | custom-call | flops 5435817984 | bytes 22437888 | tf_op jit(solution)/shard_map/pallas_call | solution.py:100
  183.4 16.0 %shard_map.156 = (f32[1024,384]{1,0:T(8,128)S(1)}, bf16[1024,1536]{1,0:T(8,128)(2,1)S(1)}, f32[8,1024]{1,0:T(8,128)S(1)}, bf16[512,1024]{1,0:T(8,128)(2,1)S(1)},...) custom-call(f32[1024,384]{1,0:T(8,128)S(1)} %get-tuple-element.65.st, ...), custom_call_target="tpu_custom_call" | custom-call | flops 3758096384 | bytes 26664960 | tf_op jit(solution)/shard_map/pallas_call | solution.py:100
  212.3 10.4 %shard_map.157 = (f32[1024,384]{1,0:T(8,128)S(1)}, f32[4,1024,192]{2,1,0:T(8,128)S(1)}, f32[120,384]{1,0:T(8,128)S(1)}, f32[8,128]{1,0:T(8,128)S(1)}) custom-call(f32[4]{0:T(128)S(1)} %pad_maximum_fusion.5.num_ref, f32[1024,384]{1,0:T(8,128)S(1)} %copy-done.21, bf16[4,1024,192]{2,1,0:T(8,128)(2,1)S(1)} %copy-done.7, bf16[128,384]{1,0:T(8,128)(2,1)S(1)} %pad.44.wu_ref, ...), custom_call_target="tpu_custom_call" | custom-call | flops 1207959552 | bytes 12582912 | tf_op jit(solution)/shard_map/pallas_call | solution.py:608
  224.6 18.4 %shard_map.158 = (f32[1024,384]{1,0:T(8,128)S(1)}, bf16[1392,16,384]{2,1,0:T(8,128)(2,1)}, f32[8,384]{1,0:T(8,128)S(1)}) custom-call(f32[1024,384]{1,0:T(8,128)S(1)} %get-tuple-element.68.grad_ref, f32[1024,384]{1,0:T(8,128)S(1)} %copy-done.10, f32[8,384]{1,0:T(8,128)S(1)} %get-tuple-element.69.stat_ref, bf16[1024,1536]{1,0:T(8,128)(2,1)S(1)} %copy-done.17, ...), custom_call_target="tpu_custom_call" | custom-call | flops 8589934592 | bytes 27660288 | tf_op jit(solution)/shard_map/pallas_call | solution.py:100
  243.0 20.3 %shard_map.159 = (f32[1024,384]{1,0:T(8,128)S(1)}, bf16[1392,16,384]{2,1,0:T(8,128)(2,1)}, f32[8,384]{1,0:T(8,128)S(1)}) custom-call(f32[1024,384]{1,0:T(8,128)S(1)} %get-tuple-element.76.grad_ref, f32[1024,384]{1,0:T(8,128)S(1)} %copy-done.33, f32[1024,384]{1,0:T(8,128)S(1)} %copy-done.35, ...), custom_call_target="tpu_custom_call", output_to_operand_aliasing={{1}: (6, {})} | custom-call | flops 10871635968 | bytes 58232832 | tf_op jit(solution)/shard_map/pallas_call | solution.py:100
  263.4 20.3 %shard_map.160 = (f32[1024,384]{1,0:T(8,128)S(1)}, bf16[1392,16,384]{2,1,0:T(8,128)(2,1)}, f32[8,384]{1,0:T(8,128)S(1)}) custom-call(f32[1024,384]{1,0:T(8,128)S(1)} %get-tuple-element.80.grad_ref, f32[1024,384]{1,0:T(8,128)S(1)} %copy-done.19, f32[1024,384]{1,0:T(8,128)S(1)} %copy-done.31, ...), custom_call_target="tpu_custom_call", output_to_operand_aliasing={{1}: (6, {})} | custom-call | flops 10871635968 | bytes 58232832 | tf_op jit(solution)/shard_map/pallas_call | solution.py:100
  283.7 7.7 %shard_map.161 = (bf16[1392,16,384]{2,1,0:T(8,128)(2,1)}, f32[320,384]{1,0:T(8,128)S(1)}) custom-call(s32[1]{0:T(128)} %bitcast.16.me_ref, f32[1024,384]{1,0:T(8,128)S(1)} %get-tuple-element.84.grad_ref, bf16[4,1024,192]{2,1,0:T(8,128)(2,1)S(1)} %copy-done.8, f32[4,1024,192]{2,1,0:T(8,128)S(1)} %get-tuple-element.85.more_ref, ...), custom_call_target="tpu_custom_call", output_to_operand_aliasing={{0}: (10, {})} | custom-call | flops 2717908992 | bytes 42672132 | tf_op jit(solution)/shard_map/pallas_call | solution.py:100
  294.1 4.9 %shard_map.162 = bf16[16,22,16,384]{3,2,1,0:T(8,128)(2,1)} custom-call(s32[16]{0:T(128)S(1)} %stack.189.starts_ref, bf16[1392,16,384]{2,1,0:T(8,128)(2,1)} %get-tuple-element.92.large_ref), custom_call_target="tpu_custom_call" | custom-call | bytes 1024 | tf_op jit(solution)/shard_map/pallas_call | solution.py:847
  299.3 5.0 %shard_map.164 = bf16[16,23,16,384]{3,2,1,0:T(8,128)(2,1)} custom-call(s32[16]{0:T(128)S(1)} %broadcast_add_fusion.starts_ref, bf16[1392,16,384]{2,1,0:T(8,128)(2,1)} %get-tuple-element.92.large_ref), custom_call_target="tpu_custom_call" | custom-call | bytes 1024 | tf_op jit(solution)/shard_map/pallas_call | solution.py:847
  306.7 5.9 %shard_map.163 = (f32[4,22,16,384]{3,2,1,0:T(8,128)S(1)}, bf16[4,22,16,384]{3,2,1,0:T(8,128)(2,1)}, f32[4,22,16,384]{3,2,1,0:T(8,128)S(1)}, bf16[4,22,16,384]{3,2,1,0:T(8,128)(2,1)}) custom-call(s32[16]{0:T(128)S(1)} %stack.159.starts_ref, bf16[1392,16,384]{2,1,0:T(8,128)(2,1)} %get-tuple-element.92.large_ref, ...), custom_call_target="tpu_custom_call" | custom-call | bytes 1024 | tf_op jit(solution)/shard_map/pallas_call | solution.py:902
  327.4 7.3 %collective-permute-done.22 = f32[160,384]{1,0:T(8,128)S(1)} collective-permute-done((f32[160,384]{1,0:T(8,128)S(1)}, f32[160,384]{1,0:T(8,128)S(1)}, u32[]{:S(2)}, u32[]{:S(2)}) %collective-permute-start.22) | collective-permute-done | bytes 245792 | tf_op jit(solution)/shard_map/ppermute | solution.py:832
  338.9 8.6 %collective-permute-done.23 = f32[160,384]{1,0:T(8,128)S(1)} collective-permute-done((f32[160,384]{1,0:T(8,128)S(1)}, f32[160,384]{1,0:T(8,128)S(1)}, u32[]{:S(2)}, u32[]{:S(2)}) %collective-permute-start.23) | collective-permute-done | bytes 245792 | tf_op jit(solution)/shard_map/ppermute | solution.py:832
  353.3 13.1 %collective-permute-done.15 = bf16[4,23,16,384]{3,2,1,0:T(8,128)(2,1)S(1)} collective-permute-done((bf16[4,23,16,384]{3,2,1,0:T(8,128)(2,1)}, bf16[4,23,16,384]{3,2,1,0:T(8,128)(2,1)S(1)}, u32[]{:S(2)}, u32[]{:S(2)}) %collective-permute-start.15) | collective-permute-done | bytes 1130528 | tf_op jit(solution)/shard_map/ppermute | solution.py:817
  372.1 12.7 %collective-permute-done.24 = f32[160,384]{1,0:T(8,128)S(1)} collective-permute-done((f32[160,384]{1,0:T(8,128)S(1)}, f32[160,384]{1,0:T(8,128)S(1)}, u32[]{:S(2)}, u32[]{:S(2)}) %collective-permute-start.24) | collective-permute-done | bytes 245792 | tf_op jit(solution)/shard_map/ppermute | solution.py:832
  387.6 7.2 %collective-permute-done.25 = f32[160,384]{1,0:T(8,128)S(1)} collective-permute-done((f32[160,384]{1,0:T(8,128)S(1)}, f32[160,384]{1,0:T(8,128)S(1)}, u32[]{:S(2)}, u32[]{:S(2)}) %collective-permute-start.25) | collective-permute-done | bytes 245792 | tf_op jit(solution)/shard_map/ppermute | solution.py:832
  399.2 6.7 %collective-permute-start.20 = (bf16[23,16,384]{2,1,0:T(8,128)(2,1)S(1)}, bf16[23,16,384]{2,1,0:T(8,128)(2,1)S(1)}, u32[]{:S(2)}, u32[]{:S(2)}) collective-permute-start(bf16[23,16,384]{2,1,0:T(8,128)(2,1)S(1)} %get-tuple-element.122), channel_id=1, source_target_pairs={{0,4},{2,6},{4,0},{6,2},{1,5},{3,7},{5,1},{7,3},{8,12},{10,14},{12... | collective-permute-start | bytes 847880 | tf_op jit(solution)/shard_map/ppermute | solution.py:817
  405.8 15.5 %collective-permute-done.13 = bf16[22,16,384]{2,1,0:T(8,128)(2,1)S(1)} collective-permute-done((bf16[22,16,384]{2,1,0:T(8,128)(2,1)S(1)}, bf16[22,16,384]{2,1,0:T(8,128)(2,1)S(1)}, u32[]{:S(2)}, u32[]{:S(2)}) %collective-permute-start.13) | collective-permute-done | bytes 270368 | tf_op jit(solution)/shard_map/ppermute | solution.py:817
  422.7 7.2 %shard_map.166 = f32[694,384]{1,0:T(8,128)S(1)} custom-call(s32[1]{0:T(128)} %bitcast.16.me_ref, f32[320,384]{1,0:T(8,128)S(1)} %pad_maximum_fusion.1.small_ref, bf16[32,192]{1,0:T(8,128)(2,1)S(1)} %pad_maximum_fusion.3.sinus_ref, f32[32,768]{1,0:T(8,128)S(1)} %get-tuple-element.109.hidden_pre_ref, bf16[32,768]{1,0:T(8,128)(2,1)S(1)} %get-tuple-element.110.hidden_ref, ...), custom_call_target="tpu_custom_call" | custom-call | bytes 1024 | tf_op jit(solution)/shard_map/pallas_call | solution.py:1133
  (267 shorter events, 137.1 us)
Async XLA Ops:
  7.2 127.1 %all-gather.2.cloned.1.call-start = ((), (), s32[]{:S(2)}) async-start(), calls=%async_computation.1 | async-start | bytes 18247680 | tf_op jit(solution)/shard_map/all_gather | solution.py:1153
  13.2 14.6 %all-to-all-start = ((f32[8,1,3584]{2,1,0:T(1,128)}), f32[8,1,3584]{2,1,0:T(1,128)S(1)}, u32[]{:S(2)}, u32[]{:S(2)}) async-start(f32[8,1,3584]{2,1,0:T(1,128)} %reshape.170), calls=%async_computation | async-start | bytes 229376 | tf_op jit(solution)/shard_map/all_to_all | solution.py:1156
  36.6 11.4 %collective-permute-start.2 = (f32[8,384]{1,0:T(8,128)S(1)}, f32[8,384]{1,0:T(8,128)S(1)}, u32[]{:S(2)}, u32[]{:S(2)}) collective-permute-start(f32[8,384]{1,0:T(8,128)S(1)} %fusion.45), channel_id=1, source_target_pairs={{0,16},{16,0},{1,17},{17,1},{2,18},{18,2},{3,19},{19,3},{4,20},{20... | collective-permute-start | bytes 36872 | tf_op jit(solution)/shard_map/ppermute | solution.py:832
  299.0 7.8 %collective-permute-start.6 = (bf16[16,22,16,384]{3,2,1,0:T(8,128)(2,1)}, bf16[16,22,16,384]{3,2,1,0:T(8,128)(2,1)}, u32[]{:S(2)}, u32[]{:S(2)}) collective-permute-start(bf16[16,22,16,384]{3,2,1,0:T(8,128)(2,1)} %shard_map.162), channel_id=1, source_target_pairs={{0,8},{8,0},{1,9},{9,1},{2,10},{10,2},{3,11},{11,3},{4,12},{12,4},... | collective-permute-start | bytes 12976136 | tf_op jit(solution)/shard_map/ppermute | solution.py:817
  304.3 13.0 %collective-permute-start.9 = (bf16[16,23,16,384]{3,2,1,0:T(8,128)(2,1)}, bf16[16,23,16,384]{3,2,1,0:T(8,128)(2,1)}, u32[]{:S(2)}, u32[]{:S(2)}) collective-permute-start(bf16[16,23,16,384]{3,2,1,0:T(8,128)(2,1)} %shard_map.164), channel_id=1, source_target_pairs={{0,8},{8,0},{1,9},{9,1},{2,10},{10,2},{3,11},{11,3},{4,12},{12,4},... | collective-permute-start | bytes 13565960 | tf_op jit(solution)/shard_map/ppermute | solution.py:817
  315.3 32.2 %collective-permute-start.7 = (bf16[4,22,16,384]{3,2,1,0:T(8,128)(2,1)}, bf16[4,22,16,384]{3,2,1,0:T(8,128)(2,1)}, u32[]{:S(2)}, u32[]{:S(2)}) collective-permute-start(bf16[4,22,16,384]{3,2,1,0:T(8,128)(2,1)} %get-tuple-element.96), channel_id=1, source_target_pairs={{0,16},{16,0},{1,17},{17,1},{2,18},{18,2},{3,19},{19,3},{4,20},{20... | collective-permute-start | bytes 3244040 | tf_op jit(solution)/shard_map/ppermute | solution.py:817
  316.8 30.8 %collective-permute-start.8 = (bf16[4,22,16,384]{3,2,1,0:T(8,128)(2,1)}, bf16[4,22,16,384]{3,2,1,0:T(8,128)(2,1)}, u32[]{:S(2)}, u32[]{:S(2)}) collective-permute-start(bf16[4,22,16,384]{3,2,1,0:T(8,128)(2,1)} %get-tuple-element.97), channel_id=1, source_target_pairs={{0,1},{1,0},{2,3},{3,2},{4,5},{5,4},{6,7},{7,6},{8,9},{9,8},{10,11... | collective-permute-start | bytes 3244040 | tf_op jit(solution)/shard_map/ppermute | solution.py:817
  327.2 7.5 %collective-permute-start.22 = (f32[160,384]{1,0:T(8,128)S(1)}, f32[160,384]{1,0:T(8,128)S(1)}, u32[]{:S(2)}, u32[]{:S(2)}) collective-permute-start(f32[160,384]{1,0:T(8,128)S(1)} %dynamic-slice_add_fusion), channel_id=1, source_target_pairs={{0,2},{2,0},{4,6},{6,4},{1,3},{3,1},{5,7},{7,5},{8,10},{10,8},{12,... | collective-permute-start | bytes 737288 | tf_op jit(solution)/shard_map/ppermute | solution.py:832
  334.7 12.8 %collective-permute-start.23 = (f32[160,384]{1,0:T(8,128)S(1)}, f32[160,384]{1,0:T(8,128)S(1)}, u32[]{:S(2)}, u32[]{:S(2)}) collective-permute-start(f32[160,384]{1,0:T(8,128)S(1)} %add.850), channel_id=1, source_target_pairs={{0,4},{2,6},{4,0},{6,2},{1,5},{3,7},{5,1},{7,3},{8,12},{10,14},{12... | collective-permute-start | bytes 737288 | tf_op jit(solution)/shard_map/ppermute | solution.py:832
  336.3 30.1 %collective-permute-start.15 = (bf16[4,23,16,384]{3,2,1,0:T(8,128)(2,1)}, bf16[4,23,16,384]{3,2,1,0:T(8,128)(2,1)S(1)}, u32[]{:S(2)}, u32[]{:S(2)}) collective-permute-start(bf16[4,23,16,384]{3,2,1,0:T(8,128)(2,1)} %copy-done.25), channel_id=1, source_target_pairs={{0,16},{16,0},{1,17},{17,1},{2,18},{18,2},{3,19},{19,3},{4,20},{20... | collective-permute-start | bytes 3391496 | tf_op jit(solution)/shard_map/ppermute | solution.py:817
  338.2 29.7 %collective-permute-start.18 = (bf16[4,23,16,384]{3,2,1,0:T(8,128)(2,1)}, bf16[4,23,16,384]{3,2,1,0:T(8,128)(2,1)S(1)}, u32[]{:S(2)}, u32[]{:S(2)}) collective-permute-start(bf16[4,23,16,384]{3,2,1,0:T(8,128)(2,1)} %copy-done.24), channel_id=1, source_target_pairs={{0,1},{1,0},{2,3},{3,2},{4,5},{5,4},{6,7},{7,6},{8,9},{9,8},{10,11... | collective-permute-start | bytes 3391496 | tf_op jit(solution)/shard_map/ppermute | solution.py:817
  351.1 36.0 %collective-permute-start.10 = (bf16[2,22,16,384]{3,2,1,0:T(8,128)(2,1)S(1)}, bf16[2,22,16,384]{3,2,1,0:T(8,128)(2,1)S(1)}, u32[]{:S(2)}, u32[]{:S(2)}) collective-permute-start(bf16[2,22,16,384]{3,2,1,0:T(8,128)(2,1)S(1)} %fusion.13), channel_id=1, source_target_pairs={{0,1},{1,0},{2,3},{3,2},{4,5},{5,4},{6,7},{7,6},{8,9},{9,8},{10,11... | collective-permute-start | bytes 1622024 | tf_op jit(solution)/shard_map/ppermute | solution.py:817
  352.7 32.8 %collective-permute-start.12 = (bf16[2,22,16,384]{3,2,1,0:T(8,128)(2,1)S(1)}, bf16[2,22,16,384]{3,2,1,0:T(8,128)(2,1)S(1)}, u32[]{:S(2)}, u32[]{:S(2)}) collective-permute-start(bf16[2,22,16,384]{3,2,1,0:T(8,128)(2,1)S(1)} %fusion.14), channel_id=1, source_target_pairs={{0,16},{16,0},{1,17},{17,1},{2,18},{18,2},{3,19},{19,3},{4,20},{20... | collective-permute-start | bytes 1622024 | tf_op jit(solution)/shard_map/ppermute | solution.py:817
  368.4 16.4 %collective-permute-start.24 = (f32[160,384]{1,0:T(8,128)S(1)}, f32[160,384]{1,0:T(8,128)S(1)}, u32[]{:S(2)}, u32[]{:S(2)}) collective-permute-start(f32[160,384]{1,0:T(8,128)S(1)} %add.851), channel_id=1, source_target_pairs={{0,1},{1,0},{2,3},{3,2},{4,5},{5,4},{6,7},{7,6},{8,9},{9,8},{10,11... | collective-permute-start | bytes 737288 | tf_op jit(solution)/shard_map/ppermute | solution.py:832
  370.0 25.9 %collective-permute-start.16 = (bf16[2,23,16,384]{3,2,1,0:T(8,128)(2,1)S(1)}, bf16[2,23,16,384]{3,2,1,0:T(8,128)(2,1)S(1)}, u32[]{:S(2)}, u32[]{:S(2)}) collective-permute-start(bf16[2,23,16,384]{3,2,1,0:T(8,128)(2,1)S(1)} %fusion.8), channel_id=1, source_target_pairs={{0,1},{1,0},{2,3},{3,2},{4,5},{5,4},{6,7},{7,6},{8,9},{9,8},{10,11... | collective-permute-start | bytes 1695752 | tf_op jit(solution)/shard_map/ppermute | solution.py:817
  370.7 24.4 %collective-permute-start.19 = (bf16[2,23,16,384]{3,2,1,0:T(8,128)(2,1)S(1)}, bf16[2,23,16,384]{3,2,1,0:T(8,128)(2,1)S(1)}, u32[]{:S(2)}, u32[]{:S(2)}) collective-permute-start(bf16[2,23,16,384]{3,2,1,0:T(8,128)(2,1)S(1)} %fusion.9), channel_id=1, source_target_pairs={{0,16},{16,0},{1,17},{17,1},{2,18},{18,2},{3,19},{19,3},{4,20},{20... | collective-permute-start | bytes 1695752 | tf_op jit(solution)/shard_map/ppermute | solution.py:817
  384.8 9.9 %collective-permute-start.25 = (f32[160,384]{1,0:T(8,128)S(1)}, f32[160,384]{1,0:T(8,128)S(1)}, u32[]{:S(2)}, u32[]{:S(2)}) collective-permute-start(f32[160,384]{1,0:T(8,128)S(1)} %add.852), channel_id=1, source_target_pairs={{0,16},{16,0},{1,17},{17,1},{2,18},{18,2},{3,19},{19,3},{4,20},{20... | collective-permute-start | bytes 737288 | tf_op jit(solution)/shard_map/ppermute | solution.py:832
  385.6 13.5 %collective-permute-start.14 = (bf16[22,16,384]{2,1,0:T(8,128)(2,1)S(1)}, bf16[22,16,384]{2,1,0:T(8,128)(2,1)S(1)}, u32[]{:S(2)}, u32[]{:S(2)}) collective-permute-start(bf16[22,16,384]{2,1,0:T(8,128)(2,1)S(1)} %get-tuple-element.125), channel_id=1, source_target_pairs={{0,6},{2,0},{4,2},{6,4},{1,7},{3,1},{5,3},{7,5},{8,14},{10,8},{12,... | collective-permute-start | bytes 811016 | tf_op jit(solution)/shard_map/ppermute | solution.py:817
  387.1 34.2 %collective-permute-start.13 = (bf16[22,16,384]{2,1,0:T(8,128)(2,1)S(1)}, bf16[22,16,384]{2,1,0:T(8,128)(2,1)S(1)}, u32[]{:S(2)}, u32[]{:S(2)}) collective-permute-start(bf16[22,16,384]{2,1,0:T(8,128)(2,1)S(1)} %get-tuple-element.124), channel_id=1, source_target_pairs={{0,4},{2,6},{4,0},{6,2},{1,5},{3,7},{5,1},{7,3},{8,12},{10,14},{12... | collective-permute-start | bytes 811016 | tf_op jit(solution)/shard_map/ppermute | solution.py:817
  394.7 26.6 %collective-permute-start.11 = (bf16[22,16,384]{2,1,0:T(8,128)(2,1)S(1)}, bf16[22,16,384]{2,1,0:T(8,128)(2,1)S(1)}, u32[]{:S(2)}, u32[]{:S(2)}) collective-permute-start(bf16[22,16,384]{2,1,0:T(8,128)(2,1)S(1)} %fusion.19), channel_id=1, source_target_pairs={{0,2},{2,4},{4,6},{6,0},{1,3},{3,5},{5,7},{7,1},{8,10},{10,12},{12... | collective-permute-start | bytes 811016 | tf_op jit(solution)/shard_map/ppermute | solution.py:817
  395.0 26.4 %collective-permute-start.26 = (f32[160,384]{1,0:T(8,128)S(1)}, f32[160,384]{1,0:T(8,128)S(1)}, u32[]{:S(2)}, u32[]{:S(2)}) collective-permute-start(f32[160,384]{1,0:T(8,128)S(1)} %add.853), channel_id=1, source_target_pairs={{0,8},{8,0},{1,9},{9,1},{2,10},{10,2},{3,11},{11,3},{4,12},{12,4},... | collective-permute-start | bytes 737288 | tf_op jit(solution)/shard_map/ppermute | solution.py:817
  395.9 34.0 %collective-permute-start.21 = (bf16[23,16,384]{2,1,0:T(8,128)(2,1)S(1)}, bf16[23,16,384]{2,1,0:T(8,128)(2,1)S(1)}, u32[]{:S(2)}, u32[]{:S(2)}) collective-permute-start(bf16[23,16,384]{2,1,0:T(8,128)(2,1)S(1)} %get-tuple-element.123), channel_id=1, source_target_pairs={{0,6},{2,0},{4,2},{6,4},{1,7},{3,1},{5,3},{7,5},{8,14},{10,8},{12,... | collective-permute-start | bytes 847880 | tf_op jit(solution)/shard_map/ppermute | solution.py:817
  399.2 34.2 %collective-permute-start.20 = (bf16[23,16,384]{2,1,0:T(8,128)(2,1)S(1)}, bf16[23,16,384]{2,1,0:T(8,128)(2,1)S(1)}, u32[]{:S(2)}, u32[]{:S(2)}) collective-permute-start(bf16[23,16,384]{2,1,0:T(8,128)(2,1)S(1)} %get-tuple-element.122), channel_id=1, source_target_pairs={{0,4},{2,6},{4,0},{6,2},{1,5},{3,7},{5,1},{7,3},{8,12},{10,14},{12... | collective-permute-start | bytes 847880 | tf_op jit(solution)/shard_map/ppermute | solution.py:817
  421.3 12.1 %collective-permute-start.17 = (bf16[23,16,384]{2,1,0:T(8,128)(2,1)S(1)}, bf16[23,16,384]{2,1,0:T(8,128)(2,1)S(1)}, u32[]{:S(2)}, u32[]{:S(2)}) collective-permute-start(bf16[23,16,384]{2,1,0:T(8,128)(2,1)S(1)} %fusion.18), channel_id=1, source_target_pairs={{0,2},{2,4},{4,6},{6,0},{1,3},{3,5},{5,7},{7,1},{8,10},{10,12},{12... | collective-permute-start | bytes 847880 | tf_op jit(solution)/shard_map/ppermute | solution.py:817
  (53 other events, 313.8 us)
Sparse Core Ops, SparseCore 0:
  12.5 121.7 all-gather.1

commit v6 on v5

--- a/solution.py
+++ b/solution.py
@@ -486,12 +486,43 @@
     return s*(1.0+v*(1.0-s))
 
 KL = 0.001
-def head_kernel(num_ref, state_ref, skip_ref, wu_ref, ws_ref, vu_ref, vs_ref, bias_ref, noise_ref, mask_ref,
+HEAD_FIRST = (ROW["head_gain"]+LEAD)//TILE
+HEAD_TILES = -(-(ROW["head_b"]+1+LEAD)//TILE)-HEAD_FIRST
+HEAD_AT = ROW["head_gain"]+LEAD-HEAD_FIRST*TILE
+
+def head_weights(low, wu_ref, ws_ref):
+    count = HEAD_TILES*TILE
+    blocks = []
+    for o in range(OUT_CH):
+        lane = lax.broadcasted_iota(jnp.int32, (64, CH), 1)
+        take = (lane == 6*lax.broadcasted_iota(jnp.int32, (64, CH), 0)+o).astype(f32).astype(narrow)
+        blocks.append(dot_nt(low, take).astype(narrow))
+    blocks = jnp.concatenate(blocks, axis=0)
+    row = lax.broadcasted_iota(jnp.int32, (128, OUT_CH*count), 0)
+    column = lax.broadcasted_iota(jnp.int32, (128, OUT_CH*count), 1)
+    valid = (row % 8 < OUT_CH) & (row < 72)
+    made = []
+    for part in range(9):
+        put = valid & (column == (row % 8)*count+HEAD_AT+3+9*(row//8)+part)
+        made.append(dot(put.astype(f32).astype(narrow), blocks))
+    wu_ref[...] = jnp.concatenate(made[:6], axis=1).astype(narrow)
+    ws_ref[...] = jnp.concatenate(made[6:], axis=1).astype(narrow)
+
+def head_kernel(rows, num_ref, state_ref, skip_ref, pieces_ref, noise_ref, mask_ref,
                 state_grad_ref, skip_grad_ref, tail_ref, loss_ref,
-                up_ref, side_ref, q_ref):
+                up_ref, side_ref, q_ref, wu_ref, ws_ref, *held):
+    rows.start(pieces_ref, *held)
+    rows.finish(pieces_ref, *held)
     log_beta, log_tilde, coefficient, sample = (num_ref[i] for i in range(4))
-    gain_u, shift_u = vu_ref[0:1, :], vu_ref[1:2, :]
-    gain_s, shift_s = vs_ref[0:1, :], vs_ref[1:2, :]
+    low = held[0][...]
+    head_weights(low, wu_ref, ws_ref)
+    wide = low.astype(f32)
+    line = lambda i: wide[HEAD_AT+i:HEAD_AT+i+1, :]
+    gain_u, gain_s = line(0), line(1)[:, :C0]
+    shift_u, shift_s = jnp.concatenate([line(1)[:, C0:], line(2)[:, :C0]], axis=1), line(2)[:, C0:]
+    own = lax.broadcasted_iota(jnp.int32, (8, CH), 0)
+    own = (own == lax.broadcasted_iota(jnp.int32, (8, CH), 1)) & (own < OUT_CH)
+    bias = jnp.sum(jnp.where(own, jnp.broadcast_to(line(ROW["head_b"]-ROW["head_gain"]), (8, CH)), 0.0), axis=1, keepdims=True)
     mu, ms = membership(CH, HEAD_PER), membership(C0, HEAD_PER, CH)
     amount = 4*PIX*HEAD_PER
     one = lambda v: jnp.sum(v, axis=0, keepdims=True)
@@ -535,7 +566,7 @@
         for t, (dy, dx) in enumerate(OFFSETS):
             at, di, dj = source(a, b, dy, dx)
             out += shift_lanes(q_ref[at, 8*t:8*t+8, :], di, dj)
-        out += bias_ref[:, 0:1]
+        out += bias
         k = 2*a+b
         error = jnp.where(row < 3, out - noise_ref[k], 0.0)
         fraction = jnp.where(row < 3, (pltpu.roll(out, 5, 0)+1.0)/2.0, 0.0)
@@ -601,14 +632,16 @@
             return _
         steps(PIX//EL, back_s, 0)
 
-def head(numbers, state, skip, wu, ws, vu, vs, bias, noise, mask):
+def head(place, numbers, state, skip, pieces, noise, mask):
+    rows = Rows(place, HEAD_FIRST, HEAD_TILES)
     spec = pl.BlockSpec(memory_space=VM)
-    ins = [numbers, state, skip, wu, ws, vu, vs, bias, noise, mask]
+    ins = [numbers, state, skip, pieces, noise, mask]
     outs = [sds((PIX, CH)), sds((4, PIX, C0)), sds((120, CH)), sds((8, 128))]
-    return pl.pallas_call(head_kernel, out_shape=outs,
-        in_specs=[pl.BlockSpec(memory_space=pltpu.SMEM)]+[spec]*(len(ins)-1), out_specs=[spec]*len(outs),
-        scratch_shapes=[pltpu.VMEM((PIX, CH), narrow), pltpu.VMEM((4, PIX, C0), narrow), pltpu.VMEM((4, 128, PIX), f32)],
-        compiler_params=pltpu.CompilerParams(vmem_limit_bytes=26*MIB),
+    return pl.pallas_call(functools.partial(head_kernel, rows), out_shape=outs,
+        in_specs=[pl.BlockSpec(memory_space=pltpu.SMEM), spec, spec, pl.BlockSpec(memory_space=pl.ANY), spec, spec], out_specs=[spec]*len(outs),
+        scratch_shapes=[pltpu.VMEM((PIX, CH), narrow), pltpu.VMEM((4, PIX, C0), narrow), pltpu.VMEM((4, 128, PIX), f32),
+                        pltpu.VMEM((128, CH), narrow), pltpu.VMEM((128, C0), narrow)]+rows.scratch(),
+        compiler_params=pltpu.CompilerParams(vmem_limit_bytes=39*MIB),
         cost_estimate=pl.CostEstimate(flops=4*2*PIX*128*(4*C0+CH), bytes_accessed=12*2**20, transcendentals=0))(*ins)
 
 HP = 128
@@ -1198,18 +1231,9 @@
     before = state
     state, qkv, log, mixed_t, attn_stat, wp, wo, attn_vec = attention_forward(place, before, pieces)
 
-    ends = rows("head_gain", 85).reshape(-1)
-    norm_u = jnp.stack([ends[:CH], ends[C0+CH:C0+2*CH]]).astype(f32)
-    norm_s = jnp.stack([ends[CH:C0+CH], ends[C0+2*CH:2*(C0+CH)]]).astype(f32)
-    head_size = 9*(C0+CH)*OUT_CH
-    head_w = ends[2*(C0+CH):2*(C0+CH)+head_size].reshape(9, C0+CH, OUT_CH)
-    head_w = jnp.transpose(head_w, (0, 2, 1))
-    wu, ws = taps_rows(head_w[..., :CH]), taps_rows(head_w[..., CH:])
-    head_b = ends[2*(C0+CH)+head_size:2*(C0+CH)+head_size+OUT_CH].astype(f32)
-    head_b = jnp.broadcast_to(jnp.pad(head_b, (0, 8-OUT_CH))[:, None], (8, 128))
     numbers = jnp.stack([jnp.log(beta), jnp.log(tilde), beta*beta/(alpha*one_minus), sample_weight])
     grad, skip_grad, head_tail, losses = head(
-        numbers, state, skip, wu, ws, norm_u, norm_s, head_b, noise_phases, mask_phases)
+        place, numbers, state, skip, pieces, noise_phases, mask_phases)
     grad, large, attn_small = attention_back(
         grad, before, attn_stat, qkv, log, mixed_t, wp, wo, attn_vec, place.tiles)
     begin, inner, stat, base, vec = blocks[1]

time: 475 us -> 459 us (0.966)
  local copies, waits for them, and re-layouts: 65.4 us -> 49.1 us
    unnamed x90 -> x58, local copies, waits for them, and re-layouts: 31.4 us -> 22.5 us
where the time goes in v6:
time: 459 us; the launch traced here: 453 us
  waiting for transfers between devices  166 us (36%)
  Pallas kernels  157 us (34%)
  local copies, waits for them, and re-layouts  49.1 us (11%)
  starting transfers between devices  41.5 us (9%)
  between operations  20 us (4%)
  other arithmetic  19.4 us (4%)
    pallas_call x8, Pallas kernels, call(): pl.pallas_call(kernel, out_shape=outs, in_specs=places, out_specs=[pl.Blo...  113 us
    all_gather x1, waiting for transfers between devices, step(): lax.all_gather(piece.reshape(place.block, TILE, WIDE), ('y', 'c', 'z', 'x...  74.5 us
    ppermute x14, waiting for transfers between devices, add_over(): lax.ppermute(value, axis, [(i, i ^ step) for i in range(size)])  49 us
    ppermute x18, waiting for transfers between devices, turn(): lax.ppermute(value, axis, [(i, (i + distance) % size) for i in range(size)])  36.6 us
    unnamed x58, local copies, waits for them, and re-layouts  22.5 us
    ppermute x18, starting transfers between devices, turn(): lax.ppermute(value, axis, [(i, (i + distance) % size) for i in range(size)])  21.2 us
    ppermute x14, starting transfers between devices, add_over(): lax.ppermute(value, axis, [(i, i ^ step) for i in range(size)])  12.9 us
    pallas_call x1, Pallas kernels, head(): pl.pallas_call(functools.partial(head_kernel, rows), out_shape=outs, in_s...  11.9 us
  transfers between devices with their start and end apart: 34, of which 19 were waited for; matrix products, arithmetic and copies ran while one was open for 7% of the time, Pallas kernels for 5%

profile of v6, /device:TPU:0, one launch (start us, length us, event | category | flops | bytes accessed | tf_op | source)
XLA Modules:
  0.0 452.7 jit_solution(15992970704963772983)
XLA Ops:
  13.2 7.3 %all-to-all-start = ((f32[8,1,3584]{2,1,0:T(1,128)}), f32[8,1,3584]{2,1,0:T(1,128)S(1)}, u32[]{:S(2)}, u32[]{:S(2)}) async-start(f32[8,1,3584]{2,1,0:T(1,128)} %reshape.153), calls=%async_computation | async-start | bytes 229376 | tf_op jit(solution)/shard_map/all_to_all | solution.py:1189
  21.9 5.9 %all-to-all-done = f32[8,1,3584]{2,1,0:T(1,128)S(1)} async-done(((f32[8,1,3584]{2,1,0:T(1,128)}), f32[8,1,3584]{2,1,0:T(1,128)S(1)}, u32[]{:S(2)}, u32[]{:S(2)}) %all-to-all-start) | async-done | bytes 114720 | tf_op jit(solution)/shard_map/all_to_all | solution.py:1189
  38.2 4.9 %mul.432 = f32[3,32,2,32,2]{4,3,2,1,0:T(8,128)} reshape(f32[1,3,8,8,64]{4,3,2,1,0:T(8,128)S(1)} %copy.47) | data formatting | bytes 98304 | tf_op jit(solution)/shard_map/mul | solution.py:1201
  43.1 4.9 %slice.110 = f32[3,32,2,32,2]{4,3,2,1,0:T(8,128)} reshape(f32[1,3,8,8,64]{4,3,2,1,0:T(8,128)S(1)} %copy.48) | data formatting | bytes 98304 | tf_op jit(solution)/shard_map/slice | solution.py:1193
  59.8 74.5 %all-gather.2.cloned.1.call-done = bf16[32,45,16,384]{3,2,1,0:T(8,128)(2,1)} async-done(((bf16[1,45,16,384]{3,2,1,0:T(8,128)(2,1)}), bf16[32,45,16,384]{3,2,1,0:T(8,128)(2,1)}) %all-gather.2.cloned.1.call-update) | async-done | bytes 17694736 | tf_op jit(solution)/shard_map/all_gather | solution.py:1186
  143.9 12.7 %shard_map.154 = (f32[1024,384]{1,0:T(8,128)S(1)}, f32[1024,384]{1,0:T(8,128)S(1)}, f32[8,384]{1,0:T(8,128)S(1)}) custom-call(f32[1024,384]{1,0:T(8,128)S(1)} %get-tuple-element.62.state_ref, bf16[32,720,384]{2,1,0:T(8,128)(2,1)} %bitcast.147, f32[8,384]{1,0:T(8,128)S(1)} %get-tuple-element.133.vec_ref), custom_call_target="tpu_custom_call" | custom-call | flops 5435817984 | bytes 22437888 | tf_op jit(solution)/shard_map/pallas_call | solution.py:100
  156.6 13.2 %shard_map.155 = (f32[1024,384]{1,0:T(8,128)S(1)}, f32[1024,384]{1,0:T(8,128)S(1)}, f32[8,384]{1,0:T(8,128)S(1)}) custom-call(f32[1024,384]{1,0:T(8,128)S(1)} %get-tuple-element.64.state_ref, bf16[32,720,384]{2,1,0:T(8,128)(2,1)} %bitcast.148, f32[8,384]{1,0:T(8,128)S(1)} %get-tuple-element.132.vec_ref), custom_call_target="tpu_custom_call" | custom-call | flops 5435817984 | bytes 22437888 | tf_op jit(solution)/shard_map/pallas_call | solution.py:100
  171.0 16.0 %shard_map.156 = (f32[1024,384]{1,0:T(8,128)S(1)}, bf16[1024,1536]{1,0:T(8,128)(2,1)S(1)}, f32[8,1024]{1,0:T(8,128)S(1)}, bf16[512,1024]{1,0:T(8,128)(2,1)S(1)},...) custom-call(f32[1024,384]{1,0:T(8,128)S(1)} %get-tuple-element.65.st, ...), custom_call_target="tpu_custom_call" | custom-call | flops 3758096384 | bytes 26664960 | tf_op jit(solution)/shard_map/pallas_call | solution.py:100
  188.7 11.9 %shard_map.157 = (f32[1024,384]{1,0:T(8,128)S(1)}, f32[4,1024,192]{2,1,0:T(8,128)S(1)}, f32[120,384]{1,0:T(8,128)S(1)}, f32[8,128]{1,0:T(8,128)S(1)}) custom-call(f32[4]{0:T(128)S(1)} %pad_maximum_fusion.5.num_ref, f32[1024,384]{1,0:T(8,128)S(1)} %get-tuple-element.66.state_ref, bf16[4,1024,192]{2,1,0:T(8,128)(2,1)S(1)} %get-tuple-element.67.skip_ref, ...), custom_call_target="tpu_custom_call" | custom-call | flops 1207959552 | bytes 12582912 | tf_op jit(solution)/shard_map/pallas_call | solution.py:640
  203.7 18.4 %shard_map.158 = (f32[1024,384]{1,0:T(8,128)S(1)}, bf16[1392,16,384]{2,1,0:T(8,128)(2,1)}, f32[8,384]{1,0:T(8,128)S(1)}) custom-call(f32[1024,384]{1,0:T(8,128)S(1)} %get-tuple-element.68.grad_ref, f32[1024,384]{1,0:T(8,128)S(1)} %get-tuple-element.65.state_ref, f32[8,384]{1,0:T(8,128)S(1)} %get-tuple-element.69.stat_ref, bf16[1024,1536]{1,0:T(8,128)(2,1)S(1)} %copy-done.10, ...), custom_call_target="tpu_custom_call" | custom-call | flops 8589934592 | bytes 27660288 | tf_op jit(solution)/shard_map/pallas_call | solution.py:100
  227.5 20.2 %shard_map.159 = (f32[1024,384]{1,0:T(8,128)S(1)}, bf16[1392,16,384]{2,1,0:T(8,128)(2,1)}, f32[8,384]{1,0:T(8,128)S(1)}) custom-call(f32[1024,384]{1,0:T(8,128)S(1)} %copy-done.20, f32[1024,384]{1,0:T(8,128)S(1)} %copy-done.16, f32[1024,384]{1,0:T(8,128)S(1)} %copy-done.18, ...), custom_call_target="tpu_custom_call", output_to_operand_aliasing={{1}: (6, {})} | custom-call | flops 10871635968 | bytes 58232832 | tf_op jit(solution)/shard_map/pallas_call | solution.py:100
  247.7 20.3 %shard_map.160 = (f32[1024,384]{1,0:T(8,128)S(1)}, bf16[1392,16,384]{2,1,0:T(8,128)(2,1)}, f32[8,384]{1,0:T(8,128)S(1)}) custom-call(f32[1024,384]{1,0:T(8,128)S(1)} %get-tuple-element.80.grad_ref, f32[1024,384]{1,0:T(8,128)S(1)} %get-tuple-element.62.state_ref, f32[1024,384]{1,0:T(8,128)S(1)} %get-tuple-element.81.inner_ref, ...), custom_call_target="tpu_custom_call", output_to_operand_aliasing={{1}: (6, {})} | custom-call | flops 10871635968 | bytes 58232832 | tf_op jit(solution)/shard_map/pallas_call | solution.py:100
  268.0 7.7 %shard_map.161 = (bf16[1392,16,384]{2,1,0:T(8,128)(2,1)}, f32[320,384]{1,0:T(8,128)S(1)}) custom-call(s32[1]{0:T(128)} %bitcast.16.me_ref, f32[1024,384]{1,0:T(8,128)S(1)} %get-tuple-element.84.grad_ref, bf16[4,1024,192]{2,1,0:T(8,128)(2,1)S(1)} %get-tuple-element.67.skip_ref, ...), custom_call_target="tpu_custom_call", output_to_operand_aliasing={{0}: (10, {})} | custom-call | flops 2717908992 | bytes 42672132 | tf_op jit(solution)/shard_map/pallas_call | solution.py:100
  278.5 4.9 %shard_map.162 = bf16[16,22,16,384]{3,2,1,0:T(8,128)(2,1)} custom-call(s32[16]{0:T(128)S(1)} %stack.165.starts_ref, bf16[1392,16,384]{2,1,0:T(8,128)(2,1)} %get-tuple-element.92.large_ref), custom_call_target="tpu_custom_call" | custom-call | bytes 1024 | tf_op jit(solution)/shard_map/pallas_call | solution.py:880
  283.7 5.0 %shard_map.164 = bf16[16,23,16,384]{3,2,1,0:T(8,128)(2,1)} custom-call(s32[16]{0:T(128)S(1)} %broadcast_add_fusion.starts_ref, bf16[1392,16,384]{2,1,0:T(8,128)(2,1)} %get-tuple-element.92.large_ref), custom_call_target="tpu_custom_call" | custom-call | bytes 1024 | tf_op jit(solution)/shard_map/pallas_call | solution.py:880
  291.1 5.9 %shard_map.163 = (f32[4,22,16,384]{3,2,1,0:T(8,128)S(1)}, bf16[4,22,16,384]{3,2,1,0:T(8,128)(2,1)}, f32[4,22,16,384]{3,2,1,0:T(8,128)S(1)}, bf16[4,22,16,384]{3,2,1,0:T(8,128)(2,1)}) custom-call(s32[16]{0:T(128)S(1)} %stack.141.starts_ref, bf16[1392,16,384]{2,1,0:T(8,128)(2,1)} %get-tuple-element.92.large_ref, ...), custom_call_target="tpu_custom_call" | custom-call | bytes 1024 | tf_op jit(solution)/shard_map/pallas_call | solution.py:935
  311.6 7.3 %collective-permute-done.22 = f32[160,384]{1,0:T(8,128)S(1)} collective-permute-done((f32[160,384]{1,0:T(8,128)S(1)}, f32[160,384]{1,0:T(8,128)S(1)}, u32[]{:S(2)}, u32[]{:S(2)}) %collective-permute-start.22) | collective-permute-done | bytes 245792 | tf_op jit(solution)/shard_map/ppermute | solution.py:865
  323.0 8.6 %collective-permute-done.23 = f32[160,384]{1,0:T(8,128)S(1)} collective-permute-done((f32[160,384]{1,0:T(8,128)S(1)}, f32[160,384]{1,0:T(8,128)S(1)}, u32[]{:S(2)}, u32[]{:S(2)}) %collective-permute-start.23) | collective-permute-done | bytes 245792 | tf_op jit(solution)/shard_map/ppermute | solution.py:865
  337.4 13.4 %collective-permute-done.15 = bf16[4,23,16,384]{3,2,1,0:T(8,128)(2,1)S(1)} collective-permute-done((bf16[4,23,16,384]{3,2,1,0:T(8,128)(2,1)}, bf16[4,23,16,384]{3,2,1,0:T(8,128)(2,1)S(1)}, u32[]{:S(2)}, u32[]{:S(2)}) %collective-permute-start.15) | collective-permute-done | bytes 1130528 | tf_op jit(solution)/shard_map/ppermute | solution.py:850
  356.8 12.4 %collective-permute-done.24 = f32[160,384]{1,0:T(8,128)S(1)} collective-permute-done((f32[160,384]{1,0:T(8,128)S(1)}, f32[160,384]{1,0:T(8,128)S(1)}, u32[]{:S(2)}, u32[]{:S(2)}) %collective-permute-start.24) | collective-permute-done | bytes 245792 | tf_op jit(solution)/shard_map/ppermute | solution.py:865
  372.0 7.2 %collective-permute-done.25 = f32[160,384]{1,0:T(8,128)S(1)} collective-permute-done((f32[160,384]{1,0:T(8,128)S(1)}, f32[160,384]{1,0:T(8,128)S(1)}, u32[]{:S(2)}, u32[]{:S(2)}) %collective-permute-start.25) | collective-permute-done | bytes 245792 | tf_op jit(solution)/shard_map/ppermute | solution.py:865
  383.6 6.7 %collective-permute-start.20 = (bf16[23,16,384]{2,1,0:T(8,128)(2,1)S(1)}, bf16[23,16,384]{2,1,0:T(8,128)(2,1)S(1)}, u32[]{:S(2)}, u32[]{:S(2)}) collective-permute-start(bf16[23,16,384]{2,1,0:T(8,128)(2,1)S(1)} %get-tuple-element.122), channel_id=1, source_target_pairs={{0,4},{2,6},{4,0},{6,2},{1,5},{3,7},{5,1},{7,3},{8,12},{10,14},{12... | collective-permute-start | bytes 847880 | tf_op jit(solution)/shard_map/ppermute | solution.py:850
  390.3 15.5 %collective-permute-done.13 = bf16[22,16,384]{2,1,0:T(8,128)(2,1)S(1)} collective-permute-done((bf16[22,16,384]{2,1,0:T(8,128)(2,1)S(1)}, bf16[22,16,384]{2,1,0:T(8,128)(2,1)S(1)}, u32[]{:S(2)}, u32[]{:S(2)}) %collective-permute-start.13) | collective-permute-done | bytes 270368 | tf_op jit(solution)/shard_map/ppermute | solution.py:850
  407.2 7.2 %shard_map.166 = f32[694,384]{1,0:T(8,128)S(1)} custom-call(s32[1]{0:T(128)} %bitcast.16.me_ref, f32[320,384]{1,0:T(8,128)S(1)} %pad_maximum_fusion.1.small_ref, bf16[32,192]{1,0:T(8,128)(2,1)S(1)} %pad_maximum_fusion.3.sinus_ref, f32[32,768]{1,0:T(8,128)S(1)} %get-tuple-element.109.hidden_pre_ref, bf16[32,768]{1,0:T(8,128)(2,1)S(1)} %get-tuple-element.110.hidden_ref, ...), custom_call_target="tpu_custom_call" | custom-call | bytes 1024 | tf_op jit(solution)/shard_map/pallas_call | solution.py:1166
  (214 shorter events, 120.9 us)
Async XLA Ops:
  7.2 127.2 %all-gather.2.cloned.1.call-start = ((), (), s32[]{:S(2)}) async-start(), calls=%async_computation.1 | async-start | bytes 18247680 | tf_op jit(solution)/shard_map/all_gather | solution.py:1186
  13.2 14.6 %all-to-all-start = ((f32[8,1,3584]{2,1,0:T(1,128)}), f32[8,1,3584]{2,1,0:T(1,128)S(1)}, u32[]{:S(2)}, u32[]{:S(2)}) async-start(f32[8,1,3584]{2,1,0:T(1,128)} %reshape.153), calls=%async_computation | async-start | bytes 229376 | tf_op jit(solution)/shard_map/all_to_all | solution.py:1189
  36.6 11.4 %collective-permute-start.2 = (f32[8,384]{1,0:T(8,128)S(1)}, f32[8,384]{1,0:T(8,128)S(1)}, u32[]{:S(2)}, u32[]{:S(2)}) collective-permute-start(f32[8,384]{1,0:T(8,128)S(1)} %fusion.44), channel_id=1, source_target_pairs={{0,16},{16,0},{1,17},{17,1},{2,18},{18,2},{3,19},{19,3},{4,20},{20... | collective-permute-start | bytes 36872 | tf_op jit(solution)/shard_map/ppermute | solution.py:865
  283.4 7.8 %collective-permute-start.6 = (bf16[16,22,16,384]{3,2,1,0:T(8,128)(2,1)}, bf16[16,22,16,384]{3,2,1,0:T(8,128)(2,1)}, u32[]{:S(2)}, u32[]{:S(2)}) collective-permute-start(bf16[16,22,16,384]{3,2,1,0:T(8,128)(2,1)} %shard_map.162), channel_id=1, source_target_pairs={{0,8},{8,0},{1,9},{9,1},{2,10},{10,2},{3,11},{11,3},{4,12},{12,4},... | collective-permute-start | bytes 12976136 | tf_op jit(solution)/shard_map/ppermute | solution.py:850
  288.7 13.0 %collective-permute-start.9 = (bf16[16,23,16,384]{3,2,1,0:T(8,128)(2,1)}, bf16[16,23,16,384]{3,2,1,0:T(8,128)(2,1)}, u32[]{:S(2)}, u32[]{:S(2)}) collective-permute-start(bf16[16,23,16,384]{3,2,1,0:T(8,128)(2,1)} %shard_map.164), channel_id=1, source_target_pairs={{0,8},{8,0},{1,9},{9,1},{2,10},{10,2},{3,11},{11,3},{4,12},{12,4},... | collective-permute-start | bytes 13565960 | tf_op jit(solution)/shard_map/ppermute | solution.py:850
  299.7 32.0 %collective-permute-start.7 = (bf16[4,22,16,384]{3,2,1,0:T(8,128)(2,1)}, bf16[4,22,16,384]{3,2,1,0:T(8,128)(2,1)}, u32[]{:S(2)}, u32[]{:S(2)}) collective-permute-start(bf16[4,22,16,384]{3,2,1,0:T(8,128)(2,1)} %get-tuple-element.96), channel_id=1, source_target_pairs={{0,16},{16,0},{1,17},{17,1},{2,18},{18,2},{3,19},{19,3},{4,20},{20... | collective-permute-start | bytes 3244040 | tf_op jit(solution)/shard_map/ppermute | solution.py:850
  301.2 30.5 %collective-permute-start.8 = (bf16[4,22,16,384]{3,2,1,0:T(8,128)(2,1)}, bf16[4,22,16,384]{3,2,1,0:T(8,128)(2,1)}, u32[]{:S(2)}, u32[]{:S(2)}) collective-permute-start(bf16[4,22,16,384]{3,2,1,0:T(8,128)(2,1)} %get-tuple-element.97), channel_id=1, source_target_pairs={{0,1},{1,0},{2,3},{3,2},{4,5},{5,4},{6,7},{7,6},{8,9},{9,8},{10,11... | collective-permute-start | bytes 3244040 | tf_op jit(solution)/shard_map/ppermute | solution.py:850
  311.3 7.5 %collective-permute-start.22 = (f32[160,384]{1,0:T(8,128)S(1)}, f32[160,384]{1,0:T(8,128)S(1)}, u32[]{:S(2)}, u32[]{:S(2)}) collective-permute-start(f32[160,384]{1,0:T(8,128)S(1)} %dynamic-slice_add_fusion), channel_id=1, source_target_pairs={{0,2},{2,0},{4,6},{6,4},{1,3},{3,1},{5,7},{7,5},{8,10},{10,8},{12,... | collective-permute-start | bytes 737288 | tf_op jit(solution)/shard_map/ppermute | solution.py:865
  318.9 12.7 %collective-permute-start.23 = (f32[160,384]{1,0:T(8,128)S(1)}, f32[160,384]{1,0:T(8,128)S(1)}, u32[]{:S(2)}, u32[]{:S(2)}) collective-permute-start(f32[160,384]{1,0:T(8,128)S(1)} %add.840), channel_id=1, source_target_pairs={{0,4},{2,6},{4,0},{6,2},{1,5},{3,7},{5,1},{7,3},{8,12},{10,14},{12... | collective-permute-start | bytes 737288 | tf_op jit(solution)/shard_map/ppermute | solution.py:865
  320.5 30.3 %collective-permute-start.15 = (bf16[4,23,16,384]{3,2,1,0:T(8,128)(2,1)}, bf16[4,23,16,384]{3,2,1,0:T(8,128)(2,1)S(1)}, u32[]{:S(2)}, u32[]{:S(2)}) collective-permute-start(bf16[4,23,16,384]{3,2,1,0:T(8,128)(2,1)} %copy-done.14), channel_id=1, source_target_pairs={{0,16},{16,0},{1,17},{17,1},{2,18},{18,2},{3,19},{19,3},{4,20},{20... | collective-permute-start | bytes 3391496 | tf_op jit(solution)/shard_map/ppermute | solution.py:850
  322.4 29.9 %collective-permute-start.18 = (bf16[4,23,16,384]{3,2,1,0:T(8,128)(2,1)}, bf16[4,23,16,384]{3,2,1,0:T(8,128)(2,1)S(1)}, u32[]{:S(2)}, u32[]{:S(2)}) collective-permute-start(bf16[4,23,16,384]{3,2,1,0:T(8,128)(2,1)} %copy-done.13), channel_id=1, source_target_pairs={{0,1},{1,0},{2,3},{3,2},{4,5},{5,4},{6,7},{7,6},{8,9},{9,8},{10,11... | collective-permute-start | bytes 3391496 | tf_op jit(solution)/shard_map/ppermute | solution.py:850
  335.2 36.3 %collective-permute-start.10 = (bf16[2,22,16,384]{3,2,1,0:T(8,128)(2,1)S(1)}, bf16[2,22,16,384]{3,2,1,0:T(8,128)(2,1)S(1)}, u32[]{:S(2)}, u32[]{:S(2)}) collective-permute-start(bf16[2,22,16,384]{3,2,1,0:T(8,128)(2,1)S(1)} %fusion.13), channel_id=1, source_target_pairs={{0,1},{1,0},{2,3},{3,2},{4,5},{5,4},{6,7},{7,6},{8,9},{9,8},{10,11... | collective-permute-start | bytes 1622024 | tf_op jit(solution)/shard_map/ppermute | solution.py:850
  336.8 33.0 %collective-permute-start.12 = (bf16[2,22,16,384]{3,2,1,0:T(8,128)(2,1)S(1)}, bf16[2,22,16,384]{3,2,1,0:T(8,128)(2,1)S(1)}, u32[]{:S(2)}, u32[]{:S(2)}) collective-permute-start(bf16[2,22,16,384]{3,2,1,0:T(8,128)(2,1)S(1)} %fusion.14), channel_id=1, source_target_pairs={{0,16},{16,0},{1,17},{17,1},{2,18},{18,2},{3,19},{19,3},{4,20},{20... | collective-permute-start | bytes 1622024 | tf_op jit(solution)/shard_map/ppermute | solution.py:850
  352.8 16.4 %collective-permute-start.24 = (f32[160,384]{1,0:T(8,128)S(1)}, f32[160,384]{1,0:T(8,128)S(1)}, u32[]{:S(2)}, u32[]{:S(2)}) collective-permute-start(f32[160,384]{1,0:T(8,128)S(1)} %add.841), channel_id=1, source_target_pairs={{0,1},{1,0},{2,3},{3,2},{4,5},{5,4},{6,7},{7,6},{8,9},{9,8},{10,11... | collective-permute-start | bytes 737288 | tf_op jit(solution)/shard_map/ppermute | solution.py:865
  354.7 25.7 %collective-permute-start.16 = (bf16[2,23,16,384]{3,2,1,0:T(8,128)(2,1)S(1)}, bf16[2,23,16,384]{3,2,1,0:T(8,128)(2,1)S(1)}, u32[]{:S(2)}, u32[]{:S(2)}) collective-permute-start(bf16[2,23,16,384]{3,2,1,0:T(8,128)(2,1)S(1)} %fusion.8), channel_id=1, source_target_pairs={{0,1},{1,0},{2,3},{3,2},{4,5},{5,4},{6,7},{7,6},{8,9},{9,8},{10,11... | collective-permute-start | bytes 1695752 | tf_op jit(solution)/shard_map/ppermute | solution.py:850
  355.4 24.1 %collective-permute-start.19 = (bf16[2,23,16,384]{3,2,1,0:T(8,128)(2,1)S(1)}, bf16[2,23,16,384]{3,2,1,0:T(8,128)(2,1)S(1)}, u32[]{:S(2)}, u32[]{:S(2)}) collective-permute-start(bf16[2,23,16,384]{3,2,1,0:T(8,128)(2,1)S(1)} %fusion.9), channel_id=1, source_target_pairs={{0,16},{16,0},{1,17},{17,1},{2,18},{18,2},{3,19},{19,3},{4,20},{20... | collective-permute-start | bytes 1695752 | tf_op jit(solution)/shard_map/ppermute | solution.py:850
  369.2 9.9 %collective-permute-start.25 = (f32[160,384]{1,0:T(8,128)S(1)}, f32[160,384]{1,0:T(8,128)S(1)}, u32[]{:S(2)}, u32[]{:S(2)}) collective-permute-start(f32[160,384]{1,0:T(8,128)S(1)} %add.842), channel_id=1, source_target_pairs={{0,16},{16,0},{1,17},{17,1},{2,18},{18,2},{3,19},{19,3},{4,20},{20... | collective-permute-start | bytes 737288 | tf_op jit(solution)/shard_map/ppermute | solution.py:865
  370.0 13.5 %collective-permute-start.14 = (bf16[22,16,384]{2,1,0:T(8,128)(2,1)S(1)}, bf16[22,16,384]{2,1,0:T(8,128)(2,1)S(1)}, u32[]{:S(2)}, u32[]{:S(2)}) collective-permute-start(bf16[22,16,384]{2,1,0:T(8,128)(2,1)S(1)} %get-tuple-element.125), channel_id=1, source_target_pairs={{0,6},{2,0},{4,2},{6,4},{1,7},{3,1},{5,3},{7,5},{8,14},{10,8},{12,... | collective-permute-start | bytes 811016 | tf_op jit(solution)/shard_map/ppermute | solution.py:850
  371.5 34.2 %collective-permute-start.13 = (bf16[22,16,384]{2,1,0:T(8,128)(2,1)S(1)}, bf16[22,16,384]{2,1,0:T(8,128)(2,1)S(1)}, u32[]{:S(2)}, u32[]{:S(2)}) collective-permute-start(bf16[22,16,384]{2,1,0:T(8,128)(2,1)S(1)} %get-tuple-element.124), channel_id=1, source_target_pairs={{0,4},{2,6},{4,0},{6,2},{1,5},{3,7},{5,1},{7,3},{8,12},{10,14},{12... | collective-permute-start | bytes 811016 | tf_op jit(solution)/shard_map/ppermute | solution.py:850
  379.1 26.6 %collective-permute-start.11 = (bf16[22,16,384]{2,1,0:T(8,128)(2,1)S(1)}, bf16[22,16,384]{2,1,0:T(8,128)(2,1)S(1)}, u32[]{:S(2)}, u32[]{:S(2)}) collective-permute-start(bf16[22,16,384]{2,1,0:T(8,128)(2,1)S(1)} %fusion.19), channel_id=1, source_target_pairs={{0,2},{2,4},{4,6},{6,0},{1,3},{3,5},{5,7},{7,1},{8,10},{10,12},{12... | collective-permute-start | bytes 811016 | tf_op jit(solution)/shard_map/ppermute | solution.py:850
  379.5 26.4 %collective-permute-start.26 = (f32[160,384]{1,0:T(8,128)S(1)}, f32[160,384]{1,0:T(8,128)S(1)}, u32[]{:S(2)}, u32[]{:S(2)}) collective-permute-start(f32[160,384]{1,0:T(8,128)S(1)} %add.843), channel_id=1, source_target_pairs={{0,8},{8,0},{1,9},{9,1},{2,10},{10,2},{3,11},{11,3},{4,12},{12,4},... | collective-permute-start | bytes 737288 | tf_op jit(solution)/shard_map/ppermute | solution.py:850
  380.3 34.1 %collective-permute-start.21 = (bf16[23,16,384]{2,1,0:T(8,128)(2,1)S(1)}, bf16[23,16,384]{2,1,0:T(8,128)(2,1)S(1)}, u32[]{:S(2)}, u32[]{:S(2)}) collective-permute-start(bf16[23,16,384]{2,1,0:T(8,128)(2,1)S(1)} %get-tuple-element.123), channel_id=1, source_target_pairs={{0,6},{2,0},{4,2},{6,4},{1,7},{3,1},{5,3},{7,5},{8,14},{10,8},{12,... | collective-permute-start | bytes 847880 | tf_op jit(solution)/shard_map/ppermute | solution.py:850
  383.6 34.2 %collective-permute-start.20 = (bf16[23,16,384]{2,1,0:T(8,128)(2,1)S(1)}, bf16[23,16,384]{2,1,0:T(8,128)(2,1)S(1)}, u32[]{:S(2)}, u32[]{:S(2)}) collective-permute-start(bf16[23,16,384]{2,1,0:T(8,128)(2,1)S(1)} %get-tuple-element.122), channel_id=1, source_target_pairs={{0,4},{2,6},{4,0},{6,2},{1,5},{3,7},{5,1},{7,3},{8,12},{10,14},{12... | collective-permute-start | bytes 847880 | tf_op jit(solution)/shard_map/ppermute | solution.py:850
  405.7 12.0 %collective-permute-start.17 = (bf16[23,16,384]{2,1,0:T(8,128)(2,1)S(1)}, bf16[23,16,384]{2,1,0:T(8,128)(2,1)S(1)}, u32[]{:S(2)}, u32[]{:S(2)}) collective-permute-start(bf16[23,16,384]{2,1,0:T(8,128)(2,1)S(1)} %fusion.18), channel_id=1, source_target_pairs={{0,2},{2,4},{4,6},{6,0},{1,3},{3,5},{5,7},{7,1},{8,10},{10,12},{12... | collective-permute-start | bytes 847880 | tf_op jit(solution)/shard_map/ppermute | solution.py:850
  (38 other events, 151.9 us)
Sparse Core Ops, SparseCore 0:
  12.5 121.8 all-gather.1
